TPU v7x, 32 devices: a whole 2x2x4 slice. The times are simulated.
32 devices in a mesh: rep: 1, ga: 32 (over z, y, x, core).
Axes of the slice: x: 2, y: 2, z: 4, core: 2. Of those that a mesh axis runs over, the one named last changes fastest.
Arguments:
- orbitals: float32 [8, 2, 128, 128, 128], P('rep', None, 'ga'), as said below
- plane_order: int32 [128], P('rep'), may hold values from 0 to 127, as said below
- potential: float32 [128, 128, 128], P('rep', 'ga'), may hold values from -1.5 to 0.5
- projectors: float32 [256, 8, 2, 8192], P(('rep', 'ga')), may hold values from -0.25 to 0.25
- slot_owner: int32 [256, 8], P(('rep', 'ga')), may hold values from 0 to 127
- strengths: float32 [32, 4], P('rep'), may hold values from 0.5 to 2
Outputs:
- residual: float32 [8, 2, 128, 128, 128], P('rep', None, 'ga')
- lagrange: float32 [2, 8, 8], P(None, 'rep')
Inputs may be any that keep to these rules, and one draw needn't show every extreme that they name: `plane_order`: A permutation: every frequency index appears at exactly one stored x-plane. `orbitals`: every band is the transform of a real field: its coefficient at frequencies (kx, ky, kz) is the complex conjugate of its coefficient at (-kx, -ky, -kz) modulo the lengths, where stored x-plane p has kx = plane_order[p].
All inputs are finite; a program needn't handle non-finite values.
Results may differ from a plain program's by a relative error of at most 0.011.
Values sent between devices are 32-bit elements; how exact they have to be, the bound alone decides.
No kernel may reach another device: no remote copies, remote signals or barrier semaphores. Data moves between devices by JAX's collectives and lax.ppermute only.
A program may use at most 128 MiB of HBM per device.

v0:
```python
import functools
import math

import jax
import jax.numpy as jnp
import numpy as np
from jax import lax
from jax.experimental import pallas as pl
from jax.experimental.pallas import tpu as pltpu
from jax.sharding import PartitionSpec as P

highest = lax.Precision.HIGHEST
f32 = jnp.float32
bf16 = jnp.bfloat16
vmem_limit = 48 * 1024 * 1024


def signed_index(values, length):
    return jnp.where(values < length // 2, values, values - length)


def dft(length, orient):
    index = np.arange(length)
    angles = (index[:, None] * index[None, :] % length) * (2.0 * math.pi / length)
    factor = 1.0 / math.sqrt(length)
    return np.cos(angles) * factor, orient * np.sin(angles) * factor


def left_table(length, orient, row_order=None, col_order=None):
    cosine, sine = dft(length, orient)
    if row_order is not None:
        cosine, sine = cosine[row_order], sine[row_order]
    if col_order is not None:
        cosine, sine = cosine[:, col_order], sine[:, col_order]
    return np.block([[cosine, -sine], [sine, cosine]])


def right_table(length, orient):
    cosine, sine = dft(length, orient)
    return np.block([[cosine, sine], [-sine, cosine]])


def split(values):
    high = values.astype(bf16)
    low = (values - high.astype(f32)).astype(bf16)
    return high, low


def split_outside(values):
    high = lax.reduce_precision(values, exponent_bits=8, mantissa_bits=7)
    return high.astype(bf16), (values - high).astype(bf16)


def const_parts(table):
    table = np.asarray(table, np.float32)
    high = table.astype(jnp.bfloat16)
    low = (table - high.astype(np.float32)).astype(jnp.bfloat16)
    return high, low


def left_const(table):
    high, low = const_parts(table)
    return jnp.asarray(np.concatenate([high, high, low], axis=1))


def right_const(table):
    high, low = const_parts(table)
    return jnp.asarray(np.concatenate([high, high, low], axis=0))


def dot_left(table, values):
    high, low = split(values)
    return jnp.dot(
        table, jnp.concatenate([high, low, high], axis=0), preferred_element_type=f32
    )


def dot_right(values, table):
    high, low = split(values)
    return jnp.dot(
        jnp.concatenate([high, low, high], axis=1), table, preferred_element_type=f32
    )


def to_rows_kernel(devices, rows, planes, psi, y_table, z_table, out):
    real = jnp.concatenate([psi[0, 0, p] - psi[1, 1, p] for p in range(planes)], axis=1)
    imag = jnp.concatenate([psi[0, 1, p] + psi[1, 0, p] for p in range(planes)], axis=1)
    span_y, span_z = psi.shape[3], psi.shape[4]
    along_y = dot_left(y_table[...], jnp.concatenate([real, imag], axis=0))
    flat = out.reshape(devices * 2 * planes * rows, span_z)
    for p in range(planes):
        cols = slice(p * span_z, (p + 1) * span_z)
        plane = jnp.concatenate([along_y[:span_y, cols], along_y[span_y:, cols]], axis=1)
        values = dot_right(plane, z_table[...])
        for part in range(2):
            for r in range(rows):
                start = (r * planes + p) * 2 + part
                flat[pl.ds(start, devices, stride=2 * planes * rows), :] = values[
                    r * devices : (r + 1) * devices, part * span_z : (part + 1) * span_z
                ]


def real_space_kernel(devices, rows, planes, recv, pot, inverse, forward, back, field):
    span_x = pot.shape[0]
    block = 2 * planes
    columns = [
        recv[:, r * block : (r + 1) * block, :].reshape(devices * block, recv.shape[2])
        for r in range(rows)
    ]
    spatial = dot_left(inverse[...], jnp.concatenate(columns, axis=1))
    for band in range(2):
        one = spatial[band * span_x : (band + 1) * span_x]
        field[band] = one
        spectral = dot_left(forward[...], one * pot[...])
        for r in range(rows):
            cols = spectral[:, r * recv.shape[2] : (r + 1) * recv.shape[2]]
            back[:, band, r * block : (r + 1) * block] = cols.reshape(devices, block, recv.shape[2])


def real_gram_kernel(bands, field, pot, out):
    pairs = [(a, b) for a in range(bands) for b in range(a, bands)]
    for weighted in range(2):

        def step(i, sums):
            rows = pl.ds(pl.multiple_of(i * 8, 8), 8)
            values = [field[a, rows, :] for a in range(bands)]
            other = [v * pot[rows, :] for v in values] if weighted else values
            result = []
            for (a, b), total in zip(pairs, sums):
                product = values[a] * other[b]
                lanes = product[:, :128]
                for c in range(128, product.shape[1], 128):
                    lanes = lanes + product[:, c : c + 128]
                result.append(total + lanes)
            return tuple(result)

        sums = lax.fori_loop(
            0, pot.shape[0] // 8, step, tuple(jnp.zeros((8, 128), f32) for _ in pairs)
        )
        for (a, b), total in zip(pairs, sums):
            line = jnp.sum(total, axis=0, keepdims=True)
            out[weighted, a, b : b + 1, :] = line
            out[weighted, b, a : a + 1, :] = line


def to_planes_kernel(devices, rows, planes, recv, base, y_table, z_table, out):
    span_y, span_z = base.shape[3], base.shape[4]
    flat = recv.reshape(devices * 2 * planes * rows, span_z)
    columns = []
    for p in range(planes):
        columns.append(
            jnp.concatenate(
                [
                    flat[pl.ds((r * planes + p) * 2 + part, devices, stride=2 * planes * rows), :]
                    for part in range(2)
                    for r in range(rows)
                ],
                axis=0,
            )
        )
    along_y = dot_left(y_table[...], jnp.concatenate(columns, axis=1))
    for p in range(planes):
        cols = slice(p * span_z, (p + 1) * span_z)
        plane = jnp.concatenate([along_y[:span_y, cols], along_y[span_y:, cols]], axis=1)
        values = dot_right(plane, z_table[...])
        for part in range(2):
            out[0, part, p] = base[0, part, p] + values[:, part * span_z : (part + 1) * span_z]


def block_rows_of(psi, beta, slots):
    bands, _, span, span_z = psi.shape
    psi_flat = psi.reshape(bands * 2 * span, span_z)
    psi_rows = [psi_flat[pl.ds(y, 2 * bands, stride=span), :] for y in range(span)]
    beta_rows = [
        jnp.concatenate(
            [beta[pl.ds(2 * y + part, slots, stride=2 * span), :] for part in range(2)], axis=0
        )
        for y in range(span)
    ]
    return psi_rows, beta_rows


def project_kernel(slots, psi, beta, kinetic, out):
    bands, _, span, span_z = psi.shape
    psi_rows, beta_rows = block_rows_of(psi, beta, slots)
    kin_rows = [psi_rows[y] * kinetic[y : y + 1, :] for y in range(span)]
    right = jnp.concatenate(split(jnp.concatenate(psi_rows, axis=1)), axis=0)
    left = jnp.concatenate(
        split(jnp.concatenate(beta_rows, axis=1)) + split(jnp.concatenate(kin_rows, axis=1)), axis=0
    )
    full = lax.dot_general(left, right, (((1,), (1,)), ((), ())), preferred_element_type=f32)
    width, height = 2 * bands, 2 * slots
    full = full[:, :width] + full[:, width:]
    out[0:height] = full[0:height] + full[height : 2 * height]
    rest = full[2 * height :]
    out[height:] = rest[0:width] + rest[width:]


def base_kernel(slots, psi, beta, kinetic, coefs, out):
    bands, _, span, span_z = psi.shape
    psi_rows, beta_rows = block_rows_of(psi, beta, slots)
    values = jnp.concatenate(
        [jnp.concatenate(psi_rows, axis=1), jnp.concatenate(beta_rows, axis=1)], axis=0
    )
    high, low = split(coefs[...])
    summed = dot_left(jnp.concatenate([high, high, low], axis=1), values)
    flat = out.reshape(bands * 2 * span, span_z)
    for y in range(span):
        flat[pl.ds(y, 2 * bands, stride=span), :] = (
            psi_rows[y] * kinetic[y : y + 1, :] + summed[:, y * span_z : (y + 1) * span_z]
        )


def whole(shape):
    return pl.BlockSpec(shape, lambda *_: (0,) * len(shape))


def subspace_solve(s_real, h_real, h_imag):
    factor = jnp.linalg.cholesky(s_real)
    solved = jax.scipy.linalg.cho_solve((factor, True), jnp.concatenate([h_real, h_imag], axis=1))
    order_size = s_real.shape[0]
    return (solved[:, :order_size], solved[:, order_size:])


def tdot(pattern, left, right):
    return jnp.einsum(pattern, left, right, precision=highest, preferred_element_type=jnp.float32)


def sum_over(values, devices):
    if devices & (devices - 1):
        return lax.psum(values, "ga")
    step = 1
    while step < devices:
        values = values + lax.ppermute(values, "ga", [(d, d ^ step) for d in range(devices)])
        step *= 2
    return values


def on_device(devices, orbitals, plane_order, potential, projectors, slot_owner, strengths):
    bands = orbitals.shape[0]
    planes = orbitals.shape[2]
    span_y = orbitals.shape[3]
    span_z = orbitals.shape[4]
    span_x = plane_order.shape[0]
    blocks, slots = slot_owner.shape
    owners = strengths.shape[0] * strengths.shape[1]
    rows = span_y // devices
    block_rows = 2 * planes * rows
    lanes = rows * span_z
    pairs = bands // 2
    block_span = projectors.shape[3] // span_z
    per_plane = span_y // block_span
    grid_x = jnp.arange(span_x, dtype=jnp.int32)
    grid_y = jnp.arange(span_y, dtype=jnp.int32)
    grid_z = jnp.arange(span_z, dtype=jnp.int32)
    params = pltpu.CompilerParams(vmem_limit_bytes=vmem_limit)

    def cost(flops, moved):
        return pl.CostEstimate(flops=flops, bytes_accessed=moved, transcendentals=0)

    row_major = (np.arange(devices)[None, :] * rows + np.arange(rows)[:, None]).reshape(-1)
    inv_y = left_const(left_table(span_y, 1.0, row_order=row_major))
    inv_z = right_const(right_table(span_z, 1.0))
    fwd_y = left_const(left_table(span_y, -1.0, col_order=row_major))
    fwd_z = right_const(right_table(span_z, -1.0))

    sent = pl.pallas_call(
        functools.partial(to_rows_kernel, devices, rows, planes),
        out_shape=jax.ShapeDtypeStruct((devices, pairs, block_rows, span_z), f32),
        grid=(pairs,),
        in_specs=[
            pl.BlockSpec((2, 2, planes, span_y, span_z), lambda j: (j, 0, 0, 0, 0)),
            whole(inv_y.shape),
            whole(inv_z.shape),
        ],
        out_specs=pl.BlockSpec((devices, None, block_rows, span_z), lambda j: (0, j, 0, 0)),
        compiler_params=params,
        cost_estimate=cost(4 * 10**9, 6 * 10**6),
        name="to_rows",
    )(orbitals, inv_y, inv_z)
    arrived = lax.all_to_all(sent, "ga", split_axis=0, concat_axis=0, tiled=True)

    phases = (plane_order[:, None] * grid_x[None, :]) % span_x
    angles = phases.astype(f32) * (2.0 * math.pi / span_x)
    factor = 1.0 / math.sqrt(span_x)
    cosine, sine = jnp.cos(angles) * factor, jnp.sin(angles) * factor
    fwd_x = jnp.stack([cosine, -sine], axis=1).reshape(2 * span_x, span_x)
    other = jnp.stack([sine, cosine], axis=1).reshape(2 * span_x, span_x)
    inv_x = jnp.concatenate([fwd_x.T, other.T], axis=0)
    high, low = split_outside(fwd_x)
    fwd_x = jnp.concatenate([high, high, low], axis=1)
    high, low = split_outside(inv_x)
    inv_x = jnp.concatenate([high, high, low], axis=1)
    pot = potential.reshape(span_x, lanes)

    local_order = lax.dynamic_slice_in_dim(plane_order, lax.axis_index("ga") * planes, planes)
    freq_x = signed_index(local_order, span_x).astype(f32) / span_x
    freq_y = signed_index(grid_y, span_y).astype(f32) / span_y
    freq_z = signed_index(grid_z, span_z).astype(f32) / span_z
    kinetic = 2.0 * (
        freq_x[:, None, None] ** 2 + freq_y[None, :, None] ** 2 + freq_z[None, None, :] ** 2
    )
    beta = projectors.reshape(blocks, slots, 2, block_span, span_z)
    beta = beta.transpose(0, 1, 3, 2, 4).reshape(blocks, slots * block_span * 2, span_z)
    block_specs = [
        pl.BlockSpec(
            (bands, 2, None, block_span, span_z),
            lambda g: (0, 0, g // per_plane, g % per_plane, 0),
        ),
        pl.BlockSpec((None, slots * block_span * 2, span_z), lambda g: (g, 0, 0)),
        pl.BlockSpec((None, block_span, span_z), lambda g: (g // per_plane, g % per_plane, 0)),
    ]
    products = pl.pallas_call(
        functools.partial(project_kernel, slots),
        out_shape=jax.ShapeDtypeStruct((blocks, 2 * slots + 2 * bands, 2 * bands), f32),
        grid=(blocks,),
        in_specs=block_specs,
        out_specs=pl.BlockSpec((None, 2 * slots + 2 * bands, 2 * bands), lambda g: (g, 0, 0)),
        compiler_params=params,
        cost_estimate=cost(8 * 10**9, 8 * 10**6),
        name="project",
    )(orbitals, beta, kinetic)
    with_real = products[:, :slots].reshape(blocks, slots, bands, 2)
    with_imag = products[:, slots : 2 * slots].reshape(blocks, slots, bands, 2)
    proj = jnp.concatenate(
        [
            with_real[..., 0] + with_imag[..., 1],
            with_real[..., 1] - with_imag[..., 0],
        ],
        axis=-1,
    )
    owned = (
        slot_owner[:, :, None] == jnp.arange(owners, dtype=jnp.int32)[None, None, :]
    ).astype(f32)
    proj = tdot("gsj,gsc->jc", owned, proj)
    kin = jnp.sum(products[:, 2 * slots :], axis=0).reshape(bands, 2, bands, 2)
    kin = kin[:, 0, :, 0] + kin[:, 1, :, 1]

    back, field = pl.pallas_call(
        functools.partial(real_space_kernel, devices, rows, planes),
        out_shape=(
            jax.ShapeDtypeStruct((devices, bands, block_rows, span_z), f32),
            jax.ShapeDtypeStruct((bands, span_x, lanes), f32),
        ),
        grid=(pairs,),
        in_specs=[
            pl.BlockSpec((devices, None, block_rows, span_z), lambda j: (0, j, 0, 0)),
            whole(pot.shape),
            whole(inv_x.shape),
            whole(fwd_x.shape),
        ],
        out_specs=(
            pl.BlockSpec((devices, 2, block_rows, span_z), lambda j: (0, j, 0, 0)),
            pl.BlockSpec((2, span_x, lanes), lambda j: (j, 0, 0)),
        ),
        compiler_params=params,
        cost_estimate=cost(4 * 10**9, 8 * 10**6),
        name="real_space",
    )(arrived, pot, inv_x, fwd_x)
    returned = lax.all_to_all(back, "ga", split_axis=0, concat_axis=0, tiled=True)

    grams = pl.pallas_call(
        functools.partial(real_gram_kernel, bands),
        out_shape=jax.ShapeDtypeStruct((2, bands, bands, 128), f32),
        compiler_params=params,
        cost_estimate=cost(10**7, 2 * 10**6),
        name="real_gram",
    )(field, pot)
    grams = jnp.sum(grams, axis=-1)
    own = jnp.concatenate([proj, jnp.concatenate([grams[0], grams[1] + kin], axis=1)], axis=0)
    total = sum_over(own, devices)
    proj, s_real, h_real = total[:owners], total[owners:, :bands], total[owners:, bands:]
    weighted = strengths.reshape(-1)[:, None] * proj
    p_real, p_imag = proj[:, :bands], proj[:, bands:]
    w_real, w_imag = weighted[:, :bands], weighted[:, bands:]
    h_real = h_real + tdot("ja,jb->ab", p_real, w_real) + tdot("ja,jb->ab", p_imag, w_imag)
    h_imag = tdot("ja,jb->ab", p_real, w_imag) - tdot("ja,jb->ab", p_imag, w_real)
    m_real, m_imag = subspace_solve(s_real, h_real, h_imag)

    coefs = tdot("gsj,jc->gcs", owned, weighted)
    c_real, c_imag = coefs[:, :bands], coefs[:, bands:]
    from_beta = jnp.stack(
        [
            jnp.concatenate([c_real, -c_imag], axis=2),
            jnp.concatenate([c_imag, c_real], axis=2),
        ],
        axis=2,
    ).reshape(blocks, 2 * bands, 2 * slots)
    from_psi = jnp.stack(
        [
            jnp.stack([-m_real.T, m_imag.T], axis=-1),
            jnp.stack([-m_imag.T, -m_real.T], axis=-1),
        ],
        axis=1,
    ).reshape(1, 2 * bands, 2 * bands)
    coefs = jnp.concatenate(
        [jnp.broadcast_to(from_psi, (blocks, 2 * bands, 2 * bands)), from_beta], axis=2
    )
    base = pl.pallas_call(
        functools.partial(base_kernel, slots),
        out_shape=jax.ShapeDtypeStruct(orbitals.shape, f32),
        grid=(blocks,),
        in_specs=block_specs
        + [pl.BlockSpec((None, 2 * bands, 2 * bands + 2 * slots), lambda g: (g, 0, 0))],
        out_specs=block_specs[0],
        compiler_params=params,
        cost_estimate=cost(8 * 10**9, 12 * 10**6),
        name="base",
    )(orbitals, beta, kinetic, coefs)

    one_band = pl.BlockSpec((1, 2, planes, span_y, span_z), lambda b: (b, 0, 0, 0, 0))
    residual = pl.pallas_call(
        functools.partial(to_planes_kernel, devices, rows, planes),
        out_shape=jax.ShapeDtypeStruct(orbitals.shape, f32),
        grid=(bands,),
        in_specs=[
            pl.BlockSpec((devices, None, block_rows, span_z), lambda b: (0, b, 0, 0)),
            one_band,
            whole(fwd_y.shape),
            whole(fwd_z.shape),
        ],
        out_specs=one_band,
        compiler_params=params,
        cost_estimate=cost(8 * 10**9, 12 * 10**6),
        name="to_planes",
    )(returned, base, fwd_y, fwd_z)
    return (residual, jnp.stack([m_real, m_imag]))


def solution(mesh):
    return jax.shard_map(
        functools.partial(on_device, mesh.shape["ga"]),
        mesh=mesh,
        in_specs=(
            P("rep", None, "ga", None, None),
            P("rep"),
            P("rep", "ga", None),
            P(("rep", "ga"), None, None, None),
            P(("rep", "ga"), None),
            P("rep", None),
        ),
        out_specs=(P("rep", None, "ga", None, None), P(None, "rep", None)),
        check_vma=False,
    )
```

profile of v0, /device:TPU:1, one launch (start us, length us, event | category | flops | bytes accessed | tf_op | source)
XLA Modules:
  0.0 199.6 jit_solution(10907055148012278969)
XLA Ops:
  0.6 1.0 copy-done.6
  1.6 1.0 copy-done.7
  2.6 5.3 %to_rows.1 = f32[32,4,32,128]{3,2,1,0:T(8,128)S(1)} custom-call(f32[8,2,4,128,128]{4,3,2,1,0:T(8,128)} %psi.5, bf16[256,768]{1,0:T(8,128)(2,1)S(1)} %copy-done.7, bf16[768,256]{1,0:T(8,128)(2,1)S(1)} %copy-done.6), custom_call_target="tpu_custom_call" | custom-call | flops 4000000000 | bytes 6000000 | tf_op jit(solution)/shard_map/to_rows/pallas_call | solution.py:267
  8.0 1.3 copy-done.2
  9.3 7.1 %all-to-all-start = ((f32[32,4,32,128]{3,2,1,0:T(8,128)}), f32[32,4,32,128]{3,2,1,0:T(8,128)S(1)}, u32[]{:S(2)}, u32[]{:S(2)}) async-start(f32[32,4,32,128]{3,2,1,0:T(8,128)} %copy-done.2), calls=%async_computation | async-start | bytes 4194304 | tf_op jit(solution)/shard_map/all_to_all | solution.py:281
  16.4 0.3 fusion.11
  16.8 0.1 copy.70
  16.9 0.1 copy.71
  17.1 0.2 copy.72.inverse
  17.2 1.0 copy.106
  18.3 46.4 %all-to-all-done.recv = f32[32,4,32,128]{3,2,1,0:T(8,128)S(1)} async-done(((f32[32,4,32,128]{3,2,1,0:T(8,128)}), f32[32,4,32,128]{3,2,1,0:T(8,128)S(1)}, u32[]{:S(2)}, u32[]{:S(2)}) %all-to-all-start) | async-done | bytes 2097184 | tf_op jit(solution)/shard_map/all_to_all | solution.py:281
  64.7 1.3 copy-done
  66.0 1.6 copy-done.1
  67.6 4.4 %real_space.1 = (f32[32,8,32,128]{3,2,1,0:T(8,128)}, f32[8,128,512]{2,1,0:T(8,128)S(1)}) custom-call(f32[32,4,32,128]{3,2,1,0:T(8,128)S(1)} %copy-done.1, f32[128,512]{1,0:T(8,128)S(1)} %bitcast.72, bf16[256,768]{1,0:T(8,128)(2,1)S(1)} %copy.72.inverse, bf16[256,384]{1,0:T(8,128)(2,1)S(1)} %pad_maximum_fusion.2.forward), custom_call_target="tpu_custom_call" | custom-call | flops 4000000000 | bytes 8000000 | tf_op jit(solution)/shard_map/real_space/pallas_call | solution.py:339
  72.0 4.7 %all-to-all-start.1 = ((f32[32,8,32,128]{3,2,1,0:T(8,128)}), f32[32,8,32,128]{3,2,1,0:T(8,128)}, u32[]{:S(2)}, u32[]{:S(2)}) async-start(f32[32,8,32,128]{3,2,1,0:T(8,128)} %get-tuple-element.4), calls=%async_computation.1 | async-start | bytes 8388608 | tf_op jit(solution)/shard_map/all_to_all | solution.py:360
  76.9 0.1 add_multiply_fusion.kinetic
  77.0 2.2 %copy-done.3 = f32[8,2,4,128,128]{4,3,2,1,0:T(8,128)S(1)} copy-done((f32[8,2,4,128,128]{4,3,2,1,0:T(8,128)S(1)}, f32[8,2,4,128,128]{4,3,2,1,0:T(8,128)}, u32[]{:S(2)}) %copy-start.3) | copy-done | bytes 4194328
  79.2 8.8 %project.1 = f32[8,32,16]{2,1,0:T(8,128)S(1)} custom-call(f32[8,2,4,128,128]{4,3,2,1,0:T(8,128)S(1)} %copy-done.3, f32[8,1024,128]{2,1,0:T(8,128)} %bitcast.84, f32[4,128,128]{2,1,0:T(8,128)S(1)} %add_multiply_fusion.kinetic), custom_call_target="tpu_custom_call" | custom-call | flops 8000000000 | bytes 8000000 | tf_op jit(solution)/shard_map/project/pallas_call | solution.py:313
  88.5 0.1 copy.99
  88.9 0.3 convolution_bitcast_fusion.1
  89.2 1.8 real_gram.1
  91.2 0.4 collective-permute-start
  91.6 0.9 collective-permute-done
  92.5 1.4 collective-permute-start.1
  93.9 9.8 %collective-permute-done.1 = f32[136,16]{0,1:T(8,128)S(1)} collective-permute-done((f32[136,16]{0,1:T(8,128)S(1)}, f32[136,16]{0,1:T(8,128)S(1)}, u32[]{:S(2)}, u32[]{:S(2)}) %collective-permute-start.1) | collective-permute-done | bytes 8736 | tf_op jit(solution)/shard_map/ppermute | solution.py:234
  103.6 1.4 collective-permute-start.2
  105.1 4.4 %collective-permute-done.2 = f32[136,16]{0,1:T(8,128)S(1)} collective-permute-done((f32[136,16]{0,1:T(8,128)S(1)}, f32[136,16]{0,1:T(8,128)S(1)}, u32[]{:S(2)}, u32[]{:S(2)}) %collective-permute-start.2) | collective-permute-done | bytes 8736 | tf_op jit(solution)/shard_map/ppermute | solution.py:234
  109.5 36.4 %collective-permute-done.3 = f32[136,16]{0,1:T(8,128)S(1)} collective-permute-done((f32[136,16]{0,1:T(8,128)S(1)}, f32[136,16]{0,1:T(8,128)S(1)}, u32[]{:S(2)}, u32[]{:S(2)}) %collective-permute-start.3) | collective-permute-done | bytes 8736 | tf_op jit(solution)/shard_map/ppermute | solution.py:234
  145.9 3.5 %collective-permute-start.4 = (f32[136,16]{0,1:T(8,128)S(1)}, f32[136,16]{0,1:T(8,128)S(1)}, u32[]{:S(2)}, u32[]{:S(2)}) collective-permute-start(f32[136,16]{0,1:T(8,128)S(1)} %add.132), channel_id=1, source_target_pairs={{0,16},{1,17},{2,18},{3,19},{4,20},{5,21},{6,22},{7,23},{8,24},{9,... | collective-permute-start | bytes 26120 | tf_op jit(solution)/shard_map/ppermute | solution.py:234
  149.4 0.1 mul.102
  149.5 21.2 %collective-permute-done.4 = f32[136,16]{0,1:T(8,128)S(1)} collective-permute-done((f32[136,16]{0,1:T(8,128)S(1)}, f32[136,16]{0,1:T(8,128)S(1)}, u32[]{:S(2)}, u32[]{:S(2)}) %collective-permute-start.4) | collective-permute-done | bytes 8736 | tf_op jit(solution)/shard_map/ppermute | solution.py:234
  170.8 0.7 cholesky.16
  171.6 0.6 compare_reduce_fusion
  172.2 0.6 fusion.19
  172.9 0.6 custom-call.10
  173.5 0.1 fusion.30
  173.6 0.1 fusion.34
  173.8 0.1 convolution_subtract_fusion
  173.9 0.1 fusion.20
  174.0 0.2 fusion.14
  174.2 0.1 fusion.22
  174.8 0.2 copy.93
  175.0 0.2 convolution_bitcast_fusion
  175.4 0.1 copy.94
  175.5 0.6 pad_maximum_fusion.8
  176.2 10.0 %base.1 = f32[8,2,4,128,128]{4,3,2,1,0:T(8,128)S(1)} custom-call(f32[8,2,4,128,128]{4,3,2,1,0:T(8,128)} %psi.5, f32[8,1024,128]{2,1,0:T(8,128)} %bitcast.85, f32[4,128,128]{2,1,0:T(8,128)S(1)} %add_multiply_fusion.kinetic, f32[8,16,32]{2,1,0:T(8,128)S(1)} %pad_maximum_fusion.6.coefs), custom_call_target="tpu_custom_call" | custom-call | flops 8000000000 | bytes 12000000 | tf_op jit(solution)/shard_map/base/pallas_call | solution.py:399
  186.2 2.0 copy-done.8
  188.2 11.4 %to_planes.1 = f32[8,2,4,128,128]{4,3,2,1,0:T(8,128)} custom-call(f32[32,8,32,128]{3,2,1,0:T(8,128)} %all-to-all-done.1.recv, f32[8,2,4,128,128]{4,3,2,1,0:T(8,128)} %copy-done.8, bf16[256,768]{1,0:T(8,128)(2,1)S(1)} %copy-done.5, bf16[768,256]{1,0:T(8,128)(2,1)S(1)} %copy-done.4), custom_call_target="tpu_custom_call" | custom-call | flops 8000000000 | bytes 12000000 | tf_op jit(solution)/shard_map/to_planes/pallas_call | solution.py:412
  (70 shorter events, 2.2 us)
Async XLA Ops:
  0.6 1.0 copy-start.6
  1.6 1.0 copy-start.7
  7.9 1.3 copy-start.2
  9.3 7.1 %copy-start.10 = (s32[128]{0:T(128)S(1)}, s32[128]{0:T(128)}, u32[]{:S(2)}) copy-start(s32[128]{0:T(128)} %param.11) | copy-start | bytes 1540
  9.3 55.4 %all-to-all-start = ((f32[32,4,32,128]{3,2,1,0:T(8,128)}), f32[32,4,32,128]{3,2,1,0:T(8,128)S(1)}, u32[]{:S(2)}, u32[]{:S(2)}) async-start(f32[32,4,32,128]{3,2,1,0:T(8,128)} %copy-done.2), calls=%async_computation | async-start | bytes 4194304 | tf_op jit(solution)/shard_map/all_to_all | solution.py:281
  64.7 1.3 copy-start
  66.0 1.6 copy-start.1
  72.0 116.2 %all-to-all-start.1 = ((f32[32,8,32,128]{3,2,1,0:T(8,128)}), f32[32,8,32,128]{3,2,1,0:T(8,128)}, u32[]{:S(2)}, u32[]{:S(2)}) async-start(f32[32,8,32,128]{3,2,1,0:T(8,128)} %get-tuple-element.4), calls=%async_computation.1 | async-start | bytes 8388608 | tf_op jit(solution)/shard_map/all_to_all | solution.py:360
  77.0 2.2 %copy-start.3 = (f32[8,2,4,128,128]{4,3,2,1,0:T(8,128)S(1)}, f32[8,2,4,128,128]{4,3,2,1,0:T(8,128)}, u32[]{:S(2)}) copy-start(f32[8,2,4,128,128]{4,3,2,1,0:T(8,128)} %psi.5) | copy-start | bytes 12582916
  79.2 9.7 %copy-start.11 = (s32[8,8]{1,0:T(8,128)S(1)}, s32[8,8]{1,0:T(8,128)}, u32[]{:S(2)}) copy-start(s32[8,8]{1,0:T(8,128)} %param.14) | copy-start | bytes 772
  88.0 61.3 %copy-start.9 = (f32[32,4]{0,1:T(4,128)S(1)}, f32[32,4]{0,1:T(4,128)}, u32[]{:S(2)}) copy-start(f32[32,4]{0,1:T(4,128)} %param.15) | copy-start | bytes 1540
  91.2 1.2 collective-permute-start
  92.5 11.2 %collective-permute-start.1 = (f32[136,16]{0,1:T(8,128)S(1)}, f32[136,16]{0,1:T(8,128)S(1)}, u32[]{:S(2)}, u32[]{:S(2)}) collective-permute-start(f32[136,16]{0,1:T(8,128)S(1)} %fusion.47), channel_id=1, source_target_pairs={{0,2},{1,3},{2,0},{3,1},{4,6},{5,7},{6,4},{7,5},{8,10},{9,11},{10,... | collective-permute-start | bytes 26120 | tf_op jit(solution)/shard_map/ppermute | solution.py:234
  103.6 5.8 %collective-permute-start.2 = (f32[136,16]{0,1:T(8,128)S(1)}, f32[136,16]{0,1:T(8,128)S(1)}, u32[]{:S(2)}, u32[]{:S(2)}) collective-permute-start(f32[136,16]{0,1:T(8,128)S(1)} %add.130), channel_id=1, source_target_pairs={{0,4},{1,5},{2,6},{3,7},{4,0},{5,1},{6,2},{7,3},{8,12},{9,13},{10,... | collective-permute-start | bytes 26120 | tf_op jit(solution)/shard_map/ppermute | solution.py:234
  109.5 36.4 %collective-permute-start.3 = (f32[136,16]{0,1:T(8,128)S(1)}, f32[136,16]{0,1:T(8,128)S(1)}, u32[]{:S(2)}, u32[]{:S(2)}) collective-permute-start(f32[136,16]{0,1:T(8,128)S(1)} %add.131), channel_id=1, source_target_pairs={{0,8},{1,9},{2,10},{3,11},{4,12},{5,13},{6,14},{7,15},{8,0},{9,1},... | collective-permute-start | bytes 26120 | tf_op jit(solution)/shard_map/ppermute | solution.py:234
  145.9 24.8 %collective-permute-start.4 = (f32[136,16]{0,1:T(8,128)S(1)}, f32[136,16]{0,1:T(8,128)S(1)}, u32[]{:S(2)}, u32[]{:S(2)}) collective-permute-start(f32[136,16]{0,1:T(8,128)S(1)} %add.132), channel_id=1, source_target_pairs={{0,16},{1,17},{2,18},{3,19},{4,20},{5,21},{6,22},{7,23},{8,24},{9,... | collective-permute-start | bytes 26120 | tf_op jit(solution)/shard_map/ppermute | solution.py:234
  176.2 12.0 %copy-start.4 = (bf16[768,256]{1,0:T(8,128)(2,1)S(1)}, bf16[768,256]{1,0:T(8,128)(2,1)}, u32[]{:S(2)}) copy-start(bf16[768,256]{1,0:T(8,128)(2,1)} %constant.102.clone.z_table) | copy-start | bytes 1179652
  176.2 12.0 %copy-start.5 = (bf16[256,768]{1,0:T(8,128)(2,1)S(1)}, bf16[256,768]{1,0:T(8,128)(2,1)}, u32[]{:S(2)}) copy-start(bf16[256,768]{1,0:T(8,128)(2,1)} %constant.101.clone.y_table) | copy-start | bytes 1179652
  186.2 2.0 %copy-start.8 = (f32[8,2,4,128,128]{4,3,2,1,0:T(8,128)}, f32[8,2,4,128,128]{4,3,2,1,0:T(8,128)S(1)}, u32[]{:S(2)}) copy-start(f32[8,2,4,128,128]{4,3,2,1,0:T(8,128)S(1)} %base.1) | copy-start | bytes 12582916
where the time goes:
time: 201 us; the launch traced here: 200 us
  waiting for transfers between devices  119 us (59%)
  Pallas kernels  41.7 us (21%)
  starting transfers between devices  18.4 us (9%)
  local copies, waits for them, and re-layouts  13.5 us (7%)
  other arithmetic  4.63 us (2%)
    ppermute x5, waiting for transfers between devices, sum_over(): lax.ppermute(values, 'ga', [(d, d ^ step) for d in range(devices)])  72.6 us
    all_to_all x1, waiting for transfers between devices, on_device(): lax.all_to_all(sent, 'ga', split_axis=0, concat_axis=0, tiled=True)  46.4 us
    unnamed x30, local copies, waits for them, and re-layouts  11.8 us
    pallas_call x1, Pallas kernels, on_device(): pl.pallas_call(functools.partial(to_planes_kernel, devices, rows, planes)...  11.4 us
    pallas_call x1, Pallas kernels, on_device(): pl.pallas_call(functools.partial(base_kernel, slots), out_shape=jax.Shape...  9.98 us
    pallas_call x1, Pallas kernels, on_device(): pl.pallas_call(functools.partial(project_kernel, slots), out_shape=jax.Sh...  8.81 us
    all_to_all x1, starting transfers between devices, on_device(): lax.all_to_all(sent, 'ga', split_axis=0, concat_axis=0, tiled=True)  7.1 us
    ppermute x5, starting transfers between devices, sum_over(): lax.ppermute(values, 'ga', [(d, d ^ step) for d in range(devices)])  6.66 us
  transfers between devices with their start and end apart: 7, of which 6 were waited for; matrix products, arithmetic and copies ran while one was open for 5% of the time, Pallas kernels for 10%

commit v1 on v0

--- a/solution.py
+++ b/solution.py
@@ -100,11 +100,14 @@
                 ]
 
 
-def real_space_kernel(devices, rows, planes, recv, pot, inverse, forward, back, field):
+def real_space_kernel(devices, rows, planes, recv, pot, inverse, forward, _, field, *rest):
+    back, staged = rest[:-1], rest[-1]
     span_x = pot.shape[0]
+    span_z = recv.shape[2]
     block = 2 * planes
+    size = block * rows
     columns = [
-        recv[:, r * block : (r + 1) * block, :].reshape(devices * block, recv.shape[2])
+        recv[:, r * block : (r + 1) * block, :].reshape(devices * block, span_z)
         for r in range(rows)
     ]
     spatial = dot_left(inverse[...], jnp.concatenate(columns, axis=1))
@@ -112,9 +115,15 @@
         one = spatial[band * span_x : (band + 1) * span_x]
         field[band] = one
         spectral = dot_left(forward[...], one * pot[...])
-        for r in range(rows):
-            cols = spectral[:, r * recv.shape[2] : (r + 1) * recv.shape[2]]
-            back[:, band, r * block : (r + 1) * block] = cols.reshape(devices, block, recv.shape[2])
+        for part in range(2):
+            for p in range(planes):
+                first = (part * planes + p) * devices
+                for r in range(rows):
+                    staged[band, pl.ds((p * rows + r) * 2 + part, devices, stride=size), :] = (
+                        spectral[first : first + devices, r * span_z : (r + 1) * span_z]
+                    )
+        for k in range(devices):
+            back[k][band] = staged[band, k * size : (k + 1) * size, :]
 
 
 def real_gram_kernel(bands, field, pot, out):
@@ -143,21 +152,13 @@
             out[weighted, b, a : a + 1, :] = line
 
 
-def to_planes_kernel(devices, rows, planes, recv, base, y_table, z_table, out):
+def to_planes_kernel(rows, planes, *refs):
+    recv, (base, y_table, z_table, out) = refs[:-4], refs[-4:]
     span_y, span_z = base.shape[3], base.shape[4]
-    flat = recv.reshape(devices * 2 * planes * rows, span_z)
     columns = []
     for p in range(planes):
-        columns.append(
-            jnp.concatenate(
-                [
-                    flat[pl.ds((r * planes + p) * 2 + part, devices, stride=2 * planes * rows), :]
-                    for part in range(2)
-                    for r in range(rows)
-                ],
-                axis=0,
-            )
-        )
+        part_rows = slice(2 * rows * p, 2 * rows * (p + 1))
+        columns.append(jnp.concatenate([one[part_rows, :] for one in recv], axis=0))
     along_y = dot_left(y_table[...], jnp.concatenate(columns, axis=1))
     for p in range(planes):
         cols = slice(p * span_z, (p + 1) * span_z)
@@ -226,13 +227,17 @@
     return jnp.einsum(pattern, left, right, precision=highest, preferred_element_type=jnp.float32)
 
 
+def partner(values, devices, k):
+    return lax.ppermute(values, "ga", [(d, d ^ k) for d in range(devices)])
+
+
 def sum_over(values, devices):
-    if devices & (devices - 1):
-        return lax.psum(values, "ga")
-    step = 1
-    while step < devices:
-        values = values + lax.ppermute(values, "ga", [(d, d ^ step) for d in range(devices)])
-        step *= 2
+    step = devices // 4
+    others = [partner(values, devices, k * step) for k in (1, 2, 3)]
+    values = (values + others[0]) + (others[1] + others[2])
+    while step > 1:
+        step //= 2
+        values = values + partner(values, devices, step)
     return values
 
 
@@ -261,7 +266,17 @@
     row_major = (np.arange(devices)[None, :] * rows + np.arange(rows)[:, None]).reshape(-1)
     inv_y = left_const(left_table(span_y, 1.0, row_order=row_major))
     inv_z = right_const(right_table(span_z, 1.0))
-    fwd_y = left_const(left_table(span_y, -1.0, col_order=row_major))
+    mine = lax.axis_index("ga")
+    source = np.arange(2 * span_y) // (2 * rows)
+    inner = np.arange(2 * span_y) % (2 * rows)
+    columns = (inner % 2) * span_y + source * rows + inner // 2
+    fwd_y = left_table(span_y, -1.0)[:, columns]
+    fwd_y = jnp.asarray(np.concatenate(const_parts(fwd_y), axis=0))
+    swap = jnp.arange(2 * span_y, dtype=jnp.int32)
+    swap = (swap[:, None] == (swap[None, :] ^ (mine * 2 * rows))).astype(bf16)
+    fwd_y = jnp.dot(fwd_y, swap, preferred_element_type=f32).astype(bf16)
+    high, low = fwd_y[: 2 * span_y], fwd_y[2 * span_y :]
+    fwd_y = jnp.concatenate([high, high, low], axis=1)
     fwd_z = right_const(right_table(span_z, -1.0))
 
     sent = pl.pallas_call(
@@ -280,13 +295,24 @@
     )(orbitals, inv_y, inv_z)
     arrived = lax.all_to_all(sent, "ga", split_axis=0, concat_axis=0, tiled=True)
 
-    phases = (plane_order[:, None] * grid_x[None, :]) % span_x
-    angles = phases.astype(f32) * (2.0 * math.pi / span_x)
-    factor = 1.0 / math.sqrt(span_x)
-    cosine, sine = jnp.cos(angles) * factor, jnp.sin(angles) * factor
-    fwd_x = jnp.stack([cosine, -sine], axis=1).reshape(2 * span_x, span_x)
-    other = jnp.stack([sine, cosine], axis=1).reshape(2 * span_x, span_x)
-    inv_x = jnp.concatenate([fwd_x.T, other.T], axis=0)
+    def along_x(order):
+        phases = (order[:, None] * grid_x[None, :]) % span_x
+        angles = phases.astype(f32) * (2.0 * math.pi / span_x)
+        factor = 1.0 / math.sqrt(span_x)
+        return jnp.cos(angles) * factor, jnp.sin(angles) * factor
+
+    members = jnp.arange(devices, dtype=jnp.int32) ^ mine
+    partner_order = jnp.take(plane_order.reshape(devices, planes), members, axis=0).T.reshape(-1)
+    cosine, sine = along_x(partner_order)
+    fwd_x = jnp.concatenate([cosine, -sine], axis=0)
+    cosine, sine = along_x(plane_order)
+    inv_x = jnp.concatenate(
+        [
+            jnp.stack([cosine, -sine], axis=1).reshape(2 * span_x, span_x).T,
+            jnp.stack([sine, cosine], axis=1).reshape(2 * span_x, span_x).T,
+        ],
+        axis=0,
+    )
     high, low = split_outside(fwd_x)
     fwd_x = jnp.concatenate([high, high, low], axis=1)
     high, low = split_outside(inv_x)
@@ -336,28 +362,27 @@
     kin = jnp.sum(products[:, 2 * slots :], axis=0).reshape(bands, 2, bands, 2)
     kin = kin[:, 0, :, 0] + kin[:, 1, :, 1]
 
-    back, field = pl.pallas_call(
+    field, *back = pl.pallas_call(
         functools.partial(real_space_kernel, devices, rows, planes),
-        out_shape=(
-            jax.ShapeDtypeStruct((devices, bands, block_rows, span_z), f32),
-            jax.ShapeDtypeStruct((bands, span_x, lanes), f32),
-        ),
+        out_shape=[jax.ShapeDtypeStruct((bands, span_x, lanes), f32)]
+        + [jax.ShapeDtypeStruct((bands, block_rows, span_z), f32)] * devices,
         grid=(pairs,),
         in_specs=[
             pl.BlockSpec((devices, None, block_rows, span_z), lambda j: (0, j, 0, 0)),
             whole(pot.shape),
             whole(inv_x.shape),
             whole(fwd_x.shape),
-        ],
-        out_specs=(
-            pl.BlockSpec((devices, 2, block_rows, span_z), lambda j: (0, j, 0, 0)),
-            pl.BlockSpec((2, span_x, lanes), lambda j: (j, 0, 0)),
-        ),
+            whole(proj.shape),
+        ],
+        out_specs=[pl.BlockSpec((2, span_x, lanes), lambda j: (j, 0, 0))]
+        + [pl.BlockSpec((2, block_rows, span_z), lambda j: (j, 0, 0))] * devices,
+        scratch_shapes=[pltpu.VMEM((2, devices * block_rows, span_z), f32)],
         compiler_params=params,
         cost_estimate=cost(4 * 10**9, 8 * 10**6),
         name="real_space",
-    )(arrived, pot, inv_x, fwd_x)
-    returned = lax.all_to_all(back, "ga", split_axis=0, concat_axis=0, tiled=True)
+    )(arrived, pot, inv_x, fwd_x, proj)
+    returned = {k: partner(back[k], devices, k) for k in range(devices - 1, 0, -1)}
+    returned = [back[0]] + [returned[k] for k in range(1, devices)]
 
     grams = pl.pallas_call(
         functools.partial(real_gram_kernel, bands),
@@ -410,11 +435,11 @@
 
     one_band = pl.BlockSpec((1, 2, planes, span_y, span_z), lambda b: (b, 0, 0, 0, 0))
     residual = pl.pallas_call(
-        functools.partial(to_planes_kernel, devices, rows, planes),
+        functools.partial(to_planes_kernel, rows, planes),
         out_shape=jax.ShapeDtypeStruct(orbitals.shape, f32),
         grid=(bands,),
-        in_specs=[
-            pl.BlockSpec((devices, None, block_rows, span_z), lambda b: (0, b, 0, 0)),
+        in_specs=[pl.BlockSpec((None, block_rows, span_z), lambda b: (b, 0, 0))] * devices
+        + [
             one_band,
             whole(fwd_y.shape),
             whole(fwd_z.shape),
@@ -423,7 +448,7 @@
         compiler_params=params,
         cost_estimate=cost(8 * 10**9, 12 * 10**6),
         name="to_planes",
-    )(returned, base, fwd_y, fwd_z)
+    )(*returned, base, fwd_y, fwd_z)
     return (residual, jnp.stack([m_real, m_imag]))
 
 

time: 201 us -> 234 us (1.16)
  the two profiles are of different devices: /device:TPU:1 before, /device:TPU:9 now
where the time goes in v1:
time: 234 us; the launch traced here: 233 us
  starting transfers between devices  77.4 us (33%)
  waiting for transfers between devices  67.6 us (29%)
  Pallas kernels  43.3 us (19%)
  local copies, waits for them, and re-layouts  31.4 us (13%)
  other arithmetic  8.52 us (4%)
  matrix products  3.19 us (1%)
    ppermute x37, starting transfers between devices, partner(): return lax.ppermute(values, 'ga', [(d, d ^ k) for d in range(devices)])  71 us
    ppermute x37, waiting for transfers between devices, partner(): return lax.ppermute(values, 'ga', [(d, d ^ k) for d in range(devices)])  35.4 us
    all_to_all x1, waiting for transfers between devices, on_device(): lax.all_to_all(sent, 'ga', split_axis=0, concat_axis=0, tiled=True)  32.2 us
    unnamed x118, local copies, waits for them, and re-layouts  27.9 us
    pallas_call x1, Pallas kernels, on_device(): pl.pallas_call(functools.partial(base_kernel, slots), out_shape=jax.Shape...  9.88 us
    pallas_call x1, Pallas kernels, on_device(): pl.pallas_call(functools.partial(to_planes_kernel, rows, planes), out_sha...  9.58 us
    pallas_call x1, Pallas kernels, on_device(): pl.pallas_call(functools.partial(project_kernel, slots), out_shape=jax.Sh...  8.84 us
    pallas_call x1, Pallas kernels, on_device(): pl.pallas_call(functools.partial(real_space_kernel, devices, rows, planes...  7.1 us
  transfers between devices with their start and end apart: 38, of which 14 were waited for; matrix products, arithmetic and copies ran while one was open for 7% of the time, Pallas kernels for 8%

profile of v1, /device:TPU:9, one launch (start us, length us, event | category | flops | bytes accessed | tf_op | source)
XLA Modules:
  0.0 232.8 jit_solution(17027409341945874868)
XLA Ops:
  1.6 1.0 copy-done.47
  2.6 6.2 %to_rows.1 = f32[32,4,32,128]{3,2,1,0:T(8,128)} custom-call(f32[8,2,4,128,128]{4,3,2,1,0:T(8,128)} %psi.5, bf16[256,768]{1,0:T(8,128)(2,1)S(1)} %copy-done.47, bf16[768,256]{1,0:T(8,128)(2,1)S(1)} %copy-done.46), custom_call_target="tpu_custom_call" | custom-call | flops 4000000000 | bytes 6000000 | tf_op jit(solution)/shard_map/to_rows/pallas_call | solution.py:282
  8.8 6.4 %all-to-all-start = ((f32[32,4,32,128]{3,2,1,0:T(8,128)}), f32[32,4,32,128]{3,2,1,0:T(8,128)S(1)}, u32[]{:S(2)}, u32[]{:S(2)}) async-start(f32[32,4,32,128]{3,2,1,0:T(8,128)} %to_rows.1), calls=%async_computation | async-start | bytes 4194304 | tf_op jit(solution)/shard_map/all_to_all | solution.py:296
  17.3 2.2 copy-done.1
  19.5 8.8 %project.1 = f32[8,32,16]{2,1,0:T(8,128)S(1)} custom-call(f32[8,2,4,128,128]{4,3,2,1,0:T(8,128)S(1)} %copy-done.1, f32[8,1024,128]{2,1,0:T(8,128)} %bitcast.90, f32[4,128,128]{2,1,0:T(8,128)S(1)} %add_multiply_fusion.kinetic), custom_call_target="tpu_custom_call" | custom-call | flops 8000000000 | bytes 8000000 | tf_op jit(solution)/shard_map/project/pallas_call | solution.py:339
  30.1 32.2 %all-to-all-done.recv = f32[32,4,32,128]{3,2,1,0:T(8,128)S(1)} async-done(((f32[32,4,32,128]{3,2,1,0:T(8,128)}), f32[32,4,32,128]{3,2,1,0:T(8,128)S(1)}, u32[]{:S(2)}, u32[]{:S(2)}) %all-to-all-start) | async-done | bytes 2097184 | tf_op jit(solution)/shard_map/all_to_all | solution.py:296
  62.3 1.3 copy-done.51
  63.7 7.1 %real_space.1 = (f32[8,128,512]{2,1,0:T(8,128)}, f32[8,32,128]{2,1,0:T(8,128)S(1)}, f32[8,32,128]{2,1,0:T(8,128)}, f32[8,32,128]{2,1,0:T(8,128)}, f32[8,32,128]{...) custom-call(f32[32,4,32,128]{3,2,1,0:T(8,128)} %copy-done.51, ...), custom_call_target="tpu_custom_call" | custom-call | flops 4000000000 | bytes 8000000 | tf_op jit(solution)/shard_map/real_space/pallas_call | solution.py:365
  78.6 1.6 copy-done
  80.2 1.7 real_gram.1
  82.2 2.0 collective-permute-start.32
  84.6 1.2 collective-permute-start.31
  87.2 1.1 collective-permute-start.34
  88.3 1.2 fusion
  89.9 1.1 collective-permute-start.35
  91.0 1.5 collective-permute-done.35
  92.5 4.9 %collective-permute-start.36 = (f32[136,16]{0,1:T(8,128)S(1)}, f32[136,16]{0,1:T(8,128)}, u32[]{:S(2)}, u32[]{:S(2)}) collective-permute-start(f32[136,16]{0,1:T(8,128)S(1)} %add.166), channel_id=1, source_target_pairs={{0,1},{1,0},{2,3},{3,2},{4,5},{5,4},{6,7},{7,6},{8,9},{9,8},{10,11... | collective-permute-start | bytes 26120 | tf_op jit(solution)/shard_map/ppermute | solution.py:231
  98.4 1.2 collective-permute-start.1
  100.5 1.0 collective-permute-start.3
  107.8 2.0 collective-permute-start.5
  109.8 1.0 collective-permute-start.6
  111.2 1.1 collective-permute-start.8
  112.3 1.4 collective-permute-start.9
  114.3 3.2 %collective-permute-start.10 = (f32[8,32,128]{2,1,0:T(8,128)}, f32[8,32,128]{2,1,0:T(8,128)S(1)}, u32[]{:S(2)}, u32[]{:S(2)}) collective-permute-start(f32[8,32,128]{2,1,0:T(8,128)} %copy-done.12), channel_id=1, source_target_pairs={{0,11},{1,10},{2,9},{3,8},{4,15},{5,14},{6,13},{7,12},{8,3},{9,2},... | collective-permute-start | bytes 393224 | tf_op jit(solution)/shard_map/ppermute | solution.py:231
  118.9 1.8 collective-permute-start.11
  122.0 1.5 collective-permute-start.13
  124.1 2.9 %collective-permute-start.14 = (f32[8,32,128]{2,1,0:T(8,128)}, f32[8,32,128]{2,1,0:T(8,128)}, u32[]{:S(2)}, u32[]{:S(2)}) collective-permute-start(f32[8,32,128]{2,1,0:T(8,128)} %copy-done.2), channel_id=1, source_target_pairs={{0,15},{1,14},{2,13},{3,12},{4,11},{5,10},{6,9},{7,8},{8,7},{9,6},... | collective-permute-start | bytes 393224 | tf_op jit(solution)/shard_map/ppermute | solution.py:231
  127.7 1.2 collective-permute-start.15
  131.5 9.1 %collective-permute-start.17 = (f32[8,32,128]{2,1,0:T(8,128)S(1)}, f32[8,32,128]{2,1,0:T(8,128)S(1)}, u32[]{:S(2)}, u32[]{:S(2)}) collective-permute-start(f32[8,32,128]{2,1,0:T(8,128)S(1)} %get-tuple-element.53), channel_id=1, source_target_pairs={{0,18},{1,19},{2,16},{3,17},{4,22},{5,23},{6,20},{7,21},{8,26},{9,... | collective-permute-start | bytes 393224 | tf_op jit(solution)/shard_map/ppermute | solution.py:231
  140.6 1.8 collective-permute-start.18
  142.3 3.8 %collective-permute-start.19 = (f32[8,32,128]{2,1,0:T(8,128)S(1)}, f32[8,32,128]{2,1,0:T(8,128)S(1)}, u32[]{:S(2)}, u32[]{:S(2)}) collective-permute-start(f32[8,32,128]{2,1,0:T(8,128)S(1)} %get-tuple-element.55), channel_id=1, source_target_pairs={{0,20},{1,21},{2,22},{3,23},{4,16},{5,17},{6,18},{7,19},{8,28},{9,... | collective-permute-start | bytes 393224 | tf_op jit(solution)/shard_map/ppermute | solution.py:231
  147.6 2.4 %collective-permute-start.21 = (f32[8,32,128]{2,1,0:T(8,128)S(1)}, f32[8,32,128]{2,1,0:T(8,128)S(1)}, u32[]{:S(2)}, u32[]{:S(2)}) collective-permute-start(f32[8,32,128]{2,1,0:T(8,128)S(1)} %get-tuple-element.57), channel_id=1, source_target_pairs={{0,22},{1,23},{2,20},{3,21},{4,18},{5,19},{6,16},{7,17},{8,30},{9,... | collective-permute-start | bytes 393224 | tf_op jit(solution)/shard_map/ppermute | solution.py:231
  150.0 7.9 %collective-permute-done.17.refs_18_ = f32[8,32,128]{2,1,0:T(8,128)S(1)} collective-permute-done((f32[8,32,128]{2,1,0:T(8,128)S(1)}, f32[8,32,128]{2,1,0:T(8,128)S(1)}, u32[]{:S(2)}, u32[]{:S(2)}) %collective-permute-start.17) | collective-permute-done | bytes 131104 | tf_op jit(solution)/shard_map/ppermute | solution.py:231
  158.5 4.8 %collective-permute-start.22 = (f32[8,32,128]{2,1,0:T(8,128)S(1)}, f32[8,32,128]{2,1,0:T(8,128)S(1)}, u32[]{:S(2)}, u32[]{:S(2)}) collective-permute-start(f32[8,32,128]{2,1,0:T(8,128)S(1)} %get-tuple-element.58), channel_id=1, source_target_pairs={{0,23},{1,22},{2,21},{3,20},{4,19},{5,18},{6,17},{7,16},{8,31},{9,... | collective-permute-start | bytes 393224 | tf_op jit(solution)/shard_map/ppermute | solution.py:231
  164.0 5.1 %collective-permute-done.19.refs_20_ = f32[8,32,128]{2,1,0:T(8,128)S(1)} collective-permute-done((f32[8,32,128]{2,1,0:T(8,128)S(1)}, f32[8,32,128]{2,1,0:T(8,128)S(1)}, u32[]{:S(2)}, u32[]{:S(2)}) %collective-permute-start.19) | collective-permute-done | bytes 131104 | tf_op jit(solution)/shard_map/ppermute | solution.py:231
  169.8 2.2 collective-permute-done.20.refs_21_
  172.4 1.0 copy.107
  173.5 1.2 collective-permute-done.21.refs_22_
  175.4 7.1 %collective-permute-start.26 = (f32[8,32,128]{2,1,0:T(8,128)S(1)}, f32[8,32,128]{2,1,0:T(8,128)S(1)}, u32[]{:S(2)}, u32[]{:S(2)}) collective-permute-start(f32[8,32,128]{2,1,0:T(8,128)S(1)} %get-tuple-element.62), channel_id=1, source_target_pairs={{0,27},{1,26},{2,25},{3,24},{4,31},{5,30},{6,29},{7,28},{8,19},{9,... | collective-permute-start | bytes 393224 | tf_op jit(solution)/shard_map/ppermute | solution.py:231
  183.8 2.9 %collective-permute-start.27 = (f32[8,32,128]{2,1,0:T(8,128)S(1)}, f32[8,32,128]{2,1,0:T(8,128)S(1)}, u32[]{:S(2)}, u32[]{:S(2)}) collective-permute-start(f32[8,32,128]{2,1,0:T(8,128)S(1)} %get-tuple-element.63), channel_id=1, source_target_pairs={{0,28},{1,29},{2,30},{3,31},{4,24},{5,25},{6,26},{7,27},{8,20},{9,... | collective-permute-start | bytes 393224 | tf_op jit(solution)/shard_map/ppermute | solution.py:231
  186.7 1.7 collective-permute-done.23.refs_24_
  189.1 3.4 %collective-permute-start.28 = (f32[8,32,128]{2,1,0:T(8,128)S(1)}, f32[8,32,128]{2,1,0:T(8,128)S(1)}, u32[]{:S(2)}, u32[]{:S(2)}) collective-permute-start(f32[8,32,128]{2,1,0:T(8,128)S(1)} %get-tuple-element.64), channel_id=1, source_target_pairs={{0,29},{1,28},{2,31},{3,30},{4,25},{5,24},{6,27},{7,26},{8,21},{9,... | collective-permute-start | bytes 393224 | tf_op jit(solution)/shard_map/ppermute | solution.py:231
  192.5 10.4 %collective-permute-done.24.refs_25_ = f32[8,32,128]{2,1,0:T(8,128)S(1)} collective-permute-done((f32[8,32,128]{2,1,0:T(8,128)S(1)}, f32[8,32,128]{2,1,0:T(8,128)S(1)}, u32[]{:S(2)}, u32[]{:S(2)}) %collective-permute-start.24) | collective-permute-done | bytes 131104 | tf_op jit(solution)/shard_map/ppermute | solution.py:231
  203.5 2.1 collective-permute-done.25.refs_26_
  206.5 4.0 %collective-permute-start.30 = (f32[8,32,128]{2,1,0:T(8,128)S(1)}, f32[8,32,128]{2,1,0:T(8,128)S(1)}, u32[]{:S(2)}, u32[]{:S(2)}) collective-permute-start(f32[8,32,128]{2,1,0:T(8,128)S(1)} %get-tuple-element.66), channel_id=1, source_target_pairs={{0,31},{1,30},{2,29},{3,28},{4,27},{5,26},{6,25},{7,24},{8,23},{9,... | collective-permute-start | bytes 393224 | tf_op jit(solution)/shard_map/ppermute | solution.py:231
  210.5 9.9 %base.1.refs_32_ = f32[8,2,4,128,128]{4,3,2,1,0:T(8,128)S(1)} custom-call(f32[8,2,4,128,128]{4,3,2,1,0:T(8,128)} %psi.5, f32[8,1024,128]{2,1,0:T(8,128)} %bitcast.91, f32[4,128,128]{2,1,0:T(8,128)S(1)} %add_multiply_fusion.kinetic, f32[8,16,32]{2,1,0:T(8,128)S(1)} %pad_maximum_fusion.8.coefs), custom_call_target="tpu_custom_call" | custom-call | flops 8000000000 | bytes 12000000 | tf_op jit(solution)/shard_map/base/pallas_call | solution.py:424
  220.4 2.0 copy-done.48
  223.2 9.6 %to_planes.1 = f32[8,2,4,128,128]{4,3,2,1,0:T(8,128)} custom-call(f32[8,32,128]{2,1,0:T(8,128)S(1)} %copy-done.50, f32[8,32,128]{2,1,0:T(8,128)S(1)} %collective-permute-done.refs_1_, f32[8,32,128]{2,1,0:T(8,128)S(1)} %collective-permute-done.1.refs_2_, f32[8,32,128]{2,1,0:T(8,128)S(1)} %collective-permute-done.2.refs_3_, ...), custom_call_target="tpu_custom_call" | custom-call | flops 8000000000 | bytes 12000000 | tf_op jit(solution)/shard_map/to_planes/pallas_call | solution.py:437
  (234 shorter events, 39.7 us)
Async XLA Ops:
  8.8 53.5 %all-to-all-start = ((f32[32,4,32,128]{3,2,1,0:T(8,128)}), f32[32,4,32,128]{3,2,1,0:T(8,128)S(1)}, u32[]{:S(2)}, u32[]{:S(2)}) async-start(f32[32,4,32,128]{3,2,1,0:T(8,128)} %to_rows.1), calls=%async_computation | async-start | bytes 4194304 | tf_op jit(solution)/shard_map/all_to_all | solution.py:296
  77.9 22.5 %copy-start.2 = (f32[8,32,128]{2,1,0:T(8,128)}, f32[8,32,128]{2,1,0:T(8,128)S(1)}, u32[]{:S(2)}) copy-start(f32[8,32,128]{2,1,0:T(8,128)S(1)} %get-tuple-element.50) | copy-start | bytes 393220
  77.9 23.6 %copy-start.3 = (f32[8,32,128]{2,1,0:T(8,128)}, f32[8,32,128]{2,1,0:T(8,128)S(1)}, u32[]{:S(2)}) copy-start(f32[8,32,128]{2,1,0:T(8,128)S(1)} %get-tuple-element.49) | copy-start | bytes 393220
  82.2 3.6 %collective-permute-start.32 = (f32[136,16]{0,1:T(8,128)S(1)}, f32[136,16]{0,1:T(8,128)S(1)}, u32[]{:S(2)}, u32[]{:S(2)}) collective-permute-start(f32[136,16]{0,1:T(8,128)S(1)} %maximum_maximum_fusion), channel_id=1, source_target_pairs={{0,16},{1,17},{2,18},{3,19},{4,20},{5,21},{6,22},{7,23},{8,24},{9,... | collective-permute-start | bytes 26120 | tf_op jit(solution)/shard_map/ppermute | solution.py:231
  84.2 2.6 %collective-permute-start.33 = (f32[136,16]{0,1:T(8,128)S(1)}, f32[136,16]{0,1:T(8,128)S(1)}, u32[]{:S(2)}, u32[]{:S(2)}) collective-permute-start(f32[136,16]{0,1:T(8,128)S(1)} %maximum_maximum_fusion), channel_id=1, source_target_pairs={{0,24},{1,25},{2,26},{3,27},{4,28},{5,29},{6,30},{7,31},{8,16},{9,... | collective-permute-start | bytes 26120 | tf_op jit(solution)/shard_map/ppermute | solution.py:231
  84.6 2.6 %collective-permute-start.31 = (f32[136,16]{0,1:T(8,128)S(1)}, f32[136,16]{0,1:T(8,128)S(1)}, u32[]{:S(2)}, u32[]{:S(2)}) collective-permute-start(f32[136,16]{0,1:T(8,128)S(1)} %maximum_maximum_fusion), channel_id=1, source_target_pairs={{0,8},{1,9},{2,10},{3,11},{4,12},{5,13},{6,14},{7,15},{8,0},{9,1},... | collective-permute-start | bytes 26120 | tf_op jit(solution)/shard_map/ppermute | solution.py:231
  87.2 2.7 %collective-permute-start.34 = (f32[136,16]{0,1:T(8,128)S(1)}, f32[136,16]{0,1:T(8,128)S(1)}, u32[]{:S(2)}, u32[]{:S(2)}) collective-permute-start(f32[136,16]{0,1:T(8,128)S(1)} %add_add_fusion), channel_id=1, source_target_pairs={{0,4},{1,5},{2,6},{3,7},{4,0},{5,1},{6,2},{7,3},{8,12},{9,13},{10,... | collective-permute-start | bytes 26120 | tf_op jit(solution)/shard_map/ppermute | solution.py:231
  89.9 2.6 %collective-permute-start.35 = (f32[136,16]{0,1:T(8,128)S(1)}, f32[136,16]{0,1:T(8,128)S(1)}, u32[]{:S(2)}, u32[]{:S(2)}) collective-permute-start(f32[136,16]{0,1:T(8,128)S(1)} %add.165), channel_id=1, source_target_pairs={{0,2},{1,3},{2,0},{3,1},{4,6},{5,7},{6,4},{7,5},{8,10},{9,11},{10,... | collective-permute-start | bytes 26120 | tf_op jit(solution)/shard_map/ppermute | solution.py:231
  92.5 9.0 %collective-permute-start.36 = (f32[136,16]{0,1:T(8,128)S(1)}, f32[136,16]{0,1:T(8,128)}, u32[]{:S(2)}, u32[]{:S(2)}) collective-permute-start(f32[136,16]{0,1:T(8,128)S(1)} %add.166), channel_id=1, source_target_pairs={{0,1},{1,0},{2,3},{3,2},{4,5},{5,4},{6,7},{7,6},{8,9},{9,8},{10,11... | collective-permute-start | bytes 26120 | tf_op jit(solution)/shard_map/ppermute | solution.py:231
  98.3 9.5 %collective-permute-start = (f32[8,32,128]{2,1,0:T(8,128)}, f32[8,32,128]{2,1,0:T(8,128)S(1)}, u32[]{:S(2)}, u32[]{:S(2)}) collective-permute-start(f32[8,32,128]{2,1,0:T(8,128)} %get-tuple-element.36), channel_id=1, source_target_pairs={{0,1},{1,0},{2,3},{3,2},{4,5},{5,4},{6,7},{7,6},{8,9},{9,8},{10,11... | collective-permute-start | bytes 393224 | tf_op jit(solution)/shard_map/ppermute | solution.py:231
  98.4 11.5 %collective-permute-start.1 = (f32[8,32,128]{2,1,0:T(8,128)}, f32[8,32,128]{2,1,0:T(8,128)S(1)}, u32[]{:S(2)}, u32[]{:S(2)}) collective-permute-start(f32[8,32,128]{2,1,0:T(8,128)} %get-tuple-element.37), channel_id=1, source_target_pairs={{0,2},{1,3},{2,0},{3,1},{4,6},{5,7},{6,4},{7,5},{8,10},{9,11},{10,... | collective-permute-start | bytes 393224 | tf_op jit(solution)/shard_map/ppermute | solution.py:231
  99.5 11.4 %collective-permute-start.2 = (f32[8,32,128]{2,1,0:T(8,128)}, f32[8,32,128]{2,1,0:T(8,128)S(1)}, u32[]{:S(2)}, u32[]{:S(2)}) collective-permute-start(f32[8,32,128]{2,1,0:T(8,128)} %copy-done.26), channel_id=1, source_target_pairs={{0,3},{1,2},{2,1},{3,0},{4,7},{5,6},{6,5},{7,4},{8,11},{9,10},{10,... | collective-permute-start | bytes 393224 | tf_op jit(solution)/shard_map/ppermute | solution.py:231
  100.5 10.8 %collective-permute-start.3 = (f32[8,32,128]{2,1,0:T(8,128)}, f32[8,32,128]{2,1,0:T(8,128)S(1)}, u32[]{:S(2)}, u32[]{:S(2)}) collective-permute-start(f32[8,32,128]{2,1,0:T(8,128)} %copy-done.25), channel_id=1, source_target_pairs={{0,4},{1,5},{2,6},{3,7},{4,0},{5,1},{6,2},{7,3},{8,12},{9,13},{10,... | collective-permute-start | bytes 393224 | tf_op jit(solution)/shard_map/ppermute | solution.py:231
  101.5 10.8 %collective-permute-start.4 = (f32[8,32,128]{2,1,0:T(8,128)}, f32[8,32,128]{2,1,0:T(8,128)S(1)}, u32[]{:S(2)}, u32[]{:S(2)}) collective-permute-start(f32[8,32,128]{2,1,0:T(8,128)} %copy-done.24), channel_id=1, source_target_pairs={{0,5},{1,4},{2,7},{3,6},{4,1},{5,0},{6,3},{7,2},{8,13},{9,12},{10,... | collective-permute-start | bytes 393224 | tf_op jit(solution)/shard_map/ppermute | solution.py:231
  107.8 5.9 %collective-permute-start.5 = (f32[8,32,128]{2,1,0:T(8,128)}, f32[8,32,128]{2,1,0:T(8,128)S(1)}, u32[]{:S(2)}, u32[]{:S(2)}) collective-permute-start(f32[8,32,128]{2,1,0:T(8,128)} %copy-done.23), channel_id=1, source_target_pairs={{0,6},{1,7},{2,4},{3,5},{4,2},{5,3},{6,0},{7,1},{8,14},{9,15},{10,... | collective-permute-start | bytes 393224 | tf_op jit(solution)/shard_map/ppermute | solution.py:231
  109.8 8.4 %collective-permute-start.6 = (f32[8,32,128]{2,1,0:T(8,128)}, f32[8,32,128]{2,1,0:T(8,128)S(1)}, u32[]{:S(2)}, u32[]{:S(2)}) collective-permute-start(f32[8,32,128]{2,1,0:T(8,128)} %copy-done.22), channel_id=1, source_target_pairs={{0,7},{1,6},{2,5},{3,4},{4,3},{5,2},{6,1},{7,0},{8,15},{9,14},{10,... | collective-permute-start | bytes 393224 | tf_op jit(solution)/shard_map/ppermute | solution.py:231
  110.9 9.8 %collective-permute-start.7 = (f32[8,32,128]{2,1,0:T(8,128)}, f32[8,32,128]{2,1,0:T(8,128)S(1)}, u32[]{:S(2)}, u32[]{:S(2)}) collective-permute-start(f32[8,32,128]{2,1,0:T(8,128)} %copy-done.21), channel_id=1, source_target_pairs={{0,8},{1,9},{2,10},{3,11},{4,12},{5,13},{6,14},{7,15},{8,0},{9,1},... | collective-permute-start | bytes 393224 | tf_op jit(solution)/shard_map/ppermute | solution.py:231
  111.2 10.1 %collective-permute-start.8 = (f32[8,32,128]{2,1,0:T(8,128)}, f32[8,32,128]{2,1,0:T(8,128)S(1)}, u32[]{:S(2)}, u32[]{:S(2)}) collective-permute-start(f32[8,32,128]{2,1,0:T(8,128)} %copy-done.18), channel_id=1, source_target_pairs={{0,9},{1,8},{2,11},{3,10},{4,13},{5,12},{6,15},{7,14},{8,1},{9,0},... | collective-permute-start | bytes 393224 | tf_op jit(solution)/shard_map/ppermute | solution.py:231
  112.3 11.2 %collective-permute-start.9 = (f32[8,32,128]{2,1,0:T(8,128)}, f32[8,32,128]{2,1,0:T(8,128)S(1)}, u32[]{:S(2)}, u32[]{:S(2)}) collective-permute-start(f32[8,32,128]{2,1,0:T(8,128)} %copy-done.15), channel_id=1, source_target_pairs={{0,10},{1,11},{2,8},{3,9},{4,14},{5,15},{6,12},{7,13},{8,2},{9,3},... | collective-permute-start | bytes 393224 | tf_op jit(solution)/shard_map/ppermute | solution.py:231
  114.3 12.7 %collective-permute-start.10 = (f32[8,32,128]{2,1,0:T(8,128)}, f32[8,32,128]{2,1,0:T(8,128)S(1)}, u32[]{:S(2)}, u32[]{:S(2)}) collective-permute-start(f32[8,32,128]{2,1,0:T(8,128)} %copy-done.12), channel_id=1, source_target_pairs={{0,11},{1,10},{2,9},{3,8},{4,15},{5,14},{6,13},{7,12},{8,3},{9,2},... | collective-permute-start | bytes 393224 | tf_op jit(solution)/shard_map/ppermute | solution.py:231
  118.9 11.1 %collective-permute-start.11 = (f32[8,32,128]{2,1,0:T(8,128)}, f32[8,32,128]{2,1,0:T(8,128)}, u32[]{:S(2)}, u32[]{:S(2)}) collective-permute-start(f32[8,32,128]{2,1,0:T(8,128)} %copy-done.7), channel_id=1, source_target_pairs={{0,12},{1,13},{2,14},{3,15},{4,8},{5,9},{6,10},{7,11},{8,4},{9,5},... | collective-permute-start | bytes 393224 | tf_op jit(solution)/shard_map/ppermute | solution.py:231
  121.3 10.2 %collective-permute-start.12 = (f32[8,32,128]{2,1,0:T(8,128)}, f32[8,32,128]{2,1,0:T(8,128)}, u32[]{:S(2)}, u32[]{:S(2)}) collective-permute-start(f32[8,32,128]{2,1,0:T(8,128)} %copy-done.4), channel_id=1, source_target_pairs={{0,13},{1,12},{2,15},{3,14},{4,9},{5,8},{6,11},{7,10},{8,5},{9,4},... | collective-permute-start | bytes 393224 | tf_op jit(solution)/shard_map/ppermute | solution.py:231
  122.0 18.5 %collective-permute-start.13 = (f32[8,32,128]{2,1,0:T(8,128)}, f32[8,32,128]{2,1,0:T(8,128)}, u32[]{:S(2)}, u32[]{:S(2)}) collective-permute-start(f32[8,32,128]{2,1,0:T(8,128)} %copy-done.3), channel_id=1, source_target_pairs={{0,14},{1,15},{2,12},{3,13},{4,10},{5,11},{6,8},{7,9},{8,6},{9,7},... | collective-permute-start | bytes 393224 | tf_op jit(solution)/shard_map/ppermute | solution.py:231
  124.1 18.2 %collective-permute-start.14 = (f32[8,32,128]{2,1,0:T(8,128)}, f32[8,32,128]{2,1,0:T(8,128)}, u32[]{:S(2)}, u32[]{:S(2)}) collective-permute-start(f32[8,32,128]{2,1,0:T(8,128)} %copy-done.2), channel_id=1, source_target_pairs={{0,15},{1,14},{2,13},{3,12},{4,11},{5,10},{6,9},{7,8},{8,7},{9,6},... | collective-permute-start | bytes 393224 | tf_op jit(solution)/shard_map/ppermute | solution.py:231
  127.7 18.5 %collective-permute-start.15 = (f32[8,32,128]{2,1,0:T(8,128)S(1)}, f32[8,32,128]{2,1,0:T(8,128)}, u32[]{:S(2)}, u32[]{:S(2)}) collective-permute-start(f32[8,32,128]{2,1,0:T(8,128)S(1)} %get-tuple-element.51), channel_id=1, source_target_pairs={{0,16},{1,17},{2,18},{3,19},{4,20},{5,21},{6,22},{7,23},{8,24},{9,... | collective-permute-start | bytes 393224 | tf_op jit(solution)/shard_map/ppermute | solution.py:231
  130.0 17.0 %collective-permute-start.16 = (f32[8,32,128]{2,1,0:T(8,128)S(1)}, f32[8,32,128]{2,1,0:T(8,128)S(1)}, u32[]{:S(2)}, u32[]{:S(2)}) collective-permute-start(f32[8,32,128]{2,1,0:T(8,128)S(1)} %get-tuple-element.52), channel_id=1, source_target_pairs={{0,17},{1,16},{2,19},{3,18},{4,21},{5,20},{6,23},{7,22},{8,25},{9,... | collective-permute-start | bytes 393224 | tf_op jit(solution)/shard_map/ppermute | solution.py:231
  131.5 26.4 %collective-permute-start.17 = (f32[8,32,128]{2,1,0:T(8,128)S(1)}, f32[8,32,128]{2,1,0:T(8,128)S(1)}, u32[]{:S(2)}, u32[]{:S(2)}) collective-permute-start(f32[8,32,128]{2,1,0:T(8,128)S(1)} %get-tuple-element.53), channel_id=1, source_target_pairs={{0,18},{1,19},{2,16},{3,17},{4,22},{5,23},{6,20},{7,21},{8,26},{9,... | collective-permute-start | bytes 393224 | tf_op jit(solution)/shard_map/ppermute | solution.py:231
  140.6 22.8 %collective-permute-start.18 = (f32[8,32,128]{2,1,0:T(8,128)S(1)}, f32[8,32,128]{2,1,0:T(8,128)S(1)}, u32[]{:S(2)}, u32[]{:S(2)}) collective-permute-start(f32[8,32,128]{2,1,0:T(8,128)S(1)} %get-tuple-element.54), channel_id=1, source_target_pairs={{0,19},{1,18},{2,17},{3,16},{4,23},{5,22},{6,21},{7,20},{8,27},{9,... | collective-permute-start | bytes 393224 | tf_op jit(solution)/shard_map/ppermute | solution.py:231
  142.3 26.8 %collective-permute-start.19 = (f32[8,32,128]{2,1,0:T(8,128)S(1)}, f32[8,32,128]{2,1,0:T(8,128)S(1)}, u32[]{:S(2)}, u32[]{:S(2)}) collective-permute-start(f32[8,32,128]{2,1,0:T(8,128)S(1)} %get-tuple-element.55), channel_id=1, source_target_pairs={{0,20},{1,21},{2,22},{3,23},{4,16},{5,17},{6,18},{7,19},{8,28},{9,... | collective-permute-start | bytes 393224 | tf_op jit(solution)/shard_map/ppermute | solution.py:231
  146.1 25.8 %collective-permute-start.20 = (f32[8,32,128]{2,1,0:T(8,128)S(1)}, f32[8,32,128]{2,1,0:T(8,128)S(1)}, u32[]{:S(2)}, u32[]{:S(2)}) collective-permute-start(f32[8,32,128]{2,1,0:T(8,128)S(1)} %get-tuple-element.56), channel_id=1, source_target_pairs={{0,21},{1,20},{2,23},{3,22},{4,17},{5,16},{6,19},{7,18},{8,29},{9,... | collective-permute-start | bytes 393224 | tf_op jit(solution)/shard_map/ppermute | solution.py:231
  147.6 27.1 %collective-permute-start.21 = (f32[8,32,128]{2,1,0:T(8,128)S(1)}, f32[8,32,128]{2,1,0:T(8,128)S(1)}, u32[]{:S(2)}, u32[]{:S(2)}) collective-permute-start(f32[8,32,128]{2,1,0:T(8,128)S(1)} %get-tuple-element.57), channel_id=1, source_target_pairs={{0,22},{1,23},{2,20},{3,21},{4,18},{5,19},{6,16},{7,17},{8,30},{9,... | collective-permute-start | bytes 393224 | tf_op jit(solution)/shard_map/ppermute | solution.py:231
  158.5 24.6 %collective-permute-start.22 = (f32[8,32,128]{2,1,0:T(8,128)S(1)}, f32[8,32,128]{2,1,0:T(8,128)S(1)}, u32[]{:S(2)}, u32[]{:S(2)}) collective-permute-start(f32[8,32,128]{2,1,0:T(8,128)S(1)} %get-tuple-element.58), channel_id=1, source_target_pairs={{0,23},{1,22},{2,21},{3,20},{4,19},{5,18},{6,17},{7,16},{8,31},{9,... | collective-permute-start | bytes 393224 | tf_op jit(solution)/shard_map/ppermute | solution.py:231
  164.0 24.4 %collective-permute-start.23 = (f32[8,32,128]{2,1,0:T(8,128)S(1)}, f32[8,32,128]{2,1,0:T(8,128)S(1)}, u32[]{:S(2)}, u32[]{:S(2)}) collective-permute-start(f32[8,32,128]{2,1,0:T(8,128)S(1)} %get-tuple-element.59), channel_id=1, source_target_pairs={{0,24},{1,25},{2,26},{3,27},{4,28},{5,29},{6,30},{7,31},{8,16},{9,... | collective-permute-start | bytes 393224 | tf_op jit(solution)/shard_map/ppermute | solution.py:231
  169.8 33.1 %collective-permute-start.24 = (f32[8,32,128]{2,1,0:T(8,128)S(1)}, f32[8,32,128]{2,1,0:T(8,128)S(1)}, u32[]{:S(2)}, u32[]{:S(2)}) collective-permute-start(f32[8,32,128]{2,1,0:T(8,128)S(1)} %get-tuple-element.60), channel_id=1, source_target_pairs={{0,25},{1,24},{2,27},{3,26},{4,29},{5,28},{6,31},{7,30},{8,17},{9,... | collective-permute-start | bytes 393224 | tf_op jit(solution)/shard_map/ppermute | solution.py:231
  171.9 33.7 %collective-permute-start.25 = (f32[8,32,128]{2,1,0:T(8,128)S(1)}, f32[8,32,128]{2,1,0:T(8,128)S(1)}, u32[]{:S(2)}, u32[]{:S(2)}) collective-permute-start(f32[8,32,128]{2,1,0:T(8,128)S(1)} %get-tuple-element.61), channel_id=1, source_target_pairs={{0,26},{1,27},{2,24},{3,25},{4,30},{5,31},{6,28},{7,29},{8,18},{9,... | collective-permute-start | bytes 393224 | tf_op jit(solution)/shard_map/ppermute | solution.py:231
  175.4 47.6 %collective-permute-start.26 = (f32[8,32,128]{2,1,0:T(8,128)S(1)}, f32[8,32,128]{2,1,0:T(8,128)S(1)}, u32[]{:S(2)}, u32[]{:S(2)}) collective-permute-start(f32[8,32,128]{2,1,0:T(8,128)S(1)} %get-tuple-element.62), channel_id=1, source_target_pairs={{0,27},{1,26},{2,25},{3,24},{4,31},{5,30},{6,29},{7,28},{8,19},{9,... | collective-permute-start | bytes 393224 | tf_op jit(solution)/shard_map/ppermute | solution.py:231
  183.8 39.2 %collective-permute-start.27 = (f32[8,32,128]{2,1,0:T(8,128)S(1)}, f32[8,32,128]{2,1,0:T(8,128)S(1)}, u32[]{:S(2)}, u32[]{:S(2)}) collective-permute-start(f32[8,32,128]{2,1,0:T(8,128)S(1)} %get-tuple-element.63), channel_id=1, source_target_pairs={{0,28},{1,29},{2,30},{3,31},{4,24},{5,25},{6,26},{7,27},{8,20},{9,... | collective-permute-start | bytes 393224 | tf_op jit(solution)/shard_map/ppermute | solution.py:231
  189.1 33.9 %collective-permute-start.28 = (f32[8,32,128]{2,1,0:T(8,128)S(1)}, f32[8,32,128]{2,1,0:T(8,128)S(1)}, u32[]{:S(2)}, u32[]{:S(2)}) collective-permute-start(f32[8,32,128]{2,1,0:T(8,128)S(1)} %get-tuple-element.64), channel_id=1, source_target_pairs={{0,29},{1,28},{2,31},{3,30},{4,25},{5,24},{6,27},{7,26},{8,21},{9,... | collective-permute-start | bytes 393224 | tf_op jit(solution)/shard_map/ppermute | solution.py:231
  203.5 19.5 %collective-permute-start.29 = (f32[8,32,128]{2,1,0:T(8,128)S(1)}, f32[8,32,128]{2,1,0:T(8,128)S(1)}, u32[]{:S(2)}, u32[]{:S(2)}) collective-permute-start(f32[8,32,128]{2,1,0:T(8,128)S(1)} %get-tuple-element.65), channel_id=1, source_target_pairs={{0,30},{1,31},{2,28},{3,29},{4,26},{5,27},{6,24},{7,25},{8,22},{9,... | collective-permute-start | bytes 393224 | tf_op jit(solution)/shard_map/ppermute | solution.py:231
  206.3 16.7 %copy-start.14 = (f32[8,32,128]{2,1,0:T(8,128)S(1)}, f32[8,32,128]{2,1,0:T(8,128)}, u32[]{:S(2)}) copy-start(f32[8,32,128]{2,1,0:T(8,128)} %copy-done.13) | copy-start | bytes 393220
  206.3 16.7 %copy-start.17 = (f32[8,32,128]{2,1,0:T(8,128)S(1)}, f32[8,32,128]{2,1,0:T(8,128)}, u32[]{:S(2)}) copy-start(f32[8,32,128]{2,1,0:T(8,128)} %copy-done.16) | copy-start | bytes 393220
  206.4 16.7 %copy-start.20 = (f32[8,32,128]{2,1,0:T(8,128)S(1)}, f32[8,32,128]{2,1,0:T(8,128)}, u32[]{:S(2)}) copy-start(f32[8,32,128]{2,1,0:T(8,128)} %copy-done.19) | copy-start | bytes 393220
  206.4 16.7 %copy-start.28 = (f32[8,32,128]{2,1,0:T(8,128)S(1)}, f32[8,32,128]{2,1,0:T(8,128)}, u32[]{:S(2)}) copy-start(f32[8,32,128]{2,1,0:T(8,128)} %copy-done.27) | copy-start | bytes 393220
  206.4 16.7 %copy-start.30 = (f32[8,32,128]{2,1,0:T(8,128)S(1)}, f32[8,32,128]{2,1,0:T(8,128)}, u32[]{:S(2)}) copy-start(f32[8,32,128]{2,1,0:T(8,128)} %copy-done.29) | copy-start | bytes 393220
  206.4 16.7 %copy-start.32 = (f32[8,32,128]{2,1,0:T(8,128)S(1)}, f32[8,32,128]{2,1,0:T(8,128)}, u32[]{:S(2)}) copy-start(f32[8,32,128]{2,1,0:T(8,128)} %copy-done.31) | copy-start | bytes 393220
  206.4 16.7 %copy-start.34 = (f32[8,32,128]{2,1,0:T(8,128)S(1)}, f32[8,32,128]{2,1,0:T(8,128)}, u32[]{:S(2)}) copy-start(f32[8,32,128]{2,1,0:T(8,128)} %copy-done.33) | copy-start | bytes 393220
  206.4 16.7 %copy-start.36 = (f32[8,32,128]{2,1,0:T(8,128)S(1)}, f32[8,32,128]{2,1,0:T(8,128)}, u32[]{:S(2)}) copy-start(f32[8,32,128]{2,1,0:T(8,128)} %copy-done.35) | copy-start | bytes 393220
  206.5 16.5 %collective-permute-start.30 = (f32[8,32,128]{2,1,0:T(8,128)S(1)}, f32[8,32,128]{2,1,0:T(8,128)S(1)}, u32[]{:S(2)}, u32[]{:S(2)}) collective-permute-start(f32[8,32,128]{2,1,0:T(8,128)S(1)} %get-tuple-element.66), channel_id=1, source_target_pairs={{0,31},{1,30},{2,29},{3,28},{4,27},{5,26},{6,25},{7,24},{8,23},{9,... | collective-permute-start | bytes 393224 | tf_op jit(solution)/shard_map/ppermute | solution.py:231
  (46 other events, 219.6 us)

commit v2 on v0

--- a/solution.py
+++ b/solution.py
@@ -12,7 +12,7 @@
 highest = lax.Precision.HIGHEST
 f32 = jnp.float32
 bf16 = jnp.bfloat16
-vmem_limit = 48 * 1024 * 1024
+vmem_limit = 60 * 1024 * 1024
 
 
 def signed_index(values, length):
@@ -82,39 +82,60 @@
     )
 
 
+def groups(count, width):
+    size = max(1, 256 // width)
+    return [list(range(i, min(i + size, count))) for i in range(0, count, size)]
+
+
+def parts_in_lanes(values, span, width):
+    items = values.shape[1] // width
+    return jnp.concatenate(
+        [
+            jnp.concatenate(
+                [values[:span, i * width : (i + 1) * width], values[span:, i * width : (i + 1) * width]],
+                axis=1,
+            )
+            for i in range(items)
+        ],
+        axis=0,
+    )
+
+
 def to_rows_kernel(devices, rows, planes, psi, y_table, z_table, out):
-    real = jnp.concatenate([psi[0, 0, p] - psi[1, 1, p] for p in range(planes)], axis=1)
-    imag = jnp.concatenate([psi[0, 1, p] + psi[1, 0, p] for p in range(planes)], axis=1)
     span_y, span_z = psi.shape[3], psi.shape[4]
-    along_y = dot_left(y_table[...], jnp.concatenate([real, imag], axis=0))
     flat = out.reshape(devices * 2 * planes * rows, span_z)
-    for p in range(planes):
-        cols = slice(p * span_z, (p + 1) * span_z)
-        plane = jnp.concatenate([along_y[:span_y, cols], along_y[span_y:, cols]], axis=1)
-        values = dot_right(plane, z_table[...])
-        for part in range(2):
-            for r in range(rows):
-                start = (r * planes + p) * 2 + part
-                flat[pl.ds(start, devices, stride=2 * planes * rows), :] = values[
-                    r * devices : (r + 1) * devices, part * span_z : (part + 1) * span_z
-                ]
-
-
-def real_space_kernel(devices, rows, planes, recv, pot, inverse, forward, back, field):
+    for group in groups(planes, span_z):
+        real = jnp.concatenate([psi[0, 0, p] - psi[1, 1, p] for p in group], axis=1)
+        imag = jnp.concatenate([psi[0, 1, p] + psi[1, 0, p] for p in group], axis=1)
+        along_y = dot_left(y_table[...], jnp.concatenate([real, imag], axis=0))
+        values = dot_right(parts_in_lanes(along_y, span_y, span_z), z_table[...])
+        for i, p in enumerate(group):
+            for part in range(2):
+                for r in range(rows):
+                    first = i * span_y + r * devices
+                    start = (r * planes + p) * 2 + part
+                    flat[pl.ds(start, devices, stride=2 * planes * rows), :] = values[
+                        first : first + devices, part * span_z : (part + 1) * span_z
+                    ]
+
+
+def real_space_kernel(devices, rows, planes, recv, pot, inverse, forward, _, back, field):
     span_x = pot.shape[0]
     block = 2 * planes
-    columns = [
-        recv[:, r * block : (r + 1) * block, :].reshape(devices * block, recv.shape[2])
-        for r in range(rows)
-    ]
-    spatial = dot_left(inverse[...], jnp.concatenate(columns, axis=1))
-    for band in range(2):
-        one = spatial[band * span_x : (band + 1) * span_x]
-        field[band] = one
-        spectral = dot_left(forward[...], one * pot[...])
-        for r in range(rows):
-            cols = spectral[:, r * recv.shape[2] : (r + 1) * recv.shape[2]]
-            back[:, band, r * block : (r + 1) * block] = cols.reshape(devices, block, recv.shape[2])
+    span_z = recv.shape[2]
+    for group in groups(rows, span_z):
+        columns = [
+            recv[:, r * block : (r + 1) * block, :].reshape(devices * block, span_z) for r in group
+        ]
+        spatial = dot_left(inverse[...], jnp.concatenate(columns, axis=1))
+        lanes = slice(group[0] * span_z, (group[-1] + 1) * span_z)
+        for band in range(2):
+            one = spatial[band * span_x : (band + 1) * span_x]
+            field[band, :, lanes] = one
+            spectral = dot_left(forward[...], one * pot[:, lanes])
+            for i, r in enumerate(group):
+                cols = spectral[:, i * span_z : (i + 1) * span_z]
+                back[:, band, r * block : (r + 1) * block] = cols.reshape(devices, block, span_z)
 
 
 def real_gram_kernel(bands, field, pot, out):
@@ -146,9 +167,8 @@
 def to_planes_kernel(devices, rows, planes, recv, base, y_table, z_table, out):
     span_y, span_z = base.shape[3], base.shape[4]
     flat = recv.reshape(devices * 2 * planes * rows, span_z)
-    columns = []
-    for p in range(planes):
-        columns.append(
+    for group in groups(planes, span_z):
+        columns = [
             jnp.concatenate(
                 [
                     flat[pl.ds((r * planes + p) * 2 + part, devices, stride=2 * planes * rows), :]
@@ -157,14 +177,15 @@
                 ],
                 axis=0,
             )
-        )
-    along_y = dot_left(y_table[...], jnp.concatenate(columns, axis=1))
-    for p in range(planes):
-        cols = slice(p * span_z, (p + 1) * span_z)
-        plane = jnp.concatenate([along_y[:span_y, cols], along_y[span_y:, cols]], axis=1)
-        values = dot_right(plane, z_table[...])
-        for part in range(2):
-            out[0, part, p] = base[0, part, p] + values[:, part * span_z : (part + 1) * span_z]
+            for p in group
+        ]
+        along_y = dot_left(y_table[...], jnp.concatenate(columns, axis=1))
+        values = dot_right(parts_in_lanes(along_y, span_y, span_z), z_table[...])
+        for i, p in enumerate(group):
+            for part in range(2):
+                out[0, part, p] = base[0, part, p] + (
+                    values[i * span_y : (i + 1) * span_y, part * span_z : (part + 1) * span_z]
+                )
 
 
 def block_rows_of(psi, beta, slots):
@@ -226,13 +247,19 @@
     return jnp.einsum(pattern, left, right, precision=highest, preferred_element_type=jnp.float32)
 
 
+def partner(values, devices, k):
+    return lax.ppermute(values, "ga", [(d, d ^ k) for d in range(devices)])
+
+
 def sum_over(values, devices):
-    if devices & (devices - 1):
+    if devices & (devices - 1) or devices < 4:
         return lax.psum(values, "ga")
-    step = 1
-    while step < devices:
-        values = values + lax.ppermute(values, "ga", [(d, d ^ step) for d in range(devices)])
-        step *= 2
+    step = devices // 4
+    others = [partner(values, devices, k * step) for k in (1, 2, 3)]
+    values = (values + others[0]) + (others[1] + others[2])
+    while step > 1:
+        step //= 2
+        values = values + partner(values, devices, step)
     return values
 
 
@@ -348,6 +375,7 @@
             whole(pot.shape),
             whole(inv_x.shape),
             whole(fwd_x.shape),
+            whole(proj.shape),
         ],
         out_specs=(
             pl.BlockSpec((devices, 2, block_rows, span_z), lambda j: (0, j, 0, 0)),
@@ -356,7 +384,7 @@
         compiler_params=params,
         cost_estimate=cost(4 * 10**9, 8 * 10**6),
         name="real_space",
-    )(arrived, pot, inv_x, fwd_x)
+    )(arrived, pot, inv_x, fwd_x, proj)
     returned = lax.all_to_all(back, "ga", split_axis=0, concat_axis=0, tiled=True)
 
     grams = pl.pallas_call(

time: 201 us -> 210 us (1.045)
  Pallas kernels: 41.7 us -> 50.5 us
  local copies, waits for them, and re-layouts: 13.5 us -> 6.44 us
  other arithmetic: 4.63 us -> 7.5 us
  starting transfers between devices: 18.4 us -> 20.6 us
    ppermute x5 -> x6, waiting for transfers between devices: 72.6 us -> 89.3 us  [partner(): return lax.ppermute(values, 'ga', [(d, d ^ k) for d in range(devices)])]
    all_to_all x1, waiting for transfers between devices: 46.4 us -> 31.8 us  [on_device(): lax.all_to_all(sent, 'ga', split_axis=0, concat_axis=0, tiled=True)]
    unnamed x30 -> x18, local copies, waits for them, and re-layouts: 11.8 us -> 2.5 us
    pallas_call x1, Pallas kernels: 1.76 us -> 3.98 us  [on_device(): pl.pallas_call(functools.partial(real_gram_kernel, bands), out_shape=jax....]
    ppermute x5 -> x6, starting transfers between devices: 6.66 us -> 8.82 us  [partner(): return lax.ppermute(values, 'ga', [(d, d ^ k) for d in range(devices)])]
    pallas_call x1, Pallas kernels: 4.44 us -> 6.58 us  [on_device(): pl.pallas_call(functools.partial(real_space_kernel, devices, rows, planes...]
  transfers between devices with their start and end apart: 7 -> 8, of which waited for: 6 -> 5; matrix products, arithmetic and copies ran while one was open for 5% -> 7% of each run, Pallas kernels for 10% -> 12%
where the time goes in v2:
time: 210 us; the launch traced here: 208 us
  waiting for transfers between devices  121 us (58%)
  Pallas kernels  50.5 us (24%)
  starting transfers between devices  20.6 us (10%)
  other arithmetic  7.5 us (4%)
  local copies, waits for them, and re-layouts  6.44 us (3%)
    ppermute x6, waiting for transfers between devices, partner(): return lax.ppermute(values, 'ga', [(d, d ^ k) for d in range(devices)])  89.3 us
    all_to_all x1, waiting for transfers between devices, on_device(): lax.all_to_all(sent, 'ga', split_axis=0, concat_axis=0, tiled=True)  31.8 us
    pallas_call x1, Pallas kernels, on_device(): pl.pallas_call(functools.partial(to_planes_kernel, devices, rows, planes)...  11.8 us
    pallas_call x1, Pallas kernels, on_device(): pl.pallas_call(functools.partial(base_kernel, slots), out_shape=jax.Shape...  11.2 us
    pallas_call x1, Pallas kernels, on_device(): pl.pallas_call(functools.partial(project_kernel, slots), out_shape=jax.Sh...  10.1 us
    ppermute x6, starting transfers between devices, partner(): return lax.ppermute(values, 'ga', [(d, d ^ k) for d in range(devices)])  8.82 us
    all_to_all x1, starting transfers between devices, on_device(): lax.all_to_all(sent, 'ga', split_axis=0, concat_axis=0, tiled=True)  7.09 us
    pallas_call x1, Pallas kernels, on_device(): pl.pallas_call(functools.partial(to_rows_kernel, devices, rows, planes),...  6.93 us
  transfers between devices with their start and end apart: 8, of which 5 were waited for; matrix products, arithmetic and copies ran while one was open for 7% of the time, Pallas kernels for 12%

profile of v2, /device:TPU:1, one launch (start us, length us, event | category | flops | bytes accessed | tf_op | source)
XLA Modules:
  0.0 208.4 jit_solution(2991070755759854584)
XLA Ops:
  0.6 6.9 %to_rows.1 = f32[32,4,32,128]{3,2,1,0:T(8,128)} custom-call(f32[8,2,4,128,128]{4,3,2,1,0:T(8,128)} %psi.5, bf16[256,768]{1,0:T(8,128)(2,1)} %constant.99.clone.y_table, bf16[768,256]{1,0:T(8,128)(2,1)} %constant.100.clone.z_table), custom_call_target="tpu_custom_call" | custom-call | flops 4000000000 | bytes 6000000 | tf_op jit(solution)/shard_map/to_rows/pallas_call | solution.py:294
  7.6 7.1 %all-to-all-start = ((f32[32,4,32,128]{3,2,1,0:T(8,128)}), f32[32,4,32,128]{3,2,1,0:T(8,128)S(1)}, u32[]{:S(2)}, u32[]{:S(2)}) async-start(f32[32,4,32,128]{3,2,1,0:T(8,128)} %to_rows.1), calls=%async_computation | async-start | bytes 4194304 | tf_op jit(solution)/shard_map/all_to_all | solution.py:308
  14.7 0.3 fusion.11
  15.1 0.1 copy.73
  15.2 0.1 copy.74
  15.4 0.9 copy.82.inverse
  16.4 0.9 add_multiply_fusion.kinetic
  17.3 10.1 %project.1 = f32[8,32,16]{2,1,0:T(8,128)} custom-call(f32[8,2,4,128,128]{4,3,2,1,0:T(8,128)} %psi.5, f32[8,1024,128]{2,1,0:T(8,128)} %bitcast.84, f32[4,128,128]{2,1,0:T(8,128)} %add_multiply_fusion.kinetic), custom_call_target="tpu_custom_call" | custom-call | flops 8000000000 | bytes 8000000 | tf_op jit(solution)/shard_map/project/pallas_call | solution.py:340
  27.4 0.8 fusion.47
  28.4 0.1 copy.76
  28.7 0.3 convolution_bitcast_fusion.1
  29.0 0.7 copy.83._
  29.7 0.7 copy.110
  30.5 0.7 pad_maximum_fusion.2.forward
  31.2 31.8 %all-to-all-done.recv = f32[32,4,32,128]{3,2,1,0:T(8,128)S(1)} async-done(((f32[32,4,32,128]{3,2,1,0:T(8,128)}), f32[32,4,32,128]{3,2,1,0:T(8,128)S(1)}, u32[]{:S(2)}, u32[]{:S(2)}) %all-to-all-start) | async-done | bytes 2097184 | tf_op jit(solution)/shard_map/all_to_all | solution.py:308
  62.9 1.3 copy-done
  64.3 6.6 %real_space.1 = (f32[32,8,32,128]{3,2,1,0:T(8,128)}, f32[8,128,512]{2,1,0:T(8,128)}) custom-call(f32[32,4,32,128]{3,2,1,0:T(8,128)} %copy-done, f32[128,512]{1,0:T(8,128)} %bitcast.74, bf16[256,768]{1,0:T(8,128)(2,1)} %copy.82.inverse, bf16[256,384]{1,0:T(8,128)(2,1)} %pad_maximum_fusion.2.forward, f32[128,16]{1,0:T(8,128)} %copy.83._), custom_call_target="tpu_custom_call" | custom-call | flops 4000000000 | bytes 8000000 | tf_op jit(solution)/shard_map/real_space/pallas_call | solution.py:366
  70.9 4.7 %all-to-all-start.1 = ((f32[32,8,32,128]{3,2,1,0:T(8,128)}), f32[32,8,32,128]{3,2,1,0:T(8,128)}, u32[]{:S(2)}, u32[]{:S(2)}) async-start(f32[32,8,32,128]{3,2,1,0:T(8,128)} %get-tuple-element.4), calls=%async_computation.1 | async-start | bytes 8388608 | tf_op jit(solution)/shard_map/all_to_all | solution.py:388
  75.8 0.1 copy.103
  75.9 4.0 %real_gram.1 = f32[2,8,8,128]{3,2,1,0:T(8,128)} custom-call(f32[8,128,512]{2,1,0:T(8,128)} %get-tuple-element.5.field, f32[128,512]{1,0:T(8,128)} %bitcast.75), custom_call_target="tpu_custom_call" | custom-call | flops 10000000 | bytes 2000000 | tf_op jit(solution)/shard_map/real_gram/pallas_call | solution.py:390
  79.9 0.9 reduce_sum.18
  81.0 2.3 %collective-permute-start.1 = (f32[136,16]{0,1:T(8,128)S(1)}, f32[136,16]{0,1:T(8,128)S(1)}, u32[]{:S(2)}, u32[]{:S(2)}) collective-permute-start(f32[136,16]{0,1:T(8,128)S(1)} %maximum_maximum_fusion), channel_id=1, source_target_pairs={{0,16},{1,17},{2,18},{3,19},{4,20},{5,21},{6,22},{7,23},{8,24},{9,... | collective-permute-start | bytes 26120 | tf_op jit(solution)/shard_map/ppermute | solution.py:251
  83.3 1.2 collective-permute-start.2
  84.5 85.4 %collective-permute-done.1 = f32[136,16]{0,1:T(8,128)S(1)} collective-permute-done((f32[136,16]{0,1:T(8,128)S(1)}, f32[136,16]{0,1:T(8,128)S(1)}, u32[]{:S(2)}, u32[]{:S(2)}) %collective-permute-start.1) | collective-permute-done | bytes 8736 | tf_op jit(solution)/shard_map/ppermute | solution.py:251
  170.0 1.0 collective-permute-start.3
  171.0 1.6 collective-permute-done.3
  172.6 1.0 collective-permute-start.4
  173.6 1.6 collective-permute-done.4
  175.2 3.2 %collective-permute-start.5 = (f32[136,16]{0,1:T(8,128)S(1)}, f32[136,16]{0,1:T(8,128)S(1)}, u32[]{:S(2)}, u32[]{:S(2)}) collective-permute-start(f32[136,16]{0,1:T(8,128)S(1)} %add.136), channel_id=1, source_target_pairs={{0,1},{1,0},{2,3},{3,2},{4,5},{5,4},{6,7},{7,6},{8,9},{9,8},{10,11... | collective-permute-start | bytes 26120 | tf_op jit(solution)/shard_map/ppermute | solution.py:251
  178.6 0.1 mul.102
  178.7 0.6 collective-permute-done.5
  179.4 0.7 cholesky.16
  180.1 0.6 compare_reduce_fusion
  180.8 0.6 fusion.19
  181.4 0.6 custom-call.10
  182.1 0.1 fusion.30
  182.2 0.1 fusion.34
  182.3 0.1 convolution_subtract_fusion
  182.5 0.1 fusion.20
  182.6 0.2 fusion.14
  182.8 0.1 fusion.22
  183.3 0.2 copy.97
  183.6 0.2 convolution_bitcast_fusion
  183.9 0.1 copy.98
  184.0 0.6 pad_maximum_fusion.8
  184.7 0.7 pad_maximum_fusion.6.coefs
  185.4 11.2 %base.1 = f32[8,2,4,128,128]{4,3,2,1,0:T(8,128)} custom-call(f32[8,2,4,128,128]{4,3,2,1,0:T(8,128)} %psi.5, f32[8,1024,128]{2,1,0:T(8,128)} %bitcast.85, f32[4,128,128]{2,1,0:T(8,128)} %add_multiply_fusion.kinetic, f32[8,16,32]{2,1,0:T(8,128)} %pad_maximum_fusion.6.coefs), custom_call_target="tpu_custom_call" | custom-call | flops 8000000000 | bytes 12000000 | tf_op jit(solution)/shard_map/base/pallas_call | solution.py:427
  196.6 11.8 %to_planes.1 = f32[8,2,4,128,128]{4,3,2,1,0:T(8,128)} custom-call(f32[32,8,32,128]{3,2,1,0:T(8,128)} %all-to-all-done.1.recv, f32[8,2,4,128,128]{4,3,2,1,0:T(8,128)} %base.1, bf16[256,768]{1,0:T(8,128)(2,1)} %constant.101.clone.y_table, bf16[768,256]{1,0:T(8,128)(2,1)} %constant.102.clone.z_table), custom_call_target="tpu_custom_call" | custom-call | flops 8000000000 | bytes 12000000 | tf_op jit(solution)/shard_map/to_planes/pallas_call | solution.py:440
  (60 shorter events, 1.9 us)
Async XLA Ops:
  7.6 7.1 %copy-start.4 = (s32[128]{0:T(128)S(1)}, s32[128]{0:T(128)}, u32[]{:S(2)}) copy-start(s32[128]{0:T(128)} %param.11) | copy-start | bytes 1540
  7.6 55.4 %all-to-all-start = ((f32[32,4,32,128]{3,2,1,0:T(8,128)}), f32[32,4,32,128]{3,2,1,0:T(8,128)S(1)}, u32[]{:S(2)}, u32[]{:S(2)}) async-start(f32[32,4,32,128]{3,2,1,0:T(8,128)} %to_rows.1), calls=%async_computation | async-start | bytes 4194304 | tf_op jit(solution)/shard_map/all_to_all | solution.py:308
  17.3 11.4 %copy-start.5 = (s32[8,8]{1,0:T(8,128)S(1)}, s32[8,8]{1,0:T(8,128)}, u32[]{:S(2)}) copy-start(s32[8,8]{1,0:T(8,128)} %param.14) | copy-start | bytes 772
  17.3 12.4 %copy-start.1 = (f32[128,4,128]{2,1,0:T(4,128)S(1)}, f32[128,4,128]{2,1,0:T(4,128)}, u32[]{:S(2)}) copy-start(f32[128,4,128]{2,1,0:T(4,128)} %param.12) | copy-start | bytes 786436
  62.9 1.3 copy-start
  70.9 4.7 %copy-start.2 = (f32[8,32,16]{2,1,0:T(8,128)S(1)}, f32[8,32,16]{2,1,0:T(8,128)}, u32[]{:S(2)}) copy-start(f32[8,32,16]{2,1,0:T(8,128)} %project.1) | copy-start | bytes 49156
  70.9 107.6 %copy-start.3 = (f32[32,4]{0,1:T(4,128)S(1)}, f32[32,4]{0,1:T(4,128)}, u32[]{:S(2)}) copy-start(f32[32,4]{0,1:T(4,128)} %param.15) | copy-start | bytes 1540
  70.9 125.7 %all-to-all-start.1 = ((f32[32,8,32,128]{3,2,1,0:T(8,128)}), f32[32,8,32,128]{3,2,1,0:T(8,128)}, u32[]{:S(2)}, u32[]{:S(2)}) async-start(f32[32,8,32,128]{3,2,1,0:T(8,128)} %get-tuple-element.4), calls=%async_computation.1 | async-start | bytes 8388608 | tf_op jit(solution)/shard_map/all_to_all | solution.py:388
  81.0 89.0 %collective-permute-start.1 = (f32[136,16]{0,1:T(8,128)S(1)}, f32[136,16]{0,1:T(8,128)S(1)}, u32[]{:S(2)}, u32[]{:S(2)}) collective-permute-start(f32[136,16]{0,1:T(8,128)S(1)} %maximum_maximum_fusion), channel_id=1, source_target_pairs={{0,16},{1,17},{2,18},{3,19},{4,20},{5,21},{6,22},{7,23},{8,24},{9,... | collective-permute-start | bytes 26120 | tf_op jit(solution)/shard_map/ppermute | solution.py:251
  83.3 86.6 %collective-permute-start.2 = (f32[136,16]{0,1:T(8,128)S(1)}, f32[136,16]{0,1:T(8,128)S(1)}, u32[]{:S(2)}, u32[]{:S(2)}) collective-permute-start(f32[136,16]{0,1:T(8,128)S(1)} %maximum_maximum_fusion), channel_id=1, source_target_pairs={{0,24},{1,25},{2,26},{3,27},{4,28},{5,29},{6,30},{7,31},{8,16},{9,... | collective-permute-start | bytes 26120 | tf_op jit(solution)/shard_map/ppermute | solution.py:251
  84.5 85.5 %collective-permute-start = (f32[136,16]{0,1:T(8,128)S(1)}, f32[136,16]{0,1:T(8,128)S(1)}, u32[]{:S(2)}, u32[]{:S(2)}) collective-permute-start(f32[136,16]{0,1:T(8,128)S(1)} %maximum_maximum_fusion), channel_id=1, source_target_pairs={{0,8},{1,9},{2,10},{3,11},{4,12},{5,13},{6,14},{7,15},{8,0},{9,1},... | collective-permute-start | bytes 26120 | tf_op jit(solution)/shard_map/ppermute | solution.py:251
  170.0 2.7 %collective-permute-start.3 = (f32[136,16]{0,1:T(8,128)S(1)}, f32[136,16]{0,1:T(8,128)S(1)}, u32[]{:S(2)}, u32[]{:S(2)}) collective-permute-start(f32[136,16]{0,1:T(8,128)S(1)} %add_add_fusion), channel_id=1, source_target_pairs={{0,4},{1,5},{2,6},{3,7},{4,0},{5,1},{6,2},{7,3},{8,12},{9,13},{10,... | collective-permute-start | bytes 26120 | tf_op jit(solution)/shard_map/ppermute | solution.py:251
  172.6 2.6 %collective-permute-start.4 = (f32[136,16]{0,1:T(8,128)S(1)}, f32[136,16]{0,1:T(8,128)S(1)}, u32[]{:S(2)}, u32[]{:S(2)}) collective-permute-start(f32[136,16]{0,1:T(8,128)S(1)} %add.135), channel_id=1, source_target_pairs={{0,2},{1,3},{2,0},{3,1},{4,6},{5,7},{6,4},{7,5},{8,10},{9,11},{10,... | collective-permute-start | bytes 26120 | tf_op jit(solution)/shard_map/ppermute | solution.py:251
  175.2 4.1 %collective-permute-start.5 = (f32[136,16]{0,1:T(8,128)S(1)}, f32[136,16]{0,1:T(8,128)S(1)}, u32[]{:S(2)}, u32[]{:S(2)}) collective-permute-start(f32[136,16]{0,1:T(8,128)S(1)} %add.136), channel_id=1, source_target_pairs={{0,1},{1,0},{2,3},{3,2},{4,5},{5,4},{6,7},{7,6},{8,9},{9,8},{10,11... | collective-permute-start | bytes 26120 | tf_op jit(solution)/shard_map/ppermute | solution.py:251

commit v3 on v2

--- a/solution.py
+++ b/solution.py
@@ -138,13 +138,15 @@
                 back[:, band, r * block : (r + 1) * block] = cols.reshape(devices, block, span_z)
 
 
-def real_gram_kernel(bands, field, pot, out):
+def real_gram_kernel(bands, *refs):
+    fields, (pot, out) = refs[:-2], refs[-2:]
+    held = fields[0].shape[0]
     pairs = [(a, b) for a in range(bands) for b in range(a, bands)]
     for weighted in range(2):
 
         def step(i, sums):
             rows = pl.ds(pl.multiple_of(i * 8, 8), 8)
-            values = [field[a, rows, :] for a in range(bands)]
+            values = [fields[a // held][a % held, rows, :] for a in range(bands)]
             other = [v * pot[rows, :] for v in values] if weighted else values
             result = []
             for (a, b), total in zip(pairs, sums):
@@ -254,13 +256,12 @@
 def sum_over(values, devices):
     if devices & (devices - 1) or devices < 4:
         return lax.psum(values, "ga")
-    step = devices // 4
+    step = 1
+    while step < devices // 4:
+        values = values + partner(values, devices, step)
+        step *= 2
     others = [partner(values, devices, k * step) for k in (1, 2, 3)]
-    values = (values + others[0]) + (others[1] + others[2])
-    while step > 1:
-        step //= 2
-        values = values + partner(values, devices, step)
-    return values
+    return (values + others[0]) + (others[1] + others[2])
 
 
 def on_device(devices, orbitals, plane_order, potential, projectors, slot_owner, strengths):
@@ -363,29 +364,36 @@
     kin = jnp.sum(products[:, 2 * slots :], axis=0).reshape(bands, 2, bands, 2)
     kin = kin[:, 0, :, 0] + kin[:, 1, :, 1]
 
-    back, field = pl.pallas_call(
-        functools.partial(real_space_kernel, devices, rows, planes),
-        out_shape=(
-            jax.ShapeDtypeStruct((devices, bands, block_rows, span_z), f32),
-            jax.ShapeDtypeStruct((bands, span_x, lanes), f32),
-        ),
-        grid=(pairs,),
-        in_specs=[
-            pl.BlockSpec((devices, None, block_rows, span_z), lambda j: (0, j, 0, 0)),
-            whole(pot.shape),
-            whole(inv_x.shape),
-            whole(fwd_x.shape),
-            whole(proj.shape),
-        ],
-        out_specs=(
-            pl.BlockSpec((devices, 2, block_rows, span_z), lambda j: (0, j, 0, 0)),
-            pl.BlockSpec((2, span_x, lanes), lambda j: (j, 0, 0)),
-        ),
-        compiler_params=params,
-        cost_estimate=cost(4 * 10**9, 8 * 10**6),
-        name="real_space",
-    )(arrived, pot, inv_x, fwd_x, proj)
-    returned = lax.all_to_all(back, "ga", split_axis=0, concat_axis=0, tiled=True)
+    parts = 2 if pairs % 2 == 0 else 1
+    share = pairs // parts
+    returned, fields = [], []
+    for c in range(parts):
+        back, field = pl.pallas_call(
+            functools.partial(real_space_kernel, devices, rows, planes),
+            out_shape=(
+                jax.ShapeDtypeStruct((devices, 2 * share, block_rows, span_z), f32),
+                jax.ShapeDtypeStruct((2 * share, span_x, lanes), f32),
+            ),
+            grid=(share,),
+            in_specs=[
+                pl.BlockSpec(
+                    (devices, None, block_rows, span_z), lambda j, c=c: (0, c * share + j, 0, 0)
+                ),
+                whole(pot.shape),
+                whole(inv_x.shape),
+                whole(fwd_x.shape),
+                whole(proj.shape),
+            ],
+            out_specs=(
+                pl.BlockSpec((devices, 2, block_rows, span_z), lambda j: (0, j, 0, 0)),
+                pl.BlockSpec((2, span_x, lanes), lambda j: (j, 0, 0)),
+            ),
+            compiler_params=params,
+            cost_estimate=cost(4 * 10**9, 8 * 10**6),
+            name="real_space",
+        )(arrived, pot, inv_x, fwd_x, proj)
+        returned.append(lax.all_to_all(back, "ga", split_axis=0, concat_axis=0, tiled=True))
+        fields.append(field)
 
     grams = pl.pallas_call(
         functools.partial(real_gram_kernel, bands),
@@ -393,7 +401,7 @@
         compiler_params=params,
         cost_estimate=cost(10**7, 2 * 10**6),
         name="real_gram",
-    )(field, pot)
+    )(*fields, pot)
     grams = jnp.sum(grams, axis=-1)
     own = jnp.concatenate([proj, jnp.concatenate([grams[0], grams[1] + kin], axis=1)], axis=0)
     total = sum_over(own, devices)
@@ -436,22 +444,27 @@
         name="base",
     )(orbitals, beta, kinetic, coefs)
 
-    one_band = pl.BlockSpec((1, 2, planes, span_y, span_z), lambda b: (b, 0, 0, 0, 0))
-    residual = pl.pallas_call(
-        functools.partial(to_planes_kernel, devices, rows, planes),
-        out_shape=jax.ShapeDtypeStruct(orbitals.shape, f32),
-        grid=(bands,),
-        in_specs=[
-            pl.BlockSpec((devices, None, block_rows, span_z), lambda b: (0, b, 0, 0)),
-            one_band,
-            whole(fwd_y.shape),
-            whole(fwd_z.shape),
-        ],
-        out_specs=one_band,
-        compiler_params=params,
-        cost_estimate=cost(8 * 10**9, 12 * 10**6),
-        name="to_planes",
-    )(returned, base, fwd_y, fwd_z)
+    residual = base
+    for c in range(parts):
+        one_band = pl.BlockSpec(
+            (1, 2, planes, span_y, span_z), lambda b, c=c: (2 * share * c + b, 0, 0, 0, 0)
+        )
+        residual = pl.pallas_call(
+            functools.partial(to_planes_kernel, devices, rows, planes),
+            out_shape=jax.ShapeDtypeStruct(orbitals.shape, f32),
+            grid=(2 * share,),
+            in_specs=[
+                pl.BlockSpec((devices, None, block_rows, span_z), lambda b: (0, b, 0, 0)),
+                one_band,
+                whole(fwd_y.shape),
+                whole(fwd_z.shape),
+            ],
+            out_specs=one_band,
+            input_output_aliases={1: 0},
+            compiler_params=params,
+            cost_estimate=cost(8 * 10**9, 12 * 10**6),
+            name="to_planes",
+        )(returned[c], residual, fwd_y, fwd_z)
     return (residual, jnp.stack([m_real, m_imag]))
 
 

time: 210 us -> 188 us (0.90)
  waiting for transfers between devices: 121 us -> 91.3 us
  Pallas kernels: 50.5 us -> 54.1 us
  starting transfers between devices: 20.6 us -> 22.8 us
    ppermute x6, waiting for transfers between devices: 89.3 us -> 33.5 us  [partner(): return lax.ppermute(values, 'ga', [(d, d ^ k) for d in range(devices)])]
    all_to_all x1 -> x2, waiting for transfers between devices: 0.01 us -> 26.1 us  [on_device(): lax.all_to_all(back, 'ga', split_axis=0, concat_axis=0, tiled=True)]
    all_to_all x1 -> x2, starting transfers between devices: 4.68 us -> 9.29 us  [on_device(): lax.all_to_all(back, 'ga', split_axis=0, concat_axis=0, tiled=True)]
    ppermute x6, starting transfers between devices: 8.82 us -> 6.4 us  [partner(): return lax.ppermute(values, 'ga', [(d, d ^ k) for d in range(devices)])]
    pallas_call x1 -> x2, Pallas kernels: 11.8 us -> 13.6 us  [on_device(): pl.pallas_call(functools.partial(to_planes_kernel, devices, rows, planes)...]
    pallas_call x1 -> x2, Pallas kernels: 6.58 us -> 8.36 us  [on_device(): pl.pallas_call(functools.partial(real_space_kernel, devices, rows, planes...]
  transfers between devices with their start and end apart: 8 -> 9, of which waited for: 5 -> 7; matrix products, arithmetic and copies ran while one was open for 7% -> 7% of each run, Pallas kernels for 12% -> 19%
where the time goes in v3:
time: 188 us; the launch traced here: 186 us
  waiting for transfers between devices  91.3 us (49%)
  Pallas kernels  54.1 us (29%)
  starting transfers between devices  22.8 us (12%)
  local copies, waits for them, and re-layouts  7.77 us (4%)
  other arithmetic  7.5 us (4%)
    ppermute x6, waiting for transfers between devices, partner(): return lax.ppermute(values, 'ga', [(d, d ^ k) for d in range(devices)])  33.5 us
    all_to_all x1, waiting for transfers between devices, on_device(): lax.all_to_all(sent, 'ga', split_axis=0, concat_axis=0, tiled=True)  31.7 us
    all_to_all x2, waiting for transfers between devices, on_device(): lax.all_to_all(back, 'ga', split_axis=0, concat_axis=0, tiled=True)  26.1 us
    pallas_call x2, Pallas kernels, on_device(): pl.pallas_call(functools.partial(to_planes_kernel, devices, rows, planes)...  13.6 us
    pallas_call x1, Pallas kernels, on_device(): pl.pallas_call(functools.partial(base_kernel, slots), out_shape=jax.Shape...  11.2 us
    pallas_call x1, Pallas kernels, on_device(): pl.pallas_call(functools.partial(project_kernel, slots), out_shape=jax.Sh...  10.1 us
    all_to_all x2, starting transfers between devices, on_device(): lax.all_to_all(back, 'ga', split_axis=0, concat_axis=0, tiled=True)  9.29 us
    pallas_call x2, Pallas kernels, on_device(): pl.pallas_call(functools.partial(real_space_kernel, devices, rows, planes...  8.36 us
  transfers between devices with their start and end apart: 9, of which 7 were waited for; matrix products, arithmetic and copies ran while one was open for 7% of the time, Pallas kernels for 19%

profile of v3, /device:TPU:1, one launch (start us, length us, event | category | flops | bytes accessed | tf_op | source)
XLA Modules:
  0.0 185.7 jit_solution(12851927236102293633)
XLA Ops:
  0.6 6.9 %to_rows.1 = f32[32,4,32,128]{3,2,1,0:T(8,128)} custom-call(f32[8,2,4,128,128]{4,3,2,1,0:T(8,128)} %psi.5, bf16[256,768]{1,0:T(8,128)(2,1)} %constant.99.clone.y_table, bf16[768,256]{1,0:T(8,128)(2,1)} %constant.100.clone.z_table), custom_call_target="tpu_custom_call" | custom-call | flops 4000000000 | bytes 6000000 | tf_op jit(solution)/shard_map/to_rows/pallas_call | solution.py:295
  7.6 7.1 %all-to-all-start = ((f32[32,4,32,128]{3,2,1,0:T(8,128)}), f32[32,4,32,128]{3,2,1,0:T(8,128)S(1)}, u32[]{:S(2)}, u32[]{:S(2)}) async-start(f32[32,4,32,128]{3,2,1,0:T(8,128)} %to_rows.1), calls=%async_computation | async-start | bytes 4194304 | tf_op jit(solution)/shard_map/all_to_all | solution.py:309
  14.7 0.3 fusion.11
  15.4 0.9 copy.90.inverse
  16.4 0.9 add_multiply_fusion.kinetic
  17.3 10.1 %project.1 = f32[8,32,16]{2,1,0:T(8,128)} custom-call(f32[8,2,4,128,128]{4,3,2,1,0:T(8,128)} %psi.5, f32[8,1024,128]{2,1,0:T(8,128)} %bitcast.85, f32[4,128,128]{2,1,0:T(8,128)} %add_multiply_fusion.kinetic), custom_call_target="tpu_custom_call" | custom-call | flops 8000000000 | bytes 8000000 | tf_op jit(solution)/shard_map/project/pallas_call | solution.py:341
  27.4 0.8 fusion.48
  28.7 0.3 convolution_bitcast_fusion.1
  29.0 0.7 copy.91._
  29.7 0.7 copy.120
  30.5 0.7 pad_maximum_fusion.2.forward
  31.2 31.7 %all-to-all-done.recv = f32[32,4,32,128]{3,2,1,0:T(8,128)S(1)} async-done(((f32[32,4,32,128]{3,2,1,0:T(8,128)}), f32[32,4,32,128]{3,2,1,0:T(8,128)S(1)}, u32[]{:S(2)}, u32[]{:S(2)}) %all-to-all-start) | async-done | bytes 2097184 | tf_op jit(solution)/shard_map/all_to_all | solution.py:309
  62.9 1.3 copy-done.1
  64.3 4.2 %real_space.3 = (f32[32,4,32,128]{3,2,1,0:T(8,128)}, f32[4,128,512]{2,1,0:T(8,128)}) custom-call(f32[32,4,32,128]{3,2,1,0:T(8,128)} %copy-done.1, f32[128,512]{1,0:T(8,128)} %bitcast.74, bf16[256,768]{1,0:T(8,128)(2,1)} %copy.90.inverse, bf16[256,384]{1,0:T(8,128)(2,1)} %pad_maximum_fusion.2.forward, f32[128,16]{1,0:T(8,128)} %copy.91._), custom_call_target="tpu_custom_call" | custom-call | flops 4000000000 | bytes 8000000 | tf_op jit(solution)/shard_map/real_space/pallas_call | solution.py:371
  68.5 4.6 %all-to-all-start.2 = ((f32[32,4,32,128]{3,2,1,0:T(8,128)}), f32[32,4,32,128]{3,2,1,0:T(8,128)S(1)}, u32[]{:S(2)}, u32[]{:S(2)}) async-start(f32[32,4,32,128]{3,2,1,0:T(8,128)} %get-tuple-element.7), calls=%async_computation.2 | async-start | bytes 4194304 | tf_op jit(solution)/shard_map/all_to_all | solution.py:395
  73.3 0.1 copy.113
  73.4 4.2 %real_space.2 = (f32[32,4,32,128]{3,2,1,0:T(8,128)}, f32[4,128,512]{2,1,0:T(8,128)}) custom-call(f32[32,4,32,128]{3,2,1,0:T(8,128)} %copy-done.1, f32[128,512]{1,0:T(8,128)} %bitcast.75, bf16[256,768]{1,0:T(8,128)(2,1)} %copy.90.inverse, bf16[256,384]{1,0:T(8,128)(2,1)} %pad_maximum_fusion.2.forward, f32[128,16]{1,0:T(8,128)} %copy.91._), custom_call_target="tpu_custom_call" | custom-call | flops 4000000000 | bytes 8000000 | tf_op jit(solution)/shard_map/real_space/pallas_call | solution.py:371
  77.6 4.0 %real_gram.1 = f32[2,8,8,128]{3,2,1,0:T(8,128)} custom-call(f32[4,128,512]{2,1,0:T(8,128)} %get-tuple-element.8.refs_0_, f32[4,128,512]{2,1,0:T(8,128)} %get-tuple-element.9.refs_1_, f32[128,512]{1,0:T(8,128)} %bitcast.76), custom_call_target="tpu_custom_call" | custom-call | flops 10000000 | bytes 2000000 | tf_op jit(solution)/shard_map/real_gram/pallas_call | solution.py:398
  81.5 0.9 reduce_sum.18
  82.6 0.3 collective-permute-start
  83.0 0.9 collective-permute-done
  83.9 1.4 collective-permute-start.1
  85.3 3.7 %collective-permute-done.1 = f32[136,16]{0,1:T(8,128)S(1)} collective-permute-done((f32[136,16]{0,1:T(8,128)S(1)}, f32[136,16]{0,1:T(8,128)S(1)}, u32[]{:S(2)}, u32[]{:S(2)}) %collective-permute-start.1) | collective-permute-done | bytes 8736 | tf_op jit(solution)/shard_map/ppermute | solution.py:253
  89.0 3.1 %collective-permute-done.2 = f32[136,16]{0,1:T(8,128)S(1)} collective-permute-done((f32[136,16]{0,1:T(8,128)S(1)}, f32[136,16]{0,1:T(8,128)S(1)}, u32[]{:S(2)}, u32[]{:S(2)}) %collective-permute-start.2) | collective-permute-done | bytes 8736 | tf_op jit(solution)/shard_map/ppermute | solution.py:253
  92.1 4.3 %collective-permute-start.5 = (f32[136,16]{0,1:T(8,128)S(1)}, f32[136,16]{0,1:T(8,128)S(1)}, u32[]{:S(2)}, u32[]{:S(2)}) collective-permute-start(f32[136,16]{0,1:T(8,128)S(1)} %add.134), channel_id=1, source_target_pairs={{0,24},{1,25},{2,26},{3,27},{4,28},{5,29},{6,30},{7,31},{8,16},{9,... | collective-permute-start | bytes 26120 | tf_op jit(solution)/shard_map/ppermute | solution.py:253
  96.5 0.4 collective-permute-start.3
  97.0 14.2 %collective-permute-done.5 = f32[136,16]{0,1:T(8,128)S(1)} collective-permute-done((f32[136,16]{0,1:T(8,128)S(1)}, f32[136,16]{0,1:T(8,128)S(1)}, u32[]{:S(2)}, u32[]{:S(2)}) %collective-permute-start.5) | collective-permute-done | bytes 8736 | tf_op jit(solution)/shard_map/ppermute | solution.py:253
  111.2 11.6 %collective-permute-done.4 = f32[136,16]{0,1:T(8,128)S(1)} collective-permute-done((f32[136,16]{0,1:T(8,128)S(1)}, f32[136,16]{0,1:T(8,128)S(1)}, u32[]{:S(2)}, u32[]{:S(2)}) %collective-permute-start.4) | collective-permute-done | bytes 8736 | tf_op jit(solution)/shard_map/ppermute | solution.py:253
  122.9 0.7 cholesky.16
  123.6 0.6 compare_reduce_fusion
  124.3 0.1 fusion.30
  124.4 0.1 fusion.34
  124.6 1.3 copy-done
  125.9 4.7 %all-to-all-start.1 = ((f32[32,4,32,128]{3,2,1,0:T(8,128)}), f32[32,4,32,128]{3,2,1,0:T(8,128)}, u32[]{:S(2)}, u32[]{:S(2)}) async-start(f32[32,4,32,128]{3,2,1,0:T(8,128)} %get-tuple-element.6), calls=%async_computation.1 | async-start | bytes 4194304 | tf_op jit(solution)/shard_map/all_to_all | solution.py:395
  130.6 0.7 fusion.19
  131.3 0.6 custom-call.10
  131.9 0.1 convolution_subtract_fusion
  132.0 0.1 fusion.20
  132.1 0.2 fusion.14
  132.3 0.1 fusion.22
  132.9 0.2 copy.107
  133.1 0.2 convolution_bitcast_fusion
  133.6 0.6 pad_maximum_fusion.8
  134.2 0.7 pad_maximum_fusion.6.coefs
  134.9 11.2 %base.1 = f32[8,2,4,128,128]{4,3,2,1,0:T(8,128)} custom-call(f32[8,2,4,128,128]{4,3,2,1,0:T(8,128)} %psi.5, f32[8,1024,128]{2,1,0:T(8,128)} %bitcast.86, f32[4,128,128]{2,1,0:T(8,128)} %add_multiply_fusion.kinetic, f32[8,16,32]{2,1,0:T(8,128)} %pad_maximum_fusion.6.coefs), custom_call_target="tpu_custom_call" | custom-call | flops 8000000000 | bytes 12000000 | tf_op jit(solution)/shard_map/base/pallas_call | solution.py:435
  146.1 6.8 %to_planes.2.base = f32[8,2,4,128,128]{4,3,2,1,0:T(8,128)} custom-call(f32[32,4,32,128]{3,2,1,0:T(8,128)} %copy-done, f32[8,2,4,128,128]{4,3,2,1,0:T(8,128)} %base.1, bf16[256,768]{1,0:T(8,128)(2,1)} %constant.101.clone.y_table, bf16[768,256]{1,0:T(8,128)(2,1)} %constant.102.clone.z_table), custom_call_target="tpu_custom_call", output_to_operand_aliasing={{}: (1, {})} | custom-call | flops 8000000000 | bytes 12000000 | tf_op jit(solution)/shard_map/to_planes/pallas_call | solution.py:452
  152.9 26.1 %all-to-all-done.1.recv = f32[32,4,32,128]{3,2,1,0:T(8,128)} async-done(((f32[32,4,32,128]{3,2,1,0:T(8,128)}), f32[32,4,32,128]{3,2,1,0:T(8,128)}, u32[]{:S(2)}, u32[]{:S(2)}) %all-to-all-start.1) | async-done | bytes 2097184 | tf_op jit(solution)/shard_map/all_to_all | solution.py:395
  178.9 6.8 %to_planes.3 = f32[8,2,4,128,128]{4,3,2,1,0:T(8,128)} custom-call(f32[32,4,32,128]{3,2,1,0:T(8,128)} %all-to-all-done.1.recv, f32[8,2,4,128,128]{4,3,2,1,0:T(8,128)} %to_planes.2.base, bf16[256,768]{1,0:T(8,128)(2,1)} %constant.101.clone.y_table, bf16[768,256]{1,0:T(8,128)(2,1)} %constant.102.clone.z_table), custom_call_target="tpu_custom_call", output_to_operand_aliasing={{}: (1, {})} | custom-call | flops 8000000000 | bytes 12000000 | tf_op jit(solution)/shard_map/to_planes/pallas_call | solution.py:452
  (66 shorter events, 2.4 us)
Async XLA Ops:
  7.6 7.1 %copy-start.5 = (s32[128]{0:T(128)S(1)}, s32[128]{0:T(128)}, u32[]{:S(2)}) copy-start(s32[128]{0:T(128)} %param.11) | copy-start | bytes 1540
  7.6 55.4 %all-to-all-start = ((f32[32,4,32,128]{3,2,1,0:T(8,128)}), f32[32,4,32,128]{3,2,1,0:T(8,128)S(1)}, u32[]{:S(2)}, u32[]{:S(2)}) async-start(f32[32,4,32,128]{3,2,1,0:T(8,128)} %to_rows.1), calls=%async_computation | async-start | bytes 4194304 | tf_op jit(solution)/shard_map/all_to_all | solution.py:309
  17.3 11.4 %copy-start.6 = (s32[8,8]{1,0:T(8,128)S(1)}, s32[8,8]{1,0:T(8,128)}, u32[]{:S(2)}) copy-start(s32[8,8]{1,0:T(8,128)} %param.14) | copy-start | bytes 772
  17.3 12.4 %copy-start.2 = (f32[128,4,128]{2,1,0:T(4,128)S(1)}, f32[128,4,128]{2,1,0:T(4,128)}, u32[]{:S(2)}) copy-start(f32[128,4,128]{2,1,0:T(4,128)} %param.12) | copy-start | bytes 786436
  62.9 1.3 copy-start.1
  68.5 4.6 %copy-start.3 = (f32[8,32,16]{2,1,0:T(8,128)S(1)}, f32[8,32,16]{2,1,0:T(8,128)}, u32[]{:S(2)}) copy-start(f32[8,32,16]{2,1,0:T(8,128)} %project.1) | copy-start | bytes 49156
  68.5 56.1 %all-to-all-start.2 = ((f32[32,4,32,128]{3,2,1,0:T(8,128)}), f32[32,4,32,128]{3,2,1,0:T(8,128)S(1)}, u32[]{:S(2)}, u32[]{:S(2)}) async-start(f32[32,4,32,128]{3,2,1,0:T(8,128)} %get-tuple-element.7), calls=%async_computation.2 | async-start | bytes 4194304 | tf_op jit(solution)/shard_map/all_to_all | solution.py:395
  77.6 19.2 %copy-start.4 = (f32[32,4]{0,1:T(4,128)S(1)}, f32[32,4]{0,1:T(4,128)}, u32[]{:S(2)}) copy-start(f32[32,4]{0,1:T(4,128)} %param.15) | copy-start | bytes 1540
  82.6 1.2 collective-permute-start
  83.9 5.1 %collective-permute-start.1 = (f32[136,16]{0,1:T(8,128)S(1)}, f32[136,16]{0,1:T(8,128)S(1)}, u32[]{:S(2)}, u32[]{:S(2)}) collective-permute-start(f32[136,16]{0,1:T(8,128)S(1)} %fusion.47), channel_id=1, source_target_pairs={{0,2},{1,3},{2,0},{3,1},{4,6},{5,7},{6,4},{7,5},{8,10},{9,11},{10,... | collective-permute-start | bytes 26120 | tf_op jit(solution)/shard_map/ppermute | solution.py:253
  89.0 3.1 %collective-permute-start.2 = (f32[136,16]{0,1:T(8,128)S(1)}, f32[136,16]{0,1:T(8,128)S(1)}, u32[]{:S(2)}, u32[]{:S(2)}) collective-permute-start(f32[136,16]{0,1:T(8,128)S(1)} %add.133), channel_id=1, source_target_pairs={{0,4},{1,5},{2,6},{3,7},{4,0},{5,1},{6,2},{7,3},{8,12},{9,13},{10,... | collective-permute-start | bytes 26120 | tf_op jit(solution)/shard_map/ppermute | solution.py:253
  92.1 19.1 %collective-permute-start.5 = (f32[136,16]{0,1:T(8,128)S(1)}, f32[136,16]{0,1:T(8,128)S(1)}, u32[]{:S(2)}, u32[]{:S(2)}) collective-permute-start(f32[136,16]{0,1:T(8,128)S(1)} %add.134), channel_id=1, source_target_pairs={{0,24},{1,25},{2,26},{3,27},{4,28},{5,29},{6,30},{7,31},{8,16},{9,... | collective-permute-start | bytes 26120 | tf_op jit(solution)/shard_map/ppermute | solution.py:253
  96.5 26.3 %collective-permute-start.4 = (f32[136,16]{0,1:T(8,128)S(1)}, f32[136,16]{0,1:T(8,128)S(1)}, u32[]{:S(2)}, u32[]{:S(2)}) collective-permute-start(f32[136,16]{0,1:T(8,128)S(1)} %add.134), channel_id=1, source_target_pairs={{0,16},{1,17},{2,18},{3,19},{4,20},{5,21},{6,22},{7,23},{8,24},{9,... | collective-permute-start | bytes 26120 | tf_op jit(solution)/shard_map/ppermute | solution.py:253
  96.5 26.3 %collective-permute-start.3 = (f32[136,16]{0,1:T(8,128)S(1)}, f32[136,16]{0,1:T(8,128)S(1)}, u32[]{:S(2)}, u32[]{:S(2)}) collective-permute-start(f32[136,16]{0,1:T(8,128)S(1)} %add.134), channel_id=1, source_target_pairs={{0,8},{1,9},{2,10},{3,11},{4,12},{5,13},{6,14},{7,15},{8,0},{9,1},... | collective-permute-start | bytes 26120 | tf_op jit(solution)/shard_map/ppermute | solution.py:253
  124.6 1.4 copy-start
  125.9 53.0 %all-to-all-start.1 = ((f32[32,4,32,128]{3,2,1,0:T(8,128)}), f32[32,4,32,128]{3,2,1,0:T(8,128)}, u32[]{:S(2)}, u32[]{:S(2)}) async-start(f32[32,4,32,128]{3,2,1,0:T(8,128)} %get-tuple-element.6), calls=%async_computation.1 | async-start | bytes 4194304 | tf_op jit(solution)/shard_map/all_to_all | solution.py:395

commit v4 on v3

--- a/solution.py
+++ b/solution.py
@@ -12,7 +12,7 @@
 highest = lax.Precision.HIGHEST
 f32 = jnp.float32
 bf16 = jnp.bfloat16
-vmem_limit = 60 * 1024 * 1024
+vmem_limit = 63 * 1024 * 1024
 
 
 def signed_index(values, length):
@@ -26,12 +26,8 @@
     return np.cos(angles) * factor, orient * np.sin(angles) * factor
 
 
-def left_table(length, orient, row_order=None, col_order=None):
+def left_table(length, orient):
     cosine, sine = dft(length, orient)
-    if row_order is not None:
-        cosine, sine = cosine[row_order], sine[row_order]
-    if col_order is not None:
-        cosine, sine = cosine[:, col_order], sine[:, col_order]
     return np.block([[cosine, -sine], [sine, cosine]])
 
 
@@ -101,41 +97,57 @@
     )
 
 
-def to_rows_kernel(devices, rows, planes, psi, y_table, z_table, out):
-    span_y, span_z = psi.shape[3], psi.shape[4]
-    flat = out.reshape(devices * 2 * planes * rows, span_z)
+def to_rows_kernel(psi, y_table, out):
+    _, _, planes, span_y, span_z = psi.shape
+    devices, block_rows, _ = out.shape
+    each = block_rows // planes
     for group in groups(planes, span_z):
         real = jnp.concatenate([psi[0, 0, p] - psi[1, 1, p] for p in group], axis=1)
         imag = jnp.concatenate([psi[0, 1, p] + psi[1, 0, p] for p in group], axis=1)
         along_y = dot_left(y_table[...], jnp.concatenate([real, imag], axis=0))
-        values = dot_right(parts_in_lanes(along_y, span_y, span_z), z_table[...])
         for i, p in enumerate(group):
-            for part in range(2):
-                for r in range(rows):
-                    first = i * span_y + r * devices
-                    start = (r * planes + p) * 2 + part
-                    flat[pl.ds(start, devices, stride=2 * planes * rows), :] = values[
-                        first : first + devices, part * span_z : (part + 1) * span_z
-                    ]
-
-
-def real_space_kernel(devices, rows, planes, recv, pot, inverse, forward, _, back, field):
-    span_x = pot.shape[0]
-    block = 2 * planes
-    span_z = recv.shape[2]
+            out[:, p * each : (p + 1) * each, :] = along_y[
+                :, i * span_z : (i + 1) * span_z
+            ].reshape(devices, each, span_z)
+
+
+def real_space_kernel(rows, planes, recv, pot, inverse, forward, inv_z, fwd_z, _, back, field):
+    devices, size, span_z = recv.shape
+    span_x = devices * planes
+    arrived = recv.reshape(devices * size, span_z)
+    leaving = back.reshape(devices * 2 * size, span_z)
     for group in groups(rows, span_z):
         columns = [
-            recv[:, r * block : (r + 1) * block, :].reshape(devices * block, span_z) for r in group
+            jnp.concatenate(
+                [
+                    arrived[pl.ds((p * rows + r) * 2 + part, devices, stride=size), :]
+                    for part in range(2)
+                    for p in range(planes)
+                ],
+                axis=0,
+            )
+            for r in group
         ]
-        spatial = dot_left(inverse[...], jnp.concatenate(columns, axis=1))
-        lanes = slice(group[0] * span_z, (group[-1] + 1) * span_z)
+        along_x = dot_left(inverse[...], jnp.concatenate(columns, axis=1))
+        spatial = dot_right(parts_in_lanes(along_x, span_x, span_z), inv_z[...])
+        here = slice(group[0] * span_x, (group[-1] + 1) * span_x)
         for band in range(2):
-            one = spatial[band * span_x : (band + 1) * span_x]
-            field[band, :, lanes] = one
-            spectral = dot_left(forward[...], one * pot[:, lanes])
+            one = spatial[:, band * span_z : (band + 1) * span_z]
+            field[band, here, :] = one
+            product = one * pot[here, :]
+            product = jnp.concatenate(
+                [product[i * span_x : (i + 1) * span_x] for i in range(len(group))], axis=1
+            )
+            spectral = dot_left(forward[...], product)
+            spectral = dot_right(parts_in_lanes(spectral, span_x, span_z), fwd_z[...])
             for i, r in enumerate(group):
-                cols = spectral[:, i * span_z : (i + 1) * span_z]
-                back[:, band, r * block : (r + 1) * block] = cols.reshape(devices, block, span_z)
+                for p in range(planes):
+                    first = i * span_x + p * devices
+                    for part in range(2):
+                        start = band * size + (p * rows + r) * 2 + part
+                        leaving[pl.ds(start, devices, stride=2 * size), :] = spectral[
+                            first : first + devices, part * span_z : (part + 1) * span_z
+                        ]
 
 
 def real_gram_kernel(bands, *refs):
@@ -166,27 +178,18 @@
             out[weighted, b, a : a + 1, :] = line
 
 
-def to_planes_kernel(devices, rows, planes, recv, base, y_table, z_table, out):
-    span_y, span_z = base.shape[3], base.shape[4]
-    flat = recv.reshape(devices * 2 * planes * rows, span_z)
+def to_planes_kernel(recv, base, y_table, out):
+    _, _, planes, span_y, span_z = base.shape
+    each = recv.shape[1] // planes
     for group in groups(planes, span_z):
         columns = [
-            jnp.concatenate(
-                [
-                    flat[pl.ds((r * planes + p) * 2 + part, devices, stride=2 * planes * rows), :]
-                    for part in range(2)
-                    for r in range(rows)
-                ],
-                axis=0,
-            )
-            for p in group
+            recv[:, p * each : (p + 1) * each, :].reshape(2 * span_y, span_z) for p in group
         ]
         along_y = dot_left(y_table[...], jnp.concatenate(columns, axis=1))
-        values = dot_right(parts_in_lanes(along_y, span_y, span_z), z_table[...])
         for i, p in enumerate(group):
             for part in range(2):
                 out[0, part, p] = base[0, part, p] + (
-                    values[i * span_y : (i + 1) * span_y, part * span_z : (part + 1) * span_z]
+                    along_y[part * span_y : (part + 1) * span_y, i * span_z : (i + 1) * span_z]
                 )
 
 
@@ -274,7 +277,6 @@
     owners = strengths.shape[0] * strengths.shape[1]
     rows = span_y // devices
     block_rows = 2 * planes * rows
-    lanes = rows * span_z
     pairs = bands // 2
     block_span = projectors.shape[3] // span_z
     per_plane = span_y // block_span
@@ -286,40 +288,46 @@
     def cost(flops, moved):
         return pl.CostEstimate(flops=flops, bytes_accessed=moved, transcendentals=0)
 
-    row_major = (np.arange(devices)[None, :] * rows + np.arange(rows)[:, None]).reshape(-1)
-    inv_y = left_const(left_table(span_y, 1.0, row_order=row_major))
+    order = np.arange(2 * span_y)
+    order = (order % 2) * span_y + order // 2
+    inv_y = left_const(left_table(span_y, 1.0)[order])
+    fwd_y = left_const(left_table(span_y, -1.0)[:, order])
     inv_z = right_const(right_table(span_z, 1.0))
-    fwd_y = left_const(left_table(span_y, -1.0, col_order=row_major))
     fwd_z = right_const(right_table(span_z, -1.0))
 
-    sent = pl.pallas_call(
-        functools.partial(to_rows_kernel, devices, rows, planes),
-        out_shape=jax.ShapeDtypeStruct((devices, pairs, block_rows, span_z), f32),
-        grid=(pairs,),
-        in_specs=[
-            pl.BlockSpec((2, 2, planes, span_y, span_z), lambda j: (j, 0, 0, 0, 0)),
-            whole(inv_y.shape),
-            whole(inv_z.shape),
-        ],
-        out_specs=pl.BlockSpec((devices, None, block_rows, span_z), lambda j: (0, j, 0, 0)),
-        compiler_params=params,
-        cost_estimate=cost(4 * 10**9, 6 * 10**6),
-        name="to_rows",
-    )(orbitals, inv_y, inv_z)
-    arrived = lax.all_to_all(sent, "ga", split_axis=0, concat_axis=0, tiled=True)
-
-    phases = (plane_order[:, None] * grid_x[None, :]) % span_x
+    parts = 2 if pairs % 2 == 0 else 1
+    share = pairs // parts
+    arrived = []
+    for c in range(parts):
+        sent = pl.pallas_call(
+            to_rows_kernel,
+            out_shape=jax.ShapeDtypeStruct((devices, share, block_rows, span_z), f32),
+            grid=(share,),
+            in_specs=[
+                pl.BlockSpec(
+                    (2, 2, planes, span_y, span_z), lambda j, c=c: (c * share + j, 0, 0, 0, 0)
+                ),
+                whole(inv_y.shape),
+            ],
+            out_specs=pl.BlockSpec((devices, None, block_rows, span_z), lambda j: (0, j, 0, 0)),
+            compiler_params=params,
+            cost_estimate=cost(4 * 10**9, 3 * 10**6),
+            name="to_rows",
+        )(orbitals, inv_y)
+        arrived.append(lax.all_to_all(sent, "ga", split_axis=0, concat_axis=0, tiled=True))
+
+    stored = plane_order.reshape(devices, planes).T.reshape(-1)
+    phases = (stored[:, None] * grid_x[None, :]) % span_x
     angles = phases.astype(f32) * (2.0 * math.pi / span_x)
     factor = 1.0 / math.sqrt(span_x)
     cosine, sine = jnp.cos(angles) * factor, jnp.sin(angles) * factor
-    fwd_x = jnp.stack([cosine, -sine], axis=1).reshape(2 * span_x, span_x)
-    other = jnp.stack([sine, cosine], axis=1).reshape(2 * span_x, span_x)
-    inv_x = jnp.concatenate([fwd_x.T, other.T], axis=0)
+    fwd_x = jnp.concatenate([cosine, -sine], axis=0)
+    inv_x = jnp.concatenate([fwd_x, jnp.concatenate([sine, cosine], axis=0)], axis=1).T
     high, low = split_outside(fwd_x)
     fwd_x = jnp.concatenate([high, high, low], axis=1)
     high, low = split_outside(inv_x)
     inv_x = jnp.concatenate([high, high, low], axis=1)
-    pot = potential.reshape(span_x, lanes)
+    pot = potential.transpose(1, 0, 2).reshape(rows * span_x, span_z)
 
     local_order = lax.dynamic_slice_in_dim(plane_order, lax.axis_index("ga") * planes, planes)
     freq_x = signed_index(local_order, span_x).astype(f32) / span_x
@@ -364,34 +372,32 @@
     kin = jnp.sum(products[:, 2 * slots :], axis=0).reshape(bands, 2, bands, 2)
     kin = kin[:, 0, :, 0] + kin[:, 1, :, 1]
 
-    parts = 2 if pairs % 2 == 0 else 1
-    share = pairs // parts
     returned, fields = [], []
     for c in range(parts):
         back, field = pl.pallas_call(
-            functools.partial(real_space_kernel, devices, rows, planes),
+            functools.partial(real_space_kernel, rows, planes),
             out_shape=(
                 jax.ShapeDtypeStruct((devices, 2 * share, block_rows, span_z), f32),
-                jax.ShapeDtypeStruct((2 * share, span_x, lanes), f32),
+                jax.ShapeDtypeStruct((2 * share, rows * span_x, span_z), f32),
             ),
             grid=(share,),
             in_specs=[
-                pl.BlockSpec(
-                    (devices, None, block_rows, span_z), lambda j, c=c: (0, c * share + j, 0, 0)
-                ),
+                pl.BlockSpec((devices, None, block_rows, span_z), lambda j: (0, j, 0, 0)),
                 whole(pot.shape),
                 whole(inv_x.shape),
                 whole(fwd_x.shape),
+                whole(inv_z.shape),
+                whole(fwd_z.shape),
                 whole(proj.shape),
             ],
             out_specs=(
                 pl.BlockSpec((devices, 2, block_rows, span_z), lambda j: (0, j, 0, 0)),
-                pl.BlockSpec((2, span_x, lanes), lambda j: (j, 0, 0)),
+                pl.BlockSpec((2, rows * span_x, span_z), lambda j: (j, 0, 0)),
             ),
             compiler_params=params,
             cost_estimate=cost(4 * 10**9, 8 * 10**6),
             name="real_space",
-        )(arrived, pot, inv_x, fwd_x, proj)
+        )(arrived[c], pot, inv_x, fwd_x, inv_z, fwd_z, proj)
         returned.append(lax.all_to_all(back, "ga", split_axis=0, concat_axis=0, tiled=True))
         fields.append(field)
 
@@ -450,21 +456,20 @@
             (1, 2, planes, span_y, span_z), lambda b, c=c: (2 * share * c + b, 0, 0, 0, 0)
         )
         residual = pl.pallas_call(
-            functools.partial(to_planes_kernel, devices, rows, planes),
+            to_planes_kernel,
             out_shape=jax.ShapeDtypeStruct(orbitals.shape, f32),
             grid=(2 * share,),
             in_specs=[
                 pl.BlockSpec((devices, None, block_rows, span_z), lambda b: (0, b, 0, 0)),
                 one_band,
                 whole(fwd_y.shape),
-                whole(fwd_z.shape),
             ],
             out_specs=one_band,
             input_output_aliases={1: 0},
             compiler_params=params,
             cost_estimate=cost(8 * 10**9, 12 * 10**6),
             name="to_planes",
-        )(returned[c], residual, fwd_y, fwd_z)
+        )(returned[c], residual, fwd_y)
     return (residual, jnp.stack([m_real, m_imag]))
 
 

time: 188 us -> 182 us (0.968)
  waiting for transfers between devices: 91.3 us -> 76.6 us
  starting transfers between devices: 22.8 us -> 29.2 us
  Pallas kernels: 54.1 us -> 59.5 us
  local copies, waits for them, and re-layouts: 7.77 us -> 5.14 us
    all_to_all x1 -> x2, waiting for transfers between devices: 31.7 us -> 22.6 us  [on_device(): lax.all_to_all(sent, 'ga', split_axis=0, concat_axis=0, tiled=True)]
    ppermute x6, waiting for transfers between devices: 33.5 us -> 26.1 us  [partner(): return lax.ppermute(values, 'ga', [(d, d ^ k) for d in range(devices)])]
    all_to_all x1 -> x2, starting transfers between devices: 7.09 us -> 11.7 us  [on_device(): lax.all_to_all(sent, 'ga', split_axis=0, concat_axis=0, tiled=True)]
    pallas_call x5 -> x6, Pallas kernels: 28.8 us -> 33.1 us  [the longest x2 17.2 us: on_device(): pl.pallas_call(functools.partial(real_space_kernel, rows, planes), out_sh...]
    unnamed x20 -> x15, local copies, waits for them, and re-layouts: 3.84 us -> 0.44 us
  transfers between devices with their start and end apart: 9 -> 10, of which waited for: 7 -> 8; matrix products, arithmetic and copies ran while one was open for 7% -> 8% of each run, Pallas kernels for 19% -> 29%
where the time goes in v4:
time: 182 us; the launch traced here: 180 us
  waiting for transfers between devices  76.6 us (42%)
  Pallas kernels  59.5 us (33%)
  starting transfers between devices  29.2 us (16%)
  other arithmetic  7.49 us (4%)
  local copies, waits for them, and re-layouts  5.14 us (3%)
    all_to_all x2, waiting for transfers between devices, on_device(): lax.all_to_all(back, 'ga', split_axis=0, concat_axis=0, tiled=True)  27.9 us
    ppermute x6, waiting for transfers between devices, partner(): return lax.ppermute(values, 'ga', [(d, d ^ k) for d in range(devices)])  26.1 us
    all_to_all x2, waiting for transfers between devices, on_device(): lax.all_to_all(sent, 'ga', split_axis=0, concat_axis=0, tiled=True)  22.6 us
    pallas_call x2, Pallas kernels, on_device(): pl.pallas_call(functools.partial(real_space_kernel, rows, planes), out_sh...  17.2 us
    all_to_all x2, starting transfers between devices, on_device(): lax.all_to_all(sent, 'ga', split_axis=0, concat_axis=0, tiled=True)  11.7 us
    pallas_call x1, Pallas kernels, on_device(): pl.pallas_call(functools.partial(base_kernel, slots), out_shape=jax.Shape...  11.2 us
    pallas_call x1, Pallas kernels, on_device(): pl.pallas_call(functools.partial(project_kernel, slots), out_shape=jax.Sh...  10.1 us
    pallas_call x2, Pallas kernels, on_device(): pl.pallas_call(to_planes_kernel, out_shape=jax.ShapeDtypeStruct(orbitals....  9.91 us
  transfers between devices with their start and end apart: 10, of which 8 were waited for; matrix products, arithmetic and copies ran while one was open for 8% of the time, Pallas kernels for 29%

profile of v4, /device:TPU:1, one launch (start us, length us, event | category | flops | bytes accessed | tf_op | source)
XLA Modules:
  0.0 180.1 jit_solution(3307044358023365070)
XLA Ops:
  0.6 3.0 %to_rows.3 = f32[32,2,32,128]{3,2,1,0:T(8,128)} custom-call(f32[8,2,4,128,128]{4,3,2,1,0:T(8,128)} %psi.7, bf16[256,768]{1,0:T(8,128)(2,1)} %constant.99.clone.y_table), custom_call_target="tpu_custom_call" | custom-call | flops 4000000000 | bytes 3000000 | tf_op jit(solution)/shard_map/to_rows/pallas_call | solution.py:302
  3.6 7.1 %all-to-all-start.2 = ((f32[32,2,32,128]{3,2,1,0:T(8,128)}), f32[32,2,32,128]{3,2,1,0:T(8,128)}, u32[]{:S(2)}, u32[]{:S(2)}) async-start(f32[32,2,32,128]{3,2,1,0:T(8,128)} %to_rows.3), calls=%async_computation.2 | async-start | bytes 2097152 | tf_op jit(solution)/shard_map/all_to_all | solution.py:317
  11.0 0.4 fusion.11
  11.5 0.9 copy.68.inverse
  12.5 0.8 add_multiply_fusion.kinetic
  13.4 3.0 %to_rows.2 = f32[32,2,32,128]{3,2,1,0:T(8,128)} custom-call(f32[8,2,4,128,128]{4,3,2,1,0:T(8,128)} %psi.7, bf16[256,768]{1,0:T(8,128)(2,1)} %constant.99.clone.y_table), custom_call_target="tpu_custom_call" | custom-call | flops 4000000000 | bytes 3000000 | tf_op jit(solution)/shard_map/to_rows/pallas_call | solution.py:302
  16.3 19.8 %all-to-all-done.2.recv = f32[32,2,32,128]{3,2,1,0:T(8,128)} async-done(((f32[32,2,32,128]{3,2,1,0:T(8,128)}), f32[32,2,32,128]{3,2,1,0:T(8,128)}, u32[]{:S(2)}, u32[]{:S(2)}) %all-to-all-start.2) | async-done | bytes 1048608 | tf_op jit(solution)/shard_map/all_to_all | solution.py:317
  36.1 4.6 %all-to-all-start = ((f32[32,2,32,128]{3,2,1,0:T(8,128)}), f32[32,2,32,128]{3,2,1,0:T(8,128)}, u32[]{:S(2)}, u32[]{:S(2)}) async-start(f32[32,2,32,128]{3,2,1,0:T(8,128)} %to_rows.2), calls=%async_computation | async-start | bytes 2097152 | tf_op jit(solution)/shard_map/all_to_all | solution.py:317
  40.7 10.1 %project.1 = f32[8,32,16]{2,1,0:T(8,128)} custom-call(f32[8,2,4,128,128]{4,3,2,1,0:T(8,128)} %psi.7, f32[8,1024,128]{2,1,0:T(8,128)} %bitcast.82, f32[4,128,128]{2,1,0:T(8,128)} %add_multiply_fusion.kinetic), custom_call_target="tpu_custom_call" | custom-call | flops 8000000000 | bytes 8000000 | tf_op jit(solution)/shard_map/project/pallas_call | solution.py:349
  50.8 0.8 fusion.48
  52.2 0.3 convolution_bitcast_fusion.1
  52.4 0.7 copy.69._
  53.2 0.7 copy.59
  53.9 0.7 pad_maximum_fusion.1.forward
  54.6 8.6 %real_space.3 = (f32[32,4,32,128]{3,2,1,0:T(8,128)}, f32[4,512,128]{2,1,0:T(8,128)}) custom-call(f32[32,2,32,128]{3,2,1,0:T(8,128)} %all-to-all-done.2.recv, f32[512,128]{1,0:T(8,128)} %bitcast.71, bf16[256,768]{1,0:T(8,128)(2,1)} %copy.68.inverse, bf16[256,384]{1,0:T(8,128)(2,1)} %pad_maximum_fusion.1.forward, bf16[768,256]{1,0:T(8,128)(2,1)} %constant.101.clone.inv_z, ...), custom_call_target="tpu_custom_call" | custom-call | flops 4000000000 | bytes 8000000 | tf_op jit(solution)/shard_map/real_space/pallas_call | solution.py:377
  63.3 2.8 %all-to-all-done.recv = f32[32,2,32,128]{3,2,1,0:T(8,128)} async-done(((f32[32,2,32,128]{3,2,1,0:T(8,128)}), f32[32,2,32,128]{3,2,1,0:T(8,128)}, u32[]{:S(2)}, u32[]{:S(2)}) %all-to-all-start) | async-done | bytes 1048608 | tf_op jit(solution)/shard_map/all_to_all | solution.py:317
  66.1 4.6 %all-to-all-start.3 = ((f32[32,4,32,128]{3,2,1,0:T(8,128)}), f32[32,4,32,128]{3,2,1,0:T(8,128)}, u32[]{:S(2)}, u32[]{:S(2)}) async-start(f32[32,4,32,128]{3,2,1,0:T(8,128)} %get-tuple-element.7), calls=%async_computation.3 | async-start | bytes 4194304 | tf_op jit(solution)/shard_map/all_to_all | solution.py:401
  70.9 0.1 copy.91
  71.0 8.6 %real_space.2 = (f32[32,4,32,128]{3,2,1,0:T(8,128)}, f32[4,512,128]{2,1,0:T(8,128)}) custom-call(f32[32,2,32,128]{3,2,1,0:T(8,128)} %all-to-all-done.recv, f32[512,128]{1,0:T(8,128)} %bitcast.72, bf16[256,768]{1,0:T(8,128)(2,1)} %copy.68.inverse, bf16[256,384]{1,0:T(8,128)(2,1)} %pad_maximum_fusion.1.forward, bf16[768,256]{1,0:T(8,128)(2,1)} %constant.101.clone.inv_z, ...), custom_call_target="tpu_custom_call" | custom-call | flops 4000000000 | bytes 8000000 | tf_op jit(solution)/shard_map/real_space/pallas_call | solution.py:377
  79.6 5.2 %real_gram.1 = f32[2,8,8,128]{3,2,1,0:T(8,128)} custom-call(f32[4,512,128]{2,1,0:T(8,128)} %get-tuple-element.8.refs_0_, f32[4,512,128]{2,1,0:T(8,128)} %get-tuple-element.9.refs_1_, f32[512,128]{1,0:T(8,128)} %bitcast.73), custom_call_target="tpu_custom_call" | custom-call | flops 10000000 | bytes 2000000 | tf_op jit(solution)/shard_map/real_gram/pallas_call | solution.py:404
  84.8 0.9 reduce_sum.18
  85.9 0.4 collective-permute-start
  86.3 0.8 collective-permute-done
  87.1 1.4 collective-permute-start.1
  88.5 1.6 collective-permute-done.1
  90.2 2.9 %collective-permute-start.2 = (f32[136,16]{0,1:T(8,128)S(1)}, f32[136,16]{0,1:T(8,128)S(1)}, u32[]{:S(2)}, u32[]{:S(2)}) collective-permute-start(f32[136,16]{0,1:T(8,128)S(1)} %add.118), channel_id=1, source_target_pairs={{0,4},{1,5},{2,6},{3,7},{4,0},{5,1},{6,2},{7,3},{8,12},{9,13},{10,... | collective-permute-start | bytes 26120 | tf_op jit(solution)/shard_map/ppermute | solution.py:256
  93.1 1.9 %collective-permute-done.2 = f32[136,16]{0,1:T(8,128)S(1)} collective-permute-done((f32[136,16]{0,1:T(8,128)S(1)}, f32[136,16]{0,1:T(8,128)S(1)}, u32[]{:S(2)}, u32[]{:S(2)}) %collective-permute-start.2) | collective-permute-done | bytes 8736 | tf_op jit(solution)/shard_map/ppermute | solution.py:256
  95.0 2.5 %collective-permute-start.5 = (f32[136,16]{0,1:T(8,128)S(1)}, f32[136,16]{0,1:T(8,128)S(1)}, u32[]{:S(2)}, u32[]{:S(2)}) collective-permute-start(f32[136,16]{0,1:T(8,128)S(1)} %add.119), channel_id=1, source_target_pairs={{0,24},{1,25},{2,26},{3,27},{4,28},{5,29},{6,30},{7,31},{8,16},{9,... | collective-permute-start | bytes 26120 | tf_op jit(solution)/shard_map/ppermute | solution.py:256
  97.5 1.0 collective-permute-start.3
  98.7 10.1 %collective-permute-done.5 = f32[136,16]{0,1:T(8,128)S(1)} collective-permute-done((f32[136,16]{0,1:T(8,128)S(1)}, f32[136,16]{0,1:T(8,128)S(1)}, u32[]{:S(2)}, u32[]{:S(2)}) %collective-permute-start.5) | collective-permute-done | bytes 8736 | tf_op jit(solution)/shard_map/ppermute | solution.py:256
  108.8 11.7 %collective-permute-done.4 = f32[136,16]{0,1:T(8,128)S(1)} collective-permute-done((f32[136,16]{0,1:T(8,128)S(1)}, f32[136,16]{0,1:T(8,128)S(1)}, u32[]{:S(2)}, u32[]{:S(2)}) %collective-permute-start.4) | collective-permute-done | bytes 8736 | tf_op jit(solution)/shard_map/ppermute | solution.py:256
  120.5 0.7 cholesky.16
  121.3 0.6 compare_reduce_fusion
  122.1 0.1 fusion.34
  122.2 4.6 %all-to-all-start.1 = ((f32[32,4,32,128]{3,2,1,0:T(8,128)}), f32[32,4,32,128]{3,2,1,0:T(8,128)}, u32[]{:S(2)}, u32[]{:S(2)}) async-start(f32[32,4,32,128]{3,2,1,0:T(8,128)} %get-tuple-element.6), calls=%async_computation.1 | async-start | bytes 4194304 | tf_op jit(solution)/shard_map/all_to_all | solution.py:401
  126.8 0.7 fusion.19
  127.5 0.6 custom-call.10
  128.2 0.1 fusion.20
  128.3 0.2 fusion.14
  128.5 0.1 fusion.22
  129.1 0.2 copy.85
  129.3 0.2 convolution_bitcast_fusion
  129.8 0.6 pad_maximum_fusion.6
  130.4 0.7 pad_maximum_fusion.4.coefs
  131.1 11.2 %base.1 = f32[8,2,4,128,128]{4,3,2,1,0:T(8,128)} custom-call(f32[8,2,4,128,128]{4,3,2,1,0:T(8,128)} %psi.7, f32[8,1024,128]{2,1,0:T(8,128)} %bitcast.83, f32[4,128,128]{2,1,0:T(8,128)} %add_multiply_fusion.kinetic, f32[8,16,32]{2,1,0:T(8,128)} %pad_maximum_fusion.4.coefs), custom_call_target="tpu_custom_call" | custom-call | flops 8000000000 | bytes 12000000 | tf_op jit(solution)/shard_map/base/pallas_call | solution.py:441
  142.3 5.0 %to_planes.2.base = f32[8,2,4,128,128]{4,3,2,1,0:T(8,128)} custom-call(f32[32,4,32,128]{3,2,1,0:T(8,128)} %all-to-all-done.3.recv, f32[8,2,4,128,128]{4,3,2,1,0:T(8,128)} %base.1, bf16[256,768]{1,0:T(8,128)(2,1)} %constant.100.clone.y_table), custom_call_target="tpu_custom_call", output_to_operand_aliasing={{}: (1, {})} | custom-call | flops 8000000000 | bytes 12000000 | tf_op jit(solution)/shard_map/to_planes/pallas_call | solution.py:458
  147.2 27.9 %all-to-all-done.1.recv = f32[32,4,32,128]{3,2,1,0:T(8,128)} async-done(((f32[32,4,32,128]{3,2,1,0:T(8,128)}), f32[32,4,32,128]{3,2,1,0:T(8,128)}, u32[]{:S(2)}, u32[]{:S(2)}) %all-to-all-start.1) | async-done | bytes 2097184 | tf_op jit(solution)/shard_map/all_to_all | solution.py:401
  175.1 4.9 %to_planes.3 = f32[8,2,4,128,128]{4,3,2,1,0:T(8,128)} custom-call(f32[32,4,32,128]{3,2,1,0:T(8,128)} %all-to-all-done.1.recv, f32[8,2,4,128,128]{4,3,2,1,0:T(8,128)} %to_planes.2.base, bf16[256,768]{1,0:T(8,128)(2,1)} %constant.100.clone.y_table), custom_call_target="tpu_custom_call", output_to_operand_aliasing={{}: (1, {})} | custom-call | flops 8000000000 | bytes 12000000 | tf_op jit(solution)/shard_map/to_planes/pallas_call | solution.py:458
  (65 shorter events, 2.6 us)
Async XLA Ops:
  0.6 10.1 %copy-start.3 = (s32[128]{0:T(128)S(1)}, s32[128]{0:T(128)}, u32[]{:S(2)}) copy-start(s32[128]{0:T(128)} %param.11) | copy-start | bytes 1540
  3.6 32.5 %all-to-all-start.2 = ((f32[32,2,32,128]{3,2,1,0:T(8,128)}), f32[32,2,32,128]{3,2,1,0:T(8,128)}, u32[]{:S(2)}, u32[]{:S(2)}) async-start(f32[32,2,32,128]{3,2,1,0:T(8,128)} %to_rows.3), calls=%async_computation.2 | async-start | bytes 2097152 | tf_op jit(solution)/shard_map/all_to_all | solution.py:317
  36.1 30.0 %all-to-all-start = ((f32[32,2,32,128]{3,2,1,0:T(8,128)}), f32[32,2,32,128]{3,2,1,0:T(8,128)}, u32[]{:S(2)}, u32[]{:S(2)}) async-start(f32[32,2,32,128]{3,2,1,0:T(8,128)} %to_rows.2), calls=%async_computation | async-start | bytes 2097152 | tf_op jit(solution)/shard_map/all_to_all | solution.py:317
  40.7 11.4 %copy-start.4 = (s32[8,8]{1,0:T(8,128)S(1)}, s32[8,8]{1,0:T(8,128)}, u32[]{:S(2)}) copy-start(s32[8,8]{1,0:T(8,128)} %param.14) | copy-start | bytes 772
  40.7 12.4 %copy-start = (f32[128,4,128]{2,1,0:T(4,128)S(1)}, f32[128,4,128]{2,1,0:T(4,128)}, u32[]{:S(2)}) copy-start(f32[128,4,128]{2,1,0:T(4,128)} %param.12) | copy-start | bytes 786436
  63.2 7.4 %copy-start.1 = (f32[8,32,16]{2,1,0:T(8,128)S(1)}, f32[8,32,16]{2,1,0:T(8,128)}, u32[]{:S(2)}) copy-start(f32[8,32,16]{2,1,0:T(8,128)} %project.1) | copy-start | bytes 49156
  66.1 56.1 %all-to-all-start.3 = ((f32[32,4,32,128]{3,2,1,0:T(8,128)}), f32[32,4,32,128]{3,2,1,0:T(8,128)}, u32[]{:S(2)}, u32[]{:S(2)}) async-start(f32[32,4,32,128]{3,2,1,0:T(8,128)} %get-tuple-element.7), calls=%async_computation.3 | async-start | bytes 4194304 | tf_op jit(solution)/shard_map/all_to_all | solution.py:401
  71.0 27.5 %copy-start.2 = (f32[32,4]{0,1:T(4,128)S(1)}, f32[32,4]{0,1:T(4,128)}, u32[]{:S(2)}) copy-start(f32[32,4]{0,1:T(4,128)} %param.15) | copy-start | bytes 1540
  85.9 1.2 collective-permute-start
  87.1 3.0 %collective-permute-start.1 = (f32[136,16]{0,1:T(8,128)S(1)}, f32[136,16]{0,1:T(8,128)S(1)}, u32[]{:S(2)}, u32[]{:S(2)}) collective-permute-start(f32[136,16]{0,1:T(8,128)S(1)} %fusion.47), channel_id=1, source_target_pairs={{0,2},{1,3},{2,0},{3,1},{4,6},{5,7},{6,4},{7,5},{8,10},{9,11},{10,... | collective-permute-start | bytes 26120 | tf_op jit(solution)/shard_map/ppermute | solution.py:256
  90.2 4.8 %collective-permute-start.2 = (f32[136,16]{0,1:T(8,128)S(1)}, f32[136,16]{0,1:T(8,128)S(1)}, u32[]{:S(2)}, u32[]{:S(2)}) collective-permute-start(f32[136,16]{0,1:T(8,128)S(1)} %add.118), channel_id=1, source_target_pairs={{0,4},{1,5},{2,6},{3,7},{4,0},{5,1},{6,2},{7,3},{8,12},{9,13},{10,... | collective-permute-start | bytes 26120 | tf_op jit(solution)/shard_map/ppermute | solution.py:256
  95.0 13.8 %collective-permute-start.5 = (f32[136,16]{0,1:T(8,128)S(1)}, f32[136,16]{0,1:T(8,128)S(1)}, u32[]{:S(2)}, u32[]{:S(2)}) collective-permute-start(f32[136,16]{0,1:T(8,128)S(1)} %add.119), channel_id=1, source_target_pairs={{0,24},{1,25},{2,26},{3,27},{4,28},{5,29},{6,30},{7,31},{8,16},{9,... | collective-permute-start | bytes 26120 | tf_op jit(solution)/shard_map/ppermute | solution.py:256
  97.5 23.0 %collective-permute-start.4 = (f32[136,16]{0,1:T(8,128)S(1)}, f32[136,16]{0,1:T(8,128)S(1)}, u32[]{:S(2)}, u32[]{:S(2)}) collective-permute-start(f32[136,16]{0,1:T(8,128)S(1)} %add.119), channel_id=1, source_target_pairs={{0,16},{1,17},{2,18},{3,19},{4,20},{5,21},{6,22},{7,23},{8,24},{9,... | collective-permute-start | bytes 26120 | tf_op jit(solution)/shard_map/ppermute | solution.py:256
  97.5 23.0 %collective-permute-start.3 = (f32[136,16]{0,1:T(8,128)S(1)}, f32[136,16]{0,1:T(8,128)S(1)}, u32[]{:S(2)}, u32[]{:S(2)}) collective-permute-start(f32[136,16]{0,1:T(8,128)S(1)} %add.119), channel_id=1, source_target_pairs={{0,8},{1,9},{2,10},{3,11},{4,12},{5,13},{6,14},{7,15},{8,0},{9,1},... | collective-permute-start | bytes 26120 | tf_op jit(solution)/shard_map/ppermute | solution.py:256
  122.2 52.9 %all-to-all-start.1 = ((f32[32,4,32,128]{3,2,1,0:T(8,128)}), f32[32,4,32,128]{3,2,1,0:T(8,128)}, u32[]{:S(2)}, u32[]{:S(2)}) async-start(f32[32,4,32,128]{3,2,1,0:T(8,128)} %get-tuple-element.6), calls=%async_computation.1 | async-start | bytes 4194304 | tf_op jit(solution)/shard_map/all_to_all | solution.py:401

commit v5 on v4

--- a/solution.py
+++ b/solution.py
@@ -193,6 +193,10 @@
                 )
 
 
+def pass_on_kernel(values, _, out):
+    out[...] = values[...]
+
+
 def block_rows_of(psi, beta, slots):
     bands, _, span, span_z = psi.shape
     psi_flat = psi.reshape(bands * 2 * span, span_z)
@@ -297,19 +301,23 @@
 
     parts = 2 if pairs % 2 == 0 else 1
     share = pairs // parts
+    some = math.gcd(planes, max(1, 256 // span_z))
+    some_rows = block_rows // planes * some
     arrived = []
     for c in range(parts):
         sent = pl.pallas_call(
             to_rows_kernel,
             out_shape=jax.ShapeDtypeStruct((devices, share, block_rows, span_z), f32),
-            grid=(share,),
+            grid=(share, planes // some),
             in_specs=[
                 pl.BlockSpec(
-                    (2, 2, planes, span_y, span_z), lambda j, c=c: (c * share + j, 0, 0, 0, 0)
+                    (2, 2, some, span_y, span_z), lambda j, p, c=c: (c * share + j, 0, p, 0, 0)
                 ),
                 whole(inv_y.shape),
             ],
-            out_specs=pl.BlockSpec((devices, None, block_rows, span_z), lambda j: (0, j, 0, 0)),
+            out_specs=pl.BlockSpec(
+                (devices, None, some_rows, span_z), lambda j, p: (0, j, p, 0)
+            ),
             compiler_params=params,
             cost_estimate=cost(4 * 10**9, 3 * 10**6),
             name="to_rows",
@@ -411,6 +419,13 @@
     grams = jnp.sum(grams, axis=-1)
     own = jnp.concatenate([proj, jnp.concatenate([grams[0], grams[1] + kin], axis=1)], axis=0)
     total = sum_over(own, devices)
+    total = pl.pallas_call(
+        pass_on_kernel,
+        out_shape=jax.ShapeDtypeStruct(total.shape, f32),
+        in_specs=[pl.BlockSpec(memory_space=pltpu.VMEM), pl.BlockSpec(memory_space=pl.ANY)],
+        out_specs=pl.BlockSpec(memory_space=pltpu.VMEM),
+        name="pass_on",
+    )(total, returned[0])
     proj, s_real, h_real = total[:owners], total[owners:, :bands], total[owners:, bands:]
     weighted = strengths.reshape(-1)[:, None] * proj
     p_real, p_imag = proj[:, :bands], proj[:, bands:]
@@ -453,14 +468,14 @@
     residual = base
     for c in range(parts):
         one_band = pl.BlockSpec(
-            (1, 2, planes, span_y, span_z), lambda b, c=c: (2 * share * c + b, 0, 0, 0, 0)
+            (1, 2, some, span_y, span_z), lambda b, p, c=c: (2 * share * c + b, 0, p, 0, 0)
         )
         residual = pl.pallas_call(
             to_planes_kernel,
             out_shape=jax.ShapeDtypeStruct(orbitals.shape, f32),
-            grid=(2 * share,),
+            grid=(2 * share, planes // some),
             in_specs=[
-                pl.BlockSpec((devices, None, block_rows, span_z), lambda b: (0, b, 0, 0)),
+                pl.BlockSpec((devices, None, some_rows, span_z), lambda b, p: (0, b, p, 0)),
                 one_band,
                 whole(fwd_y.shape),
             ],

time: 182 us -> 190 us (1.044)
  waiting for transfers between devices: 76.6 us -> 64.4 us
  Pallas kernels: 59.5 us -> 67.9 us
  matrix products: 1.33 us -> 6.01 us
  starting transfers between devices: 29.2 us -> 32.7 us
  other arithmetic: 7.49 us -> 10.1 us
    all_to_all x2, waiting for transfers between devices: 27.9 us -> 16 us  [on_device(): lax.all_to_all(back, 'ga', split_axis=0, concat_axis=0, tiled=True)]
    dot_general x6, matrix products: 0.99 us -> 5.63 us  [tdot(): jnp.einsum(pattern, left, right, precision=highest, preferred_element_typ...]
    pallas_call x2, Pallas kernels: 9.91 us -> 14.2 us  [on_device(): pl.pallas_call(to_planes_kernel, out_shape=jax.ShapeDtypeStruct(orbitals....]
    ppermute x6, starting transfers between devices: 8.26 us -> 11.7 us  [partner(): return lax.ppermute(values, 'ga', [(d, d ^ k) for d in range(devices)])]
    pallas_call x2, Pallas kernels: 5.91 us -> 8.47 us  [on_device(): pl.pallas_call(to_rows_kernel, out_shape=jax.ShapeDtypeStruct((devices, s...]
  transfers between devices with their start and end apart: 10 -> 10, of which waited for: 8 -> 8; matrix products, arithmetic and copies ran while one was open for 8% -> 11% of each run, Pallas kernels for 29% -> 30%
where the time goes in v5:
time: 190 us; the launch traced here: 187 us
  Pallas kernels  67.9 us (36%)
  waiting for transfers between devices  64.4 us (34%)
  starting transfers between devices  32.7 us (17%)
  other arithmetic  10.1 us (5%)
  matrix products  6.01 us (3%)
  local copies, waits for them, and re-layouts  4.88 us (3%)
    ppermute x6, waiting for transfers between devices, partner(): return lax.ppermute(values, 'ga', [(d, d ^ k) for d in range(devices)])  27 us
    all_to_all x2, waiting for transfers between devices, on_device(): lax.all_to_all(sent, 'ga', split_axis=0, concat_axis=0, tiled=True)  21.3 us
    pallas_call x2, Pallas kernels, on_device(): pl.pallas_call(functools.partial(real_space_kernel, rows, planes), out_sh...  17.4 us
    all_to_all x2, waiting for transfers between devices, on_device(): lax.all_to_all(back, 'ga', split_axis=0, concat_axis=0, tiled=True)  16 us
    pallas_call x2, Pallas kernels, on_device(): pl.pallas_call(to_planes_kernel, out_shape=jax.ShapeDtypeStruct(orbitals....  14.2 us
    all_to_all x2, starting transfers between devices, on_device(): lax.all_to_all(sent, 'ga', split_axis=0, concat_axis=0, tiled=True)  11.7 us
    ppermute x6, starting transfers between devices, partner(): return lax.ppermute(values, 'ga', [(d, d ^ k) for d in range(devices)])  11.7 us
    pallas_call x1, Pallas kernels, on_device(): pl.pallas_call(functools.partial(base_kernel, slots), out_shape=jax.Shape...  11.2 us
  transfers between devices with their start and end apart: 10, of which 8 were waited for; matrix products, arithmetic and copies ran while one was open for 11% of the time, Pallas kernels for 30%

profile of v5, /device:TPU:1, one launch (start us, length us, event | category | flops | bytes accessed | tf_op | source)
XLA Modules:
  0.0 187.0 jit_solution(14745148618429641606)
XLA Ops:
  0.6 4.2 %to_rows.3 = f32[32,2,32,128]{3,2,1,0:T(8,128)} custom-call(f32[8,2,4,128,128]{4,3,2,1,0:T(8,128)} %psi.7, bf16[256,768]{1,0:T(8,128)(2,1)} %constant.99.clone.y_table), custom_call_target="tpu_custom_call" | custom-call | flops 4000000000 | bytes 3000000 | tf_op jit(solution)/shard_map/to_rows/pallas_call | solution.py:308
  4.9 7.2 %all-to-all-start.2 = ((f32[32,2,32,128]{3,2,1,0:T(8,128)}), f32[32,2,32,128]{3,2,1,0:T(8,128)}, u32[]{:S(2)}, u32[]{:S(2)}) async-start(f32[32,2,32,128]{3,2,1,0:T(8,128)} %to_rows.3), calls=%async_computation.2 | async-start | bytes 2097152 | tf_op jit(solution)/shard_map/all_to_all | solution.py:325
  12.3 0.4 fusion.24
  12.7 0.9 copy.118.inverse
  13.8 0.8 add_multiply_fusion.kinetic
  14.7 4.3 %to_rows.2 = f32[32,2,32,128]{3,2,1,0:T(8,128)} custom-call(f32[8,2,4,128,128]{4,3,2,1,0:T(8,128)} %psi.7, bf16[256,768]{1,0:T(8,128)(2,1)} %constant.99.clone.y_table), custom_call_target="tpu_custom_call" | custom-call | flops 4000000000 | bytes 3000000 | tf_op jit(solution)/shard_map/to_rows/pallas_call | solution.py:308
  18.9 18.5 %all-to-all-done.2.recv = f32[32,2,32,128]{3,2,1,0:T(8,128)} async-done(((f32[32,2,32,128]{3,2,1,0:T(8,128)}), f32[32,2,32,128]{3,2,1,0:T(8,128)}, u32[]{:S(2)}, u32[]{:S(2)}) %all-to-all-start.2) | async-done | bytes 1048608 | tf_op jit(solution)/shard_map/all_to_all | solution.py:325
  37.4 4.6 %all-to-all-start = ((f32[32,2,32,128]{3,2,1,0:T(8,128)}), f32[32,2,32,128]{3,2,1,0:T(8,128)}, u32[]{:S(2)}, u32[]{:S(2)}) async-start(f32[32,2,32,128]{3,2,1,0:T(8,128)} %to_rows.2), calls=%async_computation | async-start | bytes 2097152 | tf_op jit(solution)/shard_map/all_to_all | solution.py:325
  42.0 10.1 %project.1 = f32[8,32,16]{2,1,0:T(8,128)} custom-call(f32[8,2,4,128,128]{4,3,2,1,0:T(8,128)} %psi.7, f32[8,1024,128]{2,1,0:T(8,128)} %bitcast.85, f32[4,128,128]{2,1,0:T(8,128)} %add_multiply_fusion.kinetic), custom_call_target="tpu_custom_call" | custom-call | flops 8000000000 | bytes 8000000 | tf_op jit(solution)/shard_map/project/pallas_call | solution.py:357
  52.1 0.8 fusion.47
  53.4 0.8 copy.109
  54.2 0.7 pad_maximum_fusion.1.forward
  54.9 0.9 convolution_bitcast_fusion._
  55.9 8.6 %real_space.3 = (f32[32,4,32,128]{3,2,1,0:T(8,128)}, f32[4,512,128]{2,1,0:T(8,128)}) custom-call(f32[32,2,32,128]{3,2,1,0:T(8,128)} %all-to-all-done.2.recv, f32[512,128]{1,0:T(8,128)} %bitcast.74, bf16[256,768]{1,0:T(8,128)(2,1)} %copy.118.inverse, bf16[256,384]{1,0:T(8,128)(2,1)} %pad_maximum_fusion.1.forward, bf16[768,256]{1,0:T(8,128)(2,1)} %constant.101.clone.inv_z, ...), custom_call_target="tpu_custom_call" | custom-call | flops 4000000000 | bytes 8000000 | tf_op jit(solution)/shard_map/real_space/pallas_call | solution.py:385
  64.5 2.9 %all-to-all-done.recv = f32[32,2,32,128]{3,2,1,0:T(8,128)} async-done(((f32[32,2,32,128]{3,2,1,0:T(8,128)}), f32[32,2,32,128]{3,2,1,0:T(8,128)}, u32[]{:S(2)}, u32[]{:S(2)}) %all-to-all-start) | async-done | bytes 1048608 | tf_op jit(solution)/shard_map/all_to_all | solution.py:325
  67.4 4.6 %all-to-all-start.3 = ((f32[32,4,32,128]{3,2,1,0:T(8,128)}), f32[32,4,32,128]{3,2,1,0:T(8,128)}, u32[]{:S(2)}, u32[]{:S(2)}) async-start(f32[32,4,32,128]{3,2,1,0:T(8,128)} %get-tuple-element.7), calls=%async_computation.3 | async-start | bytes 4194304 | tf_op jit(solution)/shard_map/all_to_all | solution.py:409
  72.2 8.7 %real_space.2 = (f32[32,4,32,128]{3,2,1,0:T(8,128)}, f32[4,512,128]{2,1,0:T(8,128)}) custom-call(f32[32,2,32,128]{3,2,1,0:T(8,128)} %all-to-all-done.recv, f32[512,128]{1,0:T(8,128)} %bitcast.75, bf16[256,768]{1,0:T(8,128)(2,1)} %copy.118.inverse, bf16[256,384]{1,0:T(8,128)(2,1)} %pad_maximum_fusion.1.forward, bf16[768,256]{1,0:T(8,128)(2,1)} %constant.101.clone.inv_z, ...), custom_call_target="tpu_custom_call" | custom-call | flops 4000000000 | bytes 8000000 | tf_op jit(solution)/shard_map/real_space/pallas_call | solution.py:385
  81.0 5.2 %real_gram.1 = f32[2,8,8,128]{3,2,1,0:T(8,128)} custom-call(f32[4,512,128]{2,1,0:T(8,128)} %get-tuple-element.8.refs_0_, f32[4,512,128]{2,1,0:T(8,128)} %get-tuple-element.9.refs_1_, f32[512,128]{1,0:T(8,128)} %bitcast.76), custom_call_target="tpu_custom_call" | custom-call | flops 10000000 | bytes 2000000 | tf_op jit(solution)/shard_map/real_gram/pallas_call | solution.py:412
  86.2 0.9 reduce_sum.18
  87.6 0.9 collective-permute-done
  88.5 1.4 collective-permute-start.1
  89.9 2.3 %collective-permute-done.1 = f32[136,16]{1,0:T(8,128)S(1)} collective-permute-done((f32[136,16]{1,0:T(8,128)S(1)}, f32[136,16]{1,0:T(8,128)S(1)}, u32[]{:S(2)}, u32[]{:S(2)}) %collective-permute-start.1) | collective-permute-done | bytes 8736 | tf_op jit(solution)/shard_map/ppermute | solution.py:260
  92.2 5.5 %collective-permute-start.2 = (f32[136,16]{1,0:T(8,128)S(1)}, f32[136,16]{1,0:T(8,128)S(1)}, u32[]{:S(2)}, u32[]{:S(2)}) collective-permute-start(f32[136,16]{1,0:T(8,128)S(1)} %add.118), channel_id=1, source_target_pairs={{0,4},{1,5},{2,6},{3,7},{4,0},{5,1},{6,2},{7,3},{8,12},{9,13},{10,... | collective-permute-start | bytes 26120 | tf_op jit(solution)/shard_map/ppermute | solution.py:260
  97.8 2.3 %collective-permute-done.2 = f32[136,16]{1,0:T(8,128)S(1)} collective-permute-done((f32[136,16]{1,0:T(8,128)S(1)}, f32[136,16]{1,0:T(8,128)S(1)}, u32[]{:S(2)}, u32[]{:S(2)}) %collective-permute-start.2) | collective-permute-done | bytes 8736 | tf_op jit(solution)/shard_map/ppermute | solution.py:260
  100.1 1.0 collective-permute-start.5
  101.1 3.4 %collective-permute-start.4 = (f32[136,16]{1,0:T(8,128)S(1)}, f32[136,16]{1,0:T(8,128)S(1)}, u32[]{:S(2)}, u32[]{:S(2)}) collective-permute-start(f32[136,16]{1,0:T(8,128)S(1)} %add.119), channel_id=1, source_target_pairs={{0,16},{1,17},{2,18},{3,19},{4,20},{5,21},{6,22},{7,23},{8,24},{9,... | collective-permute-start | bytes 26120 | tf_op jit(solution)/shard_map/ppermute | solution.py:260
  104.7 6.8 %collective-permute-done.5 = f32[136,16]{1,0:T(8,128)S(1)} collective-permute-done((f32[136,16]{1,0:T(8,128)S(1)}, f32[136,16]{1,0:T(8,128)S(1)}, u32[]{:S(2)}, u32[]{:S(2)}) %collective-permute-start.5) | collective-permute-done | bytes 8736 | tf_op jit(solution)/shard_map/ppermute | solution.py:260
  111.4 14.7 %collective-permute-done.4 = f32[136,16]{1,0:T(8,128)S(1)} collective-permute-done((f32[136,16]{1,0:T(8,128)S(1)}, f32[136,16]{1,0:T(8,128)S(1)}, u32[]{:S(2)}, u32[]{:S(2)}) %collective-permute-start.4) | collective-permute-done | bytes 8736 | tf_op jit(solution)/shard_map/ppermute | solution.py:260
  126.2 0.6 add_add_fusion.values
  126.8 4.7 %all-to-all-start.1 = ((f32[32,4,32,128]{3,2,1,0:T(8,128)}), f32[32,4,32,128]{3,2,1,0:T(8,128)}, u32[]{:S(2)}, u32[]{:S(2)}) async-start(f32[32,4,32,128]{3,2,1,0:T(8,128)} %get-tuple-element.6), calls=%async_computation.1 | async-start | bytes 4194304 | tf_op jit(solution)/shard_map/all_to_all | solution.py:409
  131.5 1.5 pass_on.1
  133.1 0.7 slice.119
  133.7 0.9 slice_multiply_fusion
  134.7 1.1 fusion.10
  135.8 1.1 fusion.16
  136.9 0.9 fusion.37
  137.8 0.7 cholesky.16
  138.6 0.6 compare_reduce_fusion
  139.2 0.6 fusion.27
  139.9 0.6 custom-call.10
  140.5 1.1 fusion.12
  141.6 1.1 convolution_subtract_fusion
  144.2 0.6 pad_maximum_fusion.6
  144.9 0.7 pad_maximum_fusion.4.coefs
  145.6 11.2 %base.1 = f32[8,2,4,128,128]{4,3,2,1,0:T(8,128)} custom-call(f32[8,2,4,128,128]{4,3,2,1,0:T(8,128)} %psi.7, f32[8,1024,128]{2,1,0:T(8,128)} %bitcast.86, f32[4,128,128]{2,1,0:T(8,128)} %add_multiply_fusion.kinetic, f32[8,16,32]{2,1,0:T(8,128)} %pad_maximum_fusion.4.coefs), custom_call_target="tpu_custom_call" | custom-call | flops 8000000000 | bytes 12000000 | tf_op jit(solution)/shard_map/base/pallas_call | solution.py:456
  156.8 7.1 %to_planes.2.base = f32[8,2,4,128,128]{4,3,2,1,0:T(8,128)} custom-call(f32[32,4,32,128]{3,2,1,0:T(8,128)} %all-to-all-done.3._.recv, f32[8,2,4,128,128]{4,3,2,1,0:T(8,128)} %base.1, bf16[256,768]{1,0:T(8,128)(2,1)} %constant.100.clone.y_table), custom_call_target="tpu_custom_call", output_to_operand_aliasing={{}: (1, {})} | custom-call | flops 8000000000 | bytes 12000000 | tf_op jit(solution)/shard_map/to_planes/pallas_call | solution.py:473
  163.8 16.0 %all-to-all-done.1.recv = f32[32,4,32,128]{3,2,1,0:T(8,128)} async-done(((f32[32,4,32,128]{3,2,1,0:T(8,128)}), f32[32,4,32,128]{3,2,1,0:T(8,128)}, u32[]{:S(2)}, u32[]{:S(2)}) %all-to-all-start.1) | async-done | bytes 2097184 | tf_op jit(solution)/shard_map/all_to_all | solution.py:409
  179.9 7.1 %to_planes.3 = f32[8,2,4,128,128]{4,3,2,1,0:T(8,128)} custom-call(f32[32,4,32,128]{3,2,1,0:T(8,128)} %all-to-all-done.1.recv, f32[8,2,4,128,128]{4,3,2,1,0:T(8,128)} %to_planes.2.base, bf16[256,768]{1,0:T(8,128)(2,1)} %constant.100.clone.y_table), custom_call_target="tpu_custom_call", output_to_operand_aliasing={{}: (1, {})} | custom-call | flops 8000000000 | bytes 12000000 | tf_op jit(solution)/shard_map/to_planes/pallas_call | solution.py:473
  (64 shorter events, 3.6 us)
Async XLA Ops:
  0.6 11.4 %copy-start.4 = (s32[128]{0:T(128)S(1)}, s32[128]{0:T(128)}, u32[]{:S(2)}) copy-start(s32[128]{0:T(128)} %param.11) | copy-start | bytes 1540
  4.9 32.5 %all-to-all-start.2 = ((f32[32,2,32,128]{3,2,1,0:T(8,128)}), f32[32,2,32,128]{3,2,1,0:T(8,128)}, u32[]{:S(2)}, u32[]{:S(2)}) async-start(f32[32,2,32,128]{3,2,1,0:T(8,128)} %to_rows.3), calls=%async_computation.2 | async-start | bytes 2097152 | tf_op jit(solution)/shard_map/all_to_all | solution.py:325
  37.4 30.0 %all-to-all-start = ((f32[32,2,32,128]{3,2,1,0:T(8,128)}), f32[32,2,32,128]{3,2,1,0:T(8,128)}, u32[]{:S(2)}, u32[]{:S(2)}) async-start(f32[32,2,32,128]{3,2,1,0:T(8,128)} %to_rows.2), calls=%async_computation | async-start | bytes 2097152 | tf_op jit(solution)/shard_map/all_to_all | solution.py:325
  42.0 11.4 %copy-start = (f32[128,4,128]{2,1,0:T(4,128)S(1)}, f32[128,4,128]{2,1,0:T(4,128)}, u32[]{:S(2)}) copy-start(f32[128,4,128]{2,1,0:T(4,128)} %param.12) | copy-start | bytes 786436
  42.0 12.9 %copy-start.5 = (s32[8,8]{1,0:T(8,128)S(1)}, s32[8,8]{1,0:T(8,128)}, u32[]{:S(2)}) copy-start(s32[8,8]{1,0:T(8,128)} %param.14) | copy-start | bytes 772
  64.5 7.5 %copy-start.2 = (f32[8,32,16]{2,1,0:T(8,128)S(1)}, f32[8,32,16]{2,1,0:T(8,128)}, u32[]{:S(2)}) copy-start(f32[8,32,16]{2,1,0:T(8,128)} %project.1) | copy-start | bytes 49156
  67.4 59.4 %all-to-all-start.3 = ((f32[32,4,32,128]{3,2,1,0:T(8,128)}), f32[32,4,32,128]{3,2,1,0:T(8,128)}, u32[]{:S(2)}, u32[]{:S(2)}) async-start(f32[32,4,32,128]{3,2,1,0:T(8,128)} %get-tuple-element.7), calls=%async_computation.3 | async-start | bytes 4194304 | tf_op jit(solution)/shard_map/all_to_all | solution.py:409
  72.2 14.9 %copy-start.1 = (f32[128,16]{1,0:T(8,128)S(1)}, f32[128,16]{1,0:T(8,128)}, u32[]{:S(2)}) copy-start(f32[128,16]{1,0:T(8,128)} %convolution_bitcast_fusion._) | copy-start | bytes 24580
  72.2 32.2 %copy-start.3 = (f32[32,4]{0,1:T(4,128)S(1)}, f32[32,4]{0,1:T(4,128)}, u32[]{:S(2)}) copy-start(f32[32,4]{0,1:T(4,128)} %param.15) | copy-start | bytes 1540
  87.2 1.3 collective-permute-start
  88.5 3.7 %collective-permute-start.1 = (f32[136,16]{1,0:T(8,128)S(1)}, f32[136,16]{1,0:T(8,128)S(1)}, u32[]{:S(2)}, u32[]{:S(2)}) collective-permute-start(f32[136,16]{1,0:T(8,128)S(1)} %fusion.51), channel_id=1, source_target_pairs={{0,2},{1,3},{2,0},{3,1},{4,6},{5,7},{6,4},{7,5},{8,10},{9,11},{10,... | collective-permute-start | bytes 26120 | tf_op jit(solution)/shard_map/ppermute | solution.py:260
  92.2 7.8 %collective-permute-start.2 = (f32[136,16]{1,0:T(8,128)S(1)}, f32[136,16]{1,0:T(8,128)S(1)}, u32[]{:S(2)}, u32[]{:S(2)}) collective-permute-start(f32[136,16]{1,0:T(8,128)S(1)} %add.118), channel_id=1, source_target_pairs={{0,4},{1,5},{2,6},{3,7},{4,0},{5,1},{6,2},{7,3},{8,12},{9,13},{10,... | collective-permute-start | bytes 26120 | tf_op jit(solution)/shard_map/ppermute | solution.py:260
  100.1 11.3 %collective-permute-start.5 = (f32[136,16]{1,0:T(8,128)S(1)}, f32[136,16]{1,0:T(8,128)S(1)}, u32[]{:S(2)}, u32[]{:S(2)}) collective-permute-start(f32[136,16]{1,0:T(8,128)S(1)} %add.119), channel_id=1, source_target_pairs={{0,24},{1,25},{2,26},{3,27},{4,28},{5,29},{6,30},{7,31},{8,16},{9,... | collective-permute-start | bytes 26120 | tf_op jit(solution)/shard_map/ppermute | solution.py:260
  101.1 25.1 %collective-permute-start.4 = (f32[136,16]{1,0:T(8,128)S(1)}, f32[136,16]{1,0:T(8,128)S(1)}, u32[]{:S(2)}, u32[]{:S(2)}) collective-permute-start(f32[136,16]{1,0:T(8,128)S(1)} %add.119), channel_id=1, source_target_pairs={{0,16},{1,17},{2,18},{3,19},{4,20},{5,21},{6,22},{7,23},{8,24},{9,... | collective-permute-start | bytes 26120 | tf_op jit(solution)/shard_map/ppermute | solution.py:260
  104.5 21.7 %collective-permute-start.3 = (f32[136,16]{1,0:T(8,128)S(1)}, f32[136,16]{1,0:T(8,128)S(1)}, u32[]{:S(2)}, u32[]{:S(2)}) collective-permute-start(f32[136,16]{1,0:T(8,128)S(1)} %add.119), channel_id=1, source_target_pairs={{0,8},{1,9},{2,10},{3,11},{4,12},{5,13},{6,14},{7,15},{8,0},{9,1},... | collective-permute-start | bytes 26120 | tf_op jit(solution)/shard_map/ppermute | solution.py:260
  126.8 53.1 %all-to-all-start.1 = ((f32[32,4,32,128]{3,2,1,0:T(8,128)}), f32[32,4,32,128]{3,2,1,0:T(8,128)}, u32[]{:S(2)}, u32[]{:S(2)}) async-start(f32[32,4,32,128]{3,2,1,0:T(8,128)} %get-tuple-element.6), calls=%async_computation.1 | async-start | bytes 4194304 | tf_op jit(solution)/shard_map/all_to_all | solution.py:409

commit v6 on v4

--- a/solution.py
+++ b/solution.py
@@ -109,6 +109,29 @@
             out[:, p * each : (p + 1) * each, :] = along_y[
                 :, i * span_z : (i + 1) * span_z
             ].reshape(devices, each, span_z)
+
+
+def to_rows_split_kernel(my_layer, psi, y_table, *rest):
+    outs, staged = rest[:-1], rest[-1]
+    to_rows_kernel(psi, y_table, staged)
+    each = staged.shape[0] // len(outs)
+    for k, out in enumerate(outs):
+        out[...] = staged[pl.ds((my_layer[0] ^ k) * each, each)]
+
+
+def regroup_kernel(layers, my_member, *refs):
+    arrived, outs = refs[:layers], refs[layers + 1 :]
+    for k, out in enumerate(outs):
+        for layer in range(layers):
+            out[layer] = arrived[layer][my_member[0] ^ k]
+
+
+def real_space_parts_kernel(rows, planes, members, *refs):
+    arrived, rest, staged = refs[:members], refs[members:-1], refs[-1]
+    each = staged.shape[0] // members
+    for k in range(members):
+        staged[k * each : (k + 1) * each] = arrived[k][...]
+    real_space_kernel(rows, planes, staged, *rest)
 
 
 def real_space_kernel(rows, planes, recv, pot, inverse, forward, inv_z, fwd_z, _, back, field):
@@ -193,6 +216,10 @@
                 )
 
 
+def pass_on_kernel(values, _, out):
+    out[...] = values[...]
+
+
 def block_rows_of(psi, beta, slots):
     bands, _, span, span_z = psi.shape
     psi_flat = psi.reshape(bands * 2 * span, span_z)
@@ -297,36 +324,65 @@
 
     parts = 2 if pairs % 2 == 0 else 1
     share = pairs // parts
-    arrived = []
-    for c in range(parts):
-        sent = pl.pallas_call(
-            to_rows_kernel,
-            out_shape=jax.ShapeDtypeStruct((devices, share, block_rows, span_z), f32),
+    mine = lax.axis_index("ga").astype(jnp.int32)
+    layers = 4 if parts == 2 and devices >= 8 and devices & (devices - 1) == 0 else 1
+    members = devices // layers
+    my_layer, my_member = (mine // members).reshape(1), (mine % members).reshape(1)
+    scalar = pl.BlockSpec(memory_space=pltpu.SMEM)
+
+    def to_rows(c, split):
+        spec = pl.BlockSpec((devices, None, block_rows, span_z), lambda j: (0, j, 0, 0))
+        shape = jax.ShapeDtypeStruct((devices, share, block_rows, span_z), f32)
+        if split:
+            spec = pl.BlockSpec((members, None, block_rows, span_z), lambda j: (0, j, 0, 0))
+            shape = jax.ShapeDtypeStruct((members, share, block_rows, span_z), f32)
+        return pl.pallas_call(
+            to_rows_split_kernel if split else to_rows_kernel,
+            out_shape=[shape] * layers if split else shape,
             grid=(share,),
-            in_specs=[
-                pl.BlockSpec(
-                    (2, 2, planes, span_y, span_z), lambda j, c=c: (c * share + j, 0, 0, 0, 0)
-                ),
+            in_specs=([scalar] if split else [])
+            + [
+                pl.BlockSpec((2, 2, planes, span_y, span_z), lambda j: (c * share + j, 0, 0, 0, 0)),
                 whole(inv_y.shape),
             ],
-            out_specs=pl.BlockSpec((devices, None, block_rows, span_z), lambda j: (0, j, 0, 0)),
+            out_specs=[spec] * layers if split else spec,
+            scratch_shapes=[pltpu.VMEM((devices, block_rows, span_z), f32)] if split else [],
             compiler_params=params,
             cost_estimate=cost(4 * 10**9, 3 * 10**6),
             name="to_rows",
-        )(orbitals, inv_y)
-        arrived.append(lax.all_to_all(sent, "ga", split_axis=0, concat_axis=0, tiled=True))
-
-    stored = plane_order.reshape(devices, planes).T.reshape(-1)
-    phases = (stored[:, None] * grid_x[None, :]) % span_x
-    angles = phases.astype(f32) * (2.0 * math.pi / span_x)
-    factor = 1.0 / math.sqrt(span_x)
-    cosine, sine = jnp.cos(angles) * factor, jnp.sin(angles) * factor
-    fwd_x = jnp.concatenate([cosine, -sine], axis=0)
-    inv_x = jnp.concatenate([fwd_x, jnp.concatenate([sine, cosine], axis=0)], axis=1).T
-    high, low = split_outside(fwd_x)
-    fwd_x = jnp.concatenate([high, high, low], axis=1)
-    high, low = split_outside(inv_x)
-    inv_x = jnp.concatenate([high, high, low], axis=1)
+        )(*([my_layer] if split else []), orbitals, inv_y)
+
+    arrived = []
+    for c in range(parts):
+        if c > 0 and layers > 1:
+            sent = to_rows(c, True)
+            arrived.append(
+                [sent[0]] + [partner(sent[k], devices, k * members) for k in range(1, layers)]
+            )
+        else:
+            arrived.append(
+                lax.all_to_all(to_rows(c, False), "ga", split_axis=0, concat_axis=0, tiled=True)
+            )
+
+    def tables_x(owned):
+        phases = (owned.T.reshape(-1)[:, None] * grid_x[None, :]) % span_x
+        angles = phases.astype(f32) * (2.0 * math.pi / span_x)
+        factor = 1.0 / math.sqrt(span_x)
+        cosine, sine = jnp.cos(angles) * factor, jnp.sin(angles) * factor
+        forward = jnp.concatenate([cosine, -sine], axis=0)
+        inverse = jnp.concatenate([forward, jnp.concatenate([sine, cosine], axis=0)], axis=1).T
+        tables = []
+        for table in (forward, inverse):
+            high, low = split_outside(table)
+            tables.append(jnp.concatenate([high, high, low], axis=1))
+        return tables
+
+    owned = plane_order.reshape(devices, planes)
+    fwd_x, inv_x = tables_x(owned)
+    steps = np.arange(layers)[None, :] * members + np.arange(members)[:, None]
+    _, inv_x_steps = tables_x(
+        jnp.take(owned, mine ^ jnp.asarray(steps.reshape(-1), jnp.int32), axis=0)
+    )
     pot = potential.transpose(1, 0, 2).reshape(rows * span_x, span_z)
 
     local_order = lax.dynamic_slice_in_dim(plane_order, lax.axis_index("ga") * planes, planes)
@@ -365,24 +421,46 @@
         ],
         axis=-1,
     )
-    owned = (
+    chosen = (
         slot_owner[:, :, None] == jnp.arange(owners, dtype=jnp.int32)[None, None, :]
     ).astype(f32)
-    proj = tdot("gsj,gsc->jc", owned, proj)
+    proj = tdot("gsj,gsc->jc", chosen, proj)
     kin = jnp.sum(products[:, 2 * slots :], axis=0).reshape(bands, 2, bands, 2)
     kin = kin[:, 0, :, 0] + kin[:, 1, :, 1]
 
-    returned, fields = [], []
+    returned, fields, backs = [], [], []
     for c in range(parts):
+        steps = c > 0 and layers > 1
+        if steps:
+            regrouped = pl.pallas_call(
+                functools.partial(regroup_kernel, layers),
+                out_shape=[jax.ShapeDtypeStruct((layers, share, block_rows, span_z), f32)] * members,
+                in_specs=[scalar]
+                + [pl.BlockSpec(memory_space=pltpu.VMEM)] * layers
+                + [pl.BlockSpec(memory_space=pl.ANY)],
+                out_specs=[pl.BlockSpec(memory_space=pltpu.VMEM)] * members,
+                compiler_params=params,
+                cost_estimate=cost(0, 2 * 10**6),
+                name="regroup",
+            )(my_member, *arrived[c], backs[0])
+            operands = [regrouped[0]] + [
+                partner(regrouped[k], devices, k) for k in range(1, members)
+            ]
+            kernel = functools.partial(real_space_parts_kernel, rows, planes, members)
+            spec = pl.BlockSpec((layers, None, block_rows, span_z), lambda j: (0, j, 0, 0))
+        else:
+            operands = [arrived[c]]
+            kernel = functools.partial(real_space_kernel, rows, planes)
+            spec = pl.BlockSpec((devices, None, block_rows, span_z), lambda j: (0, j, 0, 0))
         back, field = pl.pallas_call(
-            functools.partial(real_space_kernel, rows, planes),
+            kernel,
             out_shape=(
                 jax.ShapeDtypeStruct((devices, 2 * share, block_rows, span_z), f32),
                 jax.ShapeDtypeStruct((2 * share, rows * span_x, span_z), f32),
             ),
             grid=(share,),
-            in_specs=[
-                pl.BlockSpec((devices, None, block_rows, span_z), lambda j: (0, j, 0, 0)),
+            in_specs=[spec] * len(operands)
+            + [
                 whole(pot.shape),
                 whole(inv_x.shape),
                 whole(fwd_x.shape),
@@ -394,12 +472,14 @@
                 pl.BlockSpec((devices, 2, block_rows, span_z), lambda j: (0, j, 0, 0)),
                 pl.BlockSpec((2, rows * span_x, span_z), lambda j: (j, 0, 0)),
             ),
+            scratch_shapes=[pltpu.VMEM((devices, block_rows, span_z), f32)] if steps else [],
             compiler_params=params,
             cost_estimate=cost(4 * 10**9, 8 * 10**6),
             name="real_space",
-        )(arrived[c], pot, inv_x, fwd_x, inv_z, fwd_z, proj)
+        )(*operands, pot, inv_x_steps if steps else inv_x, fwd_x, inv_z, fwd_z, proj)
         returned.append(lax.all_to_all(back, "ga", split_axis=0, concat_axis=0, tiled=True))
         fields.append(field)
+        backs.append(back)
 
     grams = pl.pallas_call(
         functools.partial(real_gram_kernel, bands),
@@ -411,6 +491,13 @@
     grams = jnp.sum(grams, axis=-1)
     own = jnp.concatenate([proj, jnp.concatenate([grams[0], grams[1] + kin], axis=1)], axis=0)
     total = sum_over(own, devices)
+    total = pl.pallas_call(
+        pass_on_kernel,
+        out_shape=jax.ShapeDtypeStruct(total.shape, f32),
+        in_specs=[pl.BlockSpec(memory_space=pltpu.VMEM), pl.BlockSpec(memory_space=pl.ANY)],
+        out_specs=pl.BlockSpec(memory_space=pltpu.VMEM),
+        name="pass_on",
+    )(total, returned[0])
     proj, s_real, h_real = total[:owners], total[owners:, :bands], total[owners:, bands:]
     weighted = strengths.reshape(-1)[:, None] * proj
     p_real, p_imag = proj[:, :bands], proj[:, bands:]
@@ -419,7 +506,7 @@
     h_imag = tdot("ja,jb->ab", p_real, w_imag) - tdot("ja,jb->ab", p_imag, w_real)
     m_real, m_imag = subspace_solve(s_real, h_real, h_imag)
 
-    coefs = tdot("gsj,jc->gcs", owned, weighted)
+    coefs = tdot("gsj,jc->gcs", chosen, weighted)
     c_real, c_imag = coefs[:, :bands], coefs[:, bands:]
     from_beta = jnp.stack(
         [

time: 182 us -> 232 us (1.27)
  waiting for transfers between devices: 76.6 us -> 98.5 us
  starting transfers between devices: 29.2 us -> 41.4 us
  matrix products: 1.33 us -> 6.01 us
  Pallas kernels: 59.5 us -> 63.7 us
  other arithmetic: 7.49 us -> 11.5 us
  local copies, waits for them, and re-layouts: 5.14 us -> 8.07 us
    ppermute x6 -> x16, waiting for transfers between devices: 26.1 us -> 71.3 us  [partner(): return lax.ppermute(values, 'ga', [(d, d ^ k) for d in range(devices)])]
    ppermute x6 -> x16, starting transfers between devices: 8.26 us -> 22.1 us  [partner(): return lax.ppermute(values, 'ga', [(d, d ^ k) for d in range(devices)])]
    all_to_all x2 -> x1, waiting for transfers between devices: 22.6 us -> 8.94 us  [on_device(): lax.all_to_all(to_rows(c, False), 'ga', split_axis=0, concat_axis=0, tile...]
    all_to_all x2, waiting for transfers between devices: 27.9 us -> 18.2 us  [on_device(): lax.all_to_all(back, 'ga', split_axis=0, concat_axis=0, tiled=True)]
    dot_general x6, matrix products: 0.99 us -> 5.63 us  [tdot(): jnp.einsum(pattern, left, right, precision=highest, preferred_element_typ...]
    all_to_all x2 -> x1, starting transfers between devices: 11.7 us -> 7.15 us  [on_device(): lax.all_to_all(to_rows(c, False), 'ga', split_axis=0, concat_axis=0, tile...]
    pallas_call x4 -> x6, Pallas kernels: 23.1 us -> 27.4 us  [the longest x2 17.6 us: on_device(): pl.pallas_call(kernel, out_shape=(jax.ShapeDtypeStruct((devices, 2 * shar...]
    all_to_all x2, starting transfers between devices: 9.19 us -> 12.2 us  [on_device(): lax.all_to_all(back, 'ga', split_axis=0, concat_axis=0, tiled=True)]
  transfers between devices with their start and end apart: 10 -> 19, of which waited for: 8 -> 10; matrix products, arithmetic and copies ran while one was open for 8% -> 10% of each run, Pallas kernels for 29% -> 20%
where the time goes in v6:
time: 232 us; the launch traced here: 230 us
  waiting for transfers between devices  98.5 us (42%)
  Pallas kernels  63.7 us (27%)
  starting transfers between devices  41.4 us (18%)
  other arithmetic  11.5 us (5%)
  local copies, waits for them, and re-layouts  8.07 us (3%)
  matrix products  6.01 us (3%)
    ppermute x16, waiting for transfers between devices, partner(): return lax.ppermute(values, 'ga', [(d, d ^ k) for d in range(devices)])  71.3 us
    ppermute x16, starting transfers between devices, partner(): return lax.ppermute(values, 'ga', [(d, d ^ k) for d in range(devices)])  22.1 us
    all_to_all x2, waiting for transfers between devices, on_device(): lax.all_to_all(back, 'ga', split_axis=0, concat_axis=0, tiled=True)  18.2 us
    pallas_call x2, Pallas kernels, on_device(): pl.pallas_call(kernel, out_shape=(jax.ShapeDtypeStruct((devices, 2 * shar...  17.6 us
    all_to_all x2, starting transfers between devices, on_device(): lax.all_to_all(back, 'ga', split_axis=0, concat_axis=0, tiled=True)  12.2 us
    pallas_call x1, Pallas kernels, on_device(): pl.pallas_call(functools.partial(base_kernel, slots), out_shape=jax.Shape...  11.2 us
    pallas_call x1, Pallas kernels, on_device(): pl.pallas_call(functools.partial(project_kernel, slots), out_shape=jax.Sh...  10.1 us
    pallas_call x2, Pallas kernels, on_device(): pl.pallas_call(to_planes_kernel, out_shape=jax.ShapeDtypeStruct(orbitals....  9.91 us
  transfers between devices with their start and end apart: 19, of which 10 were waited for; matrix products, arithmetic and copies ran while one was open for 10% of the time, Pallas kernels for 20%

profile of v6, /device:TPU:1, one launch (start us, length us, event | category | flops | bytes accessed | tf_op | source)
XLA Modules:
  0.0 230.1 jit_solution(9816197145856532294)
XLA Ops:
  0.6 3.0 %to_rows.3 = f32[32,2,32,128]{3,2,1,0:T(8,128)} custom-call(f32[8,2,4,128,128]{4,3,2,1,0:T(8,128)} %psi.7, bf16[256,768]{1,0:T(8,128)(2,1)} %constant.146.clone.y_table), custom_call_target="tpu_custom_call" | custom-call | flops 4000000000 | bytes 3000000 | tf_op jit(solution)/shard_map/to_rows/pallas_call | solution.py:339
  3.6 7.2 %all-to-all-start = ((f32[32,2,32,128]{3,2,1,0:T(8,128)}), f32[32,2,32,128]{3,2,1,0:T(8,128)}, u32[]{:S(2)}, u32[]{:S(2)}) async-start(f32[32,2,32,128]{3,2,1,0:T(8,128)} %to_rows.3), calls=%async_computation | async-start | bytes 2097152 | tf_op jit(solution)/shard_map/all_to_all | solution.py:364
  11.6 0.8 add_multiply_fusion.kinetic
  12.5 0.9 copy.123.inverse
  13.4 10.1 %project.1 = f32[8,32,16]{2,1,0:T(8,128)} custom-call(f32[8,2,4,128,128]{4,3,2,1,0:T(8,128)} %psi.7, f32[8,1024,128]{2,1,0:T(8,128)} %bitcast.95, f32[4,128,128]{2,1,0:T(8,128)} %add_multiply_fusion.kinetic), custom_call_target="tpu_custom_call" | custom-call | flops 8000000000 | bytes 8000000 | tf_op jit(solution)/shard_map/project/pallas_call | solution.py:405
  23.5 0.8 fusion.55
  26.3 0.9 convolution_bitcast_fusion._.refs_13_
  27.2 8.9 %all-to-all-done.recv = f32[32,2,32,128]{3,2,1,0:T(8,128)} async-done(((f32[32,2,32,128]{3,2,1,0:T(8,128)}), f32[32,2,32,128]{3,2,1,0:T(8,128)}, u32[]{:S(2)}, u32[]{:S(2)}) %all-to-all-start) | async-done | bytes 1048608 | tf_op jit(solution)/shard_map/all_to_all | solution.py:364
  36.1 8.6 %real_space.2 = (f32[32,4,32,128]{3,2,1,0:T(8,128)}, f32[4,512,128]{2,1,0:T(8,128)}) custom-call(f32[32,2,32,128]{3,2,1,0:T(8,128)} %all-to-all-done.recv, f32[512,128]{1,0:T(8,128)} %bitcast.85, bf16[256,768]{1,0:T(8,128)(2,1)} %copy.123.inverse, bf16[256,384]{1,0:T(8,128)(2,1)} %pad_maximum_fusion.2.forward.refs_10_, ...), custom_call_target="tpu_custom_call" | custom-call | flops 4000000000 | bytes 8000000 | tf_op jit(solution)/shard_map/real_space/pallas_call | solution.py:455
  44.8 4.6 %all-to-all-start.2 = ((f32[32,4,32,128]{3,2,1,0:T(8,128)}), f32[32,4,32,128]{3,2,1,0:T(8,128)}, u32[]{:S(2)}, u32[]{:S(2)}) async-start(f32[32,4,32,128]{3,2,1,0:T(8,128)} %get-tuple-element.22.refs_4_), calls=%async_computation.2 | async-start | bytes 4194304 | tf_op jit(solution)/shard_map/all_to_all | solution.py:480
  49.4 3.1 %to_rows.2 = (f32[8,2,32,128]{3,2,1,0:T(8,128)}, f32[8,2,32,128]{3,2,1,0:T(8,128)}, f32[8,2,32,128]{3,2,1,0:T(8,128)}, f32[8,2,32,128]{3,2,1,0:T(8,128)}) custom-call(s32[1]{0:T(128)} %bitcast.1.my_layer, f32[8,2,4,128,128]{4,3,2,1,0:T(8,128)} %psi.7, bf16[256,768]{1,0:T(8,128)(2,1)} %constant.146.clone.y_table), custom_call_target="tpu_custom_call" | custom-call | flops 4000000000 | bytes 3000000 | tf_op jit(solution)/shard_map/to_rows/pallas_call | solution.py:339
  52.5 1.4 collective-permute-start
  53.9 2.1 collective-permute-start.1
  57.2 32.4 %collective-permute-done.refs_1_ = f32[8,2,32,128]{3,2,1,0:T(8,128)S(1)} collective-permute-done((f32[8,2,32,128]{3,2,1,0:T(8,128)}, f32[8,2,32,128]{3,2,1,0:T(8,128)S(1)}, u32[]{:S(2)}, u32[]{:S(2)}) %collective-permute-start) | collective-permute-done | bytes 262176 | tf_op jit(solution)/shard_map/ppermute | solution.py:283
  89.6 24.8 %collective-permute-done.1.refs_2_ = f32[8,2,32,128]{3,2,1,0:T(8,128)S(1)} collective-permute-done((f32[8,2,32,128]{3,2,1,0:T(8,128)}, f32[8,2,32,128]{3,2,1,0:T(8,128)S(1)}, u32[]{:S(2)}, u32[]{:S(2)}) %collective-permute-start.1) | collective-permute-done | bytes 262176 | tf_op jit(solution)/shard_map/ppermute | solution.py:283
  115.3 2.2 regroup.1
  117.5 1.3 collective-permute-start.3
  118.8 1.1 collective-permute-start.4
  120.6 1.0 collective-permute-start.6
  121.6 0.8 collective-permute-start.7
  122.5 1.9 collective-permute-start.8
  124.4 2.8 %collective-permute-start.9 = (f32[4,2,32,128]{3,2,1,0:T(8,128)}, f32[4,2,32,128]{3,2,1,0:T(8,128)S(1)}, u32[]{:S(2)}, u32[]{:S(2)}) collective-permute-start(f32[4,2,32,128]{3,2,1,0:T(8,128)} %get-tuple-element.30), channel_id=1, source_target_pairs={{0,7},{1,6},{2,5},{3,4},{4,3},{5,2},{6,1},{7,0},{8,15},{9,14},{10,... | collective-permute-start | bytes 393224 | tf_op jit(solution)/shard_map/ppermute | solution.py:283
  127.2 0.9 slice_reduce_fusion
  128.1 0.9 copy.126.refs_9_
  129.3 5.2 %collective-permute-done.7.refs_5_ = f32[4,2,32,128]{3,2,1,0:T(8,128)S(1)} collective-permute-done((f32[4,2,32,128]{3,2,1,0:T(8,128)}, f32[4,2,32,128]{3,2,1,0:T(8,128)S(1)}, u32[]{:S(2)}, u32[]{:S(2)}) %collective-permute-start.7) | collective-permute-done | bytes 131104 | tf_op jit(solution)/shard_map/ppermute | solution.py:283
  135.3 8.9 %real_space.3 = (f32[32,4,32,128]{3,2,1,0:T(8,128)}, f32[4,512,128]{2,1,0:T(8,128)}) custom-call(f32[4,2,32,128]{3,2,1,0:T(8,128)} %get-tuple-element.23.refs_0_, f32[4,2,32,128]{3,2,1,0:T(8,128)} %copy-done.8, f32[4,2,32,128]{3,2,1,0:T(8,128)} %copy-done.9, f32[4,2,32,128]{3,2,1,0:T(8,128)} %copy-done.10, f32[4,2,32,128]{3,2,1,0:T(8,128)} %copy-done.11, ...), custom_call_target="tpu_custom_call" | custom-call | flops 4000000000 | bytes 8000000 | tf_op jit(solution)/shard_map/real_space/pallas_call | solution.py:455
  144.2 5.2 %real_gram.1 = f32[2,8,8,128]{3,2,1,0:T(8,128)} custom-call(f32[4,512,128]{2,1,0:T(8,128)} %get-tuple-element.32.refs_0_, f32[4,512,128]{2,1,0:T(8,128)} %get-tuple-element.33.refs_1_, f32[512,128]{1,0:T(8,128)} %bitcast.87), custom_call_target="tpu_custom_call" | custom-call | flops 10000000 | bytes 2000000 | tf_op jit(solution)/shard_map/real_gram/pallas_call | solution.py:484
  149.4 0.9 reduce_sum.18
  150.5 1.2 collective-permute-done.10
  151.8 1.1 collective-permute-start.11
  152.9 2.5 %collective-permute-done.11 = f32[136,16]{1,0:T(8,128)S(1)} collective-permute-done((f32[136,16]{1,0:T(8,128)S(1)}, f32[136,16]{1,0:T(8,128)S(1)}, u32[]{:S(2)}, u32[]{:S(2)}) %collective-permute-start.11) | collective-permute-done | bytes 8736 | tf_op jit(solution)/shard_map/ppermute | solution.py:283
  155.4 1.1 collective-permute-start.12
  156.5 2.1 collective-permute-done.12
  158.7 1.1 collective-permute-start.15
  159.8 5.4 %collective-permute-start.14 = (f32[136,16]{1,0:T(8,128)S(1)}, f32[136,16]{1,0:T(8,128)S(1)}, u32[]{:S(2)}, u32[]{:S(2)}) collective-permute-start(f32[136,16]{1,0:T(8,128)S(1)} %add.140), channel_id=1, source_target_pairs={{0,16},{1,17},{2,18},{3,19},{4,20},{5,21},{6,22},{7,23},{8,24},{9,... | collective-permute-start | bytes 26120 | tf_op jit(solution)/shard_map/ppermute | solution.py:283
  165.4 2.3 %collective-permute-done.14 = f32[136,16]{1,0:T(8,128)S(1)} collective-permute-done((f32[136,16]{1,0:T(8,128)S(1)}, f32[136,16]{1,0:T(8,128)S(1)}, u32[]{:S(2)}, u32[]{:S(2)}) %collective-permute-start.14) | collective-permute-done | bytes 8736 | tf_op jit(solution)/shard_map/ppermute | solution.py:283
  169.2 7.6 %all-to-all-start.1 = ((f32[32,4,32,128]{3,2,1,0:T(8,128)}), f32[32,4,32,128]{3,2,1,0:T(8,128)}, u32[]{:S(2)}, u32[]{:S(2)}) async-start(f32[32,4,32,128]{3,2,1,0:T(8,128)} %get-tuple-element.31), calls=%async_computation.1 | async-start | bytes 4194304 | tf_op jit(solution)/shard_map/all_to_all | solution.py:480
  176.8 1.5 pass_on.1
  179.0 0.9 slice_multiply_fusion
  179.9 1.1 fusion.17
  181.0 1.1 fusion.23
  182.2 0.9 fusion.45
  185.7 1.1 fusion.19
  186.9 1.1 convolution_subtract_fusion
  190.8 11.2 %base.1 = f32[8,2,4,128,128]{4,3,2,1,0:T(8,128)} custom-call(f32[8,2,4,128,128]{4,3,2,1,0:T(8,128)} %psi.7, f32[8,1024,128]{2,1,0:T(8,128)} %bitcast.96, f32[4,128,128]{2,1,0:T(8,128)} %add_multiply_fusion.kinetic, f32[8,16,32]{2,1,0:T(8,128)} %pad_maximum_fusion.5.coefs), custom_call_target="tpu_custom_call" | custom-call | flops 8000000000 | bytes 12000000 | tf_op jit(solution)/shard_map/base/pallas_call | solution.py:528
  202.0 4.9 %to_planes.2.base = f32[8,2,4,128,128]{4,3,2,1,0:T(8,128)} custom-call(f32[32,4,32,128]{3,2,1,0:T(8,128)} %all-to-all-done.2._.recv, f32[8,2,4,128,128]{4,3,2,1,0:T(8,128)} %base.1, bf16[256,768]{1,0:T(8,128)(2,1)} %constant.147.clone.y_table), custom_call_target="tpu_custom_call", output_to_operand_aliasing={{}: (1, {})} | custom-call | flops 8000000000 | bytes 12000000 | tf_op jit(solution)/shard_map/to_planes/pallas_call | solution.py:545
  206.9 18.2 %all-to-all-done.1.recv = f32[32,4,32,128]{3,2,1,0:T(8,128)} async-done(((f32[32,4,32,128]{3,2,1,0:T(8,128)}), f32[32,4,32,128]{3,2,1,0:T(8,128)}, u32[]{:S(2)}, u32[]{:S(2)}) %all-to-all-start.1) | async-done | bytes 2097184 | tf_op jit(solution)/shard_map/all_to_all | solution.py:480
  225.1 5.0 %to_planes.3 = f32[8,2,4,128,128]{4,3,2,1,0:T(8,128)} custom-call(f32[32,4,32,128]{3,2,1,0:T(8,128)} %all-to-all-done.1.recv, f32[8,2,4,128,128]{4,3,2,1,0:T(8,128)} %to_planes.2.base, bf16[256,768]{1,0:T(8,128)(2,1)} %constant.147.clone.y_table), custom_call_target="tpu_custom_call", output_to_operand_aliasing={{}: (1, {})} | custom-call | flops 8000000000 | bytes 12000000 | tf_op jit(solution)/shard_map/to_planes/pallas_call | solution.py:545
  (115 shorter events, 14.6 us)
Async XLA Ops:
  0.6 10.2 %copy-start.6 = (s32[128]{0:T(128)S(1)}, s32[128]{0:T(128)}, u32[]{:S(2)}) copy-start(s32[128]{0:T(128)} %param.12) | copy-start | bytes 1540
  3.6 32.5 %all-to-all-start = ((f32[32,2,32,128]{3,2,1,0:T(8,128)}), f32[32,2,32,128]{3,2,1,0:T(8,128)}, u32[]{:S(2)}, u32[]{:S(2)}) async-start(f32[32,2,32,128]{3,2,1,0:T(8,128)} %to_rows.3), calls=%async_computation | async-start | bytes 2097152 | tf_op jit(solution)/shard_map/all_to_all | solution.py:364
  13.4 11.4 %copy-start = (f32[128,4,128]{2,1,0:T(4,128)S(1)}, f32[128,4,128]{2,1,0:T(4,128)}, u32[]{:S(2)}) copy-start(f32[128,4,128]{2,1,0:T(4,128)} %param.13) | copy-start | bytes 786436
  13.4 12.8 %copy-start.15 = (s32[8,8]{1,0:T(8,128)S(1)}, s32[8,8]{1,0:T(8,128)}, u32[]{:S(2)}) copy-start(s32[8,8]{1,0:T(8,128)} %param.15) | copy-start | bytes 772
  44.8 124.4 %all-to-all-start.2 = ((f32[32,4,32,128]{3,2,1,0:T(8,128)}), f32[32,4,32,128]{3,2,1,0:T(8,128)}, u32[]{:S(2)}, u32[]{:S(2)}) async-start(f32[32,4,32,128]{3,2,1,0:T(8,128)} %get-tuple-element.22.refs_4_), calls=%async_computation.2 | async-start | bytes 4194304 | tf_op jit(solution)/shard_map/all_to_all | solution.py:480
  49.4 6.7 %copy-start.7 = (s32[32]{0:T(128)S(1)}, s32[32]{0:T(128)}, u32[]{:S(2)}) copy-start(s32[32]{0:T(128)} %constant.150.clone) | copy-start | bytes 388
  52.5 37.2 %collective-permute-start = (f32[8,2,32,128]{3,2,1,0:T(8,128)}, f32[8,2,32,128]{3,2,1,0:T(8,128)S(1)}, u32[]{:S(2)}, u32[]{:S(2)}) collective-permute-start(f32[8,2,32,128]{3,2,1,0:T(8,128)} %get-tuple-element.19), channel_id=1, source_target_pairs={{0,8},{1,9},{2,10},{3,11},{4,12},{5,13},{6,14},{7,15},{8,0},{9,1},... | collective-permute-start | bytes 786440 | tf_op jit(solution)/shard_map/ppermute | solution.py:283
  53.9 60.6 %collective-permute-start.1 = (f32[8,2,32,128]{3,2,1,0:T(8,128)}, f32[8,2,32,128]{3,2,1,0:T(8,128)S(1)}, u32[]{:S(2)}, u32[]{:S(2)}) collective-permute-start(f32[8,2,32,128]{3,2,1,0:T(8,128)} %get-tuple-element.20), channel_id=1, source_target_pairs={{0,16},{1,17},{2,18},{3,19},{4,20},{5,21},{6,22},{7,23},{8,24},{9,... | collective-permute-start | bytes 786440 | tf_op jit(solution)/shard_map/ppermute | solution.py:283
  56.0 58.5 %collective-permute-start.2 = (f32[8,2,32,128]{3,2,1,0:T(8,128)}, f32[8,2,32,128]{3,2,1,0:T(8,128)S(1)}, u32[]{:S(2)}, u32[]{:S(2)}) collective-permute-start(f32[8,2,32,128]{3,2,1,0:T(8,128)} %get-tuple-element.21), channel_id=1, source_target_pairs={{0,24},{1,25},{2,26},{3,27},{4,28},{5,29},{6,30},{7,31},{8,16},{9,... | collective-permute-start | bytes 786440 | tf_op jit(solution)/shard_map/ppermute | solution.py:283
  89.6 24.8 %copy-start.2 = (f32[8,2,32,128]{3,2,1,0:T(8,128)}, f32[8,2,32,128]{3,2,1,0:T(8,128)S(1)}, u32[]{:S(2)}) copy-start(f32[8,2,32,128]{3,2,1,0:T(8,128)S(1)} %collective-permute-done.refs_1_) | copy-start | bytes 786436
  114.4 0.7 copy-start.3
  114.4 0.8 copy-start.4
  117.5 5.0 %collective-permute-start.3 = (f32[4,2,32,128]{3,2,1,0:T(8,128)}, f32[4,2,32,128]{3,2,1,0:T(8,128)S(1)}, u32[]{:S(2)}, u32[]{:S(2)}) collective-permute-start(f32[4,2,32,128]{3,2,1,0:T(8,128)} %get-tuple-element.24), channel_id=1, source_target_pairs={{0,1},{1,0},{2,3},{3,2},{4,5},{5,4},{6,7},{7,6},{8,9},{9,8},{10,11... | collective-permute-start | bytes 393224 | tf_op jit(solution)/shard_map/ppermute | solution.py:283
  118.8 5.6 %collective-permute-start.4 = (f32[4,2,32,128]{3,2,1,0:T(8,128)}, f32[4,2,32,128]{3,2,1,0:T(8,128)S(1)}, u32[]{:S(2)}, u32[]{:S(2)}) collective-permute-start(f32[4,2,32,128]{3,2,1,0:T(8,128)} %get-tuple-element.25), channel_id=1, source_target_pairs={{0,2},{1,3},{2,0},{3,1},{4,6},{5,7},{6,4},{7,5},{8,10},{9,11},{10,... | collective-permute-start | bytes 393224 | tf_op jit(solution)/shard_map/ppermute | solution.py:283
  120.0 9.2 %collective-permute-start.5 = (f32[4,2,32,128]{3,2,1,0:T(8,128)}, f32[4,2,32,128]{3,2,1,0:T(8,128)S(1)}, u32[]{:S(2)}, u32[]{:S(2)}) collective-permute-start(f32[4,2,32,128]{3,2,1,0:T(8,128)} %get-tuple-element.26), channel_id=1, source_target_pairs={{0,3},{1,2},{2,1},{3,0},{4,7},{5,6},{6,5},{7,4},{8,11},{9,10},{10,... | collective-permute-start | bytes 393224 | tf_op jit(solution)/shard_map/ppermute | solution.py:283
  120.6 8.6 %collective-permute-start.6 = (f32[4,2,32,128]{3,2,1,0:T(8,128)}, f32[4,2,32,128]{3,2,1,0:T(8,128)S(1)}, u32[]{:S(2)}, u32[]{:S(2)}) collective-permute-start(f32[4,2,32,128]{3,2,1,0:T(8,128)} %get-tuple-element.27), channel_id=1, source_target_pairs={{0,4},{1,5},{2,6},{3,7},{4,0},{5,1},{6,2},{7,3},{8,12},{9,13},{10,... | collective-permute-start | bytes 393224 | tf_op jit(solution)/shard_map/ppermute | solution.py:283
  121.6 12.8 %collective-permute-start.7 = (f32[4,2,32,128]{3,2,1,0:T(8,128)}, f32[4,2,32,128]{3,2,1,0:T(8,128)S(1)}, u32[]{:S(2)}, u32[]{:S(2)}) collective-permute-start(f32[4,2,32,128]{3,2,1,0:T(8,128)} %get-tuple-element.28), channel_id=1, source_target_pairs={{0,5},{1,4},{2,7},{3,6},{4,1},{5,0},{6,3},{7,2},{8,13},{9,12},{10,... | collective-permute-start | bytes 393224 | tf_op jit(solution)/shard_map/ppermute | solution.py:283
  122.5 12.7 %copy-start.8 = (f32[4,2,32,128]{3,2,1,0:T(8,128)}, f32[4,2,32,128]{3,2,1,0:T(8,128)S(1)}, u32[]{:S(2)}) copy-start(f32[4,2,32,128]{3,2,1,0:T(8,128)S(1)} %collective-permute-done.3.refs_1_) | copy-start | bytes 393220
  122.5 12.0 %collective-permute-start.8 = (f32[4,2,32,128]{3,2,1,0:T(8,128)}, f32[4,2,32,128]{3,2,1,0:T(8,128)S(1)}, u32[]{:S(2)}, u32[]{:S(2)}) collective-permute-start(f32[4,2,32,128]{3,2,1,0:T(8,128)} %get-tuple-element.29), channel_id=1, source_target_pairs={{0,6},{1,7},{2,4},{3,5},{4,2},{5,3},{6,0},{7,1},{8,14},{9,15},{10,... | collective-permute-start | bytes 393224 | tf_op jit(solution)/shard_map/ppermute | solution.py:283
  124.4 10.8 %copy-start.9 = (f32[4,2,32,128]{3,2,1,0:T(8,128)}, f32[4,2,32,128]{3,2,1,0:T(8,128)S(1)}, u32[]{:S(2)}) copy-start(f32[4,2,32,128]{3,2,1,0:T(8,128)S(1)} %collective-permute-done.4.refs_2_) | copy-start | bytes 393220
  124.4 10.1 %collective-permute-start.9 = (f32[4,2,32,128]{3,2,1,0:T(8,128)}, f32[4,2,32,128]{3,2,1,0:T(8,128)S(1)}, u32[]{:S(2)}, u32[]{:S(2)}) collective-permute-start(f32[4,2,32,128]{3,2,1,0:T(8,128)} %get-tuple-element.30), channel_id=1, source_target_pairs={{0,7},{1,6},{2,5},{3,4},{4,3},{5,2},{6,1},{7,0},{8,15},{9,14},{10,... | collective-permute-start | bytes 393224 | tf_op jit(solution)/shard_map/ppermute | solution.py:283
  129.3 5.9 %copy-start.10 = (f32[4,2,32,128]{3,2,1,0:T(8,128)}, f32[4,2,32,128]{3,2,1,0:T(8,128)S(1)}, u32[]{:S(2)}) copy-start(f32[4,2,32,128]{3,2,1,0:T(8,128)S(1)} %collective-permute-done.5.refs_3_) | copy-start | bytes 393220
  129.3 5.9 %copy-start.11 = (f32[4,2,32,128]{3,2,1,0:T(8,128)}, f32[4,2,32,128]{3,2,1,0:T(8,128)S(1)}, u32[]{:S(2)}) copy-start(f32[4,2,32,128]{3,2,1,0:T(8,128)S(1)} %collective-permute-done.6.refs_4_) | copy-start | bytes 393220
  134.5 0.7 copy-start.12
  134.5 0.8 copy-start.13
  134.5 0.7 copy-start.14
  135.3 15.1 %copy-start.1 = (f32[128,16]{1,0:T(8,128)S(1)}, f32[128,16]{1,0:T(8,128)}, u32[]{:S(2)}) copy-start(f32[128,16]{1,0:T(8,128)} %convolution_bitcast_fusion._.refs_13_) | copy-start | bytes 24580
  135.3 30.0 %copy-start.5 = (f32[32,4]{0,1:T(4,128)S(1)}, f32[32,4]{0,1:T(4,128)}, u32[]{:S(2)}) copy-start(f32[32,4]{0,1:T(4,128)} %param.16) | copy-start | bytes 1540
  150.4 1.3 collective-permute-start.10
  151.8 37.3 %copy-start.16 = (s32[8,8]{1,0:T(8,128)S(1)}, s32[8,8]{1,0:T(8,128)}, u32[]{:S(2)}) copy-start(s32[8,8]{1,0:T(8,128)} %param.15) | copy-start | bytes 772
  151.8 3.6 %collective-permute-start.11 = (f32[136,16]{1,0:T(8,128)S(1)}, f32[136,16]{1,0:T(8,128)S(1)}, u32[]{:S(2)}, u32[]{:S(2)}) collective-permute-start(f32[136,16]{1,0:T(8,128)S(1)} %fusion.59), channel_id=1, source_target_pairs={{0,2},{1,3},{2,0},{3,1},{4,6},{5,7},{6,4},{7,5},{8,10},{9,11},{10,... | collective-permute-start | bytes 26120 | tf_op jit(solution)/shard_map/ppermute | solution.py:283
  155.4 3.2 %collective-permute-start.12 = (f32[136,16]{1,0:T(8,128)S(1)}, f32[136,16]{1,0:T(8,128)S(1)}, u32[]{:S(2)}, u32[]{:S(2)}) collective-permute-start(f32[136,16]{1,0:T(8,128)S(1)} %add.139), channel_id=1, source_target_pairs={{0,4},{1,5},{2,6},{3,7},{4,0},{5,1},{6,2},{7,3},{8,12},{9,13},{10,... | collective-permute-start | bytes 26120 | tf_op jit(solution)/shard_map/ppermute | solution.py:283
  158.7 6.8 %collective-permute-start.15 = (f32[136,16]{1,0:T(8,128)S(1)}, f32[136,16]{1,0:T(8,128)S(1)}, u32[]{:S(2)}, u32[]{:S(2)}) collective-permute-start(f32[136,16]{1,0:T(8,128)S(1)} %add.140), channel_id=1, source_target_pairs={{0,24},{1,25},{2,26},{3,27},{4,28},{5,29},{6,30},{7,31},{8,16},{9,... | collective-permute-start | bytes 26120 | tf_op jit(solution)/shard_map/ppermute | solution.py:283
  159.8 8.0 %collective-permute-start.14 = (f32[136,16]{1,0:T(8,128)S(1)}, f32[136,16]{1,0:T(8,128)S(1)}, u32[]{:S(2)}, u32[]{:S(2)}) collective-permute-start(f32[136,16]{1,0:T(8,128)S(1)} %add.140), channel_id=1, source_target_pairs={{0,16},{1,17},{2,18},{3,19},{4,20},{5,21},{6,22},{7,23},{8,24},{9,... | collective-permute-start | bytes 26120 | tf_op jit(solution)/shard_map/ppermute | solution.py:283
  165.2 3.3 %collective-permute-start.13 = (f32[136,16]{1,0:T(8,128)S(1)}, f32[136,16]{1,0:T(8,128)S(1)}, u32[]{:S(2)}, u32[]{:S(2)}) collective-permute-start(f32[136,16]{1,0:T(8,128)S(1)} %add.140), channel_id=1, source_target_pairs={{0,8},{1,9},{2,10},{3,11},{4,12},{5,13},{6,14},{7,15},{8,0},{9,1},... | collective-permute-start | bytes 26120 | tf_op jit(solution)/shard_map/ppermute | solution.py:283
  169.2 56.0 %all-to-all-start.1 = ((f32[32,4,32,128]{3,2,1,0:T(8,128)}), f32[32,4,32,128]{3,2,1,0:T(8,128)}, u32[]{:S(2)}, u32[]{:S(2)}) async-start(f32[32,4,32,128]{3,2,1,0:T(8,128)} %get-tuple-element.31), calls=%async_computation.1 | async-start | bytes 4194304 | tf_op jit(solution)/shard_map/all_to_all | solution.py:480

commit v7 on v4

--- a/solution.py
+++ b/solution.py
@@ -179,18 +179,25 @@
 
 
 def to_planes_kernel(recv, base, y_table, out):
-    _, _, planes, span_y, span_z = base.shape
-    each = recv.shape[1] // planes
-    for group in groups(planes, span_z):
-        columns = [
-            recv[:, p * each : (p + 1) * each, :].reshape(2 * span_y, span_z) for p in group
-        ]
-        along_y = dot_left(y_table[...], jnp.concatenate(columns, axis=1))
-        for i, p in enumerate(group):
-            for part in range(2):
-                out[0, part, p] = base[0, part, p] + (
-                    along_y[part * span_y : (part + 1) * span_y, i * span_z : (i + 1) * span_z]
-                )
+    bands, _, planes, span_y, span_z = base.shape
+    each = recv.shape[2] // planes
+    for band in range(bands):
+        for group in groups(planes, span_z):
+            columns = [
+                recv[:, band, p * each : (p + 1) * each, :].reshape(2 * span_y, span_z)
+                for p in group
+            ]
+            along_y = dot_left(y_table[...], jnp.concatenate(columns, axis=1))
+            for i, p in enumerate(group):
+                for part in range(2):
+                    out[band, part, p] = base[band, part, p] + (
+                        along_y[part * span_y : (part + 1) * span_y, i * span_z : (i + 1) * span_z]
+                    )
+
+
+def last_sum_kernel(*refs):
+    first, second, third, fourth, _, out = refs
+    out[...] = (first[...] + second[...]) + (third[...] + fourth[...])
 
 
 def block_rows_of(psi, beta, slots):
@@ -256,7 +263,7 @@
     return lax.ppermute(values, "ga", [(d, d ^ k) for d in range(devices)])
 
 
-def sum_over(values, devices):
+def sum_over(values, devices, after):
     if devices & (devices - 1) or devices < 4:
         return lax.psum(values, "ga")
     step = 1
@@ -264,7 +271,14 @@
         values = values + partner(values, devices, step)
         step *= 2
     others = [partner(values, devices, k * step) for k in (1, 2, 3)]
-    return (values + others[0]) + (others[1] + others[2])
+    held = pl.BlockSpec(memory_space=pltpu.VMEM)
+    return pl.pallas_call(
+        last_sum_kernel,
+        out_shape=jax.ShapeDtypeStruct(values.shape, f32),
+        in_specs=[held] * 4 + [pl.BlockSpec(memory_space=pl.ANY)],
+        out_specs=held,
+        name="last_sum",
+    )(values, *others, after)
 
 
 def on_device(devices, orbitals, plane_order, potential, projectors, slot_owner, strengths):
@@ -410,7 +424,7 @@
     )(*fields, pot)
     grams = jnp.sum(grams, axis=-1)
     own = jnp.concatenate([proj, jnp.concatenate([grams[0], grams[1] + kin], axis=1)], axis=0)
-    total = sum_over(own, devices)
+    total = sum_over(own, devices, returned[0])
     proj, s_real, h_real = total[:owners], total[owners:, :bands], total[owners:, bands:]
     weighted = strengths.reshape(-1)[:, None] * proj
     p_real, p_imag = proj[:, :bands], proj[:, bands:]
@@ -452,19 +466,19 @@
 
     residual = base
     for c in range(parts):
-        one_band = pl.BlockSpec(
-            (1, 2, planes, span_y, span_z), lambda b, c=c: (2 * share * c + b, 0, 0, 0, 0)
+        two_bands = pl.BlockSpec(
+            (2, 2, planes, span_y, span_z), lambda j, c=c: (share * c + j, 0, 0, 0, 0)
         )
         residual = pl.pallas_call(
             to_planes_kernel,
             out_shape=jax.ShapeDtypeStruct(orbitals.shape, f32),
-            grid=(2 * share,),
+            grid=(share,),
             in_specs=[
-                pl.BlockSpec((devices, None, block_rows, span_z), lambda b: (0, b, 0, 0)),
-                one_band,
+                pl.BlockSpec((devices, 2, block_rows, span_z), lambda j: (0, j, 0, 0)),
+                two_bands,
                 whole(fwd_y.shape),
             ],
-            out_specs=one_band,
+            out_specs=two_bands,
             input_output_aliases={1: 0},
             compiler_params=params,
             cost_estimate=cost(8 * 10**9, 12 * 10**6),

time: 182 us -> 181 us (level)
  waiting for transfers between devices: 76.6 us -> 64.7 us
  matrix products: 1.33 us -> 6.01 us
  starting transfers between devices: 29.2 us -> 32.7 us
  other arithmetic: 7.49 us -> 9.48 us
    ppermute x6, waiting for transfers between devices: 26.1 us -> 5.58 us  [partner(): return lax.ppermute(values, 'ga', [(d, d ^ k) for d in range(devices)])]
    all_to_all x2, waiting for transfers between devices: 27.9 us -> 36.4 us  [on_device(): lax.all_to_all(back, 'ga', split_axis=0, concat_axis=0, tiled=True)]
    dot_general x6, matrix products: 0.99 us -> 5.63 us  [tdot(): jnp.einsum(pattern, left, right, precision=highest, preferred_element_typ...]
    ppermute x6, starting transfers between devices: 8.26 us -> 11.7 us  [partner(): return lax.ppermute(values, 'ga', [(d, d ^ k) for d in range(devices)])]
    pallas_call x2, Pallas kernels: 9.91 us -> 7.73 us  [on_device(): pl.pallas_call(to_planes_kernel, out_shape=jax.ShapeDtypeStruct(orbitals....]
  transfers between devices with their start and end apart: 10 -> 10, of which waited for: 8 -> 7; matrix products, arithmetic and copies ran while one was open for 8% -> 11% of each run, Pallas kernels for 29% -> 29%
where the time goes in v7:
time: 181 us; the launch traced here: 179 us
  waiting for transfers between devices  64.7 us (36%)
  Pallas kernels  59 us (33%)
  starting transfers between devices  32.7 us (18%)
  other arithmetic  9.48 us (5%)
  local copies, waits for them, and re-layouts  6.07 us (3%)
  matrix products  6.01 us (3%)
    all_to_all x2, waiting for transfers between devices, on_device(): lax.all_to_all(back, 'ga', split_axis=0, concat_axis=0, tiled=True)  36.4 us
    all_to_all x2, waiting for transfers between devices, on_device(): lax.all_to_all(sent, 'ga', split_axis=0, concat_axis=0, tiled=True)  22.7 us
    pallas_call x2, Pallas kernels, on_device(): pl.pallas_call(functools.partial(real_space_kernel, rows, planes), out_sh...  17.3 us
    all_to_all x2, starting transfers between devices, on_device(): lax.all_to_all(sent, 'ga', split_axis=0, concat_axis=0, tiled=True)  11.7 us
    ppermute x6, starting transfers between devices, partner(): return lax.ppermute(values, 'ga', [(d, d ^ k) for d in range(devices)])  11.7 us
    pallas_call x1, Pallas kernels, on_device(): pl.pallas_call(functools.partial(base_kernel, slots), out_shape=jax.Shape...  11.2 us
    pallas_call x1, Pallas kernels, on_device(): pl.pallas_call(functools.partial(project_kernel, slots), out_shape=jax.Sh...  10.1 us
    all_to_all x2, starting transfers between devices, on_device(): lax.all_to_all(back, 'ga', split_axis=0, concat_axis=0, tiled=True)  9.35 us
  transfers between devices with their start and end apart: 10, of which 7 were waited for; matrix products, arithmetic and copies ran while one was open for 11% of the time, Pallas kernels for 29%

profile of v7, /device:TPU:1, one launch (start us, length us, event | category | flops | bytes accessed | tf_op | source)
XLA Modules:
  0.0 179.0 jit_solution(12043780363083524169)
XLA Ops:
  0.6 3.0 %to_rows.3 = f32[32,2,32,128]{3,2,1,0:T(8,128)} custom-call(f32[8,2,4,128,128]{4,3,2,1,0:T(8,128)} %psi.7, bf16[256,768]{1,0:T(8,128)(2,1)} %constant.99.clone.y_table), custom_call_target="tpu_custom_call" | custom-call | flops 4000000000 | bytes 3000000 | tf_op jit(solution)/shard_map/to_rows/pallas_call | solution.py:316
  3.6 7.1 %all-to-all-start.2 = ((f32[32,2,32,128]{3,2,1,0:T(8,128)}), f32[32,2,32,128]{3,2,1,0:T(8,128)}, u32[]{:S(2)}, u32[]{:S(2)}) async-start(f32[32,2,32,128]{3,2,1,0:T(8,128)} %to_rows.3), calls=%async_computation.2 | async-start | bytes 2097152 | tf_op jit(solution)/shard_map/all_to_all | solution.py:331
  11.0 0.4 fusion.24
  11.5 0.9 copy.118.inverse
  12.5 0.9 add_multiply_fusion.kinetic
  13.4 3.0 %to_rows.2 = f32[32,2,32,128]{3,2,1,0:T(8,128)} custom-call(f32[8,2,4,128,128]{4,3,2,1,0:T(8,128)} %psi.7, bf16[256,768]{1,0:T(8,128)(2,1)} %constant.99.clone.y_table), custom_call_target="tpu_custom_call" | custom-call | flops 4000000000 | bytes 3000000 | tf_op jit(solution)/shard_map/to_rows/pallas_call | solution.py:316
  16.4 19.8 %all-to-all-done.2.recv = f32[32,2,32,128]{3,2,1,0:T(8,128)} async-done(((f32[32,2,32,128]{3,2,1,0:T(8,128)}), f32[32,2,32,128]{3,2,1,0:T(8,128)}, u32[]{:S(2)}, u32[]{:S(2)}) %all-to-all-start.2) | async-done | bytes 1048608 | tf_op jit(solution)/shard_map/all_to_all | solution.py:331
  36.1 4.6 %all-to-all-start = ((f32[32,2,32,128]{3,2,1,0:T(8,128)}), f32[32,2,32,128]{3,2,1,0:T(8,128)}, u32[]{:S(2)}, u32[]{:S(2)}) async-start(f32[32,2,32,128]{3,2,1,0:T(8,128)} %to_rows.2), calls=%async_computation | async-start | bytes 2097152 | tf_op jit(solution)/shard_map/all_to_all | solution.py:331
  40.7 10.1 %project.1 = f32[8,32,16]{2,1,0:T(8,128)} custom-call(f32[8,2,4,128,128]{4,3,2,1,0:T(8,128)} %psi.7, f32[8,1024,128]{2,1,0:T(8,128)} %bitcast.85, f32[4,128,128]{2,1,0:T(8,128)} %add_multiply_fusion.kinetic), custom_call_target="tpu_custom_call" | custom-call | flops 8000000000 | bytes 8000000 | tf_op jit(solution)/shard_map/project/pallas_call | solution.py:363
  50.8 0.8 fusion.47
  52.1 0.7 copy.109
  52.9 0.7 pad_maximum_fusion.1.forward
  53.6 0.9 convolution_bitcast_fusion._
  54.6 8.6 %real_space.3 = (f32[32,4,32,128]{3,2,1,0:T(8,128)}, f32[4,512,128]{2,1,0:T(8,128)}) custom-call(f32[32,2,32,128]{3,2,1,0:T(8,128)} %all-to-all-done.2.recv, f32[512,128]{1,0:T(8,128)} %bitcast.74, bf16[256,768]{1,0:T(8,128)(2,1)} %copy.118.inverse, bf16[256,384]{1,0:T(8,128)(2,1)} %pad_maximum_fusion.1.forward, bf16[768,256]{1,0:T(8,128)(2,1)} %constant.101.clone.inv_z, ...), custom_call_target="tpu_custom_call" | custom-call | flops 4000000000 | bytes 8000000 | tf_op jit(solution)/shard_map/real_space/pallas_call | solution.py:391
  63.2 2.9 %all-to-all-done.recv = f32[32,2,32,128]{3,2,1,0:T(8,128)} async-done(((f32[32,2,32,128]{3,2,1,0:T(8,128)}), f32[32,2,32,128]{3,2,1,0:T(8,128)}, u32[]{:S(2)}, u32[]{:S(2)}) %all-to-all-start) | async-done | bytes 1048608 | tf_op jit(solution)/shard_map/all_to_all | solution.py:331
  66.1 4.6 %all-to-all-start.3 = ((f32[32,4,32,128]{3,2,1,0:T(8,128)}), f32[32,4,32,128]{3,2,1,0:T(8,128)}, u32[]{:S(2)}, u32[]{:S(2)}) async-start(f32[32,4,32,128]{3,2,1,0:T(8,128)} %get-tuple-element.7), calls=%async_computation.3 | async-start | bytes 4194304 | tf_op jit(solution)/shard_map/all_to_all | solution.py:415
  71.0 8.7 %real_space.2 = (f32[32,4,32,128]{3,2,1,0:T(8,128)}, f32[4,512,128]{2,1,0:T(8,128)}) custom-call(f32[32,2,32,128]{3,2,1,0:T(8,128)} %all-to-all-done.recv, f32[512,128]{1,0:T(8,128)} %bitcast.75, bf16[256,768]{1,0:T(8,128)(2,1)} %copy.118.inverse, bf16[256,384]{1,0:T(8,128)(2,1)} %pad_maximum_fusion.1.forward, bf16[768,256]{1,0:T(8,128)(2,1)} %constant.101.clone.inv_z, ...), custom_call_target="tpu_custom_call" | custom-call | flops 4000000000 | bytes 8000000 | tf_op jit(solution)/shard_map/real_space/pallas_call | solution.py:391
  79.7 5.2 %real_gram.1 = f32[2,8,8,128]{3,2,1,0:T(8,128)} custom-call(f32[4,512,128]{2,1,0:T(8,128)} %get-tuple-element.8.refs_0_, f32[4,512,128]{2,1,0:T(8,128)} %get-tuple-element.9.refs_1_, f32[512,128]{1,0:T(8,128)} %bitcast.76), custom_call_target="tpu_custom_call" | custom-call | flops 10000000 | bytes 2000000 | tf_op jit(solution)/shard_map/real_gram/pallas_call | solution.py:418
  84.8 0.9 reduce_sum.18
  86.2 0.9 collective-permute-done
  87.2 1.4 collective-permute-start.1
  88.6 2.3 %collective-permute-done.1 = f32[136,16]{1,0:T(8,128)S(1)} collective-permute-done((f32[136,16]{1,0:T(8,128)S(1)}, f32[136,16]{1,0:T(8,128)S(1)}, u32[]{:S(2)}, u32[]{:S(2)}) %collective-permute-start.1) | collective-permute-done | bytes 8736 | tf_op jit(solution)/shard_map/ppermute | solution.py:263
  91.0 5.5 %collective-permute-start.2 = (f32[136,16]{1,0:T(8,128)S(1)}, f32[136,16]{1,0:T(8,128)S(1)}, u32[]{:S(2)}, u32[]{:S(2)}) collective-permute-start(f32[136,16]{1,0:T(8,128)S(1)} %add.109), channel_id=1, source_target_pairs={{0,4},{1,5},{2,6},{3,7},{4,0},{5,1},{6,2},{7,3},{8,12},{9,13},{10,... | collective-permute-start | bytes 26120 | tf_op jit(solution)/shard_map/ppermute | solution.py:263
  96.5 2.3 %collective-permute-done.2 = f32[136,16]{1,0:T(8,128)S(1)} collective-permute-done((f32[136,16]{1,0:T(8,128)S(1)}, f32[136,16]{1,0:T(8,128)S(1)}, u32[]{:S(2)}, u32[]{:S(2)}) %collective-permute-start.2) | collective-permute-done | bytes 8736 | tf_op jit(solution)/shard_map/ppermute | solution.py:263
  98.8 1.0 collective-permute-start.5
  99.8 3.4 %collective-permute-start.4 = (f32[136,16]{1,0:T(8,128)S(1)}, f32[136,16]{1,0:T(8,128)S(1)}, u32[]{:S(2)}, u32[]{:S(2)}) collective-permute-start(f32[136,16]{1,0:T(8,128)S(1)} %add.110.refs_0_), channel_id=1, source_target_pairs={{0,16},{1,17},{2,18},{3,19},{4,20},{5,21},{6,22},{7,23},{8,24},{9,... | collective-permute-start | bytes 26120 | tf_op jit(solution)/shard_map/ppermute | solution.py:263
  103.4 18.6 %all-to-all-done.3.refs_4_.recv = f32[32,4,32,128]{3,2,1,0:T(8,128)} async-done(((f32[32,4,32,128]{3,2,1,0:T(8,128)}), f32[32,4,32,128]{3,2,1,0:T(8,128)}, u32[]{:S(2)}, u32[]{:S(2)}) %all-to-all-start.3) | async-done | bytes 2097184 | tf_op jit(solution)/shard_map/all_to_all | solution.py:415
  122.0 4.8 %all-to-all-start.1 = ((f32[32,4,32,128]{3,2,1,0:T(8,128)}), f32[32,4,32,128]{3,2,1,0:T(8,128)}, u32[]{:S(2)}, u32[]{:S(2)}) async-start(f32[32,4,32,128]{3,2,1,0:T(8,128)} %get-tuple-element.6), calls=%async_computation.1 | async-start | bytes 4194304 | tf_op jit(solution)/shard_map/all_to_all | solution.py:415
  126.8 0.6 copy-done.4
  127.4 0.6 copy-done.6
  128.1 1.6 last_sum.1
  129.7 0.7 slice.119
  130.4 0.9 slice_multiply_fusion
  131.3 1.1 fusion.10
  132.4 1.1 fusion.16
  133.6 0.9 fusion.37
  134.5 0.7 cholesky.16
  135.2 0.6 compare_reduce_fusion
  135.8 0.6 fusion.27
  136.5 0.6 custom-call.10
  137.1 1.1 fusion.12
  138.3 1.1 convolution_subtract_fusion
  140.9 0.6 pad_maximum_fusion.6
  141.5 0.7 pad_maximum_fusion.4.coefs
  142.2 11.2 %base.1 = f32[8,2,4,128,128]{4,3,2,1,0:T(8,128)} custom-call(f32[8,2,4,128,128]{4,3,2,1,0:T(8,128)} %psi.7, f32[8,1024,128]{2,1,0:T(8,128)} %bitcast.86, f32[4,128,128]{2,1,0:T(8,128)} %add_multiply_fusion.kinetic, f32[8,16,32]{2,1,0:T(8,128)} %pad_maximum_fusion.4.coefs), custom_call_target="tpu_custom_call" | custom-call | flops 8000000000 | bytes 12000000 | tf_op jit(solution)/shard_map/base/pallas_call | solution.py:455
  153.4 3.9 %to_planes.2.base = f32[8,2,4,128,128]{4,3,2,1,0:T(8,128)} custom-call(f32[32,4,32,128]{3,2,1,0:T(8,128)} %all-to-all-done.3.refs_4_.recv, f32[8,2,4,128,128]{4,3,2,1,0:T(8,128)} %base.1, bf16[256,768]{1,0:T(8,128)(2,1)} %constant.100.clone.y_table), custom_call_target="tpu_custom_call", output_to_operand_aliasing={{}: (1, {})} | custom-call | flops 8000000000 | bytes 12000000 | tf_op jit(solution)/shard_map/to_planes/pallas_call | solution.py:472
  157.2 17.9 %all-to-all-done.1.recv = f32[32,4,32,128]{3,2,1,0:T(8,128)} async-done(((f32[32,4,32,128]{3,2,1,0:T(8,128)}), f32[32,4,32,128]{3,2,1,0:T(8,128)}, u32[]{:S(2)}, u32[]{:S(2)}) %all-to-all-start.1) | async-done | bytes 2097184 | tf_op jit(solution)/shard_map/all_to_all | solution.py:415
  175.1 3.9 %to_planes.3 = f32[8,2,4,128,128]{4,3,2,1,0:T(8,128)} custom-call(f32[32,4,32,128]{3,2,1,0:T(8,128)} %all-to-all-done.1.recv, f32[8,2,4,128,128]{4,3,2,1,0:T(8,128)} %to_planes.2.base, bf16[256,768]{1,0:T(8,128)(2,1)} %constant.100.clone.y_table), custom_call_target="tpu_custom_call", output_to_operand_aliasing={{}: (1, {})} | custom-call | flops 8000000000 | bytes 12000000 | tf_op jit(solution)/shard_map/to_planes/pallas_call | solution.py:472
  (71 shorter events, 3.6 us)
Async XLA Ops:
  0.6 10.1 %copy-start.8 = (s32[128]{0:T(128)S(1)}, s32[128]{0:T(128)}, u32[]{:S(2)}) copy-start(s32[128]{0:T(128)} %param.11) | copy-start | bytes 1540
  3.6 32.5 %all-to-all-start.2 = ((f32[32,2,32,128]{3,2,1,0:T(8,128)}), f32[32,2,32,128]{3,2,1,0:T(8,128)}, u32[]{:S(2)}, u32[]{:S(2)}) async-start(f32[32,2,32,128]{3,2,1,0:T(8,128)} %to_rows.3), calls=%async_computation.2 | async-start | bytes 2097152 | tf_op jit(solution)/shard_map/all_to_all | solution.py:331
  36.1 30.0 %all-to-all-start = ((f32[32,2,32,128]{3,2,1,0:T(8,128)}), f32[32,2,32,128]{3,2,1,0:T(8,128)}, u32[]{:S(2)}, u32[]{:S(2)}) async-start(f32[32,2,32,128]{3,2,1,0:T(8,128)} %to_rows.2), calls=%async_computation | async-start | bytes 2097152 | tf_op jit(solution)/shard_map/all_to_all | solution.py:331
  40.7 11.4 %copy-start.1 = (f32[128,4,128]{2,1,0:T(4,128)S(1)}, f32[128,4,128]{2,1,0:T(4,128)}, u32[]{:S(2)}) copy-start(f32[128,4,128]{2,1,0:T(4,128)} %param.12) | copy-start | bytes 786436
  40.7 12.9 %copy-start.9 = (s32[8,8]{1,0:T(8,128)S(1)}, s32[8,8]{1,0:T(8,128)}, u32[]{:S(2)}) copy-start(s32[8,8]{1,0:T(8,128)} %param.14) | copy-start | bytes 772
  63.2 7.5 %copy-start.3 = (f32[8,32,16]{2,1,0:T(8,128)S(1)}, f32[8,32,16]{2,1,0:T(8,128)}, u32[]{:S(2)}) copy-start(f32[8,32,16]{2,1,0:T(8,128)} %project.1) | copy-start | bytes 49156
  66.1 55.9 %all-to-all-start.3 = ((f32[32,4,32,128]{3,2,1,0:T(8,128)}), f32[32,4,32,128]{3,2,1,0:T(8,128)}, u32[]{:S(2)}, u32[]{:S(2)}) async-start(f32[32,4,32,128]{3,2,1,0:T(8,128)} %get-tuple-element.7), calls=%async_computation.3 | async-start | bytes 4194304 | tf_op jit(solution)/shard_map/all_to_all | solution.py:415
  70.9 14.8 %copy-start.2 = (f32[128,16]{1,0:T(8,128)S(1)}, f32[128,16]{1,0:T(8,128)}, u32[]{:S(2)}) copy-start(f32[128,16]{1,0:T(8,128)} %convolution_bitcast_fusion._) | copy-start | bytes 24580
  71.0 32.3 %copy-start.7 = (f32[32,4]{0,1:T(4,128)S(1)}, f32[32,4]{0,1:T(4,128)}, u32[]{:S(2)}) copy-start(f32[32,4]{0,1:T(4,128)} %param.15) | copy-start | bytes 1540
  85.9 1.3 collective-permute-start
  87.2 3.7 %collective-permute-start.1 = (f32[136,16]{1,0:T(8,128)S(1)}, f32[136,16]{1,0:T(8,128)S(1)}, u32[]{:S(2)}, u32[]{:S(2)}) collective-permute-start(f32[136,16]{1,0:T(8,128)S(1)} %fusion.51), channel_id=1, source_target_pairs={{0,2},{1,3},{2,0},{3,1},{4,6},{5,7},{6,4},{7,5},{8,10},{9,11},{10,... | collective-permute-start | bytes 26120 | tf_op jit(solution)/shard_map/ppermute | solution.py:263
  91.0 7.9 %collective-permute-start.2 = (f32[136,16]{1,0:T(8,128)S(1)}, f32[136,16]{1,0:T(8,128)S(1)}, u32[]{:S(2)}, u32[]{:S(2)}) collective-permute-start(f32[136,16]{1,0:T(8,128)S(1)} %add.109), channel_id=1, source_target_pairs={{0,4},{1,5},{2,6},{3,7},{4,0},{5,1},{6,2},{7,3},{8,12},{9,13},{10,... | collective-permute-start | bytes 26120 | tf_op jit(solution)/shard_map/ppermute | solution.py:263
  98.8 28.0 %copy-start = (f32[136,16]{1,0:T(8,128)}, f32[136,16]{1,0:T(8,128)S(1)}, u32[]{:S(2)}) copy-start(f32[136,16]{1,0:T(8,128)S(1)} %add.110.refs_0_) | copy-start | bytes 26116
  98.8 27.9 %collective-permute-start.5 = (f32[136,16]{1,0:T(8,128)S(1)}, f32[136,16]{1,0:T(8,128)S(1)}, u32[]{:S(2)}, u32[]{:S(2)}) collective-permute-start(f32[136,16]{1,0:T(8,128)S(1)} %add.110.refs_0_), channel_id=1, source_target_pairs={{0,24},{1,25},{2,26},{3,27},{4,28},{5,29},{6,30},{7,31},{8,16},{9,... | collective-permute-start | bytes 26120 | tf_op jit(solution)/shard_map/ppermute | solution.py:263
  99.8 27.0 %collective-permute-start.4 = (f32[136,16]{1,0:T(8,128)S(1)}, f32[136,16]{1,0:T(8,128)S(1)}, u32[]{:S(2)}, u32[]{:S(2)}) collective-permute-start(f32[136,16]{1,0:T(8,128)S(1)} %add.110.refs_0_), channel_id=1, source_target_pairs={{0,16},{1,17},{2,18},{3,19},{4,20},{5,21},{6,22},{7,23},{8,24},{9,... | collective-permute-start | bytes 26120 | tf_op jit(solution)/shard_map/ppermute | solution.py:263
  103.2 23.6 %collective-permute-start.3 = (f32[136,16]{1,0:T(8,128)S(1)}, f32[136,16]{1,0:T(8,128)S(1)}, u32[]{:S(2)}, u32[]{:S(2)}) collective-permute-start(f32[136,16]{1,0:T(8,128)S(1)} %add.110.refs_0_), channel_id=1, source_target_pairs={{0,8},{1,9},{2,10},{3,11},{4,12},{5,13},{6,14},{7,15},{8,0},{9,1},... | collective-permute-start | bytes 26120 | tf_op jit(solution)/shard_map/ppermute | solution.py:263
  122.0 53.1 %all-to-all-start.1 = ((f32[32,4,32,128]{3,2,1,0:T(8,128)}), f32[32,4,32,128]{3,2,1,0:T(8,128)}, u32[]{:S(2)}, u32[]{:S(2)}) async-start(f32[32,4,32,128]{3,2,1,0:T(8,128)} %get-tuple-element.6), calls=%async_computation.1 | async-start | bytes 4194304 | tf_op jit(solution)/shard_map/all_to_all | solution.py:415
  126.8 0.6 copy-start.4
  126.8 0.6 copy-start.5
  127.4 0.6 copy-start.6

commit v8 on v7

--- a/solution.py
+++ b/solution.py
@@ -111,11 +111,11 @@
             ].reshape(devices, each, span_z)
 
 
-def real_space_kernel(rows, planes, recv, pot, inverse, forward, inv_z, fwd_z, _, back, field):
+def real_space_kernel(rows, planes, recv, pot, inverse, forward, inv_z, fwd_z, _, *refs):
     devices, size, span_z = recv.shape
     span_x = devices * planes
     arrived = recv.reshape(devices * size, span_z)
-    leaving = back.reshape(devices * 2 * size, span_z)
+    field, back, staged = refs[-devices - 2], refs[-devices - 1 : -1], refs[-1]
     for group in groups(rows, span_z):
         columns = [
             jnp.concatenate(
@@ -144,14 +144,17 @@
                 for p in range(planes):
                     first = i * span_x + p * devices
                     for part in range(2):
-                        start = band * size + (p * rows + r) * 2 + part
-                        leaving[pl.ds(start, devices, stride=2 * size), :] = spectral[
+                        start = (p * rows + r) * 2 + part
+                        staged[band, pl.ds(start, devices, stride=size), :] = spectral[
                             first : first + devices, part * span_z : (part + 1) * span_z
                         ]
+    for k in range(devices):
+        for band in range(2):
+            back[k][band] = staged[band, k * size : (k + 1) * size, :]
 
 
 def real_gram_kernel(bands, *refs):
-    fields, (pot, out) = refs[:-2], refs[-2:]
+    fields, (pot, _, out) = refs[:-3], refs[-3:]
     held = fields[0].shape[0]
     pairs = [(a, b) for a in range(bands) for b in range(a, bands)]
     for weighted in range(2):
@@ -178,13 +181,14 @@
             out[weighted, b, a : a + 1, :] = line
 
 
-def to_planes_kernel(recv, base, y_table, out):
+def to_planes_kernel(*refs):
+    recv, (base, y_table, out) = refs[:-3], refs[-3:]
     bands, _, planes, span_y, span_z = base.shape
-    each = recv.shape[2] // planes
+    each = recv[0].shape[1] // planes
     for band in range(bands):
         for group in groups(planes, span_z):
             columns = [
-                recv[:, band, p * each : (p + 1) * each, :].reshape(2 * span_y, span_z)
+                jnp.concatenate([one[band, p * each : (p + 1) * each, :] for one in recv], axis=0)
                 for p in group
             ]
             along_y = dot_left(y_table[...], jnp.concatenate(columns, axis=1))
@@ -193,11 +197,6 @@
                     out[band, part, p] = base[band, part, p] + (
                         along_y[part * span_y : (part + 1) * span_y, i * span_z : (i + 1) * span_z]
                     )
-
-
-def last_sum_kernel(*refs):
-    first, second, third, fourth, _, out = refs
-    out[...] = (first[...] + second[...]) + (third[...] + fourth[...])
 
 
 def block_rows_of(psi, beta, slots):
@@ -263,7 +262,7 @@
     return lax.ppermute(values, "ga", [(d, d ^ k) for d in range(devices)])
 
 
-def sum_over(values, devices, after):
+def sum_over(values, devices):
     if devices & (devices - 1) or devices < 4:
         return lax.psum(values, "ga")
     step = 1
@@ -271,14 +270,7 @@
         values = values + partner(values, devices, step)
         step *= 2
     others = [partner(values, devices, k * step) for k in (1, 2, 3)]
-    held = pl.BlockSpec(memory_space=pltpu.VMEM)
-    return pl.pallas_call(
-        last_sum_kernel,
-        out_shape=jax.ShapeDtypeStruct(values.shape, f32),
-        in_specs=[held] * 4 + [pl.BlockSpec(memory_space=pl.ANY)],
-        out_specs=held,
-        name="last_sum",
-    )(values, *others, after)
+    return (values + others[0]) + (others[1] + others[2])
 
 
 def on_device(devices, orbitals, plane_order, potential, projectors, slot_owner, strengths):
@@ -305,7 +297,13 @@
     order = np.arange(2 * span_y)
     order = (order % 2) * span_y + order // 2
     inv_y = left_const(left_table(span_y, 1.0)[order])
-    fwd_y = left_const(left_table(span_y, -1.0)[:, order])
+    mine = lax.axis_index("ga").astype(jnp.int32)
+    fwd_y = jnp.asarray(np.concatenate(const_parts(left_table(span_y, -1.0)[:, order]), axis=0))
+    swap = jnp.arange(2 * span_y, dtype=jnp.int32)
+    swap = (swap[:, None] == (swap[None, :] ^ (mine * 2 * rows))).astype(bf16)
+    fwd_y = jnp.dot(fwd_y, swap, preferred_element_type=f32).astype(bf16)
+    high, low = fwd_y[: 2 * span_y], fwd_y[2 * span_y :]
+    fwd_y = jnp.concatenate([high, high, low], axis=1)
     inv_z = right_const(right_table(span_z, 1.0))
     fwd_z = right_const(right_table(span_z, -1.0))
 
@@ -330,17 +328,24 @@
         )(orbitals, inv_y)
         arrived.append(lax.all_to_all(sent, "ga", split_axis=0, concat_axis=0, tiled=True))
 
-    stored = plane_order.reshape(devices, planes).T.reshape(-1)
-    phases = (stored[:, None] * grid_x[None, :]) % span_x
-    angles = phases.astype(f32) * (2.0 * math.pi / span_x)
-    factor = 1.0 / math.sqrt(span_x)
-    cosine, sine = jnp.cos(angles) * factor, jnp.sin(angles) * factor
-    fwd_x = jnp.concatenate([cosine, -sine], axis=0)
-    inv_x = jnp.concatenate([fwd_x, jnp.concatenate([sine, cosine], axis=0)], axis=1).T
-    high, low = split_outside(fwd_x)
+    def along_x(owned):
+        phases = (owned.T.reshape(-1)[:, None] * grid_x[None, :]) % span_x
+        angles = phases.astype(f32) * (2.0 * math.pi / span_x)
+        factor = 1.0 / math.sqrt(span_x)
+        return jnp.cos(angles) * factor, jnp.sin(angles) * factor
+
+    owned = plane_order.reshape(devices, planes)
+    cosine, sine = along_x(owned)
+    high, low = split_outside(
+        jnp.concatenate(
+            [jnp.concatenate([cosine, -sine], axis=0), jnp.concatenate([sine, cosine], axis=0)],
+            axis=1,
+        ).T
+    )
+    inv_x = jnp.concatenate([high, high, low], axis=1)
+    cosine, sine = along_x(jnp.take(owned, mine ^ jnp.arange(devices, dtype=jnp.int32), axis=0))
+    high, low = split_outside(jnp.concatenate([cosine, -sine], axis=0))
     fwd_x = jnp.concatenate([high, high, low], axis=1)
-    high, low = split_outside(inv_x)
-    inv_x = jnp.concatenate([high, high, low], axis=1)
     pot = potential.transpose(1, 0, 2).reshape(rows * span_x, span_z)
 
     local_order = lax.dynamic_slice_in_dim(plane_order, lax.axis_index("ga") * planes, planes)
@@ -386,14 +391,13 @@
     kin = jnp.sum(products[:, 2 * slots :], axis=0).reshape(bands, 2, bands, 2)
     kin = kin[:, 0, :, 0] + kin[:, 1, :, 1]
 
-    returned, fields = [], []
+    fields, back = [], []
     for c in range(parts):
-        back, field = pl.pallas_call(
+        held = len(back)
+        field, *back = pl.pallas_call(
             functools.partial(real_space_kernel, rows, planes),
-            out_shape=(
-                jax.ShapeDtypeStruct((devices, 2 * share, block_rows, span_z), f32),
-                jax.ShapeDtypeStruct((2 * share, rows * span_x, span_z), f32),
-            ),
+            out_shape=[jax.ShapeDtypeStruct((2 * share, rows * span_x, span_z), f32)]
+            + [jax.ShapeDtypeStruct((bands, block_rows, span_z), f32)] * devices,
             grid=(share,),
             in_specs=[
                 pl.BlockSpec((devices, None, block_rows, span_z), lambda j: (0, j, 0, 0)),
@@ -403,28 +407,44 @@
                 whole(inv_z.shape),
                 whole(fwd_z.shape),
                 whole(proj.shape),
-            ],
-            out_specs=(
-                pl.BlockSpec((devices, 2, block_rows, span_z), lambda j: (0, j, 0, 0)),
-                pl.BlockSpec((2, rows * span_x, span_z), lambda j: (j, 0, 0)),
-            ),
+            ]
+            + [pl.BlockSpec(memory_space=pl.ANY)] * held,
+            out_specs=[pl.BlockSpec((2, rows * span_x, span_z), lambda j: (j, 0, 0))]
+            + [
+                pl.BlockSpec((2, block_rows, span_z), lambda j, c=c: (c * share + j, 0, 0))
+            ] * devices,
+            scratch_shapes=[pltpu.VMEM((2, devices * block_rows, span_z), f32)],
+            input_output_aliases={7 + k: 1 + k for k in range(held)},
             compiler_params=params,
             cost_estimate=cost(4 * 10**9, 8 * 10**6),
             name="real_space",
-        )(arrived[c], pot, inv_x, fwd_x, inv_z, fwd_z, proj)
-        returned.append(lax.all_to_all(back, "ga", split_axis=0, concat_axis=0, tiled=True))
+        )(arrived[c], pot, inv_x, fwd_x, inv_z, fwd_z, proj, *back)
         fields.append(field)
+    layers = min(4, devices)
+    rest = devices // layers
+    sequence = [
+        j * rest + (2 * ((j + i) % max(1, rest // 2)) + c) % rest
+        for c in range(min(2, rest))
+        for i in range(max(1, rest // 2))
+        for j in range(layers)
+    ]
+    sequence = [k for k in sequence if k > 0]
+    returned = {k: partner(back[k], devices, k) for k in sequence}
+    early = returned[sequence[min(4, len(sequence) - 1)]]
+    returned = [back[0]] + [returned[k] for k in range(1, devices)]
 
     grams = pl.pallas_call(
         functools.partial(real_gram_kernel, bands),
         out_shape=jax.ShapeDtypeStruct((2, bands, bands, 128), f32),
+        in_specs=[pl.BlockSpec(memory_space=pltpu.VMEM)] * (parts + 1)
+        + [pl.BlockSpec(memory_space=pl.ANY)],
         compiler_params=params,
         cost_estimate=cost(10**7, 2 * 10**6),
         name="real_gram",
-    )(*fields, pot)
+    )(*fields, pot, early)
     grams = jnp.sum(grams, axis=-1)
     own = jnp.concatenate([proj, jnp.concatenate([grams[0], grams[1] + kin], axis=1)], axis=0)
-    total = sum_over(own, devices, returned[0])
+    total = sum_over(own, devices)
     proj, s_real, h_real = total[:owners], total[owners:, :bands], total[owners:, bands:]
     weighted = strengths.reshape(-1)[:, None] * proj
     p_real, p_imag = proj[:, :bands], proj[:, bands:]
@@ -464,26 +484,18 @@
         name="base",
     )(orbitals, beta, kinetic, coefs)
 
-    residual = base
-    for c in range(parts):
-        two_bands = pl.BlockSpec(
-            (2, 2, planes, span_y, span_z), lambda j, c=c: (share * c + j, 0, 0, 0, 0)
-        )
-        residual = pl.pallas_call(
-            to_planes_kernel,
-            out_shape=jax.ShapeDtypeStruct(orbitals.shape, f32),
-            grid=(share,),
-            in_specs=[
-                pl.BlockSpec((devices, 2, block_rows, span_z), lambda j: (0, j, 0, 0)),
-                two_bands,
-                whole(fwd_y.shape),
-            ],
-            out_specs=two_bands,
-            input_output_aliases={1: 0},
-            compiler_params=params,
-            cost_estimate=cost(8 * 10**9, 12 * 10**6),
-            name="to_planes",
-        )(returned[c], residual, fwd_y)
+    two_bands = pl.BlockSpec((2, 2, planes, span_y, span_z), lambda j: (j, 0, 0, 0, 0))
+    residual = pl.pallas_call(
+        to_planes_kernel,
+        out_shape=jax.ShapeDtypeStruct(orbitals.shape, f32),
+        grid=(pairs,),
+        in_specs=[pl.BlockSpec((2, block_rows, span_z), lambda j: (j, 0, 0))] * devices
+        + [two_bands, whole(fwd_y.shape)],
+        out_specs=two_bands,
+        compiler_params=params,
+        cost_estimate=cost(8 * 10**9, 12 * 10**6),
+        name="to_planes",
+    )(*returned, base, fwd_y)
     return (residual, jnp.stack([m_real, m_imag]))
 
 

time: 181 us -> 242 us (1.34)
  starting transfers between devices: 32.7 us -> 88.8 us
  waiting for transfers between devices: 64.7 us -> 76.2 us
  matrix products: 6.01 us -> 1.57 us
    ppermute x6 -> x37, starting transfers between devices: 11.7 us -> 77.1 us  [partner(): return lax.ppermute(values, 'ga', [(d, d ^ k) for d in range(devices)])]
    ppermute x6 -> x37, waiting for transfers between devices: 5.58 us -> 54.9 us  [partner(): return lax.ppermute(values, 'ga', [(d, d ^ k) for d in range(devices)])]
    all_to_all x2 -> x0, waiting for transfers between devices: 36.4 us -> none  [on_device(): lax.all_to_all(back, 'ga', split_axis=0, concat_axis=0, tiled=True)]
    all_to_all x2 -> x0, starting transfers between devices: 9.35 us -> none  [on_device(): lax.all_to_all(back, 'ga', split_axis=0, concat_axis=0, tiled=True)]
    dot_general x6, matrix products: 5.63 us -> 1 us  [tdot(): jnp.einsum(pattern, left, right, precision=highest, preferred_element_typ...]
    pallas_call x2 -> x1, Pallas kernels: 7.73 us -> 7.12 us  [on_device(): pl.pallas_call(to_planes_kernel, out_shape=jax.ShapeDtypeStruct(orbitals....]
  transfers between devices with their start and end apart: 10 -> 39, of which waited for: 7 -> 18; matrix products, arithmetic and copies ran while one was open for 11% -> 6% of each run, Pallas kernels for 29% -> 14%
where the time goes in v8:
time: 242 us; the launch traced here: 241 us
  starting transfers between devices  88.8 us (37%)
  waiting for transfers between devices  76.2 us (31%)
  Pallas kernels  56.9 us (24%)
  other arithmetic  8.71 us (4%)
  local copies, waits for them, and re-layouts  7.3 us (3%)
    ppermute x37, starting transfers between devices, partner(): return lax.ppermute(values, 'ga', [(d, d ^ k) for d in range(devices)])  77.1 us
    ppermute x37, waiting for transfers between devices, partner(): return lax.ppermute(values, 'ga', [(d, d ^ k) for d in range(devices)])  54.9 us
    all_to_all x2, waiting for transfers between devices, on_device(): lax.all_to_all(sent, 'ga', split_axis=0, concat_axis=0, tiled=True)  21.3 us
    pallas_call x2, Pallas kernels, on_device(): pl.pallas_call(functools.partial(real_space_kernel, rows, planes), out_sh...  17.5 us
    all_to_all x2, starting transfers between devices, on_device(): lax.all_to_all(sent, 'ga', split_axis=0, concat_axis=0, tiled=True)  11.7 us
    pallas_call x1, Pallas kernels, on_device(): pl.pallas_call(functools.partial(base_kernel, slots), out_shape=jax.Shape...  11.2 us
    pallas_call x1, Pallas kernels, on_device(): pl.pallas_call(functools.partial(project_kernel, slots), out_shape=jax.Sh...  10 us
    pallas_call x1, Pallas kernels, on_device(): pl.pallas_call(to_planes_kernel, out_shape=jax.ShapeDtypeStruct(orbitals....  7.12 us
  transfers between devices with their start and end apart: 39, of which 18 were waited for; matrix products, arithmetic and copies ran while one was open for 6% of the time, Pallas kernels for 14%

profile of v8, /device:TPU:1, one launch (start us, length us, event | category | flops | bytes accessed | tf_op | source)
XLA Modules:
  0.0 240.6 jit_solution(8710321013961884195)
XLA Ops:
  0.6 3.0 %to_rows.3 = f32[32,2,32,128]{3,2,1,0:T(8,128)} custom-call(f32[8,2,4,128,128]{4,3,2,1,0:T(8,128)} %psi.7, bf16[256,768]{1,0:T(8,128)(2,1)} %constant.122.clone.y_table), custom_call_target="tpu_custom_call" | custom-call | flops 4000000000 | bytes 3000000 | tf_op jit(solution)/shard_map/to_rows/pallas_call | solution.py:314
  3.6 7.1 %all-to-all-start.1 = ((f32[32,2,32,128]{3,2,1,0:T(8,128)}), f32[32,2,32,128]{3,2,1,0:T(8,128)}, u32[]{:S(2)}, u32[]{:S(2)}) async-start(f32[32,2,32,128]{3,2,1,0:T(8,128)} %to_rows.3), calls=%async_computation.1 | async-start | bytes 2097152 | tf_op jit(solution)/shard_map/all_to_all | solution.py:329
  11.8 10.0 %project.1 = f32[8,32,16]{2,1,0:T(8,128)} custom-call(f32[8,2,4,128,128]{4,3,2,1,0:T(8,128)} %psi.7, f32[8,1024,128]{2,1,0:T(8,128)} %bitcast.89, f32[4,128,128]{2,1,0:T(8,128)} %add_multiply_fusion.kinetic), custom_call_target="tpu_custom_call" | custom-call | flops 8000000000 | bytes 8000000 | tf_op jit(solution)/shard_map/project/pallas_call | solution.py:368
  23.1 3.0 %to_rows.2 = f32[32,2,32,128]{3,2,1,0:T(8,128)} custom-call(f32[8,2,4,128,128]{4,3,2,1,0:T(8,128)} %psi.7, bf16[256,768]{1,0:T(8,128)(2,1)} %constant.122.clone.y_table), custom_call_target="tpu_custom_call" | custom-call | flops 4000000000 | bytes 3000000 | tf_op jit(solution)/shard_map/to_rows/pallas_call | solution.py:314
  26.1 10.0 %all-to-all-done.1.recv = f32[32,2,32,128]{3,2,1,0:T(8,128)} async-done(((f32[32,2,32,128]{3,2,1,0:T(8,128)}), f32[32,2,32,128]{3,2,1,0:T(8,128)}, u32[]{:S(2)}, u32[]{:S(2)}) %all-to-all-start.1) | async-done | bytes 1048608 | tf_op jit(solution)/shard_map/all_to_all | solution.py:329
  36.1 4.6 %all-to-all-start = ((f32[32,2,32,128]{3,2,1,0:T(8,128)}), f32[32,2,32,128]{3,2,1,0:T(8,128)}, u32[]{:S(2)}, u32[]{:S(2)}) async-start(f32[32,2,32,128]{3,2,1,0:T(8,128)} %to_rows.2), calls=%async_computation | async-start | bytes 2097152 | tf_op jit(solution)/shard_map/all_to_all | solution.py:329
  46.2 8.7 %real_space.2 = (f32[4,512,128]{2,1,0:T(8,128)}, f32[8,32,128]{2,1,0:T(8,128)}, f32[8,32,128]{2,1,0:T(8,128)}, f32[8,32,128]{2,1,0:T(8,128)}, f32[8,32,128]{2,1,...) custom-call(f32[32,2,32,128]{3,2,1,0:T(8,128)} %all-to-all-done.1.re, ...), custom_call_target="tpu_custom_call" | custom-call | flops 4000000000 | bytes 8000000 | tf_op jit(solution)/shard_map/real_space/pallas_call | solution.py:397
  54.9 11.2 %all-to-all-done.recv = f32[32,2,32,128]{3,2,1,0:T(8,128)} async-done(((f32[32,2,32,128]{3,2,1,0:T(8,128)}), f32[32,2,32,128]{3,2,1,0:T(8,128)}, u32[]{:S(2)}, u32[]{:S(2)}) %all-to-all-start) | async-done | bytes 1048608 | tf_op jit(solution)/shard_map/all_to_all | solution.py:329
  66.1 8.7 %real_space.3 = (f32[4,512,128]{2,1,0:T(8,128)}, f32[8,32,128]{2,1,0:T(8,128)}, f32[8,32,128]{2,1,0:T(8,128)}, f32[8,32,128]{2,1,0:T(8,128)}, f32[8,32,128]{2,1,...) custom-call(f32[32,2,32,128]{3,2,1,0:T(8,128)} %all-to-all-done.recv, ...), custom_call_target="tpu_custom_call", output_to_operand_aliasing={{1}: (7, {}), {2}: (8, {}), {3}: (9, {}), {4}: (10, {}), {5... | custom-call | flops 4000000000 | bytes 8000000 | tf_op jit(solution)/shard_map/real_space/pallas_call | solution.py:397
  75.8 4.1 %collective-permute-done.11.refs_3_.refs_12_ = f32[8,32,128]{2,1,0:T(8,128)S(1)} collective-permute-done((f32[8,32,128]{2,1,0:T(8,128)}, f32[8,32,128]{2,1,0:T(8,128)S(1)}, u32[]{:S(2)}, u32[]{:S(2)}) %collective-permute-start.11) | collective-permute-done | bytes 131104 | tf_op jit(solution)/shard_map/ppermute | solution.py:262
  80.5 5.2 %real_gram.1 = f32[2,8,8,128]{3,2,1,0:T(8,128)} custom-call(f32[4,512,128]{2,1,0:T(8,128)} %get-tuple-element.132.refs_0_, f32[4,512,128]{2,1,0:T(8,128)} %get-tuple-element.133.refs_1_, f32[512,128]{1,0:T(8,128)} %bitcast.81, f32[8,32,128]{2,1,0:T(8,128)} %copy-done.2), custom_call_target="tpu_custom_call" | custom-call | flops 10000000 | bytes 2000000 | tf_op jit(solution)/shard_map/real_gram/pallas_call | solution.py:436
  86.8 2.4 collective-permute-start.31
  90.0 1.4 collective-permute-start.32
  92.6 1.2 collective-permute-start.33
  93.8 1.4 collective-permute-done.33
  95.2 1.1 collective-permute-start.34
  97.0 1.8 collective-permute-start.36
  99.8 3.5 %collective-permute-start = (f32[8,32,128]{2,1,0:T(8,128)S(1)}, f32[8,32,128]{2,1,0:T(8,128)S(1)}, u32[]{:S(2)}, u32[]{:S(2)}) collective-permute-start(f32[8,32,128]{2,1,0:T(8,128)S(1)} %copy-done.31), channel_id=1, source_target_pairs={{0,1},{1,0},{2,3},{3,2},{4,5},{5,4},{6,7},{7,6},{8,9},{9,8},{10,11... | collective-permute-start | bytes 393224 | tf_op jit(solution)/shard_map/ppermute | solution.py:262
  103.3 1.4 collective-permute-start.1
  105.0 2.2 collective-permute-start.12
  107.2 1.1 collective-permute-start.13
  112.3 2.7 %collective-permute-start.14 = (f32[8,32,128]{2,1,0:T(8,128)}, f32[8,32,128]{2,1,0:T(8,128)S(1)}, u32[]{:S(2)}, u32[]{:S(2)}) collective-permute-start(f32[8,32,128]{2,1,0:T(8,128)} %get-tuple-element.115), channel_id=1, source_target_pairs={{0,15},{1,14},{2,13},{3,12},{4,11},{5,10},{6,9},{7,8},{8,7},{9,6},... | collective-permute-start | bytes 393224 | tf_op jit(solution)/shard_map/ppermute | solution.py:262
  115.3 2.1 collective-permute-start.16
  118.4 2.8 %collective-permute-start.18 = (f32[8,32,128]{2,1,0:T(8,128)}, f32[8,32,128]{2,1,0:T(8,128)S(1)}, u32[]{:S(2)}, u32[]{:S(2)}) collective-permute-start(f32[8,32,128]{2,1,0:T(8,128)} %get-tuple-element.119), channel_id=1, source_target_pairs={{0,19},{1,18},{2,17},{3,16},{4,23},{5,22},{6,21},{7,20},{8,27},{9,... | collective-permute-start | bytes 393224 | tf_op jit(solution)/shard_map/ppermute | solution.py:262
  121.9 1.0 collective-permute-start.19
  122.9 12.4 %collective-permute-done.15.refs_16_ = f32[8,32,128]{2,1,0:T(8,128)S(1)} collective-permute-done((f32[8,32,128]{2,1,0:T(8,128)}, f32[8,32,128]{2,1,0:T(8,128)S(1)}, u32[]{:S(2)}, u32[]{:S(2)}) %collective-permute-start.15) | collective-permute-done | bytes 131104 | tf_op jit(solution)/shard_map/ppermute | solution.py:262
  135.4 2.2 collective-permute-start.2
  137.5 1.0 collective-permute-done.16.refs_17_
  138.6 3.3 %collective-permute-done.17.refs_18_ = f32[8,32,128]{2,1,0:T(8,128)S(1)} collective-permute-done((f32[8,32,128]{2,1,0:T(8,128)}, f32[8,32,128]{2,1,0:T(8,128)S(1)}, u32[]{:S(2)}, u32[]{:S(2)}) %collective-permute-start.17) | collective-permute-done | bytes 131104 | tf_op jit(solution)/shard_map/ppermute | solution.py:262
  142.7 8.4 %collective-permute-done.18.refs_19_ = f32[8,32,128]{2,1,0:T(8,128)S(1)} collective-permute-done((f32[8,32,128]{2,1,0:T(8,128)}, f32[8,32,128]{2,1,0:T(8,128)S(1)}, u32[]{:S(2)}, u32[]{:S(2)}) %collective-permute-start.18) | collective-permute-done | bytes 131104 | tf_op jit(solution)/shard_map/ppermute | solution.py:262
  151.3 1.0 collective-permute-done.19.refs_20_
  152.3 1.3 collective-permute-start.23
  153.6 3.0 %collective-permute-start.24 = (f32[8,32,128]{2,1,0:T(8,128)}, f32[8,32,128]{2,1,0:T(8,128)S(1)}, u32[]{:S(2)}, u32[]{:S(2)}) collective-permute-start(f32[8,32,128]{2,1,0:T(8,128)} %get-tuple-element.125), channel_id=1, source_target_pairs={{0,25},{1,24},{2,27},{3,26},{4,29},{5,28},{6,31},{7,30},{8,17},{9,... | collective-permute-start | bytes 393224 | tf_op jit(solution)/shard_map/ppermute | solution.py:262
  156.7 7.1 %collective-permute-done.20.refs_21_ = f32[8,32,128]{2,1,0:T(8,128)S(1)} collective-permute-done((f32[8,32,128]{2,1,0:T(8,128)}, f32[8,32,128]{2,1,0:T(8,128)S(1)}, u32[]{:S(2)}, u32[]{:S(2)}) %collective-permute-start.20) | collective-permute-done | bytes 131104 | tf_op jit(solution)/shard_map/ppermute | solution.py:262
  163.8 2.1 collective-permute-start.25
  165.9 1.5 collective-permute-done.21.refs_22_
  167.4 2.1 collective-permute-start.26
  169.5 3.9 %collective-permute-done.22.refs_23_ = f32[8,32,128]{2,1,0:T(8,128)S(1)} collective-permute-done((f32[8,32,128]{2,1,0:T(8,128)}, f32[8,32,128]{2,1,0:T(8,128)S(1)}, u32[]{:S(2)}, u32[]{:S(2)}) %collective-permute-start.22) | collective-permute-done | bytes 131104 | tf_op jit(solution)/shard_map/ppermute | solution.py:262
  173.4 5.4 %collective-permute-start.27 = (f32[8,32,128]{2,1,0:T(8,128)}, f32[8,32,128]{2,1,0:T(8,128)S(1)}, u32[]{:S(2)}, u32[]{:S(2)}) collective-permute-start(f32[8,32,128]{2,1,0:T(8,128)} %get-tuple-element.128), channel_id=1, source_target_pairs={{0,28},{1,29},{2,30},{3,31},{4,24},{5,25},{6,26},{7,27},{8,20},{9,... | collective-permute-start | bytes 393224 | tf_op jit(solution)/shard_map/ppermute | solution.py:262
  178.9 1.3 collective-permute-start.29
  180.3 4.4 %collective-permute-start.30 = (f32[8,32,128]{2,1,0:T(8,128)}, f32[8,32,128]{2,1,0:T(8,128)S(1)}, u32[]{:S(2)}, u32[]{:S(2)}) collective-permute-start(f32[8,32,128]{2,1,0:T(8,128)} %get-tuple-element.131), channel_id=1, source_target_pairs={{0,31},{1,30},{2,29},{3,28},{4,27},{5,26},{6,25},{7,24},{8,23},{9,... | collective-permute-start | bytes 393224 | tf_op jit(solution)/shard_map/ppermute | solution.py:262
  184.6 1.2 collective-permute-start.4
  188.4 2.2 collective-permute-start.6
  190.5 7.0 %collective-permute-done.3.refs_4_ = f32[8,32,128]{2,1,0:T(8,128)S(1)} collective-permute-done((f32[8,32,128]{2,1,0:T(8,128)}, f32[8,32,128]{2,1,0:T(8,128)S(1)}, u32[]{:S(2)}, u32[]{:S(2)}) %collective-permute-start.3) | collective-permute-done | bytes 131104 | tf_op jit(solution)/shard_map/ppermute | solution.py:262
  197.6 19.9 %collective-permute-start.7 = (f32[8,32,128]{2,1,0:T(8,128)}, f32[8,32,128]{2,1,0:T(8,128)}, u32[]{:S(2)}, u32[]{:S(2)}) collective-permute-start(f32[8,32,128]{2,1,0:T(8,128)} %get-tuple-element.108), channel_id=1, source_target_pairs={{0,8},{1,9},{2,10},{3,11},{4,12},{5,13},{6,14},{7,15},{8,0},{9,1},... | collective-permute-start | bytes 393224 | tf_op jit(solution)/shard_map/ppermute | solution.py:262
  218.7 2.9 %collective-permute-start.9 = (f32[8,32,128]{2,1,0:T(8,128)}, f32[8,32,128]{2,1,0:T(8,128)}, u32[]{:S(2)}, u32[]{:S(2)}) collective-permute-start(f32[8,32,128]{2,1,0:T(8,128)} %get-tuple-element.110), channel_id=1, source_target_pairs={{0,10},{1,11},{2,8},{3,9},{4,14},{5,15},{6,12},{7,13},{8,2},{9,3},... | collective-permute-start | bytes 393224 | tf_op jit(solution)/shard_map/ppermute | solution.py:262
  221.6 11.2 %base.1.refs_32_ = f32[8,2,4,128,128]{4,3,2,1,0:T(8,128)} custom-call(f32[8,2,4,128,128]{4,3,2,1,0:T(8,128)} %psi.7, f32[8,1024,128]{2,1,0:T(8,128)} %bitcast.90, f32[4,128,128]{2,1,0:T(8,128)} %add_multiply_fusion.kinetic, f32[8,16,32]{2,1,0:T(8,128)} %pad_maximum_fusion.5.coefs), custom_call_target="tpu_custom_call" | custom-call | flops 8000000000 | bytes 12000000 | tf_op jit(solution)/shard_map/base/pallas_call | solution.py:475
  233.5 7.1 %to_planes.1 = f32[8,2,4,128,128]{4,3,2,1,0:T(8,128)} custom-call(f32[8,32,128]{2,1,0:T(8,128)} %get-tuple-element.100.refs_0_, f32[8,32,128]{2,1,0:T(8,128)} %copy-done.6, f32[8,32,128]{2,1,0:T(8,128)} %copy-done.7, f32[8,32,128]{2,1,0:T(8,128)} %copy-done.17, f32[8,32,128]{2,1,0:T(8,128)} %copy-done.28, f32[8,32,128]{2,1,0:T(8,128)} %copy-done.30, ...), custom_call_target="tpu_custom_call" | custom-call | flops 8000000000 | bytes 12000000 | tf_op jit(solution)/shard_map/to_planes/pallas_call | solution.py:488
  (192 shorter events, 25.7 us)
Async XLA Ops:
  3.6 32.5 %all-to-all-start.1 = ((f32[32,2,32,128]{3,2,1,0:T(8,128)}), f32[32,2,32,128]{3,2,1,0:T(8,128)}, u32[]{:S(2)}, u32[]{:S(2)}) async-start(f32[32,2,32,128]{3,2,1,0:T(8,128)} %to_rows.3), calls=%async_computation.1 | async-start | bytes 2097152 | tf_op jit(solution)/shard_map/all_to_all | solution.py:329
  36.1 30.0 %all-to-all-start = ((f32[32,2,32,128]{3,2,1,0:T(8,128)}), f32[32,2,32,128]{3,2,1,0:T(8,128)}, u32[]{:S(2)}, u32[]{:S(2)}) async-start(f32[32,2,32,128]{3,2,1,0:T(8,128)} %to_rows.2), calls=%async_computation | async-start | bytes 2097152 | tf_op jit(solution)/shard_map/all_to_all | solution.py:329
  74.9 5.0 %collective-permute-start.11 = (f32[8,32,128]{2,1,0:T(8,128)}, f32[8,32,128]{2,1,0:T(8,128)S(1)}, u32[]{:S(2)}, u32[]{:S(2)}) collective-permute-start(f32[8,32,128]{2,1,0:T(8,128)} %get-tuple-element.112), channel_id=1, source_target_pairs={{0,12},{1,13},{2,14},{3,15},{4,8},{5,9},{6,10},{7,11},{8,4},{9,5},... | collective-permute-start | bytes 393224 | tf_op jit(solution)/shard_map/ppermute | solution.py:262
  86.8 3.2 %collective-permute-start.31 = (f32[136,16]{0,1:T(8,128)S(1)}, f32[136,16]{0,1:T(8,128)S(1)}, u32[]{:S(2)}, u32[]{:S(2)}) collective-permute-start(f32[136,16]{0,1:T(8,128)S(1)} %maximum_maximum_fusion), channel_id=1, source_target_pairs={{0,1},{1,0},{2,3},{3,2},{4,5},{5,4},{6,7},{7,6},{8,9},{9,8},{10,11... | collective-permute-start | bytes 26120 | tf_op jit(solution)/shard_map/ppermute | solution.py:262
  90.0 2.6 %collective-permute-start.32 = (f32[136,16]{0,1:T(8,128)S(1)}, f32[136,16]{0,1:T(8,128)S(1)}, u32[]{:S(2)}, u32[]{:S(2)}) collective-permute-start(f32[136,16]{0,1:T(8,128)S(1)} %fusion.56), channel_id=1, source_target_pairs={{0,2},{1,3},{2,0},{3,1},{4,6},{5,7},{6,4},{7,5},{8,10},{9,11},{10,... | collective-permute-start | bytes 26120 | tf_op jit(solution)/shard_map/ppermute | solution.py:262
  92.6 2.6 %collective-permute-start.33 = (f32[136,16]{0,1:T(8,128)S(1)}, f32[136,16]{0,1:T(8,128)S(1)}, u32[]{:S(2)}, u32[]{:S(2)}) collective-permute-start(f32[136,16]{0,1:T(8,128)S(1)} %add.148), channel_id=1, source_target_pairs={{0,4},{1,5},{2,6},{3,7},{4,0},{5,1},{6,2},{7,3},{8,12},{9,13},{10,... | collective-permute-start | bytes 26120 | tf_op jit(solution)/shard_map/ppermute | solution.py:262
  95.2 9.6 %collective-permute-start.34 = (f32[136,16]{0,1:T(8,128)S(1)}, f32[136,16]{0,1:T(8,128)S(1)}, u32[]{:S(2)}, u32[]{:S(2)}) collective-permute-start(f32[136,16]{0,1:T(8,128)S(1)} %add.149), channel_id=1, source_target_pairs={{0,8},{1,9},{2,10},{3,11},{4,12},{5,13},{6,14},{7,15},{8,0},{9,1},... | collective-permute-start | bytes 26120 | tf_op jit(solution)/shard_map/ppermute | solution.py:262
  96.3 8.6 %collective-permute-start.35 = (f32[136,16]{0,1:T(8,128)S(1)}, f32[136,16]{0,1:T(8,128)S(1)}, u32[]{:S(2)}, u32[]{:S(2)}) collective-permute-start(f32[136,16]{0,1:T(8,128)S(1)} %add.149), channel_id=1, source_target_pairs={{0,16},{1,17},{2,18},{3,19},{4,20},{5,21},{6,22},{7,23},{8,24},{9,... | collective-permute-start | bytes 26120 | tf_op jit(solution)/shard_map/ppermute | solution.py:262
  97.0 10.2 %collective-permute-start.36 = (f32[136,16]{0,1:T(8,128)S(1)}, f32[136,16]{0,1:T(8,128)S(1)}, u32[]{:S(2)}, u32[]{:S(2)}) collective-permute-start(f32[136,16]{0,1:T(8,128)S(1)} %add.149), channel_id=1, source_target_pairs={{0,24},{1,25},{2,26},{3,27},{4,28},{5,29},{6,30},{7,31},{8,16},{9,... | collective-permute-start | bytes 26120 | tf_op jit(solution)/shard_map/ppermute | solution.py:262
  99.8 12.5 %collective-permute-start = (f32[8,32,128]{2,1,0:T(8,128)S(1)}, f32[8,32,128]{2,1,0:T(8,128)S(1)}, u32[]{:S(2)}, u32[]{:S(2)}) collective-permute-start(f32[8,32,128]{2,1,0:T(8,128)S(1)} %copy-done.31), channel_id=1, source_target_pairs={{0,1},{1,0},{2,3},{3,2},{4,5},{5,4},{6,7},{7,6},{8,9},{9,8},{10,11... | collective-permute-start | bytes 393224 | tf_op jit(solution)/shard_map/ppermute | solution.py:262
  103.3 11.7 %collective-permute-start.1 = (f32[8,32,128]{2,1,0:T(8,128)S(1)}, f32[8,32,128]{2,1,0:T(8,128)S(1)}, u32[]{:S(2)}, u32[]{:S(2)}) collective-permute-start(f32[8,32,128]{2,1,0:T(8,128)S(1)} %copy-done.32), channel_id=1, source_target_pairs={{0,2},{1,3},{2,0},{3,1},{4,6},{5,7},{6,4},{7,5},{8,10},{9,11},{10,... | collective-permute-start | bytes 393224 | tf_op jit(solution)/shard_map/ppermute | solution.py:262
  104.8 10.5 %collective-permute-start.10 = (f32[8,32,128]{2,1,0:T(8,128)}, f32[8,32,128]{2,1,0:T(8,128)S(1)}, u32[]{:S(2)}, u32[]{:S(2)}) collective-permute-start(f32[8,32,128]{2,1,0:T(8,128)} %get-tuple-element.111), channel_id=1, source_target_pairs={{0,11},{1,10},{2,9},{3,8},{4,15},{5,14},{6,13},{7,12},{8,3},{9,2},... | collective-permute-start | bytes 393224 | tf_op jit(solution)/shard_map/ppermute | solution.py:262
  105.0 12.5 %collective-permute-start.12 = (f32[8,32,128]{2,1,0:T(8,128)}, f32[8,32,128]{2,1,0:T(8,128)S(1)}, u32[]{:S(2)}, u32[]{:S(2)}) collective-permute-start(f32[8,32,128]{2,1,0:T(8,128)} %get-tuple-element.113), channel_id=1, source_target_pairs={{0,13},{1,12},{2,15},{3,14},{4,9},{5,8},{6,11},{7,10},{8,5},{9,4},... | collective-permute-start | bytes 393224 | tf_op jit(solution)/shard_map/ppermute | solution.py:262
  107.2 11.2 %collective-permute-start.13 = (f32[8,32,128]{2,1,0:T(8,128)}, f32[8,32,128]{2,1,0:T(8,128)S(1)}, u32[]{:S(2)}, u32[]{:S(2)}) collective-permute-start(f32[8,32,128]{2,1,0:T(8,128)} %get-tuple-element.114), channel_id=1, source_target_pairs={{0,14},{1,15},{2,12},{3,13},{4,10},{5,11},{6,8},{7,9},{8,6},{9,7},... | collective-permute-start | bytes 393224 | tf_op jit(solution)/shard_map/ppermute | solution.py:262
  112.2 120.6 %copy-start.6 = (f32[8,32,128]{2,1,0:T(8,128)}, f32[8,32,128]{2,1,0:T(8,128)S(1)}, u32[]{:S(2)}) copy-start(f32[8,32,128]{2,1,0:T(8,128)S(1)} %collective-permute-done.refs_1_) | copy-start | bytes 393220
  112.3 9.7 %collective-permute-start.14 = (f32[8,32,128]{2,1,0:T(8,128)}, f32[8,32,128]{2,1,0:T(8,128)S(1)}, u32[]{:S(2)}, u32[]{:S(2)}) collective-permute-start(f32[8,32,128]{2,1,0:T(8,128)} %get-tuple-element.115), channel_id=1, source_target_pairs={{0,15},{1,14},{2,13},{3,12},{4,11},{5,10},{6,9},{7,8},{8,7},{9,6},... | collective-permute-start | bytes 393224 | tf_op jit(solution)/shard_map/ppermute | solution.py:262
  115.0 117.8 %copy-start.7 = (f32[8,32,128]{2,1,0:T(8,128)}, f32[8,32,128]{2,1,0:T(8,128)S(1)}, u32[]{:S(2)}) copy-start(f32[8,32,128]{2,1,0:T(8,128)S(1)} %collective-permute-done.1.refs_2_) | copy-start | bytes 393220
  115.0 20.4 %collective-permute-start.15 = (f32[8,32,128]{2,1,0:T(8,128)}, f32[8,32,128]{2,1,0:T(8,128)S(1)}, u32[]{:S(2)}, u32[]{:S(2)}) collective-permute-start(f32[8,32,128]{2,1,0:T(8,128)} %get-tuple-element.116), channel_id=1, source_target_pairs={{0,16},{1,17},{2,18},{3,19},{4,20},{5,21},{6,22},{7,23},{8,24},{9,... | collective-permute-start | bytes 393224 | tf_op jit(solution)/shard_map/ppermute | solution.py:262
  115.3 117.5 %copy-start.8 = (f32[8,32,128]{2,1,0:T(8,128)}, f32[8,32,128]{2,1,0:T(8,128)S(1)}, u32[]{:S(2)}) copy-start(f32[8,32,128]{2,1,0:T(8,128)S(1)} %collective-permute-done.10.refs_11_) | copy-start | bytes 393220
  115.3 23.2 %collective-permute-start.16 = (f32[8,32,128]{2,1,0:T(8,128)}, f32[8,32,128]{2,1,0:T(8,128)S(1)}, u32[]{:S(2)}, u32[]{:S(2)}) collective-permute-start(f32[8,32,128]{2,1,0:T(8,128)} %get-tuple-element.117), channel_id=1, source_target_pairs={{0,17},{1,16},{2,19},{3,18},{4,21},{5,20},{6,23},{7,22},{8,25},{9,... | collective-permute-start | bytes 393224 | tf_op jit(solution)/shard_map/ppermute | solution.py:262
  117.4 115.4 %copy-start.9 = (f32[8,32,128]{2,1,0:T(8,128)}, f32[8,32,128]{2,1,0:T(8,128)S(1)}, u32[]{:S(2)}) copy-start(f32[8,32,128]{2,1,0:T(8,128)S(1)} %collective-permute-done.12.refs_13_) | copy-start | bytes 393220
  117.4 24.5 %collective-permute-start.17 = (f32[8,32,128]{2,1,0:T(8,128)}, f32[8,32,128]{2,1,0:T(8,128)S(1)}, u32[]{:S(2)}, u32[]{:S(2)}) collective-permute-start(f32[8,32,128]{2,1,0:T(8,128)} %get-tuple-element.118), channel_id=1, source_target_pairs={{0,18},{1,19},{2,16},{3,17},{4,22},{5,23},{6,20},{7,21},{8,26},{9,... | collective-permute-start | bytes 393224 | tf_op jit(solution)/shard_map/ppermute | solution.py:262
  118.4 114.4 %copy-start.10 = (f32[8,32,128]{2,1,0:T(8,128)}, f32[8,32,128]{2,1,0:T(8,128)S(1)}, u32[]{:S(2)}) copy-start(f32[8,32,128]{2,1,0:T(8,128)S(1)} %collective-permute-done.13.refs_14_) | copy-start | bytes 393220
  118.4 32.6 %collective-permute-start.18 = (f32[8,32,128]{2,1,0:T(8,128)}, f32[8,32,128]{2,1,0:T(8,128)S(1)}, u32[]{:S(2)}, u32[]{:S(2)}) collective-permute-start(f32[8,32,128]{2,1,0:T(8,128)} %get-tuple-element.119), channel_id=1, source_target_pairs={{0,19},{1,18},{2,17},{3,16},{4,23},{5,22},{6,21},{7,20},{8,27},{9,... | collective-permute-start | bytes 393224 | tf_op jit(solution)/shard_map/ppermute | solution.py:262
  121.9 110.9 %copy-start.11 = (f32[8,32,128]{2,1,0:T(8,128)}, f32[8,32,128]{2,1,0:T(8,128)S(1)}, u32[]{:S(2)}) copy-start(f32[8,32,128]{2,1,0:T(8,128)S(1)} %collective-permute-done.14.refs_15_) | copy-start | bytes 393220
  121.9 30.4 %collective-permute-start.19 = (f32[8,32,128]{2,1,0:T(8,128)}, f32[8,32,128]{2,1,0:T(8,128)S(1)}, u32[]{:S(2)}, u32[]{:S(2)}) collective-permute-start(f32[8,32,128]{2,1,0:T(8,128)} %get-tuple-element.120), channel_id=1, source_target_pairs={{0,20},{1,21},{2,22},{3,23},{4,16},{5,17},{6,18},{7,19},{8,28},{9,... | collective-permute-start | bytes 393224 | tf_op jit(solution)/shard_map/ppermute | solution.py:262
  135.4 97.5 %copy-start.12 = (f32[8,32,128]{2,1,0:T(8,128)}, f32[8,32,128]{2,1,0:T(8,128)S(1)}, u32[]{:S(2)}) copy-start(f32[8,32,128]{2,1,0:T(8,128)S(1)} %collective-permute-done.15.refs_16_) | copy-start | bytes 393220
  135.4 18.2 %collective-permute-start.2 = (f32[8,32,128]{2,1,0:T(8,128)}, f32[8,32,128]{2,1,0:T(8,128)S(1)}, u32[]{:S(2)}, u32[]{:S(2)}) collective-permute-start(f32[8,32,128]{2,1,0:T(8,128)} %get-tuple-element.103), channel_id=1, source_target_pairs={{0,3},{1,2},{2,1},{3,0},{4,7},{5,6},{6,5},{7,4},{8,11},{9,10},{10,... | collective-permute-start | bytes 393224 | tf_op jit(solution)/shard_map/ppermute | solution.py:262
  138.6 25.2 %collective-permute-start.20 = (f32[8,32,128]{2,1,0:T(8,128)}, f32[8,32,128]{2,1,0:T(8,128)S(1)}, u32[]{:S(2)}, u32[]{:S(2)}) collective-permute-start(f32[8,32,128]{2,1,0:T(8,128)} %get-tuple-element.121), channel_id=1, source_target_pairs={{0,21},{1,20},{2,23},{3,22},{4,17},{5,16},{6,19},{7,18},{8,29},{9,... | collective-permute-start | bytes 393224 | tf_op jit(solution)/shard_map/ppermute | solution.py:262
  141.9 45.0 %copy-start.14 = (f32[8,32,128]{2,1,0:T(8,128)}, f32[8,32,128]{2,1,0:T(8,128)S(1)}, u32[]{:S(2)}) copy-start(f32[8,32,128]{2,1,0:T(8,128)S(1)} %collective-permute-done.17.refs_18_) | copy-start | bytes 393220
  141.9 25.5 %collective-permute-start.21 = (f32[8,32,128]{2,1,0:T(8,128)}, f32[8,32,128]{2,1,0:T(8,128)S(1)}, u32[]{:S(2)}, u32[]{:S(2)}) collective-permute-start(f32[8,32,128]{2,1,0:T(8,128)} %get-tuple-element.122), channel_id=1, source_target_pairs={{0,22},{1,23},{2,20},{3,21},{4,18},{5,19},{6,16},{7,17},{8,30},{9,... | collective-permute-start | bytes 393224 | tf_op jit(solution)/shard_map/ppermute | solution.py:262
  151.0 22.4 %collective-permute-start.22 = (f32[8,32,128]{2,1,0:T(8,128)}, f32[8,32,128]{2,1,0:T(8,128)S(1)}, u32[]{:S(2)}, u32[]{:S(2)}) collective-permute-start(f32[8,32,128]{2,1,0:T(8,128)} %get-tuple-element.123), channel_id=1, source_target_pairs={{0,23},{1,22},{2,21},{3,20},{4,19},{5,18},{6,17},{7,16},{8,31},{9,... | collective-permute-start | bytes 393224 | tf_op jit(solution)/shard_map/ppermute | solution.py:262
  152.3 26.5 %collective-permute-start.23 = (f32[8,32,128]{2,1,0:T(8,128)}, f32[8,32,128]{2,1,0:T(8,128)S(1)}, u32[]{:S(2)}, u32[]{:S(2)}) collective-permute-start(f32[8,32,128]{2,1,0:T(8,128)} %get-tuple-element.124), channel_id=1, source_target_pairs={{0,24},{1,25},{2,26},{3,27},{4,28},{5,29},{6,30},{7,31},{8,16},{9,... | collective-permute-start | bytes 393224 | tf_op jit(solution)/shard_map/ppermute | solution.py:262
  153.6 25.3 %collective-permute-start.24 = (f32[8,32,128]{2,1,0:T(8,128)}, f32[8,32,128]{2,1,0:T(8,128)S(1)}, u32[]{:S(2)}, u32[]{:S(2)}) collective-permute-start(f32[8,32,128]{2,1,0:T(8,128)} %get-tuple-element.125), channel_id=1, source_target_pairs={{0,25},{1,24},{2,27},{3,26},{4,29},{5,28},{6,31},{7,30},{8,17},{9,... | collective-permute-start | bytes 393224 | tf_op jit(solution)/shard_map/ppermute | solution.py:262
  163.8 16.5 %collective-permute-start.25 = (f32[8,32,128]{2,1,0:T(8,128)}, f32[8,32,128]{2,1,0:T(8,128)S(1)}, u32[]{:S(2)}, u32[]{:S(2)}) collective-permute-start(f32[8,32,128]{2,1,0:T(8,128)} %get-tuple-element.126), channel_id=1, source_target_pairs={{0,26},{1,27},{2,24},{3,25},{4,30},{5,31},{6,28},{7,29},{8,18},{9,... | collective-permute-start | bytes 393224 | tf_op jit(solution)/shard_map/ppermute | solution.py:262
  167.4 12.8 %collective-permute-start.26 = (f32[8,32,128]{2,1,0:T(8,128)}, f32[8,32,128]{2,1,0:T(8,128)S(1)}, u32[]{:S(2)}, u32[]{:S(2)}) collective-permute-start(f32[8,32,128]{2,1,0:T(8,128)} %get-tuple-element.127), channel_id=1, source_target_pairs={{0,27},{1,26},{2,25},{3,24},{4,31},{5,30},{6,29},{7,28},{8,19},{9,... | collective-permute-start | bytes 393224 | tf_op jit(solution)/shard_map/ppermute | solution.py:262
  173.4 11.2 %collective-permute-start.27 = (f32[8,32,128]{2,1,0:T(8,128)}, f32[8,32,128]{2,1,0:T(8,128)S(1)}, u32[]{:S(2)}, u32[]{:S(2)}) collective-permute-start(f32[8,32,128]{2,1,0:T(8,128)} %get-tuple-element.128), channel_id=1, source_target_pairs={{0,28},{1,29},{2,30},{3,31},{4,24},{5,25},{6,26},{7,27},{8,20},{9,... | collective-permute-start | bytes 393224 | tf_op jit(solution)/shard_map/ppermute | solution.py:262
  178.8 8.7 %collective-permute-start.28 = (f32[8,32,128]{2,1,0:T(8,128)}, f32[8,32,128]{2,1,0:T(8,128)S(1)}, u32[]{:S(2)}, u32[]{:S(2)}) collective-permute-start(f32[8,32,128]{2,1,0:T(8,128)} %get-tuple-element.129), channel_id=1, source_target_pairs={{0,29},{1,28},{2,31},{3,30},{4,25},{5,24},{6,27},{7,26},{8,21},{9,... | collective-permute-start | bytes 393224 | tf_op jit(solution)/shard_map/ppermute | solution.py:262
  178.9 9.4 %collective-permute-start.29 = (f32[8,32,128]{2,1,0:T(8,128)}, f32[8,32,128]{2,1,0:T(8,128)S(1)}, u32[]{:S(2)}, u32[]{:S(2)}) collective-permute-start(f32[8,32,128]{2,1,0:T(8,128)} %get-tuple-element.130), channel_id=1, source_target_pairs={{0,30},{1,31},{2,28},{3,29},{4,26},{5,27},{6,24},{7,25},{8,22},{9,... | collective-permute-start | bytes 393224 | tf_op jit(solution)/shard_map/ppermute | solution.py:262
  180.2 37.2 %copy-start.23 = (f32[8,32,128]{2,1,0:T(8,128)}, f32[8,32,128]{2,1,0:T(8,128)S(1)}, u32[]{:S(2)}) copy-start(f32[8,32,128]{2,1,0:T(8,128)S(1)} %collective-permute-done.25.refs_26_) | copy-start | bytes 393220
  180.2 17.3 %collective-permute-start.3 = (f32[8,32,128]{2,1,0:T(8,128)}, f32[8,32,128]{2,1,0:T(8,128)S(1)}, u32[]{:S(2)}, u32[]{:S(2)}) collective-permute-start(f32[8,32,128]{2,1,0:T(8,128)} %get-tuple-element.104), channel_id=1, source_target_pairs={{0,4},{1,5},{2,6},{3,7},{4,0},{5,1},{6,2},{7,3},{8,12},{9,13},{10,... | collective-permute-start | bytes 393224 | tf_op jit(solution)/shard_map/ppermute | solution.py:262
  180.3 37.2 %collective-permute-start.30 = (f32[8,32,128]{2,1,0:T(8,128)}, f32[8,32,128]{2,1,0:T(8,128)S(1)}, u32[]{:S(2)}, u32[]{:S(2)}) collective-permute-start(f32[8,32,128]{2,1,0:T(8,128)} %get-tuple-element.131), channel_id=1, source_target_pairs={{0,31},{1,30},{2,29},{3,28},{4,27},{5,26},{6,25},{7,24},{8,23},{9,... | collective-permute-start | bytes 393224 | tf_op jit(solution)/shard_map/ppermute | solution.py:262
  184.6 33.4 %collective-permute-start.4 = (f32[8,32,128]{2,1,0:T(8,128)}, f32[8,32,128]{2,1,0:T(8,128)S(1)}, u32[]{:S(2)}, u32[]{:S(2)}) collective-permute-start(f32[8,32,128]{2,1,0:T(8,128)} %get-tuple-element.105), channel_id=1, source_target_pairs={{0,5},{1,4},{2,7},{3,6},{4,1},{5,0},{6,3},{7,2},{8,13},{9,12},{10,... | collective-permute-start | bytes 393224 | tf_op jit(solution)/shard_map/ppermute | solution.py:262
  187.5 45.9 %collective-permute-start.5 = (f32[8,32,128]{2,1,0:T(8,128)}, f32[8,32,128]{2,1,0:T(8,128)}, u32[]{:S(2)}, u32[]{:S(2)}) collective-permute-start(f32[8,32,128]{2,1,0:T(8,128)} %get-tuple-element.106), channel_id=1, source_target_pairs={{0,6},{1,7},{2,4},{3,5},{4,2},{5,3},{6,0},{7,1},{8,14},{9,15},{10,... | collective-permute-start | bytes 393224 | tf_op jit(solution)/shard_map/ppermute | solution.py:262
  188.4 45.1 %collective-permute-start.6 = (f32[8,32,128]{2,1,0:T(8,128)}, f32[8,32,128]{2,1,0:T(8,128)}, u32[]{:S(2)}, u32[]{:S(2)}) collective-permute-start(f32[8,32,128]{2,1,0:T(8,128)} %get-tuple-element.107), channel_id=1, source_target_pairs={{0,7},{1,6},{2,5},{3,4},{4,3},{5,2},{6,1},{7,0},{8,15},{9,14},{10,... | collective-permute-start | bytes 393224 | tf_op jit(solution)/shard_map/ppermute | solution.py:262
  197.6 35.9 %collective-permute-start.7 = (f32[8,32,128]{2,1,0:T(8,128)}, f32[8,32,128]{2,1,0:T(8,128)}, u32[]{:S(2)}, u32[]{:S(2)}) collective-permute-start(f32[8,32,128]{2,1,0:T(8,128)} %get-tuple-element.108), channel_id=1, source_target_pairs={{0,8},{1,9},{2,10},{3,11},{4,12},{5,13},{6,14},{7,15},{8,0},{9,1},... | collective-permute-start | bytes 393224 | tf_op jit(solution)/shard_map/ppermute | solution.py:262
  217.5 16.0 %collective-permute-start.8 = (f32[8,32,128]{2,1,0:T(8,128)}, f32[8,32,128]{2,1,0:T(8,128)}, u32[]{:S(2)}, u32[]{:S(2)}) collective-permute-start(f32[8,32,128]{2,1,0:T(8,128)} %get-tuple-element.109), channel_id=1, source_target_pairs={{0,9},{1,8},{2,11},{3,10},{4,13},{5,12},{6,15},{7,14},{8,1},{9,0},... | collective-permute-start | bytes 393224 | tf_op jit(solution)/shard_map/ppermute | solution.py:262
  218.7 14.8 %collective-permute-start.9 = (f32[8,32,128]{2,1,0:T(8,128)}, f32[8,32,128]{2,1,0:T(8,128)}, u32[]{:S(2)}, u32[]{:S(2)}) collective-permute-start(f32[8,32,128]{2,1,0:T(8,128)} %get-tuple-element.110), channel_id=1, source_target_pairs={{0,10},{1,11},{2,8},{3,9},{4,14},{5,15},{6,12},{7,13},{8,2},{9,3},... | collective-permute-start | bytes 393224 | tf_op jit(solution)/shard_map/ppermute | solution.py:262
  (25 other events, 539.1 us)

commit v9 on v7

--- a/solution.py
+++ b/solution.py
@@ -116,49 +116,49 @@
     span_x = devices * planes
     arrived = recv.reshape(devices * size, span_z)
     leaving = back.reshape(devices * 2 * size, span_z)
-    for group in groups(rows, span_z):
-        columns = [
-            jnp.concatenate(
-                [
-                    arrived[pl.ds((p * rows + r) * 2 + part, devices, stride=size), :]
-                    for part in range(2)
-                    for p in range(planes)
-                ],
-                axis=0,
-            )
-            for r in group
-        ]
-        along_x = dot_left(inverse[...], jnp.concatenate(columns, axis=1))
-        spatial = dot_right(parts_in_lanes(along_x, span_x, span_z), inv_z[...])
-        here = slice(group[0] * span_x, (group[-1] + 1) * span_x)
-        for band in range(2):
-            one = spatial[:, band * span_z : (band + 1) * span_z]
-            field[band, here, :] = one
-            product = one * pot[here, :]
-            product = jnp.concatenate(
-                [product[i * span_x : (i + 1) * span_x] for i in range(len(group))], axis=1
-            )
-            spectral = dot_left(forward[...], product)
-            spectral = dot_right(parts_in_lanes(spectral, span_x, span_z), fwd_z[...])
-            for i, r in enumerate(group):
-                for p in range(planes):
-                    first = i * span_x + p * devices
-                    for part in range(2):
-                        start = band * size + (p * rows + r) * 2 + part
-                        leaving[pl.ds(start, devices, stride=2 * size), :] = spectral[
-                            first : first + devices, part * span_z : (part + 1) * span_z
-                        ]
+    columns = [
+        jnp.concatenate(
+            [
+                arrived[pl.ds((p * rows + r) * 2 + part, devices, stride=size), :]
+                for part in range(2)
+                for p in range(planes)
+            ],
+            axis=0,
+        )
+        for r in range(rows)
+    ]
+    along_x = dot_left(inverse[...], jnp.concatenate(columns, axis=1))
+    spatial = dot_right(parts_in_lanes(along_x, span_x, span_z), inv_z[...])
+    spectral = []
+    for band in range(2):
+        one = spatial[:, band * span_z : (band + 1) * span_z]
+        field[band] = one
+        product = one * pot[...]
+        product = jnp.concatenate(
+            [product[r * span_x : (r + 1) * span_x] for r in range(rows)], axis=1
+        )
+        spectral.append(parts_in_lanes(dot_left(forward[...], product), span_x, span_z))
+    spectral = dot_right(jnp.concatenate(spectral, axis=0), fwd_z[...])
+    for band in range(2):
+        for r in range(rows):
+            for p in range(planes):
+                first = ((band * rows + r) * planes + p) * devices
+                for part in range(2):
+                    start = band * size + (p * rows + r) * 2 + part
+                    leaving[pl.ds(start, devices, stride=2 * size), :] = spectral[
+                        first : first + devices, part * span_z : (part + 1) * span_z
+                    ]
 
 
 def real_gram_kernel(bands, *refs):
     fields, (pot, out) = refs[:-2], refs[-2:]
-    held = fields[0].shape[0]
+    lines = [(one, i) for one in fields for i in range(one.shape[0])]
     pairs = [(a, b) for a in range(bands) for b in range(a, bands)]
     for weighted in range(2):
 
         def step(i, sums):
             rows = pl.ds(pl.multiple_of(i * 8, 8), 8)
-            values = [fields[a // held][a % held, rows, :] for a in range(bands)]
+            values = [one[i, rows, :] for one, i in lines]
             other = [v * pot[rows, :] for v in values] if weighted else values
             result = []
             for (a, b), total in zip(pairs, sums):
@@ -195,9 +195,8 @@
                     )
 
 
-def last_sum_kernel(*refs):
-    first, second, third, fourth, _, out = refs
-    out[...] = (first[...] + second[...]) + (third[...] + fourth[...])
+def pass_on_kernel(values, _, out):
+    out[...] = values[...]
 
 
 def block_rows_of(psi, beta, slots):
@@ -266,19 +265,21 @@
 def sum_over(values, devices, after):
     if devices & (devices - 1) or devices < 4:
         return lax.psum(values, "ga")
-    step = 1
-    while step < devices // 4:
+    step = devices // 4
+    others = [partner(values, devices, k * step) for k in (1, 2, 3)]
+    values = (values + others[0]) + (others[1] + others[2])
+    held = pl.BlockSpec(memory_space=pltpu.VMEM)
+    values = pl.pallas_call(
+        pass_on_kernel,
+        out_shape=jax.ShapeDtypeStruct(values.shape, f32),
+        in_specs=[held, pl.BlockSpec(memory_space=pl.ANY)],
+        out_specs=held,
+        name="pass_on",
+    )(values, after)
+    while step > 1:
+        step //= 2
         values = values + partner(values, devices, step)
-        step *= 2
-    others = [partner(values, devices, k * step) for k in (1, 2, 3)]
-    held = pl.BlockSpec(memory_space=pltpu.VMEM)
-    return pl.pallas_call(
-        last_sum_kernel,
-        out_shape=jax.ShapeDtypeStruct(values.shape, f32),
-        in_specs=[held] * 4 + [pl.BlockSpec(memory_space=pl.ANY)],
-        out_specs=held,
-        name="last_sum",
-    )(values, *others, after)
+    return values
 
 
 def on_device(devices, orbitals, plane_order, potential, projectors, slot_owner, strengths):
@@ -309,26 +310,20 @@
     inv_z = right_const(right_table(span_z, 1.0))
     fwd_z = right_const(right_table(span_z, -1.0))
 
-    parts = 2 if pairs % 2 == 0 else 1
-    share = pairs // parts
-    arrived = []
-    for c in range(parts):
-        sent = pl.pallas_call(
-            to_rows_kernel,
-            out_shape=jax.ShapeDtypeStruct((devices, share, block_rows, span_z), f32),
-            grid=(share,),
-            in_specs=[
-                pl.BlockSpec(
-                    (2, 2, planes, span_y, span_z), lambda j, c=c: (c * share + j, 0, 0, 0, 0)
-                ),
-                whole(inv_y.shape),
-            ],
-            out_specs=pl.BlockSpec((devices, None, block_rows, span_z), lambda j: (0, j, 0, 0)),
-            compiler_params=params,
-            cost_estimate=cost(4 * 10**9, 3 * 10**6),
-            name="to_rows",
-        )(orbitals, inv_y)
-        arrived.append(lax.all_to_all(sent, "ga", split_axis=0, concat_axis=0, tiled=True))
+    sent = pl.pallas_call(
+        to_rows_kernel,
+        out_shape=jax.ShapeDtypeStruct((devices, pairs, block_rows, span_z), f32),
+        grid=(pairs,),
+        in_specs=[
+            pl.BlockSpec((2, 2, planes, span_y, span_z), lambda j: (j, 0, 0, 0, 0)),
+            whole(inv_y.shape),
+        ],
+        out_specs=pl.BlockSpec((devices, None, block_rows, span_z), lambda j: (0, j, 0, 0)),
+        compiler_params=params,
+        cost_estimate=cost(4 * 10**9, 6 * 10**6),
+        name="to_rows",
+    )(orbitals, inv_y)
+    arrived = lax.all_to_all(sent, "ga", split_axis=0, concat_axis=0, tiled=True)
 
     stored = plane_order.reshape(devices, planes).T.reshape(-1)
     phases = (stored[:, None] * grid_x[None, :]) % span_x
@@ -386,8 +381,10 @@
     kin = jnp.sum(products[:, 2 * slots :], axis=0).reshape(bands, 2, bands, 2)
     kin = kin[:, 0, :, 0] + kin[:, 1, :, 1]
 
+    parts = [(0, 1), (1, pairs)] if pairs > 1 else [(0, pairs)]
     returned, fields = [], []
-    for c in range(parts):
+    for first, end in parts:
+        share = end - first
         back, field = pl.pallas_call(
             functools.partial(real_space_kernel, rows, planes),
             out_shape=(
@@ -396,7 +393,9 @@
             ),
             grid=(share,),
             in_specs=[
-                pl.BlockSpec((devices, None, block_rows, span_z), lambda j: (0, j, 0, 0)),
+                pl.BlockSpec(
+                    (devices, None, block_rows, span_z), lambda j, first=first: (0, first + j, 0, 0)
+                ),
                 whole(pot.shape),
                 whole(inv_x.shape),
                 whole(fwd_x.shape),
@@ -411,7 +410,7 @@
             compiler_params=params,
             cost_estimate=cost(4 * 10**9, 8 * 10**6),
             name="real_space",
-        )(arrived[c], pot, inv_x, fwd_x, inv_z, fwd_z, proj)
+        )(arrived, pot, inv_x, fwd_x, inv_z, fwd_z, proj)
         returned.append(lax.all_to_all(back, "ga", split_axis=0, concat_axis=0, tiled=True))
         fields.append(field)
 
@@ -465,14 +464,14 @@
     )(orbitals, beta, kinetic, coefs)
 
     residual = base
-    for c in range(parts):
+    for (first, end), one_return in zip(parts, returned):
         two_bands = pl.BlockSpec(
-            (2, 2, planes, span_y, span_z), lambda j, c=c: (share * c + j, 0, 0, 0, 0)
+            (2, 2, planes, span_y, span_z), lambda j, first=first: (first + j, 0, 0, 0, 0)
         )
         residual = pl.pallas_call(
             to_planes_kernel,
             out_shape=jax.ShapeDtypeStruct(orbitals.shape, f32),
-            grid=(share,),
+            grid=(end - first,),
             in_specs=[
                 pl.BlockSpec((devices, 2, block_rows, span_z), lambda j: (0, j, 0, 0)),
                 two_bands,
@@ -483,7 +482,7 @@
             compiler_params=params,
             cost_estimate=cost(8 * 10**9, 12 * 10**6),
             name="to_planes",
-        )(returned[c], residual, fwd_y)
+        )(one_return, residual, fwd_y)
     return (residual, jnp.stack([m_real, m_imag]))
 
 

time: 181 us -> 217 us (1.20)
  waiting for transfers between devices: 64.7 us -> 116 us
  starting transfers between devices: 32.7 us -> 25.5 us
  matrix products: 6.01 us -> 2.03 us
    ppermute x6, waiting for transfers between devices: 5.58 us -> 75.6 us  [partner(): return lax.ppermute(values, 'ga', [(d, d ^ k) for d in range(devices)])]
    all_to_all x2, waiting for transfers between devices: 36.4 us -> 8.27 us  [on_device(): lax.all_to_all(back, 'ga', split_axis=0, concat_axis=0, tiled=True)]
    all_to_all x2 -> x1, waiting for transfers between devices: 22.7 us -> 31.8 us  [on_device(): lax.all_to_all(sent, 'ga', split_axis=0, concat_axis=0, tiled=True)]
    all_to_all x2 -> x1, starting transfers between devices: 11.7 us -> 7.15 us  [on_device(): lax.all_to_all(sent, 'ga', split_axis=0, concat_axis=0, tiled=True)]
    dot_general x6, matrix products: 5.63 us -> 1.69 us  [tdot(): jnp.einsum(pattern, left, right, precision=highest, preferred_element_typ...]
    ppermute x6, starting transfers between devices: 11.7 us -> 9.08 us  [partner(): return lax.ppermute(values, 'ga', [(d, d ^ k) for d in range(devices)])]
    pallas_call x3 -> x2, Pallas kernels: 7.55 us -> 6.52 us  [the longest x1 5.01 us: on_device(): pl.pallas_call(to_rows_kernel, out_shape=jax.ShapeDtypeStruct((devices, p...]
  transfers between devices with their start and end apart: 10 -> 9, of which waited for: 7 -> 6; matrix products, arithmetic and copies ran while one was open for 11% -> 7% of each run, Pallas kernels for 29% -> 19%
where the time goes in v9:
time: 217 us; the launch traced here: 216 us
  waiting for transfers between devices  116 us (53%)
  Pallas kernels  58.2 us (27%)
  starting transfers between devices  25.5 us (12%)
  other arithmetic  8.37 us (4%)
  local copies, waits for them, and re-layouts  5.14 us (2%)
    ppermute x6, waiting for transfers between devices, partner(): return lax.ppermute(values, 'ga', [(d, d ^ k) for d in range(devices)])  75.6 us
    all_to_all x1, waiting for transfers between devices, on_device(): lax.all_to_all(sent, 'ga', split_axis=0, concat_axis=0, tiled=True)  31.8 us
    pallas_call x2, Pallas kernels, on_device(): pl.pallas_call(functools.partial(real_space_kernel, rows, planes), out_sh...  15.9 us
    pallas_call x1, Pallas kernels, on_device(): pl.pallas_call(functools.partial(base_kernel, slots), out_shape=jax.Shape...  11.2 us
    pallas_call x1, Pallas kernels, on_device(): pl.pallas_call(functools.partial(project_kernel, slots), out_shape=jax.Sh...  10 us
    pallas_call x2, Pallas kernels, on_device(): pl.pallas_call(to_planes_kernel, out_shape=jax.ShapeDtypeStruct(orbitals....  9.33 us
    all_to_all x2, starting transfers between devices, on_device(): lax.all_to_all(back, 'ga', split_axis=0, concat_axis=0, tiled=True)  9.25 us
    ppermute x6, starting transfers between devices, partner(): return lax.ppermute(values, 'ga', [(d, d ^ k) for d in range(devices)])  9.08 us
  transfers between devices with their start and end apart: 9, of which 6 were waited for; matrix products, arithmetic and copies ran while one was open for 7% of the time, Pallas kernels for 19%

profile of v9, /device:TPU:1, one launch (start us, length us, event | category | flops | bytes accessed | tf_op | source)
XLA Modules:
  0.0 215.7 jit_solution(12162077287449684920)
XLA Ops:
  0.6 5.0 %to_rows.1 = f32[32,4,32,128]{3,2,1,0:T(8,128)} custom-call(f32[8,2,4,128,128]{4,3,2,1,0:T(8,128)} %psi.5, bf16[256,768]{1,0:T(8,128)(2,1)} %constant.99.clone.y_table), custom_call_target="tpu_custom_call" | custom-call | flops 4000000000 | bytes 6000000 | tf_op jit(solution)/shard_map/to_rows/pallas_call | solution.py:313
  5.6 7.2 %all-to-all-start = ((f32[32,4,32,128]{3,2,1,0:T(8,128)}), f32[32,4,32,128]{3,2,1,0:T(8,128)}, u32[]{:S(2)}, u32[]{:S(2)}) async-start(f32[32,4,32,128]{3,2,1,0:T(8,128)} %to_rows.1), calls=%async_computation | async-start | bytes 4194304 | tf_op jit(solution)/shard_map/all_to_all | solution.py:326
  13.1 0.4 fusion.12
  13.5 1.0 copy.128.inverse
  14.7 0.9 add_multiply_fusion.kinetic
  15.5 10.0 %project.1 = f32[8,32,16]{2,1,0:T(8,128)} custom-call(f32[8,2,4,128,128]{4,3,2,1,0:T(8,128)} %psi.5, f32[8,1024,128]{2,1,0:T(8,128)} %bitcast.85, f32[4,128,128]{2,1,0:T(8,128)} %add_multiply_fusion.kinetic), custom_call_target="tpu_custom_call" | custom-call | flops 8000000000 | bytes 8000000 | tf_op jit(solution)/shard_map/project/pallas_call | solution.py:358
  25.6 0.8 fusion.49
  26.9 0.7 copy.119
  27.7 0.7 pad_maximum_fusion.1.forward
  28.4 0.9 convolution_bitcast_fusion._
  29.4 31.8 %all-to-all-done.recv = f32[32,4,32,128]{3,2,1,0:T(8,128)} async-done(((f32[32,4,32,128]{3,2,1,0:T(8,128)}), f32[32,4,32,128]{3,2,1,0:T(8,128)}, u32[]{:S(2)}, u32[]{:S(2)}) %all-to-all-start) | async-done | bytes 2097184 | tf_op jit(solution)/shard_map/all_to_all | solution.py:326
  61.1 5.2 %real_space.3 = (f32[32,2,32,128]{3,2,1,0:T(8,128)}, f32[2,512,128]{2,1,0:T(8,128)}) custom-call(f32[32,4,32,128]{3,2,1,0:T(8,128)} %all-to-all-done.recv, f32[512,128]{1,0:T(8,128)} %bitcast.74, bf16[256,768]{1,0:T(8,128)(2,1)} %copy.128.inverse, bf16[256,384]{1,0:T(8,128)(2,1)} %pad_maximum_fusion.1.forward, bf16[768,256]{1,0:T(8,128)(2,1)} %constant.101.clone.inv_z, ...), custom_call_target="tpu_custom_call" | custom-call | flops 4000000000 | bytes 8000000 | tf_op jit(solution)/shard_map/real_space/pallas_call | solution.py:388
  66.3 4.7 %all-to-all-start.2 = ((f32[32,2,32,128]{3,2,1,0:T(8,128)}), f32[32,2,32,128]{3,2,1,0:T(8,128)}, u32[]{:S(2)}, u32[]{:S(2)}) async-start(f32[32,2,32,128]{3,2,1,0:T(8,128)} %get-tuple-element.7), calls=%async_computation.2 | async-start | bytes 2097152 | tf_op jit(solution)/shard_map/all_to_all | solution.py:414
  71.1 0.2 fusion.8
  71.3 10.7 %real_space.2 = (f32[32,6,32,128]{3,2,1,0:T(8,128)}, f32[6,512,128]{2,1,0:T(8,128)}) custom-call(f32[32,4,32,128]{3,2,1,0:T(8,128)} %all-to-all-done.recv, f32[512,128]{1,0:T(8,128)} %bitcast.75, bf16[256,768]{1,0:T(8,128)(2,1)} %copy.128.inverse, bf16[256,384]{1,0:T(8,128)(2,1)} %pad_maximum_fusion.1.forward, bf16[768,256]{1,0:T(8,128)(2,1)} %constant.101.clone.inv_z, ...), custom_call_target="tpu_custom_call" | custom-call | flops 4000000000 | bytes 8000000 | tf_op jit(solution)/shard_map/real_space/pallas_call | solution.py:388
  82.0 5.2 %real_gram.1 = f32[2,8,8,128]{3,2,1,0:T(8,128)} custom-call(f32[2,512,128]{2,1,0:T(8,128)} %get-tuple-element.8.refs_0_, f32[6,512,128]{2,1,0:T(8,128)} %get-tuple-element.9.refs_1_, f32[512,128]{1,0:T(8,128)} %bitcast.76), custom_call_target="tpu_custom_call" | custom-call | flops 10000000 | bytes 2000000 | tf_op jit(solution)/shard_map/real_gram/pallas_call | solution.py:417
  87.2 0.9 reduce_sum.18
  88.1 8.3 %all-to-all-done.2._.recv = f32[32,2,32,128]{3,2,1,0:T(8,128)} async-done(((f32[32,2,32,128]{3,2,1,0:T(8,128)}), f32[32,2,32,128]{3,2,1,0:T(8,128)}, u32[]{:S(2)}, u32[]{:S(2)}) %all-to-all-start.2) | async-done | bytes 1048608 | tf_op jit(solution)/shard_map/all_to_all | solution.py:414
  96.4 4.6 %all-to-all-start.1 = ((f32[32,6,32,128]{3,2,1,0:T(8,128)}), f32[32,6,32,128]{3,2,1,0:T(8,128)}, u32[]{:S(2)}, u32[]{:S(2)}) async-start(f32[32,6,32,128]{3,2,1,0:T(8,128)} %get-tuple-element.6), calls=%async_computation.1 | async-start | bytes 6291456 | tf_op jit(solution)/shard_map/all_to_all | solution.py:414
  101.1 2.3 %collective-permute-start.1 = (f32[136,16]{1,0:T(8,128)S(1)}, f32[136,16]{1,0:T(8,128)S(1)}, u32[]{:S(2)}, u32[]{:S(2)}) collective-permute-start(f32[136,16]{1,0:T(8,128)S(1)} %maximum_maximum_fusion), channel_id=1, source_target_pairs={{0,16},{1,17},{2,18},{3,19},{4,20},{5,21},{6,22},{7,23},{8,24},{9,... | collective-permute-start | bytes 26120 | tf_op jit(solution)/shard_map/ppermute | solution.py:262
  103.4 1.2 collective-permute-start.2
  104.6 71.6 %collective-permute-done.1 = f32[136,16]{1,0:T(8,128)S(1)} collective-permute-done((f32[136,16]{1,0:T(8,128)S(1)}, f32[136,16]{1,0:T(8,128)S(1)}, u32[]{:S(2)}, u32[]{:S(2)}) %collective-permute-start.1) | collective-permute-done | bytes 8736 | tf_op jit(solution)/shard_map/ppermute | solution.py:262
  176.3 0.7 add_add_fusion.values
  177.0 1.5 pass_on.1
  178.5 0.9 copy.134
  179.4 1.0 collective-permute-start.3
  180.4 1.7 collective-permute-done.3
  182.1 1.0 collective-permute-start.4
  183.0 1.6 collective-permute-done.4
  184.7 3.6 %collective-permute-start.5 = (f32[136,16]{0,1:T(8,128)S(1)}, f32[136,16]{0,1:T(8,128)S(1)}, u32[]{:S(2)}, u32[]{:S(2)}) collective-permute-start(f32[136,16]{0,1:T(8,128)S(1)} %add.121), channel_id=1, source_target_pairs={{0,1},{1,0},{2,3},{3,2},{4,5},{5,4},{6,7},{7,6},{8,9},{9,8},{10,11... | collective-permute-start | bytes 26120 | tf_op jit(solution)/shard_map/ppermute | solution.py:262
  188.5 0.6 collective-permute-done.5
  189.2 0.7 cholesky.16
  190.0 0.6 compare_reduce_fusion
  190.6 0.6 fusion.20
  191.3 0.6 custom-call.10
  191.9 0.1 fusion.32
  192.1 0.1 fusion.36
  192.2 0.1 convolution_subtract_fusion
  192.3 0.1 fusion.21
  192.5 0.2 fusion.15
  192.7 0.1 fusion.24
  193.2 0.2 copy.145
  193.4 0.2 convolution_bitcast_fusion.1
  193.9 0.6 pad_maximum_fusion.6
  194.5 0.7 pad_maximum_fusion.4.coefs
  195.2 11.2 %base.1 = f32[8,2,4,128,128]{4,3,2,1,0:T(8,128)} custom-call(f32[8,2,4,128,128]{4,3,2,1,0:T(8,128)} %psi.5, f32[8,1024,128]{2,1,0:T(8,128)} %bitcast.86, f32[4,128,128]{2,1,0:T(8,128)} %add_multiply_fusion.kinetic, f32[8,16,32]{2,1,0:T(8,128)} %pad_maximum_fusion.4.coefs), custom_call_target="tpu_custom_call" | custom-call | flops 8000000000 | bytes 12000000 | tf_op jit(solution)/shard_map/base/pallas_call | solution.py:454
  206.4 3.2 %to_planes.2.base = f32[8,2,4,128,128]{4,3,2,1,0:T(8,128)} custom-call(f32[32,2,32,128]{3,2,1,0:T(8,128)} %all-to-all-done.2._.recv, f32[8,2,4,128,128]{4,3,2,1,0:T(8,128)} %base.1, bf16[256,768]{1,0:T(8,128)(2,1)} %constant.100.clone.y_table), custom_call_target="tpu_custom_call", output_to_operand_aliasing={{}: (1, {})} | custom-call | flops 8000000000 | bytes 12000000 | tf_op jit(solution)/shard_map/to_planes/pallas_call | solution.py:471
  209.6 6.1 %to_planes.3 = f32[8,2,4,128,128]{4,3,2,1,0:T(8,128)} custom-call(f32[32,6,32,128]{3,2,1,0:T(8,128)} %all-to-all-done.1.recv, f32[8,2,4,128,128]{4,3,2,1,0:T(8,128)} %to_planes.2.base, bf16[256,768]{1,0:T(8,128)(2,1)} %constant.100.clone.y_table), custom_call_target="tpu_custom_call", output_to_operand_aliasing={{}: (1, {})} | custom-call | flops 8000000000 | bytes 12000000 | tf_op jit(solution)/shard_map/to_planes/pallas_call | solution.py:471
  (62 shorter events, 2.3 us)
Async XLA Ops:
  5.6 7.2 %copy-start.4 = (s32[128]{0:T(128)S(1)}, s32[128]{0:T(128)}, u32[]{:S(2)}) copy-start(s32[128]{0:T(128)} %param.11) | copy-start | bytes 1540
  5.6 55.5 %all-to-all-start = ((f32[32,4,32,128]{3,2,1,0:T(8,128)}), f32[32,4,32,128]{3,2,1,0:T(8,128)}, u32[]{:S(2)}, u32[]{:S(2)}) async-start(f32[32,4,32,128]{3,2,1,0:T(8,128)} %to_rows.1), calls=%async_computation | async-start | bytes 4194304 | tf_op jit(solution)/shard_map/all_to_all | solution.py:326
  15.5 11.4 %copy-start = (f32[128,4,128]{2,1,0:T(4,128)S(1)}, f32[128,4,128]{2,1,0:T(4,128)}, u32[]{:S(2)}) copy-start(f32[128,4,128]{2,1,0:T(4,128)} %param.12) | copy-start | bytes 786436
  15.5 12.9 %copy-start.5 = (s32[8,8]{1,0:T(8,128)S(1)}, s32[8,8]{1,0:T(8,128)}, u32[]{:S(2)}) copy-start(s32[8,8]{1,0:T(8,128)} %param.14) | copy-start | bytes 772
  61.1 9.9 %copy-start.2 = (f32[8,32,16]{2,1,0:T(8,128)S(1)}, f32[8,32,16]{2,1,0:T(8,128)}, u32[]{:S(2)}) copy-start(f32[8,32,16]{2,1,0:T(8,128)} %project.1) | copy-start | bytes 49156
  66.3 30.1 %all-to-all-start.2 = ((f32[32,2,32,128]{3,2,1,0:T(8,128)}), f32[32,2,32,128]{3,2,1,0:T(8,128)}, u32[]{:S(2)}, u32[]{:S(2)}) async-start(f32[32,2,32,128]{3,2,1,0:T(8,128)} %get-tuple-element.7), calls=%async_computation.2 | async-start | bytes 2097152 | tf_op jit(solution)/shard_map/all_to_all | solution.py:414
  82.0 19.0 %copy-start.1 = (f32[128,16]{1,0:T(8,128)S(1)}, f32[128,16]{1,0:T(8,128)}, u32[]{:S(2)}) copy-start(f32[128,16]{1,0:T(8,128)} %convolution_bitcast_fusion._) | copy-start | bytes 24580
  87.2 101.1 %copy-start.3 = (f32[32,4]{0,1:T(4,128)S(1)}, f32[32,4]{0,1:T(4,128)}, u32[]{:S(2)}) copy-start(f32[32,4]{0,1:T(4,128)} %param.15) | copy-start | bytes 1540
  96.4 113.2 %all-to-all-start.1 = ((f32[32,6,32,128]{3,2,1,0:T(8,128)}), f32[32,6,32,128]{3,2,1,0:T(8,128)}, u32[]{:S(2)}, u32[]{:S(2)}) async-start(f32[32,6,32,128]{3,2,1,0:T(8,128)} %get-tuple-element.6), calls=%async_computation.1 | async-start | bytes 6291456 | tf_op jit(solution)/shard_map/all_to_all | solution.py:414
  101.1 75.2 %collective-permute-start.1 = (f32[136,16]{1,0:T(8,128)S(1)}, f32[136,16]{1,0:T(8,128)S(1)}, u32[]{:S(2)}, u32[]{:S(2)}) collective-permute-start(f32[136,16]{1,0:T(8,128)S(1)} %maximum_maximum_fusion), channel_id=1, source_target_pairs={{0,16},{1,17},{2,18},{3,19},{4,20},{5,21},{6,22},{7,23},{8,24},{9,... | collective-permute-start | bytes 26120 | tf_op jit(solution)/shard_map/ppermute | solution.py:262
  103.4 72.9 %collective-permute-start.2 = (f32[136,16]{1,0:T(8,128)S(1)}, f32[136,16]{1,0:T(8,128)S(1)}, u32[]{:S(2)}, u32[]{:S(2)}) collective-permute-start(f32[136,16]{1,0:T(8,128)S(1)} %maximum_maximum_fusion), channel_id=1, source_target_pairs={{0,24},{1,25},{2,26},{3,27},{4,28},{5,29},{6,30},{7,31},{8,16},{9,... | collective-permute-start | bytes 26120 | tf_op jit(solution)/shard_map/ppermute | solution.py:262
  104.6 71.7 %collective-permute-start = (f32[136,16]{1,0:T(8,128)S(1)}, f32[136,16]{1,0:T(8,128)S(1)}, u32[]{:S(2)}, u32[]{:S(2)}) collective-permute-start(f32[136,16]{1,0:T(8,128)S(1)} %maximum_maximum_fusion), channel_id=1, source_target_pairs={{0,8},{1,9},{2,10},{3,11},{4,12},{5,13},{6,14},{7,15},{8,0},{9,1},... | collective-permute-start | bytes 26120 | tf_op jit(solution)/shard_map/ppermute | solution.py:262
  179.4 2.6 %collective-permute-start.3 = (f32[136,16]{0,1:T(8,128)S(1)}, f32[136,16]{0,1:T(8,128)S(1)}, u32[]{:S(2)}, u32[]{:S(2)}) collective-permute-start(f32[136,16]{0,1:T(8,128)S(1)} %copy.134), channel_id=1, source_target_pairs={{0,4},{1,5},{2,6},{3,7},{4,0},{5,1},{6,2},{7,3},{8,12},{9,13},{10,... | collective-permute-start | bytes 26120 | tf_op jit(solution)/shard_map/ppermute | solution.py:262
  182.1 2.6 %collective-permute-start.4 = (f32[136,16]{0,1:T(8,128)S(1)}, f32[136,16]{0,1:T(8,128)S(1)}, u32[]{:S(2)}, u32[]{:S(2)}) collective-permute-start(f32[136,16]{0,1:T(8,128)S(1)} %add.120), channel_id=1, source_target_pairs={{0,2},{1,3},{2,0},{3,1},{4,6},{5,7},{6,4},{7,5},{8,10},{9,11},{10,... | collective-permute-start | bytes 26120 | tf_op jit(solution)/shard_map/ppermute | solution.py:262
  184.7 4.5 %collective-permute-start.5 = (f32[136,16]{0,1:T(8,128)S(1)}, f32[136,16]{0,1:T(8,128)S(1)}, u32[]{:S(2)}, u32[]{:S(2)}) collective-permute-start(f32[136,16]{0,1:T(8,128)S(1)} %add.121), channel_id=1, source_target_pairs={{0,1},{1,0},{2,3},{3,2},{4,5},{5,4},{6,7},{7,6},{8,9},{9,8},{10,11... | collective-permute-start | bytes 26120 | tf_op jit(solution)/shard_map/ppermute | solution.py:262

commit v10 on v9

--- a/solution.py
+++ b/solution.py
@@ -109,6 +109,29 @@
             out[:, p * each : (p + 1) * each, :] = along_y[
                 :, i * span_z : (i + 1) * span_z
             ].reshape(devices, each, span_z)
+
+
+def to_rows_split_kernel(my_layer, psi, y_table, *rest):
+    outs, staged = rest[:-1], rest[-1]
+    to_rows_kernel(psi, y_table, staged)
+    each = staged.shape[0] // len(outs)
+    for k, out in enumerate(outs):
+        out[...] = staged[pl.ds((my_layer[0] ^ k) * each, each)]
+
+
+def regroup_kernel(layers, my_member, *refs):
+    arrived, outs = refs[:layers], refs[layers + 1 : -1]
+    for k, out in enumerate(outs):
+        for layer in range(layers):
+            out[layer] = arrived[layer][my_member[0] ^ k]
+
+
+def real_space_parts_kernel(rows, planes, members, *refs):
+    arrived, rest, staged = refs[:members], refs[members:-1], refs[-1]
+    each = staged.shape[0] // members
+    for k in range(members):
+        staged[k * each : (k + 1) * each] = arrived[k][...]
+    real_space_kernel(rows, planes, staged, *rest)
 
 
 def real_space_kernel(rows, planes, recv, pot, inverse, forward, inv_z, fwd_z, _, back, field):
@@ -152,13 +175,13 @@
 
 def real_gram_kernel(bands, *refs):
     fields, (pot, out) = refs[:-2], refs[-2:]
-    lines = [(one, i) for one in fields for i in range(one.shape[0])]
+    held = fields[0].shape[0]
     pairs = [(a, b) for a in range(bands) for b in range(a, bands)]
     for weighted in range(2):
 
         def step(i, sums):
             rows = pl.ds(pl.multiple_of(i * 8, 8), 8)
-            values = [one[i, rows, :] for one, i in lines]
+            values = [fields[a // held][a % held, rows, :] for a in range(bands)]
             other = [v * pot[rows, :] for v in values] if weighted else values
             result = []
             for (a, b), total in zip(pairs, sums):
@@ -195,8 +218,9 @@
                     )
 
 
-def pass_on_kernel(values, _, out):
-    out[...] = values[...]
+def last_sum_kernel(*refs):
+    first, second, third, fourth, _, out = refs
+    out[...] = (first[...] + second[...]) + (third[...] + fourth[...])
 
 
 def block_rows_of(psi, beta, slots):
@@ -265,21 +289,19 @@
 def sum_over(values, devices, after):
     if devices & (devices - 1) or devices < 4:
         return lax.psum(values, "ga")
-    step = devices // 4
+    step = 1
+    while step < devices // 4:
+        values = values + partner(values, devices, step)
+        step *= 2
     others = [partner(values, devices, k * step) for k in (1, 2, 3)]
-    values = (values + others[0]) + (others[1] + others[2])
     held = pl.BlockSpec(memory_space=pltpu.VMEM)
-    values = pl.pallas_call(
-        pass_on_kernel,
+    return pl.pallas_call(
+        last_sum_kernel,
         out_shape=jax.ShapeDtypeStruct(values.shape, f32),
-        in_specs=[held, pl.BlockSpec(memory_space=pl.ANY)],
+        in_specs=[held] * 4 + [pl.BlockSpec(memory_space=pl.ANY)],
         out_specs=held,
-        name="pass_on",
-    )(values, after)
-    while step > 1:
-        step //= 2
-        values = values + partner(values, devices, step)
-    return values
+        name="last_sum",
+    )(values, *others, after)
 
 
 def on_device(devices, orbitals, plane_order, potential, projectors, slot_owner, strengths):
@@ -310,32 +332,82 @@
     inv_z = right_const(right_table(span_z, 1.0))
     fwd_z = right_const(right_table(span_z, -1.0))
 
-    sent = pl.pallas_call(
-        to_rows_kernel,
-        out_shape=jax.ShapeDtypeStruct((devices, pairs, block_rows, span_z), f32),
-        grid=(pairs,),
-        in_specs=[
-            pl.BlockSpec((2, 2, planes, span_y, span_z), lambda j: (j, 0, 0, 0, 0)),
-            whole(inv_y.shape),
-        ],
-        out_specs=pl.BlockSpec((devices, None, block_rows, span_z), lambda j: (0, j, 0, 0)),
-        compiler_params=params,
-        cost_estimate=cost(4 * 10**9, 6 * 10**6),
-        name="to_rows",
-    )(orbitals, inv_y)
-    arrived = lax.all_to_all(sent, "ga", split_axis=0, concat_axis=0, tiled=True)
-
-    stored = plane_order.reshape(devices, planes).T.reshape(-1)
-    phases = (stored[:, None] * grid_x[None, :]) % span_x
-    angles = phases.astype(f32) * (2.0 * math.pi / span_x)
-    factor = 1.0 / math.sqrt(span_x)
-    cosine, sine = jnp.cos(angles) * factor, jnp.sin(angles) * factor
-    fwd_x = jnp.concatenate([cosine, -sine], axis=0)
-    inv_x = jnp.concatenate([fwd_x, jnp.concatenate([sine, cosine], axis=0)], axis=1).T
-    high, low = split_outside(fwd_x)
-    fwd_x = jnp.concatenate([high, high, low], axis=1)
-    high, low = split_outside(inv_x)
-    inv_x = jnp.concatenate([high, high, low], axis=1)
+    parts = 2 if pairs % 2 == 0 else 1
+    share = pairs // parts
+    mine = lax.axis_index("ga").astype(jnp.int32)
+    layers = 4 if parts == 2 and devices >= 8 and devices & (devices - 1) == 0 else 1
+    members = devices // layers
+    my_layer, my_member = (mine // members).reshape(1), (mine % members).reshape(1)
+    scalar = pl.BlockSpec(memory_space=pltpu.SMEM)
+
+    def to_rows(c, split):
+        spec = pl.BlockSpec((devices, None, block_rows, span_z), lambda j: (0, j, 0, 0))
+        shape = jax.ShapeDtypeStruct((devices, share, block_rows, span_z), f32)
+        if split:
+            spec = pl.BlockSpec((members, None, block_rows, span_z), lambda j: (0, j, 0, 0))
+            shape = jax.ShapeDtypeStruct((members, share, block_rows, span_z), f32)
+        return pl.pallas_call(
+            to_rows_split_kernel if split else to_rows_kernel,
+            out_shape=[shape] * layers if split else shape,
+            grid=(share,),
+            in_specs=([scalar] if split else [])
+            + [
+                pl.BlockSpec((2, 2, planes, span_y, span_z), lambda j: (c * share + j, 0, 0, 0, 0)),
+                whole(inv_y.shape),
+            ],
+            out_specs=[spec] * layers if split else spec,
+            scratch_shapes=[pltpu.VMEM((devices, block_rows, span_z), f32)] if split else [],
+            compiler_params=params,
+            cost_estimate=cost(4 * 10**9, 3 * 10**6),
+            name="to_rows",
+        )(*([my_layer] if split else []), orbitals, inv_y)
+
+    sent = [to_rows(c, c == 0 and layers > 1) for c in range(parts)]
+    arrived = []
+    if layers > 1:
+        crossed = [sent[0][0]] + [
+            partner(sent[0][k], devices, k * members) for k in range(1, layers)
+        ]
+        *regrouped, sent[1] = pl.pallas_call(
+            functools.partial(regroup_kernel, layers),
+            out_shape=[jax.ShapeDtypeStruct((layers, share, block_rows, span_z), f32)] * members
+            + [jax.ShapeDtypeStruct(sent[1].shape, f32)],
+            in_specs=[scalar]
+            + [pl.BlockSpec(memory_space=pltpu.VMEM)] * layers
+            + [pl.BlockSpec(memory_space=pl.ANY)],
+            out_specs=[pl.BlockSpec(memory_space=pltpu.VMEM)] * members
+            + [pl.BlockSpec(memory_space=pl.ANY)],
+            input_output_aliases={1 + layers: members},
+            compiler_params=params,
+            cost_estimate=cost(0, 2 * 10**6),
+            name="regroup",
+        )(my_member, *crossed, sent[1])
+        arrived.append(
+            [regrouped[0]] + [partner(regrouped[k], devices, k) for k in range(1, members)]
+        )
+        sent = sent[1:]
+    for one in sent:
+        arrived.append([lax.all_to_all(one, "ga", split_axis=0, concat_axis=0, tiled=True)])
+
+    def tables_x(owned):
+        phases = (owned.T.reshape(-1)[:, None] * grid_x[None, :]) % span_x
+        angles = phases.astype(f32) * (2.0 * math.pi / span_x)
+        factor = 1.0 / math.sqrt(span_x)
+        cosine, sine = jnp.cos(angles) * factor, jnp.sin(angles) * factor
+        forward = jnp.concatenate([cosine, -sine], axis=0)
+        inverse = jnp.concatenate([forward, jnp.concatenate([sine, cosine], axis=0)], axis=1).T
+        tables = []
+        for table in (forward, inverse):
+            high, low = split_outside(table)
+            tables.append(jnp.concatenate([high, high, low], axis=1))
+        return tables
+
+    owned = plane_order.reshape(devices, planes)
+    fwd_x, inv_x = tables_x(owned)
+    steps = np.arange(layers)[None, :] * members + np.arange(members)[:, None]
+    _, inv_x_steps = tables_x(
+        jnp.take(owned, mine ^ jnp.asarray(steps.reshape(-1), jnp.int32), axis=0)
+    )
     pot = potential.transpose(1, 0, 2).reshape(rows * span_x, span_z)
 
     local_order = lax.dynamic_slice_in_dim(plane_order, lax.axis_index("ga") * planes, planes)
@@ -374,43 +446,48 @@
         ],
         axis=-1,
     )
-    owned = (
+    chosen = (
         slot_owner[:, :, None] == jnp.arange(owners, dtype=jnp.int32)[None, None, :]
     ).astype(f32)
-    proj = tdot("gsj,gsc->jc", owned, proj)
+    proj = tdot("gsj,gsc->jc", chosen, proj)
     kin = jnp.sum(products[:, 2 * slots :], axis=0).reshape(bands, 2, bands, 2)
     kin = kin[:, 0, :, 0] + kin[:, 1, :, 1]
 
-    parts = [(0, 1), (1, pairs)] if pairs > 1 else [(0, pairs)]
     returned, fields = [], []
-    for first, end in parts:
-        share = end - first
+    before = proj
+    for operands in arrived:
+        steps = len(operands) > 1
+        held = devices // len(operands)
+        kernel = functools.partial(real_space_kernel, rows, planes)
+        if steps:
+            kernel = functools.partial(real_space_parts_kernel, rows, planes, members)
         back, field = pl.pallas_call(
-            functools.partial(real_space_kernel, rows, planes),
+            kernel,
             out_shape=(
                 jax.ShapeDtypeStruct((devices, 2 * share, block_rows, span_z), f32),
                 jax.ShapeDtypeStruct((2 * share, rows * span_x, span_z), f32),
             ),
             grid=(share,),
-            in_specs=[
-                pl.BlockSpec(
-                    (devices, None, block_rows, span_z), lambda j, first=first: (0, first + j, 0, 0)
-                ),
+            in_specs=[pl.BlockSpec((held, None, block_rows, span_z), lambda j: (0, j, 0, 0))]
+            * len(operands)
+            + [
                 whole(pot.shape),
                 whole(inv_x.shape),
                 whole(fwd_x.shape),
                 whole(inv_z.shape),
                 whole(fwd_z.shape),
-                whole(proj.shape),
+                pl.BlockSpec(memory_space=pl.ANY),
             ],
             out_specs=(
                 pl.BlockSpec((devices, 2, block_rows, span_z), lambda j: (0, j, 0, 0)),
                 pl.BlockSpec((2, rows * span_x, span_z), lambda j: (j, 0, 0)),
             ),
+            scratch_shapes=[pltpu.VMEM((devices, block_rows, span_z), f32)] if steps else [],
             compiler_params=params,
             cost_estimate=cost(4 * 10**9, 8 * 10**6),
             name="real_space",
-        )(arrived, pot, inv_x, fwd_x, inv_z, fwd_z, proj)
+        )(*operands, pot, inv_x_steps if steps else inv_x, fwd_x, inv_z, fwd_z, before)
+        before = back
         returned.append(lax.all_to_all(back, "ga", split_axis=0, concat_axis=0, tiled=True))
         fields.append(field)
 
@@ -432,7 +509,7 @@
     h_imag = tdot("ja,jb->ab", p_real, w_imag) - tdot("ja,jb->ab", p_imag, w_real)
     m_real, m_imag = subspace_solve(s_real, h_real, h_imag)
 
-    coefs = tdot("gsj,jc->gcs", owned, weighted)
+    coefs = tdot("gsj,jc->gcs", chosen, weighted)
     c_real, c_imag = coefs[:, :bands], coefs[:, bands:]
     from_beta = jnp.stack(
         [
@@ -464,14 +541,14 @@
     )(orbitals, beta, kinetic, coefs)
 
     residual = base
-    for (first, end), one_return in zip(parts, returned):
+    for c in range(parts):
         two_bands = pl.BlockSpec(
-            (2, 2, planes, span_y, span_z), lambda j, first=first: (first + j, 0, 0, 0, 0)
+            (2, 2, planes, span_y, span_z), lambda j, c=c: (share * c + j, 0, 0, 0, 0)
         )
         residual = pl.pallas_call(
             to_planes_kernel,
             out_shape=jax.ShapeDtypeStruct(orbitals.shape, f32),
-            grid=(end - first,),
+            grid=(share,),
             in_specs=[
                 pl.BlockSpec((devices, 2, block_rows, span_z), lambda j: (0, j, 0, 0)),
                 two_bands,
@@ -482,7 +559,7 @@
             compiler_params=params,
             cost_estimate=cost(8 * 10**9, 12 * 10**6),
             name="to_planes",
-        )(one_return, residual, fwd_y)
+        )(returned[c], residual, fwd_y)
     return (residual, jnp.stack([m_real, m_imag]))
 
 

time: 217 us -> 189 us (0.87)
  waiting for transfers between devices: 116 us -> 55.2 us
  starting transfers between devices: 25.5 us -> 44.6 us
  local copies, waits for them, and re-layouts: 5.14 us -> 9.21 us
  matrix products: 2.03 us -> 6.01 us
    ppermute x6 -> x16, waiting for transfers between devices: 75.6 us -> 18.8 us  [partner(): return lax.ppermute(values, 'ga', [(d, d ^ k) for d in range(devices)])]
    all_to_all x1, waiting for transfers between devices: 31.8 us -> 0.01 us  [on_device(): lax.all_to_all(one, 'ga', split_axis=0, concat_axis=0, tiled=True)]
    all_to_all x2, waiting for transfers between devices: 8.27 us -> 36.4 us  [on_device(): lax.all_to_all(back, 'ga', split_axis=0, concat_axis=0, tiled=True)]
    ppermute x6 -> x16, starting transfers between devices: 9.08 us -> 25 us  [partner(): return lax.ppermute(values, 'ga', [(d, d ^ k) for d in range(devices)])]
    dot_general x6, matrix products: 1.69 us -> 5.63 us  [tdot(): jnp.einsum(pattern, left, right, precision=highest, preferred_element_typ...]
    all_to_all x1, starting transfers between devices: 7.15 us -> 11 us  [on_device(): lax.all_to_all(one, 'ga', split_axis=0, concat_axis=0, tiled=True)]
    pallas_call x4 -> x6, Pallas kernels: 22.4 us -> 26.2 us  [the longest x2 16.3 us: on_device(): pl.pallas_call(kernel, out_shape=(jax.ShapeDtypeStruct((devices, 2 * shar...]
    unnamed x17 -> x60, local copies, waits for them, and re-layouts: 0.43 us -> 3.18 us
  transfers between devices with their start and end apart: 9 -> 19, of which waited for: 6 -> 9; matrix products, arithmetic and copies ran while one was open for 7% -> 12% of each run, Pallas kernels for 19% -> 27%
where the time goes in v10:
time: 189 us; the launch traced here: 186 us
  Pallas kernels  60.3 us (32%)
  waiting for transfers between devices  55.2 us (29%)
  starting transfers between devices  44.6 us (24%)
  other arithmetic  9.97 us (5%)
  local copies, waits for them, and re-layouts  9.21 us (5%)
  matrix products  6.01 us (3%)
    all_to_all x2, waiting for transfers between devices, on_device(): lax.all_to_all(back, 'ga', split_axis=0, concat_axis=0, tiled=True)  36.4 us
    ppermute x16, starting transfers between devices, partner(): return lax.ppermute(values, 'ga', [(d, d ^ k) for d in range(devices)])  25 us
    ppermute x16, waiting for transfers between devices, partner(): return lax.ppermute(values, 'ga', [(d, d ^ k) for d in range(devices)])  18.8 us
    pallas_call x2, Pallas kernels, on_device(): pl.pallas_call(kernel, out_shape=(jax.ShapeDtypeStruct((devices, 2 * shar...  16.3 us
    pallas_call x1, Pallas kernels, on_device(): pl.pallas_call(functools.partial(base_kernel, slots), out_shape=jax.Shape...  11.2 us
    all_to_all x1, starting transfers between devices, on_device(): lax.all_to_all(one, 'ga', split_axis=0, concat_axis=0, tiled=True)  11 us
    pallas_call x1, Pallas kernels, on_device(): pl.pallas_call(functools.partial(project_kernel, slots), out_shape=jax.Sh...  10 us
    all_to_all x2, starting transfers between devices, on_device(): lax.all_to_all(back, 'ga', split_axis=0, concat_axis=0, tiled=True)  8.56 us
  transfers between devices with their start and end apart: 19, of which 9 were waited for; matrix products, arithmetic and copies ran while one was open for 12% of the time, Pallas kernels for 27%

profile of v10, /device:TPU:1, one launch (start us, length us, event | category | flops | bytes accessed | tf_op | source)
XLA Modules:
  0.0 186.4 jit_solution(13480063479566912633)
XLA Ops:
  0.7 3.0 %to_rows.2 = (f32[8,2,32,128]{3,2,1,0:T(8,128)}, f32[8,2,32,128]{3,2,1,0:T(8,128)}, f32[8,2,32,128]{3,2,1,0:T(8,128)}, f32[8,2,32,128]{3,2,1,0:T(8,128)}) custom-call(s32[1]{0:T(128)} %bitcast.1.my_layer, f32[8,2,4,128,128]{4,3,2,1,0:T(8,128)} %psi.7, bf16[256,768]{1,0:T(8,128)(2,1)} %constant.146.clone.y_table), custom_call_target="tpu_custom_call" | custom-call | flops 4000000000 | bytes 3000000 | tf_op jit(solution)/shard_map/to_rows/pallas_call | solution.py:349
  3.7 2.1 %collective-permute-start = (f32[8,2,32,128]{3,2,1,0:T(8,128)}, f32[8,2,32,128]{3,2,1,0:T(8,128)S(1)}, u32[]{:S(2)}, u32[]{:S(2)}) collective-permute-start(f32[8,2,32,128]{3,2,1,0:T(8,128)} %get-tuple-element.20), channel_id=1, source_target_pairs={{0,8},{1,9},{2,10},{3,11},{4,12},{5,13},{6,14},{7,15},{8,0},{9,1},... | collective-permute-start | bytes 786440 | tf_op jit(solution)/shard_map/ppermute | solution.py:286
  5.8 2.3 %collective-permute-start.1 = (f32[8,2,32,128]{3,2,1,0:T(8,128)}, f32[8,2,32,128]{3,2,1,0:T(8,128)S(1)}, u32[]{:S(2)}, u32[]{:S(2)}) collective-permute-start(f32[8,2,32,128]{3,2,1,0:T(8,128)} %get-tuple-element.21), channel_id=1, source_target_pairs={{0,16},{1,17},{2,18},{3,19},{4,20},{5,21},{6,22},{7,23},{8,24},{9,... | collective-permute-start | bytes 786440 | tf_op jit(solution)/shard_map/ppermute | solution.py:286
  9.4 0.9 add_multiply_fusion.kinetic
  10.3 10.0 %project.1 = f32[8,32,16]{2,1,0:T(8,128)} custom-call(f32[8,2,4,128,128]{4,3,2,1,0:T(8,128)} %psi.7, f32[8,1024,128]{2,1,0:T(8,128)} %bitcast.94, f32[4,128,128]{2,1,0:T(8,128)} %add_multiply_fusion.kinetic), custom_call_target="tpu_custom_call" | custom-call | flops 8000000000 | bytes 8000000 | tf_op jit(solution)/shard_map/project/pallas_call | solution.py:430
  20.3 0.8 fusion.55
  21.2 3.0 %to_rows.3.refs_4_ = f32[32,2,32,128]{3,2,1,0:T(8,128)} custom-call(f32[8,2,4,128,128]{4,3,2,1,0:T(8,128)} %psi.7, bf16[256,768]{1,0:T(8,128)(2,1)} %constant.146.clone.y_table), custom_call_target="tpu_custom_call" | custom-call | flops 4000000000 | bytes 3000000 | tf_op jit(solution)/shard_map/to_rows/pallas_call | solution.py:349
  24.2 1.0 collective-permute-done.2.refs_3_
  25.9 2.2 %regroup.1 = (f32[4,2,32,128]{3,2,1,0:T(8,128)}, f32[4,2,32,128]{3,2,1,0:T(8,128)}, f32[4,2,32,128]{3,2,1,0:T(8,128)}, f32[4,2,32,128]{3,2,1,0:T(8,128)}, f32[4,...) custom-call(s32[1]{0:T(128)} %bitcast.my_member, ...), custom_call_target="tpu_custom_call", output_to_operand_aliasing={{8}: (5, {})} | custom-call | bytes 2000000 | tf_op jit(solution)/shard_map/regroup/pallas_call | solution.py:371
  28.2 11.0 %all-to-all-start = ((f32[32,2,32,128]{3,2,1,0:T(8,128)}), f32[32,2,32,128]{3,2,1,0:T(8,128)}, u32[]{:S(2)}, u32[]{:S(2)}) async-start(f32[32,2,32,128]{3,2,1,0:T(8,128)} %get-tuple-element.23), calls=%async_computation | async-start | bytes 2097152 | tf_op jit(solution)/shard_map/all_to_all | solution.py:390
  40.8 1.4 collective-permute-start.4
  42.8 1.4 collective-permute-start.6
  44.5 2.3 %collective-permute-start.8 = (f32[4,2,32,128]{3,2,1,0:T(8,128)S(1)}, f32[4,2,32,128]{3,2,1,0:T(8,128)S(1)}, u32[]{:S(2)}, u32[]{:S(2)}) collective-permute-start(f32[4,2,32,128]{3,2,1,0:T(8,128)S(1)} %copy-done.14), channel_id=1, source_target_pairs={{0,6},{1,7},{2,4},{3,5},{4,2},{5,3},{6,0},{7,1},{8,14},{9,15},{10,... | collective-permute-start | bytes 393224 | tf_op jit(solution)/shard_map/ppermute | solution.py:286
  46.8 5.1 %collective-permute-done.4.refs_2_ = f32[4,2,32,128]{3,2,1,0:T(8,128)S(1)} collective-permute-done((f32[4,2,32,128]{3,2,1,0:T(8,128)}, f32[4,2,32,128]{3,2,1,0:T(8,128)S(1)}, u32[]{:S(2)}, u32[]{:S(2)}) %collective-permute-start.4) | collective-permute-done | bytes 131104 | tf_op jit(solution)/shard_map/ppermute | solution.py:286
  51.9 3.0 %collective-permute-start.9 = (f32[4,2,32,128]{3,2,1,0:T(8,128)S(1)}, f32[4,2,32,128]{3,2,1,0:T(8,128)S(1)}, u32[]{:S(2)}, u32[]{:S(2)}) collective-permute-start(f32[4,2,32,128]{3,2,1,0:T(8,128)S(1)} %copy-done.13), channel_id=1, source_target_pairs={{0,7},{1,6},{2,5},{3,4},{4,3},{5,2},{6,1},{7,0},{8,15},{9,14},{10,... | collective-permute-start | bytes 393224 | tf_op jit(solution)/shard_map/ppermute | solution.py:286
  54.9 0.7 pad_maximum_fusion.2.refs_10_.forward
  55.6 0.9 copy.121.refs_9_
  56.5 0.7 copy.111
  57.3 0.9 convolution_bitcast_fusion.refs_13_
  58.3 2.0 %collective-permute-done.8.refs_6_ = f32[4,2,32,128]{3,2,1,0:T(8,128)S(1)} collective-permute-done((f32[4,2,32,128]{3,2,1,0:T(8,128)S(1)}, f32[4,2,32,128]{3,2,1,0:T(8,128)S(1)}, u32[]{:S(2)}, u32[]{:S(2)}) %collective-permute-start.8) | collective-permute-done | bytes 131104 | tf_op jit(solution)/shard_map/ppermute | solution.py:286
  60.3 5.0 %collective-permute-done.9.refs_7_ = f32[4,2,32,128]{3,2,1,0:T(8,128)S(1)} collective-permute-done((f32[4,2,32,128]{3,2,1,0:T(8,128)S(1)}, f32[4,2,32,128]{3,2,1,0:T(8,128)S(1)}, u32[]{:S(2)}, u32[]{:S(2)}) %collective-permute-start.9) | collective-permute-done | bytes 131104 | tf_op jit(solution)/shard_map/ppermute | solution.py:286
  66.0 8.3 %real_space.2 = (f32[32,4,32,128]{3,2,1,0:T(8,128)}, f32[4,512,128]{2,1,0:T(8,128)}) custom-call(f32[4,2,32,128]{3,2,1,0:T(8,128)} %get-tuple-element.24.refs_0_, f32[4,2,32,128]{3,2,1,0:T(8,128)} %copy-done.18, f32[4,2,32,128]{3,2,1,0:T(8,128)} %copy-done.19, f32[4,2,32,128]{3,2,1,0:T(8,128)} %copy-done.20, f32[4,2,32,128]{3,2,1,0:T(8,128)} %copy-done.21, ...), custom_call_target="tpu_custom_call" | custom-call | flops 4000000000 | bytes 8000000 | tf_op jit(solution)/shard_map/real_space/pallas_call | solution.py:464
  74.3 3.8 %all-to-all-start.2 = ((f32[32,4,32,128]{3,2,1,0:T(8,128)}), f32[32,4,32,128]{3,2,1,0:T(8,128)}, u32[]{:S(2)}, u32[]{:S(2)}) async-start(f32[32,4,32,128]{3,2,1,0:T(8,128)} %get-tuple-element.32._), calls=%async_computation.2 | async-start | bytes 4194304 | tf_op jit(solution)/shard_map/all_to_all | solution.py:491
  78.2 1.0 copy.123.inverse
  79.4 8.0 %real_space.3 = (f32[32,4,32,128]{3,2,1,0:T(8,128)}, f32[4,512,128]{2,1,0:T(8,128)}) custom-call(f32[32,2,32,128]{3,2,1,0:T(8,128)} %all-to-all-done.recv, f32[512,128]{1,0:T(8,128)} %bitcast.85, bf16[256,768]{1,0:T(8,128)(2,1)} %copy.123.inverse, bf16[256,384]{1,0:T(8,128)(2,1)} %pad_maximum_fusion.2.refs_10_.forward, ...), custom_call_target="tpu_custom_call" | custom-call | flops 4000000000 | bytes 8000000 | tf_op jit(solution)/shard_map/real_space/pallas_call | solution.py:464
  87.4 5.2 %real_gram.1 = f32[2,8,8,128]{3,2,1,0:T(8,128)} custom-call(f32[4,512,128]{2,1,0:T(8,128)} %get-tuple-element.34.refs_0_, f32[4,512,128]{2,1,0:T(8,128)} %get-tuple-element.35.refs_1_, f32[512,128]{1,0:T(8,128)} %bitcast.86), custom_call_target="tpu_custom_call" | custom-call | flops 10000000 | bytes 2000000 | tf_op jit(solution)/shard_map/real_gram/pallas_call | solution.py:494
  92.6 0.9 reduce_sum.18
  94.0 0.9 collective-permute-done.10
  95.0 1.4 collective-permute-start.11
  96.4 2.4 %collective-permute-done.11 = f32[136,16]{1,0:T(8,128)S(1)} collective-permute-done((f32[136,16]{1,0:T(8,128)S(1)}, f32[136,16]{1,0:T(8,128)S(1)}, u32[]{:S(2)}, u32[]{:S(2)}) %collective-permute-start.11) | collective-permute-done | bytes 8736 | tf_op jit(solution)/shard_map/ppermute | solution.py:286
  98.8 5.1 %collective-permute-start.12 = (f32[136,16]{1,0:T(8,128)S(1)}, f32[136,16]{1,0:T(8,128)S(1)}, u32[]{:S(2)}, u32[]{:S(2)}) collective-permute-start(f32[136,16]{1,0:T(8,128)S(1)} %add.130), channel_id=1, source_target_pairs={{0,4},{1,5},{2,6},{3,7},{4,0},{5,1},{6,2},{7,3},{8,12},{9,13},{10,... | collective-permute-start | bytes 26120 | tf_op jit(solution)/shard_map/ppermute | solution.py:286
  103.9 2.3 %collective-permute-done.12 = f32[136,16]{1,0:T(8,128)S(1)} collective-permute-done((f32[136,16]{1,0:T(8,128)S(1)}, f32[136,16]{1,0:T(8,128)S(1)}, u32[]{:S(2)}, u32[]{:S(2)}) %collective-permute-start.12) | collective-permute-done | bytes 8736 | tf_op jit(solution)/shard_map/ppermute | solution.py:286
  106.2 1.1 collective-permute-start.15
  107.3 3.4 %collective-permute-start.14 = (f32[136,16]{1,0:T(8,128)S(1)}, f32[136,16]{1,0:T(8,128)S(1)}, u32[]{:S(2)}, u32[]{:S(2)}) collective-permute-start(f32[136,16]{1,0:T(8,128)S(1)} %add.131.refs_0_), channel_id=1, source_target_pairs={{0,16},{1,17},{2,18},{3,19},{4,20},{5,21},{6,22},{7,23},{8,24},{9,... | collective-permute-start | bytes 26120 | tf_op jit(solution)/shard_map/ppermute | solution.py:286
  110.9 18.5 %all-to-all-done.2.refs_4_.recv = f32[32,4,32,128]{3,2,1,0:T(8,128)} async-done(((f32[32,4,32,128]{3,2,1,0:T(8,128)}), f32[32,4,32,128]{3,2,1,0:T(8,128)}, u32[]{:S(2)}, u32[]{:S(2)}) %all-to-all-start.2) | async-done | bytes 2097184 | tf_op jit(solution)/shard_map/all_to_all | solution.py:491
  129.4 4.8 %all-to-all-start.1 = ((f32[32,4,32,128]{3,2,1,0:T(8,128)}), f32[32,4,32,128]{3,2,1,0:T(8,128)}, u32[]{:S(2)}, u32[]{:S(2)}) async-start(f32[32,4,32,128]{3,2,1,0:T(8,128)} %get-tuple-element.33), calls=%async_computation.1 | async-start | bytes 4194304 | tf_op jit(solution)/shard_map/all_to_all | solution.py:491
  135.5 1.6 last_sum.1
  137.8 0.9 slice_multiply_fusion
  138.7 1.1 fusion.17
  139.8 1.1 fusion.23
  141.0 0.9 fusion.45
  144.5 1.1 fusion.19
  145.6 1.1 convolution_subtract_fusion
  148.9 0.7 pad_maximum_fusion.5.coefs
  149.6 11.2 %base.1 = f32[8,2,4,128,128]{4,3,2,1,0:T(8,128)} custom-call(f32[8,2,4,128,128]{4,3,2,1,0:T(8,128)} %psi.7, f32[8,1024,128]{2,1,0:T(8,128)} %bitcast.95, f32[4,128,128]{2,1,0:T(8,128)} %add_multiply_fusion.kinetic, f32[8,16,32]{2,1,0:T(8,128)} %pad_maximum_fusion.5.coefs), custom_call_target="tpu_custom_call" | custom-call | flops 8000000000 | bytes 12000000 | tf_op jit(solution)/shard_map/base/pallas_call | solution.py:531
  160.8 3.9 %to_planes.2.base = f32[8,2,4,128,128]{4,3,2,1,0:T(8,128)} custom-call(f32[32,4,32,128]{3,2,1,0:T(8,128)} %all-to-all-done.2.refs_4_.recv, f32[8,2,4,128,128]{4,3,2,1,0:T(8,128)} %base.1, bf16[256,768]{1,0:T(8,128)(2,1)} %constant.147.clone.y_table), custom_call_target="tpu_custom_call", output_to_operand_aliasing={{}: (1, {})} | custom-call | flops 8000000000 | bytes 12000000 | tf_op jit(solution)/shard_map/to_planes/pallas_call | solution.py:548
  164.6 17.9 %all-to-all-done.1.recv = f32[32,4,32,128]{3,2,1,0:T(8,128)} async-done(((f32[32,4,32,128]{3,2,1,0:T(8,128)}), f32[32,4,32,128]{3,2,1,0:T(8,128)}, u32[]{:S(2)}, u32[]{:S(2)}) %all-to-all-start.1) | async-done | bytes 2097184 | tf_op jit(solution)/shard_map/all_to_all | solution.py:491
  182.6 3.9 %to_planes.3 = f32[8,2,4,128,128]{4,3,2,1,0:T(8,128)} custom-call(f32[32,4,32,128]{3,2,1,0:T(8,128)} %all-to-all-done.1.recv, f32[8,2,4,128,128]{4,3,2,1,0:T(8,128)} %to_planes.2.base, bf16[256,768]{1,0:T(8,128)(2,1)} %constant.147.clone.y_table), custom_call_target="tpu_custom_call", output_to_operand_aliasing={{}: (1, {})} | custom-call | flops 8000000000 | bytes 12000000 | tf_op jit(solution)/shard_map/to_planes/pallas_call | solution.py:548
  (134 shorter events, 13.0 us)
Async XLA Ops:
  0.6 7.5 %copy-start.11 = (s32[128]{0:T(128)S(1)}, s32[128]{0:T(128)}, u32[]{:S(2)}) copy-start(s32[128]{0:T(128)} %param.12) | copy-start | bytes 1540
  0.7 7.7 %copy-start.12 = (s32[32]{0:T(128)S(1)}, s32[32]{0:T(128)}, u32[]{:S(2)}) copy-start(s32[32]{0:T(128)} %constant.150.clone) | copy-start | bytes 388
  3.7 20.4 %collective-permute-start = (f32[8,2,32,128]{3,2,1,0:T(8,128)}, f32[8,2,32,128]{3,2,1,0:T(8,128)S(1)}, u32[]{:S(2)}, u32[]{:S(2)}) collective-permute-start(f32[8,2,32,128]{3,2,1,0:T(8,128)} %get-tuple-element.20), channel_id=1, source_target_pairs={{0,8},{1,9},{2,10},{3,11},{4,12},{5,13},{6,14},{7,15},{8,0},{9,1},... | collective-permute-start | bytes 786440 | tf_op jit(solution)/shard_map/ppermute | solution.py:286
  5.8 18.3 %collective-permute-start.1 = (f32[8,2,32,128]{3,2,1,0:T(8,128)}, f32[8,2,32,128]{3,2,1,0:T(8,128)S(1)}, u32[]{:S(2)}, u32[]{:S(2)}) collective-permute-start(f32[8,2,32,128]{3,2,1,0:T(8,128)} %get-tuple-element.21), channel_id=1, source_target_pairs={{0,16},{1,17},{2,18},{3,19},{4,20},{5,21},{6,22},{7,23},{8,24},{9,... | collective-permute-start | bytes 786440 | tf_op jit(solution)/shard_map/ppermute | solution.py:286
  8.1 17.1 %collective-permute-start.2 = (f32[8,2,32,128]{3,2,1,0:T(8,128)}, f32[8,2,32,128]{3,2,1,0:T(8,128)S(1)}, u32[]{:S(2)}, u32[]{:S(2)}) collective-permute-start(f32[8,2,32,128]{3,2,1,0:T(8,128)} %get-tuple-element.22), channel_id=1, source_target_pairs={{0,24},{1,25},{2,26},{3,27},{4,28},{5,29},{6,30},{7,31},{8,16},{9,... | collective-permute-start | bytes 786440 | tf_op jit(solution)/shard_map/ppermute | solution.py:286
  24.2 1.1 copy-start.1
  24.2 1.1 copy-start.2
  25.2 0.7 copy-start.3
  28.2 14.1 %copy-start.17 = (f32[4,2,32,128]{3,2,1,0:T(8,128)S(1)}, f32[4,2,32,128]{3,2,1,0:T(8,128)}, u32[]{:S(2)}) copy-start(f32[4,2,32,128]{3,2,1,0:T(8,128)} %get-tuple-element.27) | copy-start | bytes 393220
  28.2 14.6 %copy-start.16 = (f32[4,2,32,128]{3,2,1,0:T(8,128)S(1)}, f32[4,2,32,128]{3,2,1,0:T(8,128)}, u32[]{:S(2)}) copy-start(f32[4,2,32,128]{3,2,1,0:T(8,128)} %get-tuple-element.28) | copy-start | bytes 393220
  28.2 16.0 %copy-start.15 = (f32[4,2,32,128]{3,2,1,0:T(8,128)S(1)}, f32[4,2,32,128]{3,2,1,0:T(8,128)}, u32[]{:S(2)}) copy-start(f32[4,2,32,128]{3,2,1,0:T(8,128)} %get-tuple-element.29) | copy-start | bytes 393220
  28.2 16.4 %copy-start.14 = (f32[4,2,32,128]{3,2,1,0:T(8,128)S(1)}, f32[4,2,32,128]{3,2,1,0:T(8,128)}, u32[]{:S(2)}) copy-start(f32[4,2,32,128]{3,2,1,0:T(8,128)} %get-tuple-element.30) | copy-start | bytes 393220
  28.2 23.7 %copy-start.13 = (f32[4,2,32,128]{3,2,1,0:T(8,128)S(1)}, f32[4,2,32,128]{3,2,1,0:T(8,128)}, u32[]{:S(2)}) copy-start(f32[4,2,32,128]{3,2,1,0:T(8,128)} %get-tuple-element.31) | copy-start | bytes 393220
  28.2 28.4 %copy-start.4 = (f32[128,4,128]{2,1,0:T(4,128)S(1)}, f32[128,4,128]{2,1,0:T(4,128)}, u32[]{:S(2)}) copy-start(f32[128,4,128]{2,1,0:T(4,128)} %param.13) | copy-start | bytes 786436
  28.2 29.1 %copy-start.25 = (s32[8,8]{1,0:T(8,128)S(1)}, s32[8,8]{1,0:T(8,128)}, u32[]{:S(2)}) copy-start(s32[8,8]{1,0:T(8,128)} %param.15) | copy-start | bytes 772
  28.2 46.1 %all-to-all-start = ((f32[32,2,32,128]{3,2,1,0:T(8,128)}), f32[32,2,32,128]{3,2,1,0:T(8,128)}, u32[]{:S(2)}, u32[]{:S(2)}) async-start(f32[32,2,32,128]{3,2,1,0:T(8,128)} %get-tuple-element.23), calls=%async_computation | async-start | bytes 2097152 | tf_op jit(solution)/shard_map/all_to_all | solution.py:390
  40.4 4.1 %collective-permute-start.3 = (f32[4,2,32,128]{3,2,1,0:T(8,128)}, f32[4,2,32,128]{3,2,1,0:T(8,128)S(1)}, u32[]{:S(2)}, u32[]{:S(2)}) collective-permute-start(f32[4,2,32,128]{3,2,1,0:T(8,128)} %get-tuple-element.25), channel_id=1, source_target_pairs={{0,1},{1,0},{2,3},{3,2},{4,5},{5,4},{6,7},{7,6},{8,9},{9,8},{10,11... | collective-permute-start | bytes 393224 | tf_op jit(solution)/shard_map/ppermute | solution.py:286
  40.8 11.1 %collective-permute-start.4 = (f32[4,2,32,128]{3,2,1,0:T(8,128)}, f32[4,2,32,128]{3,2,1,0:T(8,128)S(1)}, u32[]{:S(2)}, u32[]{:S(2)}) collective-permute-start(f32[4,2,32,128]{3,2,1,0:T(8,128)} %get-tuple-element.26), channel_id=1, source_target_pairs={{0,2},{1,3},{2,0},{3,1},{4,6},{5,7},{6,4},{7,5},{8,10},{9,11},{10,... | collective-permute-start | bytes 393224 | tf_op jit(solution)/shard_map/ppermute | solution.py:286
  42.3 15.9 %collective-permute-start.5 = (f32[4,2,32,128]{3,2,1,0:T(8,128)S(1)}, f32[4,2,32,128]{3,2,1,0:T(8,128)S(1)}, u32[]{:S(2)}, u32[]{:S(2)}) collective-permute-start(f32[4,2,32,128]{3,2,1,0:T(8,128)S(1)} %copy-done.17), channel_id=1, source_target_pairs={{0,3},{1,2},{2,1},{3,0},{4,7},{5,6},{6,5},{7,4},{8,11},{9,10},{10,... | collective-permute-start | bytes 393224 | tf_op jit(solution)/shard_map/ppermute | solution.py:286
  42.8 15.5 %collective-permute-start.6 = (f32[4,2,32,128]{3,2,1,0:T(8,128)S(1)}, f32[4,2,32,128]{3,2,1,0:T(8,128)S(1)}, u32[]{:S(2)}, u32[]{:S(2)}) collective-permute-start(f32[4,2,32,128]{3,2,1,0:T(8,128)S(1)} %copy-done.16), channel_id=1, source_target_pairs={{0,4},{1,5},{2,6},{3,7},{4,0},{5,1},{6,2},{7,3},{8,12},{9,13},{10,... | collective-permute-start | bytes 393224 | tf_op jit(solution)/shard_map/ppermute | solution.py:286
  44.2 14.1 %collective-permute-start.7 = (f32[4,2,32,128]{3,2,1,0:T(8,128)S(1)}, f32[4,2,32,128]{3,2,1,0:T(8,128)S(1)}, u32[]{:S(2)}, u32[]{:S(2)}) collective-permute-start(f32[4,2,32,128]{3,2,1,0:T(8,128)S(1)} %copy-done.15), channel_id=1, source_target_pairs={{0,5},{1,4},{2,7},{3,6},{4,1},{5,0},{6,3},{7,2},{8,13},{9,12},{10,... | collective-permute-start | bytes 393224 | tf_op jit(solution)/shard_map/ppermute | solution.py:286
  44.5 21.5 %copy-start.18 = (f32[4,2,32,128]{3,2,1,0:T(8,128)}, f32[4,2,32,128]{3,2,1,0:T(8,128)S(1)}, u32[]{:S(2)}) copy-start(f32[4,2,32,128]{3,2,1,0:T(8,128)S(1)} %collective-permute-done.3.refs_1_) | copy-start | bytes 393220
  44.5 15.7 %collective-permute-start.8 = (f32[4,2,32,128]{3,2,1,0:T(8,128)S(1)}, f32[4,2,32,128]{3,2,1,0:T(8,128)S(1)}, u32[]{:S(2)}, u32[]{:S(2)}) collective-permute-start(f32[4,2,32,128]{3,2,1,0:T(8,128)S(1)} %copy-done.14), channel_id=1, source_target_pairs={{0,6},{1,7},{2,4},{3,5},{4,2},{5,3},{6,0},{7,1},{8,14},{9,15},{10,... | collective-permute-start | bytes 393224 | tf_op jit(solution)/shard_map/ppermute | solution.py:286
  51.9 14.1 %copy-start.19 = (f32[4,2,32,128]{3,2,1,0:T(8,128)}, f32[4,2,32,128]{3,2,1,0:T(8,128)S(1)}, u32[]{:S(2)}) copy-start(f32[4,2,32,128]{3,2,1,0:T(8,128)S(1)} %collective-permute-done.4.refs_2_) | copy-start | bytes 393220
  51.9 13.5 %collective-permute-start.9 = (f32[4,2,32,128]{3,2,1,0:T(8,128)S(1)}, f32[4,2,32,128]{3,2,1,0:T(8,128)S(1)}, u32[]{:S(2)}, u32[]{:S(2)}) collective-permute-start(f32[4,2,32,128]{3,2,1,0:T(8,128)S(1)} %copy-done.13), channel_id=1, source_target_pairs={{0,7},{1,6},{2,5},{3,4},{4,3},{5,2},{6,1},{7,0},{8,15},{9,14},{10,... | collective-permute-start | bytes 393224 | tf_op jit(solution)/shard_map/ppermute | solution.py:286
  58.2 7.1 %copy-start.20 = (f32[4,2,32,128]{3,2,1,0:T(8,128)}, f32[4,2,32,128]{3,2,1,0:T(8,128)S(1)}, u32[]{:S(2)}) copy-start(f32[4,2,32,128]{3,2,1,0:T(8,128)S(1)} %collective-permute-done.5.refs_3_) | copy-start | bytes 393220
  58.2 7.1 %copy-start.21 = (f32[4,2,32,128]{3,2,1,0:T(8,128)}, f32[4,2,32,128]{3,2,1,0:T(8,128)S(1)}, u32[]{:S(2)}) copy-start(f32[4,2,32,128]{3,2,1,0:T(8,128)S(1)} %collective-permute-done.6.refs_4_) | copy-start | bytes 393220
  58.3 7.1 %copy-start.22 = (f32[4,2,32,128]{3,2,1,0:T(8,128)}, f32[4,2,32,128]{3,2,1,0:T(8,128)S(1)}, u32[]{:S(2)}) copy-start(f32[4,2,32,128]{3,2,1,0:T(8,128)S(1)} %collective-permute-done.7.refs_5_) | copy-start | bytes 393220
  60.3 5.1 %copy-start.23 = (f32[4,2,32,128]{3,2,1,0:T(8,128)}, f32[4,2,32,128]{3,2,1,0:T(8,128)S(1)}, u32[]{:S(2)}) copy-start(f32[4,2,32,128]{3,2,1,0:T(8,128)S(1)} %collective-permute-done.8.refs_6_) | copy-start | bytes 393220
  65.3 0.7 copy-start.24
  74.3 4.9 %copy-start.6 = (f32[8,32,16]{2,1,0:T(8,128)S(1)}, f32[8,32,16]{2,1,0:T(8,128)}, u32[]{:S(2)}) copy-start(f32[8,32,16]{2,1,0:T(8,128)} %project.1) | copy-start | bytes 49156
  74.3 55.1 %all-to-all-start.2 = ((f32[32,4,32,128]{3,2,1,0:T(8,128)}), f32[32,4,32,128]{3,2,1,0:T(8,128)}, u32[]{:S(2)}, u32[]{:S(2)}) async-start(f32[32,4,32,128]{3,2,1,0:T(8,128)} %get-tuple-element.32._), calls=%async_computation.2 | async-start | bytes 4194304 | tf_op jit(solution)/shard_map/all_to_all | solution.py:491
  79.4 14.2 %copy-start.5 = (f32[128,16]{1,0:T(8,128)S(1)}, f32[128,16]{1,0:T(8,128)}, u32[]{:S(2)}) copy-start(f32[128,16]{1,0:T(8,128)} %convolution_bitcast_fusion.refs_13_) | copy-start | bytes 24580
  79.4 31.3 %copy-start.10 = (f32[32,4]{0,1:T(4,128)S(1)}, f32[32,4]{0,1:T(4,128)}, u32[]{:S(2)}) copy-start(f32[32,4]{0,1:T(4,128)} %param.16) | copy-start | bytes 1540
  93.7 54.2 %copy-start.26 = (s32[8,8]{1,0:T(8,128)S(1)}, s32[8,8]{1,0:T(8,128)}, u32[]{:S(2)}) copy-start(s32[8,8]{1,0:T(8,128)} %param.15) | copy-start | bytes 772
  93.7 1.3 collective-permute-start.10
  95.0 3.8 %collective-permute-start.11 = (f32[136,16]{1,0:T(8,128)S(1)}, f32[136,16]{1,0:T(8,128)S(1)}, u32[]{:S(2)}, u32[]{:S(2)}) collective-permute-start(f32[136,16]{1,0:T(8,128)S(1)} %fusion.59), channel_id=1, source_target_pairs={{0,2},{1,3},{2,0},{3,1},{4,6},{5,7},{6,4},{7,5},{8,10},{9,11},{10,... | collective-permute-start | bytes 26120 | tf_op jit(solution)/shard_map/ppermute | solution.py:286
  98.8 7.4 %collective-permute-start.12 = (f32[136,16]{1,0:T(8,128)S(1)}, f32[136,16]{1,0:T(8,128)S(1)}, u32[]{:S(2)}, u32[]{:S(2)}) collective-permute-start(f32[136,16]{1,0:T(8,128)S(1)} %add.130), channel_id=1, source_target_pairs={{0,4},{1,5},{2,6},{3,7},{4,0},{5,1},{6,2},{7,3},{8,12},{9,13},{10,... | collective-permute-start | bytes 26120 | tf_op jit(solution)/shard_map/ppermute | solution.py:286
  106.2 28.0 %copy-start = (f32[136,16]{1,0:T(8,128)}, f32[136,16]{1,0:T(8,128)S(1)}, u32[]{:S(2)}) copy-start(f32[136,16]{1,0:T(8,128)S(1)} %add.131.refs_0_) | copy-start | bytes 26116
  106.2 28.0 %collective-permute-start.15 = (f32[136,16]{1,0:T(8,128)S(1)}, f32[136,16]{1,0:T(8,128)S(1)}, u32[]{:S(2)}, u32[]{:S(2)}) collective-permute-start(f32[136,16]{1,0:T(8,128)S(1)} %add.131.refs_0_), channel_id=1, source_target_pairs={{0,24},{1,25},{2,26},{3,27},{4,28},{5,29},{6,30},{7,31},{8,16},{9,... | collective-permute-start | bytes 26120 | tf_op jit(solution)/shard_map/ppermute | solution.py:286
  107.3 26.9 %collective-permute-start.14 = (f32[136,16]{1,0:T(8,128)S(1)}, f32[136,16]{1,0:T(8,128)S(1)}, u32[]{:S(2)}, u32[]{:S(2)}) collective-permute-start(f32[136,16]{1,0:T(8,128)S(1)} %add.131.refs_0_), channel_id=1, source_target_pairs={{0,16},{1,17},{2,18},{3,19},{4,20},{5,21},{6,22},{7,23},{8,24},{9,... | collective-permute-start | bytes 26120 | tf_op jit(solution)/shard_map/ppermute | solution.py:286
  110.7 23.6 %collective-permute-start.13 = (f32[136,16]{1,0:T(8,128)S(1)}, f32[136,16]{1,0:T(8,128)S(1)}, u32[]{:S(2)}, u32[]{:S(2)}) collective-permute-start(f32[136,16]{1,0:T(8,128)S(1)} %add.131.refs_0_), channel_id=1, source_target_pairs={{0,8},{1,9},{2,10},{3,11},{4,12},{5,13},{6,14},{7,15},{8,0},{9,1},... | collective-permute-start | bytes 26120 | tf_op jit(solution)/shard_map/ppermute | solution.py:286
  129.4 53.2 %all-to-all-start.1 = ((f32[32,4,32,128]{3,2,1,0:T(8,128)}), f32[32,4,32,128]{3,2,1,0:T(8,128)}, u32[]{:S(2)}, u32[]{:S(2)}) async-start(f32[32,4,32,128]{3,2,1,0:T(8,128)} %get-tuple-element.33), calls=%async_computation.1 | async-start | bytes 4194304 | tf_op jit(solution)/shard_map/all_to_all | solution.py:491
  134.2 0.6 copy-start.7
  134.2 0.7 copy-start.8
  134.9 0.6 copy-start.9

commit v11 on v10

--- a/solution.py
+++ b/solution.py
@@ -119,8 +119,9 @@
         out[...] = staged[pl.ds((my_layer[0] ^ k) * each, each)]
 
 
-def regroup_kernel(layers, my_member, *refs):
-    arrived, outs = refs[:layers], refs[layers + 1 : -1]
+def regroup_kernel(layers, members, my_member, *refs):
+    passed = (len(refs) - layers - members) // 2
+    arrived, outs = refs[:layers], refs[layers + passed : layers + passed + members]
     for k, out in enumerate(outs):
         for layer in range(layers):
             out[layer] = arrived[layer][my_member[0] ^ k]
@@ -134,7 +135,8 @@
     real_space_kernel(rows, planes, staged, *rest)
 
 
-def real_space_kernel(rows, planes, recv, pot, inverse, forward, inv_z, fwd_z, _, back, field):
+def real_space_kernel(rows, planes, recv, pot, inverse, forward, inv_z, fwd_z, *refs):
+    back, field = refs[-2:]
     devices, size, span_z = recv.shape
     span_x = devices * planes
     arrived = recv.reshape(devices * size, span_z)
@@ -362,32 +364,39 @@
             name="to_rows",
         )(*([my_layer] if split else []), orbitals, inv_y)
 
-    sent = [to_rows(c, c == 0 and layers > 1) for c in range(parts)]
-    arrived = []
-    if layers > 1:
-        crossed = [sent[0][0]] + [
-            partner(sent[0][k], devices, k * members) for k in range(1, layers)
-        ]
-        *regrouped, sent[1] = pl.pallas_call(
-            functools.partial(regroup_kernel, layers),
-            out_shape=[jax.ShapeDtypeStruct((layers, share, block_rows, span_z), f32)] * members
-            + [jax.ShapeDtypeStruct(sent[1].shape, f32)],
-            in_specs=[scalar]
-            + [pl.BlockSpec(memory_space=pltpu.VMEM)] * layers
-            + [pl.BlockSpec(memory_space=pl.ANY)],
-            out_specs=[pl.BlockSpec(memory_space=pltpu.VMEM)] * members
-            + [pl.BlockSpec(memory_space=pl.ANY)],
-            input_output_aliases={1 + layers: members},
+    sent = [to_rows(c, layers > 1) for c in range(parts)]
+
+    def cross(one):
+        return [one[0]] + [partner(one[k], devices, k * members) for k in range(1, layers)]
+
+    def regroup(crossed, through):
+        anywhere = pl.BlockSpec(memory_space=pl.ANY)
+        held = pl.BlockSpec(memory_space=pltpu.VMEM)
+        shape = jax.ShapeDtypeStruct((layers, share, block_rows, span_z), f32)
+        outs = pl.pallas_call(
+            functools.partial(regroup_kernel, layers, members),
+            out_shape=[shape] * members
+            + [jax.ShapeDtypeStruct(one.shape, f32) for one in through],
+            in_specs=[scalar] + [held] * layers + [anywhere] * len(through),
+            out_specs=[held] * members + [anywhere] * len(through),
+            input_output_aliases={1 + layers + i: members + i for i in range(len(through))},
             compiler_params=params,
             cost_estimate=cost(0, 2 * 10**6),
             name="regroup",
-        )(my_member, *crossed, sent[1])
-        arrived.append(
-            [regrouped[0]] + [partner(regrouped[k], devices, k) for k in range(1, members)]
-        )
-        sent = sent[1:]
-    for one in sent:
-        arrived.append([lax.all_to_all(one, "ga", split_axis=0, concat_axis=0, tiled=True)])
+        )(my_member, *crossed, *through)
+        return outs[:members], outs[members:]
+
+    def spread(one):
+        return [one[0]] + [partner(one[k], devices, k) for k in range(1, members)]
+
+    if layers > 1:
+        one, sent[1] = regroup(cross(sent[0]), sent[1])
+        crossed = cross(sent[1])
+        arrived = [spread(one), crossed]
+    else:
+        arrived = [
+            [lax.all_to_all(one, "ga", split_axis=0, concat_axis=0, tiled=True)] for one in sent
+        ]
 
     def tables_x(owned):
         phases = (owned.T.reshape(-1)[:, None] * grid_x[None, :]) % span_x
@@ -455,8 +464,10 @@
 
     returned, fields = [], []
     before = proj
-    for operands in arrived:
-        steps = len(operands) > 1
+    for c, operands in enumerate(arrived):
+        steps = layers > 1
+        if steps and c > 0:
+            operands = spread(operands)
         held = devices // len(operands)
         kernel = functools.partial(real_space_kernel, rows, planes)
         if steps:
@@ -476,17 +487,19 @@
                 whole(fwd_x.shape),
                 whole(inv_z.shape),
                 whole(fwd_z.shape),
-                pl.BlockSpec(memory_space=pl.ANY),
-            ],
+            ]
+            + [pl.BlockSpec(memory_space=pl.ANY)],
             out_specs=(
                 pl.BlockSpec((devices, 2, block_rows, span_z), lambda j: (0, j, 0, 0)),
                 pl.BlockSpec((2, rows * span_x, span_z), lambda j: (j, 0, 0)),
             ),
             scratch_shapes=[pltpu.VMEM((devices, block_rows, span_z), f32)] if steps else [],
             compiler_params=params,
-            cost_estimate=cost(4 * 10**9, 8 * 10**6),
+            cost_estimate=cost(10**6, 10**4),
             name="real_space",
         )(*operands, pot, inv_x_steps if steps else inv_x, fwd_x, inv_z, fwd_z, before)
+        if steps and c == 0:
+            arrived[1], (back,) = regroup(arrived[1], [back])
         before = back
         returned.append(lax.all_to_all(back, "ga", split_axis=0, concat_axis=0, tiled=True))
         fields.append(field)

time: 189 us -> 199 us (1.053)
  waiting for transfers between devices: 55.2 us -> 46.8 us
  starting transfers between devices: 44.6 us -> 52.1 us
  other arithmetic: 9.97 us -> 14.2 us
  local copies, waits for them, and re-layouts: 9.21 us -> 12.1 us
  Pallas kernels: 60.3 us -> 62.9 us
    all_to_all x2, waiting for transfers between devices: 36.4 us -> 17.9 us  [on_device(): lax.all_to_all(back, 'ga', split_axis=0, concat_axis=0, tiled=True)]
    ppermute x16 -> x26, starting transfers between devices: 25 us -> 39.3 us  [partner(): return lax.ppermute(values, 'ga', [(d, d ^ k) for d in range(devices)])]
    all_to_all x1 -> x0, starting transfers between devices: 11 us -> none  [on_device(): lax.all_to_all(one, 'ga', split_axis=0, concat_axis=0, tiled=True)]
    ppermute x16 -> x26, waiting for transfers between devices: 18.8 us -> 28.9 us  [partner(): return lax.ppermute(values, 'ga', [(d, d ^ k) for d in range(devices)])]
    all_to_all x2, starting transfers between devices: 8.56 us -> 12.8 us  [on_device(): lax.all_to_all(back, 'ga', split_axis=0, concat_axis=0, tiled=True)]
    unnamed x60 -> x72, local copies, waits for them, and re-layouts: 3.18 us -> 6.11 us
    pallas_call x1 -> x2, Pallas kernels: 2.24 us -> 4.47 us  [regroup(): pl.pallas_call(functools.partial(regroup_kernel, layers, members), out_sh...]
  transfers between devices with their start and end apart: 19 -> 28, of which waited for: 9 -> 9; matrix products, arithmetic and copies ran while one was open for 12% -> 14% of each run, Pallas kernels for 27% -> 26%
where the time goes in v11:
time: 199 us; the launch traced here: 196 us
  Pallas kernels  62.9 us (32%)
  starting transfers between devices  52.1 us (26%)
  waiting for transfers between devices  46.8 us (24%)
  other arithmetic  14.2 us (7%)
  local copies, waits for them, and re-layouts  12.1 us (6%)
  matrix products  6.8 us (3%)
    ppermute x26, starting transfers between devices, partner(): return lax.ppermute(values, 'ga', [(d, d ^ k) for d in range(devices)])  39.3 us
    ppermute x26, waiting for transfers between devices, partner(): return lax.ppermute(values, 'ga', [(d, d ^ k) for d in range(devices)])  28.9 us
    all_to_all x2, waiting for transfers between devices, on_device(): lax.all_to_all(back, 'ga', split_axis=0, concat_axis=0, tiled=True)  17.9 us
    pallas_call x2, Pallas kernels, on_device(): pl.pallas_call(kernel, out_shape=(jax.ShapeDtypeStruct((devices, 2 * shar...  16.6 us
    all_to_all x2, starting transfers between devices, on_device(): lax.all_to_all(back, 'ga', split_axis=0, concat_axis=0, tiled=True)  12.8 us
    pallas_call x1, Pallas kernels, on_device(): pl.pallas_call(functools.partial(base_kernel, slots), out_shape=jax.Shape...  11.2 us
    pallas_call x1, Pallas kernels, on_device(): pl.pallas_call(functools.partial(project_kernel, slots), out_shape=jax.Sh...  10 us
    pallas_call x2, Pallas kernels, on_device(): pl.pallas_call(to_planes_kernel, out_shape=jax.ShapeDtypeStruct(orbitals....  7.73 us
  transfers between devices with their start and end apart: 28, of which 9 were waited for; matrix products, arithmetic and copies ran while one was open for 14% of the time, Pallas kernels for 26%

profile of v11, /device:TPU:1, one launch (start us, length us, event | category | flops | bytes accessed | tf_op | source)
XLA Modules:
  0.0 196.1 jit_solution(6832900538342415441)
XLA Ops:
  0.6 3.0 %to_rows.2 = (f32[8,2,32,128]{3,2,1,0:T(8,128)}, f32[8,2,32,128]{3,2,1,0:T(8,128)}, f32[8,2,32,128]{3,2,1,0:T(8,128)}, f32[8,2,32,128]{3,2,1,0:T(8,128)}) custom-call(s32[1]{0:T(128)} %bitcast.1.my_layer, f32[8,2,4,128,128]{4,3,2,1,0:T(8,128)} %psi.7, bf16[256,768]{1,0:T(8,128)(2,1)} %constant.146.clone.y_table), custom_call_target="tpu_custom_call" | custom-call | flops 4000000000 | bytes 3000000 | tf_op jit(solution)/shard_map/to_rows/pallas_call | solution.py:351
  3.7 2.1 %collective-permute-start = (f32[8,2,32,128]{3,2,1,0:T(8,128)}, f32[8,2,32,128]{3,2,1,0:T(8,128)S(1)}, u32[]{:S(2)}, u32[]{:S(2)}) collective-permute-start(f32[8,2,32,128]{3,2,1,0:T(8,128)} %get-tuple-element.36), channel_id=1, source_target_pairs={{0,8},{1,9},{2,10},{3,11},{4,12},{5,13},{6,14},{7,15},{8,0},{9,1},... | collective-permute-start | bytes 786440 | tf_op jit(solution)/shard_map/ppermute | solution.py:288
  5.8 2.3 %collective-permute-start.1 = (f32[8,2,32,128]{3,2,1,0:T(8,128)}, f32[8,2,32,128]{3,2,1,0:T(8,128)S(1)}, u32[]{:S(2)}, u32[]{:S(2)}) collective-permute-start(f32[8,2,32,128]{3,2,1,0:T(8,128)} %get-tuple-element.37), channel_id=1, source_target_pairs={{0,16},{1,17},{2,18},{3,19},{4,20},{5,21},{6,22},{7,23},{8,24},{9,... | collective-permute-start | bytes 786440 | tf_op jit(solution)/shard_map/ppermute | solution.py:288
  8.2 3.1 %to_rows.3 = (f32[8,2,32,128]{3,2,1,0:T(8,128)}, f32[8,2,32,128]{3,2,1,0:T(8,128)}, f32[8,2,32,128]{3,2,1,0:T(8,128)}, f32[8,2,32,128]{3,2,1,0:T(8,128)}) custom-call(s32[1]{0:T(128)} %bitcast.1.my_layer, f32[8,2,4,128,128]{4,3,2,1,0:T(8,128)} %psi.7, bf16[256,768]{1,0:T(8,128)(2,1)} %constant.146.clone.y_table), custom_call_target="tpu_custom_call" | custom-call | flops 4000000000 | bytes 3000000 | tf_op jit(solution)/shard_map/to_rows/pallas_call | solution.py:351
  12.2 1.0 cosine_multiply_fusion
  14.1 10.0 %project.1 = f32[8,32,16]{2,1,0:T(8,128)} custom-call(f32[8,2,4,128,128]{4,3,2,1,0:T(8,128)} %psi.7, f32[8,1024,128]{2,1,0:T(8,128)} %bitcast.88, f32[4,128,128]{2,1,0:T(8,128)} %add_multiply_fusion.kinetic), custom_call_target="tpu_custom_call" | custom-call | flops 8000000000 | bytes 8000000 | tf_op jit(solution)/shard_map/project/pallas_call | solution.py:439
  27.6 2.2 %regroup.2 = (f32[4,2,32,128]{3,2,1,0:T(8,128)}, f32[4,2,32,128]{3,2,1,0:T(8,128)}, f32[4,2,32,128]{3,2,1,0:T(8,128)}, f32[4,2,32,128]{3,2,1,0:T(8,128)}, f32[4,...) custom-call(s32[1]{0:T(128)} %bitcast.my_member, ...), custom_call_target="tpu_custom_call", output_to_operand_aliasing={{8}: (5, {}), {9}: (6, {}), {10}: (7, {}), {11}: (8, {})} | custom-call | bytes 2000000 | tf_op jit(solution)/shard_map/regroup/pallas_call | solution.py:376
  29.8 1.6 collective-permute-start.6
  31.4 1.2 collective-permute-start.7
  33.1 1.3 collective-permute-start.9
  35.1 4.4 %collective-permute-start.3 = (f32[8,2,32,128]{3,2,1,0:T(8,128)}, f32[8,2,32,128]{3,2,1,0:T(8,128)S(1)}, u32[]{:S(2)}, u32[]{:S(2)}) collective-permute-start(f32[8,2,32,128]{3,2,1,0:T(8,128)} %get-tuple-element.44), channel_id=1, source_target_pairs={{0,8},{1,9},{2,10},{3,11},{4,12},{5,13},{6,14},{7,15},{8,0},{9,1},... | collective-permute-start | bytes 786440 | tf_op jit(solution)/shard_map/ppermute | solution.py:288
  40.1 2.6 %collective-permute-start.4 = (f32[8,2,32,128]{3,2,1,0:T(8,128)}, f32[8,2,32,128]{3,2,1,0:T(8,128)S(1)}, u32[]{:S(2)}, u32[]{:S(2)}) collective-permute-start(f32[8,2,32,128]{3,2,1,0:T(8,128)} %get-tuple-element.45), channel_id=1, source_target_pairs={{0,16},{1,17},{2,18},{3,19},{4,20},{5,21},{6,22},{7,23},{8,24},{9,... | collective-permute-start | bytes 786440 | tf_op jit(solution)/shard_map/ppermute | solution.py:288
  43.4 1.1 collective-permute-start.5
  45.4 2.2 %collective-permute-start.11 = (f32[4,2,32,128]{3,2,1,0:T(8,128)}, f32[4,2,32,128]{3,2,1,0:T(8,128)}, u32[]{:S(2)}, u32[]{:S(2)}) collective-permute-start(f32[4,2,32,128]{3,2,1,0:T(8,128)} %get-tuple-element.53), channel_id=1, source_target_pairs={{0,6},{1,7},{2,4},{3,5},{4,2},{5,3},{6,0},{7,1},{8,14},{9,15},{10,... | collective-permute-start | bytes 393224 | tf_op jit(solution)/shard_map/ppermute | solution.py:288
  47.6 2.2 %collective-permute-start.12 = (f32[4,2,32,128]{3,2,1,0:T(8,128)}, f32[4,2,32,128]{3,2,1,0:T(8,128)}, u32[]{:S(2)}, u32[]{:S(2)}) collective-permute-start(f32[4,2,32,128]{3,2,1,0:T(8,128)} %get-tuple-element.54), channel_id=1, source_target_pairs={{0,7},{1,6},{2,5},{3,4},{4,3},{5,2},{6,1},{7,0},{8,15},{9,14},{10,... | collective-permute-start | bytes 393224 | tf_op jit(solution)/shard_map/ppermute | solution.py:288
  51.5 1.7 copy.115
  53.1 1.7 convolution_bitcast_fusion.refs_13_
  55.3 8.3 %real_space.2 = (f32[32,4,32,128]{3,2,1,0:T(8,128)}, f32[4,512,128]{2,1,0:T(8,128)}) custom-call(f32[4,2,32,128]{3,2,1,0:T(8,128)} %get-tuple-element.47.refs_0_, f32[4,2,32,128]{3,2,1,0:T(8,128)} %copy-done.15, f32[4,2,32,128]{3,2,1,0:T(8,128)} %copy-done.16, f32[4,2,32,128]{3,2,1,0:T(8,128)} %copy-done.17, f32[4,2,32,128]{3,2,1,0:T(8,128)} %copy-done.18, ...), custom_call_target="tpu_custom_call" | custom-call | flops 1000000 | bytes 10000 | tf_op jit(solution)/shard_map/real_space/pallas_call | solution.py:475
  64.5 2.2 %regroup.3 = (f32[4,2,32,128]{3,2,1,0:T(8,128)}, f32[4,2,32,128]{3,2,1,0:T(8,128)}, f32[4,2,32,128]{3,2,1,0:T(8,128)}, f32[4,2,32,128]{3,2,1,0:T(8,128)}, f32[4,...) custom-call(s32[1]{0:T(128)} %bitcast.my_member, ...), custom_call_target="tpu_custom_call", output_to_operand_aliasing={{8}: (5, {})} | custom-call | bytes 2000000 | tf_op jit(solution)/shard_map/regroup/pallas_call | solution.py:376
  66.8 6.7 %all-to-all-start.1 = ((f32[32,4,32,128]{3,2,1,0:T(8,128)}), f32[32,4,32,128]{3,2,1,0:T(8,128)}, u32[]{:S(2)}, u32[]{:S(2)}) async-start(f32[32,4,32,128]{3,2,1,0:T(8,128)} %get-tuple-element.64.refs_13_), calls=%async_computation.1 | async-start | bytes 4194304 | tf_op jit(solution)/shard_map/all_to_all | solution.py:504
  73.9 1.4 collective-permute-start.14
  75.7 1.4 collective-permute-start.16
  77.5 2.3 %collective-permute-start.18 = (f32[4,2,32,128]{3,2,1,0:T(8,128)S(1)}, f32[4,2,32,128]{3,2,1,0:T(8,128)S(1)}, u32[]{:S(2)}, u32[]{:S(2)}) collective-permute-start(f32[4,2,32,128]{3,2,1,0:T(8,128)S(1)} %copy-done.26), channel_id=1, source_target_pairs={{0,6},{1,7},{2,4},{3,5},{4,2},{5,3},{6,0},{7,1},{8,14},{9,15},{10,... | collective-permute-start | bytes 393224 | tf_op jit(solution)/shard_map/ppermute | solution.py:288
  79.8 11.9 %collective-permute-done.14.refs_2_ = f32[4,2,32,128]{3,2,1,0:T(8,128)S(1)} collective-permute-done((f32[4,2,32,128]{3,2,1,0:T(8,128)S(1)}, f32[4,2,32,128]{3,2,1,0:T(8,128)S(1)}, u32[]{:S(2)}, u32[]{:S(2)}) %collective-permute-start.14) | collective-permute-done | bytes 131104 | tf_op jit(solution)/shard_map/ppermute | solution.py:288
  91.7 4.5 %collective-permute-start.19 = (f32[4,2,32,128]{3,2,1,0:T(8,128)S(1)}, f32[4,2,32,128]{3,2,1,0:T(8,128)S(1)}, u32[]{:S(2)}, u32[]{:S(2)}) collective-permute-start(f32[4,2,32,128]{3,2,1,0:T(8,128)S(1)} %copy-done.25), channel_id=1, source_target_pairs={{0,7},{1,6},{2,5},{3,4},{4,3},{5,2},{6,1},{7,0},{8,15},{9,14},{10,... | collective-permute-start | bytes 393224 | tf_op jit(solution)/shard_map/ppermute | solution.py:288
  97.8 2.2 %collective-permute-done.15.refs_3_ = f32[4,2,32,128]{3,2,1,0:T(8,128)S(1)} collective-permute-done((f32[4,2,32,128]{3,2,1,0:T(8,128)S(1)}, f32[4,2,32,128]{3,2,1,0:T(8,128)S(1)}, u32[]{:S(2)}, u32[]{:S(2)}) %collective-permute-start.15) | collective-permute-done | bytes 131104 | tf_op jit(solution)/shard_map/ppermute | solution.py:288
  100.1 3.3 %collective-permute-done.18.refs_6_ = f32[4,2,32,128]{3,2,1,0:T(8,128)S(1)} collective-permute-done((f32[4,2,32,128]{3,2,1,0:T(8,128)S(1)}, f32[4,2,32,128]{3,2,1,0:T(8,128)S(1)}, u32[]{:S(2)}, u32[]{:S(2)}) %collective-permute-start.18) | collective-permute-done | bytes 131104 | tf_op jit(solution)/shard_map/ppermute | solution.py:288
  103.4 4.4 %collective-permute-done.19.refs_7_ = f32[4,2,32,128]{3,2,1,0:T(8,128)S(1)} collective-permute-done((f32[4,2,32,128]{3,2,1,0:T(8,128)S(1)}, f32[4,2,32,128]{3,2,1,0:T(8,128)S(1)}, u32[]{:S(2)}, u32[]{:S(2)}) %collective-permute-start.19) | collective-permute-done | bytes 131104 | tf_op jit(solution)/shard_map/ppermute | solution.py:288
  108.5 8.3 %real_space.3 = (f32[32,4,32,128]{3,2,1,0:T(8,128)}, f32[4,512,128]{2,1,0:T(8,128)}) custom-call(f32[4,2,32,128]{3,2,1,0:T(8,128)} %get-tuple-element.56.refs_0_, f32[4,2,32,128]{3,2,1,0:T(8,128)} %copy-done.8, f32[4,2,32,128]{3,2,1,0:T(8,128)} %copy-done.9, f32[4,2,32,128]{3,2,1,0:T(8,128)} %copy-done.10, f32[4,2,32,128]{3,2,1,0:T(8,128)} %copy-done.11, ...), custom_call_target="tpu_custom_call" | custom-call | flops 1000000 | bytes 10000 | tf_op jit(solution)/shard_map/real_space/pallas_call | solution.py:475
  116.8 5.2 %real_gram.1 = f32[2,8,8,128]{3,2,1,0:T(8,128)} custom-call(f32[4,512,128]{2,1,0:T(8,128)} %get-tuple-element.66.refs_0_, f32[4,512,128]{2,1,0:T(8,128)} %get-tuple-element.67.refs_1_, f32[512,128]{1,0:T(8,128)} %bitcast.79), custom_call_target="tpu_custom_call" | custom-call | flops 10000000 | bytes 2000000 | tf_op jit(solution)/shard_map/real_gram/pallas_call | solution.py:507
  122.0 0.9 reduce_sum.18
  123.9 1.1 collective-permute-done.20
  125.1 2.6 %collective-permute-start.21 = (f32[136,16]{1,0:T(8,128)S(1)}, f32[136,16]{1,0:T(8,128)S(1)}, u32[]{:S(2)}, u32[]{:S(2)}) collective-permute-start(f32[136,16]{1,0:T(8,128)S(1)} %fusion.57), channel_id=1, source_target_pairs={{0,2},{1,3},{2,0},{3,1},{4,6},{5,7},{6,4},{7,5},{8,10},{9,11},{10,... | collective-permute-start | bytes 26120 | tf_op jit(solution)/shard_map/ppermute | solution.py:288
  127.7 2.4 %collective-permute-done.21 = f32[136,16]{1,0:T(8,128)S(1)} collective-permute-done((f32[136,16]{1,0:T(8,128)S(1)}, f32[136,16]{1,0:T(8,128)S(1)}, u32[]{:S(2)}, u32[]{:S(2)}) %collective-permute-start.21) | collective-permute-done | bytes 8736 | tf_op jit(solution)/shard_map/ppermute | solution.py:288
  130.2 3.1 %collective-permute-done.22 = f32[136,16]{1,0:T(8,128)S(1)} collective-permute-done((f32[136,16]{1,0:T(8,128)S(1)}, f32[136,16]{1,0:T(8,128)S(1)}, u32[]{:S(2)}, u32[]{:S(2)}) %collective-permute-start.22) | collective-permute-done | bytes 8736 | tf_op jit(solution)/shard_map/ppermute | solution.py:288
  133.3 2.0 %collective-permute-start.25 = (f32[136,16]{1,0:T(8,128)S(1)}, f32[136,16]{1,0:T(8,128)S(1)}, u32[]{:S(2)}, u32[]{:S(2)}) collective-permute-start(f32[136,16]{1,0:T(8,128)S(1)} %add.131.refs_0_), channel_id=1, source_target_pairs={{0,24},{1,25},{2,26},{3,27},{4,28},{5,29},{6,30},{7,31},{8,16},{9,... | collective-permute-start | bytes 26120 | tf_op jit(solution)/shard_map/ppermute | solution.py:288
  135.4 1.6 collective-permute-start.23
  137.8 6.1 %all-to-all-start = ((f32[32,4,32,128]{3,2,1,0:T(8,128)}), f32[32,4,32,128]{3,2,1,0:T(8,128)}, u32[]{:S(2)}, u32[]{:S(2)}) async-start(f32[32,4,32,128]{3,2,1,0:T(8,128)} %get-tuple-element.65), calls=%async_computation | async-start | bytes 4194304 | tf_op jit(solution)/shard_map/all_to_all | solution.py:504
  145.2 1.6 last_sum.1
  147.5 0.9 slice_multiply_fusion
  148.4 1.1 fusion.16
  149.5 1.1 fusion.22
  154.2 1.1 fusion.18
  155.4 1.1 convolution_subtract_fusion
  159.3 11.2 %base.1 = f32[8,2,4,128,128]{4,3,2,1,0:T(8,128)} custom-call(f32[8,2,4,128,128]{4,3,2,1,0:T(8,128)} %psi.7, f32[8,1024,128]{2,1,0:T(8,128)} %bitcast.89, f32[4,128,128]{2,1,0:T(8,128)} %add_multiply_fusion.kinetic, f32[8,16,32]{2,1,0:T(8,128)} %pad_maximum_fusion.4.coefs), custom_call_target="tpu_custom_call" | custom-call | flops 8000000000 | bytes 12000000 | tf_op jit(solution)/shard_map/base/pallas_call | solution.py:544
  170.5 3.9 %to_planes.2.base = f32[8,2,4,128,128]{4,3,2,1,0:T(8,128)} custom-call(f32[32,4,32,128]{3,2,1,0:T(8,128)} %all-to-all-done.1.refs_4_.recv, f32[8,2,4,128,128]{4,3,2,1,0:T(8,128)} %base.1, bf16[256,768]{1,0:T(8,128)(2,1)} %constant.147.clone.y_table), custom_call_target="tpu_custom_call", output_to_operand_aliasing={{}: (1, {})} | custom-call | flops 8000000000 | bytes 12000000 | tf_op jit(solution)/shard_map/to_planes/pallas_call | solution.py:561
  174.4 17.9 %all-to-all-done.recv = f32[32,4,32,128]{3,2,1,0:T(8,128)} async-done(((f32[32,4,32,128]{3,2,1,0:T(8,128)}), f32[32,4,32,128]{3,2,1,0:T(8,128)}, u32[]{:S(2)}, u32[]{:S(2)}) %all-to-all-start) | async-done | bytes 2097184 | tf_op jit(solution)/shard_map/all_to_all | solution.py:504
  192.3 3.9 %to_planes.3 = f32[8,2,4,128,128]{4,3,2,1,0:T(8,128)} custom-call(f32[32,4,32,128]{3,2,1,0:T(8,128)} %all-to-all-done.recv, f32[8,2,4,128,128]{4,3,2,1,0:T(8,128)} %to_planes.2.base, bf16[256,768]{1,0:T(8,128)(2,1)} %constant.147.clone.y_table), custom_call_target="tpu_custom_call", output_to_operand_aliasing={{}: (1, {})} | custom-call | flops 8000000000 | bytes 12000000 | tf_op jit(solution)/shard_map/to_planes/pallas_call | solution.py:561
  (162 shorter events, 25.4 us)
Async XLA Ops:
  3.7 23.0 %collective-permute-start = (f32[8,2,32,128]{3,2,1,0:T(8,128)}, f32[8,2,32,128]{3,2,1,0:T(8,128)S(1)}, u32[]{:S(2)}, u32[]{:S(2)}) collective-permute-start(f32[8,2,32,128]{3,2,1,0:T(8,128)} %get-tuple-element.36), channel_id=1, source_target_pairs={{0,8},{1,9},{2,10},{3,11},{4,12},{5,13},{6,14},{7,15},{8,0},{9,1},... | collective-permute-start | bytes 786440 | tf_op jit(solution)/shard_map/ppermute | solution.py:288
  5.8 20.9 %collective-permute-start.1 = (f32[8,2,32,128]{3,2,1,0:T(8,128)}, f32[8,2,32,128]{3,2,1,0:T(8,128)S(1)}, u32[]{:S(2)}, u32[]{:S(2)}) collective-permute-start(f32[8,2,32,128]{3,2,1,0:T(8,128)} %get-tuple-element.37), channel_id=1, source_target_pairs={{0,16},{1,17},{2,18},{3,19},{4,20},{5,21},{6,22},{7,23},{8,24},{9,... | collective-permute-start | bytes 786440 | tf_op jit(solution)/shard_map/ppermute | solution.py:288
  8.1 18.6 %collective-permute-start.2 = (f32[8,2,32,128]{3,2,1,0:T(8,128)}, f32[8,2,32,128]{3,2,1,0:T(8,128)S(1)}, u32[]{:S(2)}, u32[]{:S(2)}) collective-permute-start(f32[8,2,32,128]{3,2,1,0:T(8,128)} %get-tuple-element.38), channel_id=1, source_target_pairs={{0,24},{1,25},{2,26},{3,27},{4,28},{5,29},{6,30},{7,31},{8,16},{9,... | collective-permute-start | bytes 786440 | tf_op jit(solution)/shard_map/ppermute | solution.py:288
  8.1 3.3 %copy-start.24 = (s32[32]{0:T(128)S(1)}, s32[32]{0:T(128)}, u32[]{:S(2)}) copy-start(s32[32]{0:T(128)} %constant.150.clone) | copy-start | bytes 388
  29.8 5.2 %collective-permute-start.6 = (f32[4,2,32,128]{3,2,1,0:T(8,128)}, f32[4,2,32,128]{3,2,1,0:T(8,128)S(1)}, u32[]{:S(2)}, u32[]{:S(2)}) collective-permute-start(f32[4,2,32,128]{3,2,1,0:T(8,128)} %get-tuple-element.48), channel_id=1, source_target_pairs={{0,1},{1,0},{2,3},{3,2},{4,5},{5,4},{6,7},{7,6},{8,9},{9,8},{10,11... | collective-permute-start | bytes 393224 | tf_op jit(solution)/shard_map/ppermute | solution.py:288
  31.4 8.1 %collective-permute-start.7 = (f32[4,2,32,128]{3,2,1,0:T(8,128)}, f32[4,2,32,128]{3,2,1,0:T(8,128)S(1)}, u32[]{:S(2)}, u32[]{:S(2)}) collective-permute-start(f32[4,2,32,128]{3,2,1,0:T(8,128)} %get-tuple-element.49), channel_id=1, source_target_pairs={{0,2},{1,3},{2,0},{3,1},{4,6},{5,7},{6,4},{7,5},{8,10},{9,11},{10,... | collective-permute-start | bytes 393224 | tf_op jit(solution)/shard_map/ppermute | solution.py:288
  32.6 10.1 %collective-permute-start.8 = (f32[4,2,32,128]{3,2,1,0:T(8,128)}, f32[4,2,32,128]{3,2,1,0:T(8,128)S(1)}, u32[]{:S(2)}, u32[]{:S(2)}) collective-permute-start(f32[4,2,32,128]{3,2,1,0:T(8,128)} %get-tuple-element.50), channel_id=1, source_target_pairs={{0,3},{1,2},{2,1},{3,0},{4,7},{5,6},{6,5},{7,4},{8,11},{9,10},{10,... | collective-permute-start | bytes 393224 | tf_op jit(solution)/shard_map/ppermute | solution.py:288
  33.1 12.2 %collective-permute-start.9 = (f32[4,2,32,128]{3,2,1,0:T(8,128)}, f32[4,2,32,128]{3,2,1,0:T(8,128)S(1)}, u32[]{:S(2)}, u32[]{:S(2)}) collective-permute-start(f32[4,2,32,128]{3,2,1,0:T(8,128)} %get-tuple-element.51), channel_id=1, source_target_pairs={{0,4},{1,5},{2,6},{3,7},{4,0},{5,1},{6,2},{7,3},{8,12},{9,13},{10,... | collective-permute-start | bytes 393224 | tf_op jit(solution)/shard_map/ppermute | solution.py:288
  34.4 13.2 %collective-permute-start.10 = (f32[4,2,32,128]{3,2,1,0:T(8,128)}, f32[4,2,32,128]{3,2,1,0:T(8,128)S(1)}, u32[]{:S(2)}, u32[]{:S(2)}) collective-permute-start(f32[4,2,32,128]{3,2,1,0:T(8,128)} %get-tuple-element.52), channel_id=1, source_target_pairs={{0,5},{1,4},{2,7},{3,6},{4,1},{5,0},{6,3},{7,2},{8,13},{9,12},{10,... | collective-permute-start | bytes 393224 | tf_op jit(solution)/shard_map/ppermute | solution.py:288
  35.0 16.4 %copy-start.15 = (f32[4,2,32,128]{3,2,1,0:T(8,128)}, f32[4,2,32,128]{3,2,1,0:T(8,128)S(1)}, u32[]{:S(2)}) copy-start(f32[4,2,32,128]{3,2,1,0:T(8,128)S(1)} %collective-permute-done.6.refs_1_) | copy-start | bytes 393220
  35.1 28.5 %collective-permute-start.3 = (f32[8,2,32,128]{3,2,1,0:T(8,128)}, f32[8,2,32,128]{3,2,1,0:T(8,128)S(1)}, u32[]{:S(2)}, u32[]{:S(2)}) collective-permute-start(f32[8,2,32,128]{3,2,1,0:T(8,128)} %get-tuple-element.44), channel_id=1, source_target_pairs={{0,8},{1,9},{2,10},{3,11},{4,12},{5,13},{6,14},{7,15},{8,0},{9,1},... | collective-permute-start | bytes 786440 | tf_op jit(solution)/shard_map/ppermute | solution.py:288
  40.1 23.5 %collective-permute-start.4 = (f32[8,2,32,128]{3,2,1,0:T(8,128)}, f32[8,2,32,128]{3,2,1,0:T(8,128)S(1)}, u32[]{:S(2)}, u32[]{:S(2)}) collective-permute-start(f32[8,2,32,128]{3,2,1,0:T(8,128)} %get-tuple-element.45), channel_id=1, source_target_pairs={{0,16},{1,17},{2,18},{3,19},{4,20},{5,21},{6,22},{7,23},{8,24},{9,... | collective-permute-start | bytes 786440 | tf_op jit(solution)/shard_map/ppermute | solution.py:288
  43.4 20.2 %collective-permute-start.5 = (f32[8,2,32,128]{3,2,1,0:T(8,128)}, f32[8,2,32,128]{3,2,1,0:T(8,128)S(1)}, u32[]{:S(2)}, u32[]{:S(2)}) collective-permute-start(f32[8,2,32,128]{3,2,1,0:T(8,128)} %get-tuple-element.46), channel_id=1, source_target_pairs={{0,24},{1,25},{2,26},{3,27},{4,28},{5,29},{6,30},{7,31},{8,16},{9,... | collective-permute-start | bytes 786440 | tf_op jit(solution)/shard_map/ppermute | solution.py:288
  45.4 9.9 %copy-start.18 = (f32[4,2,32,128]{3,2,1,0:T(8,128)}, f32[4,2,32,128]{3,2,1,0:T(8,128)S(1)}, u32[]{:S(2)}) copy-start(f32[4,2,32,128]{3,2,1,0:T(8,128)S(1)} %collective-permute-done.9.refs_4_) | copy-start | bytes 393220
  45.4 9.5 %collective-permute-start.11 = (f32[4,2,32,128]{3,2,1,0:T(8,128)}, f32[4,2,32,128]{3,2,1,0:T(8,128)}, u32[]{:S(2)}, u32[]{:S(2)}) collective-permute-start(f32[4,2,32,128]{3,2,1,0:T(8,128)} %get-tuple-element.53), channel_id=1, source_target_pairs={{0,6},{1,7},{2,4},{3,5},{4,2},{5,3},{6,0},{7,1},{8,14},{9,15},{10,... | collective-permute-start | bytes 393224 | tf_op jit(solution)/shard_map/ppermute | solution.py:288
  47.6 3.8 %copy-start.19 = (f32[4,2,32,128]{3,2,1,0:T(8,128)}, f32[4,2,32,128]{3,2,1,0:T(8,128)S(1)}, u32[]{:S(2)}) copy-start(f32[4,2,32,128]{3,2,1,0:T(8,128)S(1)} %collective-permute-done.10.refs_5_) | copy-start | bytes 393220
  47.6 7.7 %collective-permute-start.12 = (f32[4,2,32,128]{3,2,1,0:T(8,128)}, f32[4,2,32,128]{3,2,1,0:T(8,128)}, u32[]{:S(2)}, u32[]{:S(2)}) collective-permute-start(f32[4,2,32,128]{3,2,1,0:T(8,128)} %get-tuple-element.54), channel_id=1, source_target_pairs={{0,7},{1,6},{2,5},{3,4},{4,3},{5,2},{6,1},{7,0},{8,15},{9,14},{10,... | collective-permute-start | bytes 393224 | tf_op jit(solution)/shard_map/ppermute | solution.py:288
  66.7 6.8 %copy-start.31 = (f32[4,2,32,128]{3,2,1,0:T(8,128)S(1)}, f32[4,2,32,128]{3,2,1,0:T(8,128)}, u32[]{:S(2)}) copy-start(f32[4,2,32,128]{3,2,1,0:T(8,128)} %get-tuple-element.57) | copy-start | bytes 393220
  66.8 7.2 %copy-start.30 = (f32[4,2,32,128]{3,2,1,0:T(8,128)S(1)}, f32[4,2,32,128]{3,2,1,0:T(8,128)}, u32[]{:S(2)}) copy-start(f32[4,2,32,128]{3,2,1,0:T(8,128)} %get-tuple-element.58) | copy-start | bytes 393220
  66.8 8.6 %copy-start.29 = (f32[4,2,32,128]{3,2,1,0:T(8,128)S(1)}, f32[4,2,32,128]{3,2,1,0:T(8,128)}, u32[]{:S(2)}) copy-start(f32[4,2,32,128]{3,2,1,0:T(8,128)} %get-tuple-element.59) | copy-start | bytes 393220
  66.8 9.0 %copy-start.28 = (f32[4,2,32,128]{3,2,1,0:T(8,128)S(1)}, f32[4,2,32,128]{3,2,1,0:T(8,128)}, u32[]{:S(2)}) copy-start(f32[4,2,32,128]{3,2,1,0:T(8,128)} %get-tuple-element.60) | copy-start | bytes 393220
  66.8 10.4 %copy-start.27 = (f32[4,2,32,128]{3,2,1,0:T(8,128)S(1)}, f32[4,2,32,128]{3,2,1,0:T(8,128)}, u32[]{:S(2)}) copy-start(f32[4,2,32,128]{3,2,1,0:T(8,128)} %get-tuple-element.61) | copy-start | bytes 393220
  66.8 10.8 %copy-start.26 = (f32[4,2,32,128]{3,2,1,0:T(8,128)S(1)}, f32[4,2,32,128]{3,2,1,0:T(8,128)}, u32[]{:S(2)}) copy-start(f32[4,2,32,128]{3,2,1,0:T(8,128)} %get-tuple-element.62) | copy-start | bytes 393220
  66.8 24.9 %copy-start.25 = (f32[4,2,32,128]{3,2,1,0:T(8,128)S(1)}, f32[4,2,32,128]{3,2,1,0:T(8,128)}, u32[]{:S(2)}) copy-start(f32[4,2,32,128]{3,2,1,0:T(8,128)} %get-tuple-element.63) | copy-start | bytes 393220
  66.8 71.0 %all-to-all-start.1 = ((f32[32,4,32,128]{3,2,1,0:T(8,128)}), f32[32,4,32,128]{3,2,1,0:T(8,128)}, u32[]{:S(2)}, u32[]{:S(2)}) async-start(f32[32,4,32,128]{3,2,1,0:T(8,128)} %get-tuple-element.64.refs_13_), calls=%async_computation.1 | async-start | bytes 4194304 | tf_op jit(solution)/shard_map/all_to_all | solution.py:504
  73.5 50.1 %copy-start = (f32[128,16]{1,0:T(8,128)S(1)}, f32[128,16]{1,0:T(8,128)}, u32[]{:S(2)}) copy-start(f32[128,16]{1,0:T(8,128)} %convolution_bitcast_fusion.refs_13_) | copy-start | bytes 24580
  73.5 4.0 %collective-permute-start.13 = (f32[4,2,32,128]{3,2,1,0:T(8,128)S(1)}, f32[4,2,32,128]{3,2,1,0:T(8,128)S(1)}, u32[]{:S(2)}, u32[]{:S(2)}) collective-permute-start(f32[4,2,32,128]{3,2,1,0:T(8,128)S(1)} %copy-done.31), channel_id=1, source_target_pairs={{0,1},{1,0},{2,3},{3,2},{4,5},{5,4},{6,7},{7,6},{8,9},{9,8},{10,11... | collective-permute-start | bytes 393224 | tf_op jit(solution)/shard_map/ppermute | solution.py:288
  73.9 17.7 %collective-permute-start.14 = (f32[4,2,32,128]{3,2,1,0:T(8,128)S(1)}, f32[4,2,32,128]{3,2,1,0:T(8,128)S(1)}, u32[]{:S(2)}, u32[]{:S(2)}) collective-permute-start(f32[4,2,32,128]{3,2,1,0:T(8,128)S(1)} %copy-done.30), channel_id=1, source_target_pairs={{0,2},{1,3},{2,0},{3,1},{4,6},{5,7},{6,4},{7,5},{8,10},{9,11},{10,... | collective-permute-start | bytes 393224 | tf_op jit(solution)/shard_map/ppermute | solution.py:288
  75.3 24.7 %collective-permute-start.15 = (f32[4,2,32,128]{3,2,1,0:T(8,128)S(1)}, f32[4,2,32,128]{3,2,1,0:T(8,128)S(1)}, u32[]{:S(2)}, u32[]{:S(2)}) collective-permute-start(f32[4,2,32,128]{3,2,1,0:T(8,128)S(1)} %copy-done.29), channel_id=1, source_target_pairs={{0,3},{1,2},{2,1},{3,0},{4,7},{5,6},{6,5},{7,4},{8,11},{9,10},{10,... | collective-permute-start | bytes 393224 | tf_op jit(solution)/shard_map/ppermute | solution.py:288
  75.7 24.3 %collective-permute-start.16 = (f32[4,2,32,128]{3,2,1,0:T(8,128)S(1)}, f32[4,2,32,128]{3,2,1,0:T(8,128)S(1)}, u32[]{:S(2)}, u32[]{:S(2)}) collective-permute-start(f32[4,2,32,128]{3,2,1,0:T(8,128)S(1)} %copy-done.28), channel_id=1, source_target_pairs={{0,4},{1,5},{2,6},{3,7},{4,0},{5,1},{6,2},{7,3},{8,12},{9,13},{10,... | collective-permute-start | bytes 393224 | tf_op jit(solution)/shard_map/ppermute | solution.py:288
  77.2 22.9 %collective-permute-start.17 = (f32[4,2,32,128]{3,2,1,0:T(8,128)S(1)}, f32[4,2,32,128]{3,2,1,0:T(8,128)S(1)}, u32[]{:S(2)}, u32[]{:S(2)}) collective-permute-start(f32[4,2,32,128]{3,2,1,0:T(8,128)S(1)} %copy-done.27), channel_id=1, source_target_pairs={{0,5},{1,4},{2,7},{3,6},{4,1},{5,0},{6,3},{7,2},{8,13},{9,12},{10,... | collective-permute-start | bytes 393224 | tf_op jit(solution)/shard_map/ppermute | solution.py:288
  77.5 30.3 %copy-start.8 = (f32[4,2,32,128]{3,2,1,0:T(8,128)}, f32[4,2,32,128]{3,2,1,0:T(8,128)S(1)}, u32[]{:S(2)}) copy-start(f32[4,2,32,128]{3,2,1,0:T(8,128)S(1)} %collective-permute-done.13.refs_1_) | copy-start | bytes 393220
  77.5 25.9 %collective-permute-start.18 = (f32[4,2,32,128]{3,2,1,0:T(8,128)S(1)}, f32[4,2,32,128]{3,2,1,0:T(8,128)S(1)}, u32[]{:S(2)}, u32[]{:S(2)}) collective-permute-start(f32[4,2,32,128]{3,2,1,0:T(8,128)S(1)} %copy-done.26), channel_id=1, source_target_pairs={{0,6},{1,7},{2,4},{3,5},{4,2},{5,3},{6,0},{7,1},{8,14},{9,15},{10,... | collective-permute-start | bytes 393224 | tf_op jit(solution)/shard_map/ppermute | solution.py:288
  91.7 16.1 %copy-start.9 = (f32[4,2,32,128]{3,2,1,0:T(8,128)}, f32[4,2,32,128]{3,2,1,0:T(8,128)S(1)}, u32[]{:S(2)}) copy-start(f32[4,2,32,128]{3,2,1,0:T(8,128)S(1)} %collective-permute-done.14.refs_2_) | copy-start | bytes 393220
  91.7 16.1 %collective-permute-start.19 = (f32[4,2,32,128]{3,2,1,0:T(8,128)S(1)}, f32[4,2,32,128]{3,2,1,0:T(8,128)S(1)}, u32[]{:S(2)}, u32[]{:S(2)}) collective-permute-start(f32[4,2,32,128]{3,2,1,0:T(8,128)S(1)} %copy-done.25), channel_id=1, source_target_pairs={{0,7},{1,6},{2,5},{3,4},{4,3},{5,2},{6,1},{7,0},{8,15},{9,14},{10,... | collective-permute-start | bytes 393224 | tf_op jit(solution)/shard_map/ppermute | solution.py:288
  100.1 7.7 %copy-start.10 = (f32[4,2,32,128]{3,2,1,0:T(8,128)}, f32[4,2,32,128]{3,2,1,0:T(8,128)S(1)}, u32[]{:S(2)}) copy-start(f32[4,2,32,128]{3,2,1,0:T(8,128)S(1)} %collective-permute-done.15.refs_3_) | copy-start | bytes 393220
  100.1 7.7 %copy-start.11 = (f32[4,2,32,128]{3,2,1,0:T(8,128)}, f32[4,2,32,128]{3,2,1,0:T(8,128)S(1)}, u32[]{:S(2)}) copy-start(f32[4,2,32,128]{3,2,1,0:T(8,128)S(1)} %collective-permute-done.16.refs_4_) | copy-start | bytes 393220
  100.1 7.7 %copy-start.12 = (f32[4,2,32,128]{3,2,1,0:T(8,128)}, f32[4,2,32,128]{3,2,1,0:T(8,128)S(1)}, u32[]{:S(2)}) copy-start(f32[4,2,32,128]{3,2,1,0:T(8,128)S(1)} %collective-permute-done.17.refs_5_) | copy-start | bytes 393220
  103.4 4.4 %copy-start.13 = (f32[4,2,32,128]{3,2,1,0:T(8,128)}, f32[4,2,32,128]{3,2,1,0:T(8,128)S(1)}, u32[]{:S(2)}) copy-start(f32[4,2,32,128]{3,2,1,0:T(8,128)S(1)} %collective-permute-done.18.refs_6_) | copy-start | bytes 393220
  123.7 33.8 %copy-start.32 = (s32[8,8]{1,0:T(8,128)S(1)}, s32[8,8]{1,0:T(8,128)}, u32[]{:S(2)}) copy-start(s32[8,8]{1,0:T(8,128)} %param.15) | copy-start | bytes 772
  123.7 1.3 collective-permute-start.20
  125.1 5.0 %collective-permute-start.21 = (f32[136,16]{1,0:T(8,128)S(1)}, f32[136,16]{1,0:T(8,128)S(1)}, u32[]{:S(2)}, u32[]{:S(2)}) collective-permute-start(f32[136,16]{1,0:T(8,128)S(1)} %fusion.57), channel_id=1, source_target_pairs={{0,2},{1,3},{2,0},{3,1},{4,6},{5,7},{6,4},{7,5},{8,10},{9,11},{10,... | collective-permute-start | bytes 26120 | tf_op jit(solution)/shard_map/ppermute | solution.py:288
  130.1 3.2 %collective-permute-start.22 = (f32[136,16]{1,0:T(8,128)S(1)}, f32[136,16]{1,0:T(8,128)S(1)}, u32[]{:S(2)}, u32[]{:S(2)}) collective-permute-start(f32[136,16]{1,0:T(8,128)S(1)} %add.130), channel_id=1, source_target_pairs={{0,4},{1,5},{2,6},{3,7},{4,0},{5,1},{6,2},{7,3},{8,12},{9,13},{10,... | collective-permute-start | bytes 26120 | tf_op jit(solution)/shard_map/ppermute | solution.py:288
  133.3 10.6 %copy-start.1 = (f32[136,16]{1,0:T(8,128)}, f32[136,16]{1,0:T(8,128)S(1)}, u32[]{:S(2)}) copy-start(f32[136,16]{1,0:T(8,128)S(1)} %add.131.refs_0_) | copy-start | bytes 26116
  133.3 10.6 %collective-permute-start.25 = (f32[136,16]{1,0:T(8,128)S(1)}, f32[136,16]{1,0:T(8,128)S(1)}, u32[]{:S(2)}, u32[]{:S(2)}) collective-permute-start(f32[136,16]{1,0:T(8,128)S(1)} %add.131.refs_0_), channel_id=1, source_target_pairs={{0,24},{1,25},{2,26},{3,27},{4,28},{5,29},{6,30},{7,31},{8,16},{9,... | collective-permute-start | bytes 26120 | tf_op jit(solution)/shard_map/ppermute | solution.py:288
  135.4 8.5 %collective-permute-start.24 = (f32[136,16]{1,0:T(8,128)S(1)}, f32[136,16]{1,0:T(8,128)S(1)}, u32[]{:S(2)}, u32[]{:S(2)}) collective-permute-start(f32[136,16]{1,0:T(8,128)S(1)} %add.131.refs_0_), channel_id=1, source_target_pairs={{0,16},{1,17},{2,18},{3,19},{4,20},{5,21},{6,22},{7,23},{8,24},{9,... | collective-permute-start | bytes 26120 | tf_op jit(solution)/shard_map/ppermute | solution.py:288
  135.4 8.6 %collective-permute-start.23 = (f32[136,16]{1,0:T(8,128)S(1)}, f32[136,16]{1,0:T(8,128)S(1)}, u32[]{:S(2)}, u32[]{:S(2)}) collective-permute-start(f32[136,16]{1,0:T(8,128)S(1)} %add.131.refs_0_), channel_id=1, source_target_pairs={{0,8},{1,9},{2,10},{3,11},{4,12},{5,13},{6,14},{7,15},{8,0},{9,1},... | collective-permute-start | bytes 26120 | tf_op jit(solution)/shard_map/ppermute | solution.py:288
  137.8 54.4 %all-to-all-start = ((f32[32,4,32,128]{3,2,1,0:T(8,128)}), f32[32,4,32,128]{3,2,1,0:T(8,128)}, u32[]{:S(2)}, u32[]{:S(2)}) async-start(f32[32,4,32,128]{3,2,1,0:T(8,128)} %get-tuple-element.65), calls=%async_computation | async-start | bytes 4194304 | tf_op jit(solution)/shard_map/all_to_all | solution.py:504
  (13 other events, 11.7 us)

commit v12 on v7

--- a/solution.py
+++ b/solution.py
@@ -116,38 +116,38 @@
     span_x = devices * planes
     arrived = recv.reshape(devices * size, span_z)
     leaving = back.reshape(devices * 2 * size, span_z)
-    for group in groups(rows, span_z):
-        columns = [
-            jnp.concatenate(
-                [
-                    arrived[pl.ds((p * rows + r) * 2 + part, devices, stride=size), :]
-                    for part in range(2)
-                    for p in range(planes)
-                ],
-                axis=0,
-            )
-            for r in group
-        ]
-        along_x = dot_left(inverse[...], jnp.concatenate(columns, axis=1))
-        spatial = dot_right(parts_in_lanes(along_x, span_x, span_z), inv_z[...])
-        here = slice(group[0] * span_x, (group[-1] + 1) * span_x)
-        for band in range(2):
-            one = spatial[:, band * span_z : (band + 1) * span_z]
-            field[band, here, :] = one
-            product = one * pot[here, :]
-            product = jnp.concatenate(
-                [product[i * span_x : (i + 1) * span_x] for i in range(len(group))], axis=1
-            )
-            spectral = dot_left(forward[...], product)
-            spectral = dot_right(parts_in_lanes(spectral, span_x, span_z), fwd_z[...])
-            for i, r in enumerate(group):
-                for p in range(planes):
-                    first = i * span_x + p * devices
-                    for part in range(2):
-                        start = band * size + (p * rows + r) * 2 + part
-                        leaving[pl.ds(start, devices, stride=2 * size), :] = spectral[
-                            first : first + devices, part * span_z : (part + 1) * span_z
-                        ]
+    columns = [
+        jnp.concatenate(
+            [
+                arrived[pl.ds((p * rows + r) * 2 + part, devices, stride=size), :]
+                for part in range(2)
+                for p in range(planes)
+            ],
+            axis=0,
+        )
+        for r in range(rows)
+    ]
+    along_x = dot_left(inverse[...], jnp.concatenate(columns, axis=1))
+    spatial = dot_right(parts_in_lanes(along_x, span_x, span_z), inv_z[...])
+    spectral = []
+    for band in range(2):
+        one = spatial[:, band * span_z : (band + 1) * span_z]
+        field[band] = one
+        product = one * pot[...]
+        product = jnp.concatenate(
+            [product[r * span_x : (r + 1) * span_x] for r in range(rows)], axis=1
+        )
+        spectral.append(parts_in_lanes(dot_left(forward[...], product), span_x, span_z))
+    spectral = dot_right(jnp.concatenate(spectral, axis=0), fwd_z[...])
+    for band in range(2):
+        for r in range(rows):
+            for p in range(planes):
+                first = ((band * rows + r) * planes + p) * devices
+                for part in range(2):
+                    start = band * size + (p * rows + r) * 2 + part
+                    leaving[pl.ds(start, devices, stride=2 * size), :] = spectral[
+                        first : first + devices, part * span_z : (part + 1) * span_z
+                    ]
 
 
 def real_gram_kernel(bands, *refs):
@@ -178,7 +178,8 @@
             out[weighted, b, a : a + 1, :] = line
 
 
-def to_planes_kernel(recv, base, y_table, out):
+def to_planes_kernel(recv, base, y_table, *refs):
+    out = refs[-1]
     bands, _, planes, span_y, span_z = base.shape
     each = recv.shape[2] // planes
     for band in range(bands):
@@ -195,9 +196,8 @@
                     )
 
 
-def last_sum_kernel(*refs):
-    first, second, third, fourth, _, out = refs
-    out[...] = (first[...] + second[...]) + (third[...] + fourth[...])
+def last_sum_kernel(first, second, _, out):
+    out[...] = first[...] + second[...]
 
 
 def block_rows_of(psi, beta, slots):
@@ -264,21 +264,20 @@
 
 
 def sum_over(values, devices, after):
-    if devices & (devices - 1) or devices < 4:
+    if devices & (devices - 1) or devices < 2:
         return lax.psum(values, "ga")
     step = 1
-    while step < devices // 4:
+    while step < devices // 2:
         values = values + partner(values, devices, step)
         step *= 2
-    others = [partner(values, devices, k * step) for k in (1, 2, 3)]
     held = pl.BlockSpec(memory_space=pltpu.VMEM)
     return pl.pallas_call(
         last_sum_kernel,
         out_shape=jax.ShapeDtypeStruct(values.shape, f32),
-        in_specs=[held] * 4 + [pl.BlockSpec(memory_space=pl.ANY)],
+        in_specs=[held] * 2 + [pl.BlockSpec(memory_space=pl.ANY)],
         out_specs=held,
         name="last_sum",
-    )(values, *others, after)
+    )(values, partner(values, devices, step), after)
 
 
 def on_device(devices, orbitals, plane_order, potential, projectors, slot_owner, strengths):
@@ -298,6 +297,7 @@
     grid_y = jnp.arange(span_y, dtype=jnp.int32)
     grid_z = jnp.arange(span_z, dtype=jnp.int32)
     params = pltpu.CompilerParams(vmem_limit_bytes=vmem_limit)
+    tail_params = pltpu.CompilerParams(vmem_limit_bytes=vmem_limit // 2)
 
     def cost(flops, moved):
         return pl.CostEstimate(flops=flops, bytes_accessed=moved, transcendentals=0)
@@ -459,12 +459,12 @@
         in_specs=block_specs
         + [pl.BlockSpec((None, 2 * bands, 2 * bands + 2 * slots), lambda g: (g, 0, 0))],
         out_specs=block_specs[0],
-        compiler_params=params,
+        compiler_params=tail_params,
         cost_estimate=cost(8 * 10**9, 12 * 10**6),
         name="base",
     )(orbitals, beta, kinetic, coefs)
 
-    residual = base
+    earlier = []
     for c in range(parts):
         two_bands = pl.BlockSpec(
             (2, 2, planes, span_y, span_z), lambda j, c=c: (share * c + j, 0, 0, 0, 0)
@@ -477,13 +477,15 @@
                 pl.BlockSpec((devices, 2, block_rows, span_z), lambda j: (0, j, 0, 0)),
                 two_bands,
                 whole(fwd_y.shape),
-            ],
+            ]
+            + [pl.BlockSpec(memory_space=pl.ANY)] * len(earlier),
             out_specs=two_bands,
-            input_output_aliases={1: 0},
-            compiler_params=params,
+            input_output_aliases={3: 0} if earlier else {},
+            compiler_params=tail_params,
             cost_estimate=cost(8 * 10**9, 12 * 10**6),
             name="to_planes",
-        )(returned[c], residual, fwd_y)
+        )(returned[c], base, fwd_y, *earlier)
+        earlier = [residual]
     return (residual, jnp.stack([m_real, m_imag]))
 
 

time: 181 us -> 180 us (level)
  local copies, waits for them, and re-layouts: 6.07 us -> 14 us
  Pallas kernels: 59 us -> 52.8 us
  waiting for transfers between devices: 64.7 us -> 60.6 us
  starting transfers between devices: 32.7 us -> 34.8 us
    all_to_all x2, waiting for transfers between devices: 36.4 us -> 26.1 us  [on_device(): lax.all_to_all(back, 'ga', split_axis=0, concat_axis=0, tiled=True)]
    unnamed x26 -> x34, local copies, waits for them, and re-layouts: 1.76 us -> 9.65 us
    ppermute x6 -> x5, waiting for transfers between devices: 5.58 us -> 11.2 us  [partner(): return lax.ppermute(values, 'ga', [(d, d ^ k) for d in range(devices)])]
    pallas_call x1, Pallas kernels: 11.2 us -> 8.15 us  [on_device(): pl.pallas_call(functools.partial(base_kernel, slots), out_shape=jax.Shape...]
    ppermute x6 -> x5, starting transfers between devices: 11.7 us -> 13.8 us  [partner(): return lax.ppermute(values, 'ga', [(d, d ^ k) for d in range(devices)])]
    pallas_call x2, Pallas kernels: 7.73 us -> 5.74 us  [on_device(): pl.pallas_call(to_planes_kernel, out_shape=jax.ShapeDtypeStruct(orbitals....]
  transfers between devices with their start and end apart: 10 -> 9, of which waited for: 7 -> 8; matrix products, arithmetic and copies ran while one was open for 11% -> 11% of each run, Pallas kernels for 29% -> 27%
where the time goes in v12:
time: 180 us; the launch traced here: 178 us
  waiting for transfers between devices  60.6 us (34%)
  Pallas kernels  52.8 us (29%)
  starting transfers between devices  34.8 us (19%)
  local copies, waits for them, and re-layouts  14 us (8%)
  other arithmetic  8.88 us (5%)
  matrix products  6.02 us (3%)
    all_to_all x2, waiting for transfers between devices, on_device(): lax.all_to_all(back, 'ga', split_axis=0, concat_axis=0, tiled=True)  26.1 us
    all_to_all x2, waiting for transfers between devices, on_device(): lax.all_to_all(sent, 'ga', split_axis=0, concat_axis=0, tiled=True)  23.3 us
    pallas_call x2, Pallas kernels, on_device(): pl.pallas_call(functools.partial(real_space_kernel, rows, planes), out_sh...  16.2 us
    ppermute x5, starting transfers between devices, partner(): return lax.ppermute(values, 'ga', [(d, d ^ k) for d in range(devices)])  13.8 us
    all_to_all x2, starting transfers between devices, on_device(): lax.all_to_all(sent, 'ga', split_axis=0, concat_axis=0, tiled=True)  11.7 us
    ppermute x5, waiting for transfers between devices, partner(): return lax.ppermute(values, 'ga', [(d, d ^ k) for d in range(devices)])  11.2 us
    pallas_call x1, Pallas kernels, on_device(): pl.pallas_call(functools.partial(project_kernel, slots), out_shape=jax.Sh...  10.1 us
    unnamed x34, local copies, waits for them, and re-layouts  9.65 us
  transfers between devices with their start and end apart: 9, of which 8 were waited for; matrix products, arithmetic and copies ran while one was open for 11% of the time, Pallas kernels for 27%

profile of v12, /device:TPU:1, one launch (start us, length us, event | category | flops | bytes accessed | tf_op | source)
XLA Modules:
  0.0 178.0 jit_solution(17437034489446073593)
XLA Ops:
  0.6 3.0 %to_rows.3 = f32[32,2,32,128]{3,2,1,0:T(8,128)} custom-call(f32[8,2,4,128,128]{4,3,2,1,0:T(8,128)} %psi.7, bf16[256,768]{1,0:T(8,128)(2,1)} %constant.99.clone.y_table), custom_call_target="tpu_custom_call" | custom-call | flops 4000000000 | bytes 3000000 | tf_op jit(solution)/shard_map/to_rows/pallas_call | solution.py:316
  3.6 7.1 %all-to-all-start.2 = ((f32[32,2,32,128]{3,2,1,0:T(8,128)}), f32[32,2,32,128]{3,2,1,0:T(8,128)}, u32[]{:S(2)}, u32[]{:S(2)}) async-start(f32[32,2,32,128]{3,2,1,0:T(8,128)} %to_rows.3), calls=%async_computation.2 | async-start | bytes 2097152 | tf_op jit(solution)/shard_map/all_to_all | solution.py:331
  11.5 0.9 copy.117.inverse
  12.5 0.9 add_multiply_fusion.kinetic
  13.4 3.0 %to_rows.2 = f32[32,2,32,128]{3,2,1,0:T(8,128)} custom-call(f32[8,2,4,128,128]{4,3,2,1,0:T(8,128)} %psi.7, bf16[256,768]{1,0:T(8,128)(2,1)} %constant.99.clone.y_table), custom_call_target="tpu_custom_call" | custom-call | flops 4000000000 | bytes 3000000 | tf_op jit(solution)/shard_map/to_rows/pallas_call | solution.py:316
  16.4 19.7 %all-to-all-done.2.recv = f32[32,2,32,128]{3,2,1,0:T(8,128)} async-done(((f32[32,2,32,128]{3,2,1,0:T(8,128)}), f32[32,2,32,128]{3,2,1,0:T(8,128)}, u32[]{:S(2)}, u32[]{:S(2)}) %all-to-all-start.2) | async-done | bytes 1048608 | tf_op jit(solution)/shard_map/all_to_all | solution.py:331
  36.1 4.6 %all-to-all-start = ((f32[32,2,32,128]{3,2,1,0:T(8,128)}), f32[32,2,32,128]{3,2,1,0:T(8,128)}, u32[]{:S(2)}, u32[]{:S(2)}) async-start(f32[32,2,32,128]{3,2,1,0:T(8,128)} %to_rows.2), calls=%async_computation | async-start | bytes 2097152 | tf_op jit(solution)/shard_map/all_to_all | solution.py:331
  40.7 10.1 %project.1 = f32[8,32,16]{2,1,0:T(8,128)} custom-call(f32[8,2,4,128,128]{4,3,2,1,0:T(8,128)} %psi.7, f32[8,1024,128]{2,1,0:T(8,128)} %bitcast.74, f32[4,128,128]{2,1,0:T(8,128)} %add_multiply_fusion.kinetic), custom_call_target="tpu_custom_call" | custom-call | flops 8000000000 | bytes 8000000 | tf_op jit(solution)/shard_map/project/pallas_call | solution.py:363
  50.8 0.8 fusion.47
  52.1 0.7 copy.108
  52.9 0.7 pad_maximum_fusion.1.forward
  53.6 1.0 convolution_bitcast_fusion._
  54.6 8.0 %real_space.3 = (f32[32,4,32,128]{3,2,1,0:T(8,128)}, f32[4,512,128]{2,1,0:T(8,128)}) custom-call(f32[32,2,32,128]{3,2,1,0:T(8,128)} %all-to-all-done.2.recv, f32[512,128]{1,0:T(8,128)} %bitcast.76, bf16[256,768]{1,0:T(8,128)(2,1)} %copy.117.inverse, bf16[256,384]{1,0:T(8,128)(2,1)} %pad_maximum_fusion.1.forward, bf16[768,256]{1,0:T(8,128)(2,1)} %constant.101.clone.inv_z, ...), custom_call_target="tpu_custom_call" | custom-call | flops 4000000000 | bytes 8000000 | tf_op jit(solution)/shard_map/real_space/pallas_call | solution.py:391
  62.5 3.6 %all-to-all-done.recv = f32[32,2,32,128]{3,2,1,0:T(8,128)} async-done(((f32[32,2,32,128]{3,2,1,0:T(8,128)}), f32[32,2,32,128]{3,2,1,0:T(8,128)}, u32[]{:S(2)}, u32[]{:S(2)}) %all-to-all-start) | async-done | bytes 1048608 | tf_op jit(solution)/shard_map/all_to_all | solution.py:331
  66.1 4.6 %all-to-all-start.3 = ((f32[32,4,32,128]{3,2,1,0:T(8,128)}), f32[32,4,32,128]{3,2,1,0:T(8,128)}, u32[]{:S(2)}, u32[]{:S(2)}) async-start(f32[32,4,32,128]{3,2,1,0:T(8,128)} %get-tuple-element.9), calls=%async_computation.3 | async-start | bytes 4194304 | tf_op jit(solution)/shard_map/all_to_all | solution.py:415
  71.0 8.2 %real_space.2 = (f32[32,4,32,128]{3,2,1,0:T(8,128)}, f32[4,512,128]{2,1,0:T(8,128)}) custom-call(f32[32,2,32,128]{3,2,1,0:T(8,128)} %all-to-all-done.recv, f32[512,128]{1,0:T(8,128)} %bitcast.77, bf16[256,768]{1,0:T(8,128)(2,1)} %copy.117.inverse, bf16[256,384]{1,0:T(8,128)(2,1)} %pad_maximum_fusion.1.forward, bf16[768,256]{1,0:T(8,128)(2,1)} %constant.101.clone.inv_z, ...), custom_call_target="tpu_custom_call" | custom-call | flops 4000000000 | bytes 8000000 | tf_op jit(solution)/shard_map/real_space/pallas_call | solution.py:391
  79.2 5.2 %real_gram.1 = f32[2,8,8,128]{3,2,1,0:T(8,128)} custom-call(f32[4,512,128]{2,1,0:T(8,128)} %get-tuple-element.7.refs_0_, f32[4,512,128]{2,1,0:T(8,128)} %get-tuple-element.8.refs_1_, f32[512,128]{1,0:T(8,128)} %bitcast.78), custom_call_target="tpu_custom_call" | custom-call | flops 10000000 | bytes 2000000 | tf_op jit(solution)/shard_map/real_gram/pallas_call | solution.py:418
  84.4 0.9 reduce_sum.18
  85.8 0.9 collective-permute-done
  86.8 1.4 collective-permute-start.1
  88.2 2.4 %collective-permute-done.1 = f32[136,16]{1,0:T(8,128)S(1)} collective-permute-done((f32[136,16]{1,0:T(8,128)S(1)}, f32[136,16]{1,0:T(8,128)S(1)}, u32[]{:S(2)}, u32[]{:S(2)}) %collective-permute-start.1) | collective-permute-done | bytes 8736 | tf_op jit(solution)/shard_map/ppermute | solution.py:263
  90.6 5.9 %collective-permute-start.2 = (f32[136,16]{1,0:T(8,128)S(1)}, f32[136,16]{1,0:T(8,128)S(1)}, u32[]{:S(2)}, u32[]{:S(2)}) collective-permute-start(f32[136,16]{1,0:T(8,128)S(1)} %add.112), channel_id=1, source_target_pairs={{0,4},{1,5},{2,6},{3,7},{4,0},{5,1},{6,2},{7,3},{8,12},{9,13},{10,... | collective-permute-start | bytes 26120 | tf_op jit(solution)/shard_map/ppermute | solution.py:263
  96.5 2.3 %collective-permute-done.2 = f32[136,16]{1,0:T(8,128)S(1)} collective-permute-done((f32[136,16]{1,0:T(8,128)S(1)}, f32[136,16]{1,0:T(8,128)S(1)}, u32[]{:S(2)}, u32[]{:S(2)}) %collective-permute-start.2) | collective-permute-done | bytes 8736 | tf_op jit(solution)/shard_map/ppermute | solution.py:263
  98.8 2.9 %collective-permute-start.3 = (f32[136,16]{1,0:T(8,128)S(1)}, f32[136,16]{1,0:T(8,128)S(1)}, u32[]{:S(2)}, u32[]{:S(2)}) collective-permute-start(f32[136,16]{1,0:T(8,128)S(1)} %add.113), channel_id=1, source_target_pairs={{0,8},{1,9},{2,10},{3,11},{4,12},{5,13},{6,14},{7,15},{8,0},{9,1},... | collective-permute-start | bytes 26120 | tf_op jit(solution)/shard_map/ppermute | solution.py:263
  101.7 5.5 %collective-permute-done.3 = f32[136,16]{1,0:T(8,128)S(1)} collective-permute-done((f32[136,16]{1,0:T(8,128)S(1)}, f32[136,16]{1,0:T(8,128)S(1)}, u32[]{:S(2)}, u32[]{:S(2)}) %collective-permute-start.3) | collective-permute-done | bytes 8736 | tf_op jit(solution)/shard_map/ppermute | solution.py:263
  107.3 3.3 %collective-permute-start.4 = (f32[136,16]{1,0:T(8,128)S(1)}, f32[136,16]{1,0:T(8,128)S(1)}, u32[]{:S(2)}, u32[]{:S(2)}) collective-permute-start(f32[136,16]{1,0:T(8,128)S(1)} %add.114.first), channel_id=1, source_target_pairs={{0,16},{1,17},{2,18},{3,19},{4,20},{5,21},{6,22},{7,23},{8,24},{9,... | collective-permute-start | bytes 26120 | tf_op jit(solution)/shard_map/ppermute | solution.py:263
  110.7 9.8 %all-to-all-done.3._.recv = f32[32,4,32,128]{3,2,1,0:T(8,128)} async-done(((f32[32,4,32,128]{3,2,1,0:T(8,128)}), f32[32,4,32,128]{3,2,1,0:T(8,128)}, u32[]{:S(2)}, u32[]{:S(2)}) %all-to-all-start.3) | async-done | bytes 2097184 | tf_op jit(solution)/shard_map/all_to_all | solution.py:415
  120.5 4.7 %all-to-all-start.1 = ((f32[32,4,32,128]{3,2,1,0:T(8,128)}), f32[32,4,32,128]{3,2,1,0:T(8,128)S(1)}, u32[]{:S(2)}, u32[]{:S(2)}) async-start(f32[32,4,32,128]{3,2,1,0:T(8,128)} %get-tuple-element.6), calls=%async_computation.1 | async-start | bytes 4194304 | tf_op jit(solution)/shard_map/all_to_all | solution.py:415
  125.8 1.5 last_sum.1
  127.4 0.7 slice.119
  128.1 0.9 slice_multiply_fusion
  129.0 1.1 fusion.10
  130.1 1.1 fusion.16
  131.3 0.9 fusion.37
  132.1 0.7 cholesky.16
  132.9 0.6 compare_reduce_fusion
  133.5 0.6 fusion.27
  134.2 0.6 custom-call.10
  134.8 1.1 fusion.12
  135.9 1.1 convolution_subtract_fusion
  139.3 2.2 %copy-done.1 = f32[8,2,4,128,128]{4,3,2,1,0:T(8,128)S(1)} copy-done((f32[8,2,4,128,128]{4,3,2,1,0:T(8,128)S(1)}, f32[8,2,4,128,128]{4,3,2,1,0:T(8,128)}, u32[]{:S(2)}) %copy-start.1) | copy-done | bytes 4194328
  141.5 2.2 %copy-done.2 = f32[8,8,2,8192]{3,2,1,0:T(2,128)S(1)} copy-done((f32[8,8,2,8192]{3,2,1,0:T(2,128)S(1)}, f32[8,8,2,8192]{3,2,1,0:T(2,128)}, u32[]{:S(2)}) %copy-start.2) | copy-done | bytes 4194328
  143.7 8.1 %base.1 = f32[8,2,4,128,128]{4,3,2,1,0:T(8,128)S(1)} custom-call(f32[8,2,4,128,128]{4,3,2,1,0:T(8,128)S(1)} %copy-done.1, f32[8,1024,128]{2,1,0:T(8,128)S(1)} %bitcast.75, f32[4,128,128]{2,1,0:T(8,128)S(1)} %copy-done, f32[8,16,32]{2,1,0:T(8,128)S(1)} %pad_maximum_fusion.4.coefs), custom_call_target="tpu_custom_call" | custom-call | flops 8000000000 | bytes 12000000 | tf_op jit(solution)/shard_map/base/pallas_call | solution.py:455
  151.8 3.4 %to_planes.2.refs_0_ = f32[8,2,4,128,128]{4,3,2,1,0:T(8,128)} custom-call(f32[32,4,32,128]{3,2,1,0:T(8,128)} %all-to-all-done.3._.recv, f32[8,2,4,128,128]{4,3,2,1,0:T(8,128)S(1)} %base.1, bf16[256,768]{1,0:T(8,128)(2,1)S(1)} %copy-done.3), custom_call_target="tpu_custom_call" | custom-call | flops 8000000000 | bytes 12000000 | tf_op jit(solution)/shard_map/to_planes/pallas_call | solution.py:472
  155.2 1.9 %copy-done.4 = f32[8,2,4,128,128]{4,3,2,1,0:T(8,128)} copy-done((f32[8,2,4,128,128]{4,3,2,1,0:T(8,128)}, f32[8,2,4,128,128]{4,3,2,1,0:T(8,128)S(1)}, u32[]{:S(2)}) %copy-start.4) | copy-done | bytes 4194328
  157.2 16.3 %all-to-all-done.1.recv = f32[32,4,32,128]{3,2,1,0:T(8,128)S(1)} async-done(((f32[32,4,32,128]{3,2,1,0:T(8,128)}), f32[32,4,32,128]{3,2,1,0:T(8,128)S(1)}, u32[]{:S(2)}, u32[]{:S(2)}) %all-to-all-start.1) | async-done | bytes 2097184 | tf_op jit(solution)/shard_map/all_to_all | solution.py:415
  173.5 2.2 %copy-done.5 = f32[8,2,4,128,128]{4,3,2,1,0:T(8,128)S(1)} copy-done((f32[8,2,4,128,128]{4,3,2,1,0:T(8,128)S(1)}, f32[8,2,4,128,128]{4,3,2,1,0:T(8,128)}, u32[]{:S(2)}) %copy-start.5) | copy-done | bytes 4194328
  175.7 2.3 %to_planes.3 = f32[8,2,4,128,128]{4,3,2,1,0:T(8,128)} custom-call(f32[32,4,32,128]{3,2,1,0:T(8,128)S(1)} %all-to-all-done.1.recv, f32[8,2,4,128,128]{4,3,2,1,0:T(8,128)S(1)} %copy-done.5, bf16[256,768]{1,0:T(8,128)(2,1)S(1)} %copy-done.3, f32[8,2,4,128,128]{4,3,2,1,0:T(8,128)} %to_planes.2.refs_0_), custom_call_target="tpu_custom_call", output_to_operand_aliasing={{}: (3, {})} | custom-call | flops 8000000000 | bytes 12000000 | tf_op jit(solution)/shard_map/to_planes/pallas_call | solution.py:472
  (78 shorter events, 5.3 us)
Async XLA Ops:
  0.6 10.1 %copy-start.12 = (s32[128]{0:T(128)S(1)}, s32[128]{0:T(128)}, u32[]{:S(2)}) copy-start(s32[128]{0:T(128)} %param.11) | copy-start | bytes 1540
  3.6 32.5 %all-to-all-start.2 = ((f32[32,2,32,128]{3,2,1,0:T(8,128)}), f32[32,2,32,128]{3,2,1,0:T(8,128)}, u32[]{:S(2)}, u32[]{:S(2)}) async-start(f32[32,2,32,128]{3,2,1,0:T(8,128)} %to_rows.3), calls=%async_computation.2 | async-start | bytes 2097152 | tf_op jit(solution)/shard_map/all_to_all | solution.py:331
  36.1 30.0 %all-to-all-start = ((f32[32,2,32,128]{3,2,1,0:T(8,128)}), f32[32,2,32,128]{3,2,1,0:T(8,128)}, u32[]{:S(2)}, u32[]{:S(2)}) async-start(f32[32,2,32,128]{3,2,1,0:T(8,128)} %to_rows.2), calls=%async_computation | async-start | bytes 2097152 | tf_op jit(solution)/shard_map/all_to_all | solution.py:331
  40.7 11.4 %copy-start.7 = (f32[128,4,128]{2,1,0:T(4,128)S(1)}, f32[128,4,128]{2,1,0:T(4,128)}, u32[]{:S(2)}) copy-start(f32[128,4,128]{2,1,0:T(4,128)} %param.12) | copy-start | bytes 786436
  40.7 12.9 %copy-start.13 = (s32[8,8]{1,0:T(8,128)S(1)}, s32[8,8]{1,0:T(8,128)}, u32[]{:S(2)}) copy-start(s32[8,8]{1,0:T(8,128)} %param.14) | copy-start | bytes 772
  62.5 8.2 %copy-start.9 = (f32[8,32,16]{2,1,0:T(8,128)S(1)}, f32[8,32,16]{2,1,0:T(8,128)}, u32[]{:S(2)}) copy-start(f32[8,32,16]{2,1,0:T(8,128)} %project.1) | copy-start | bytes 49156
  66.1 54.4 %all-to-all-start.3 = ((f32[32,4,32,128]{3,2,1,0:T(8,128)}), f32[32,4,32,128]{3,2,1,0:T(8,128)}, u32[]{:S(2)}, u32[]{:S(2)}) async-start(f32[32,4,32,128]{3,2,1,0:T(8,128)} %get-tuple-element.9), calls=%async_computation.3 | async-start | bytes 4194304 | tf_op jit(solution)/shard_map/all_to_all | solution.py:415
  70.9 14.4 %copy-start.8 = (f32[128,16]{1,0:T(8,128)S(1)}, f32[128,16]{1,0:T(8,128)}, u32[]{:S(2)}) copy-start(f32[128,16]{1,0:T(8,128)} %convolution_bitcast_fusion._) | copy-start | bytes 24580
  71.0 39.6 %copy-start.11 = (f32[32,4]{0,1:T(4,128)S(1)}, f32[32,4]{0,1:T(4,128)}, u32[]{:S(2)}) copy-start(f32[32,4]{0,1:T(4,128)} %param.15) | copy-start | bytes 1540
  85.4 1.3 collective-permute-start
  86.8 3.8 %collective-permute-start.1 = (f32[136,16]{1,0:T(8,128)S(1)}, f32[136,16]{1,0:T(8,128)S(1)}, u32[]{:S(2)}, u32[]{:S(2)}) collective-permute-start(f32[136,16]{1,0:T(8,128)S(1)} %fusion.51), channel_id=1, source_target_pairs={{0,2},{1,3},{2,0},{3,1},{4,6},{5,7},{6,4},{7,5},{8,10},{9,11},{10,... | collective-permute-start | bytes 26120 | tf_op jit(solution)/shard_map/ppermute | solution.py:263
  90.6 8.2 %collective-permute-start.2 = (f32[136,16]{1,0:T(8,128)S(1)}, f32[136,16]{1,0:T(8,128)S(1)}, u32[]{:S(2)}, u32[]{:S(2)}) collective-permute-start(f32[136,16]{1,0:T(8,128)S(1)} %add.112), channel_id=1, source_target_pairs={{0,4},{1,5},{2,6},{3,7},{4,0},{5,1},{6,2},{7,3},{8,12},{9,13},{10,... | collective-permute-start | bytes 26120 | tf_op jit(solution)/shard_map/ppermute | solution.py:263
  98.8 8.4 %collective-permute-start.3 = (f32[136,16]{1,0:T(8,128)S(1)}, f32[136,16]{1,0:T(8,128)S(1)}, u32[]{:S(2)}, u32[]{:S(2)}) collective-permute-start(f32[136,16]{1,0:T(8,128)S(1)} %add.113), channel_id=1, source_target_pairs={{0,8},{1,9},{2,10},{3,11},{4,12},{5,13},{6,14},{7,15},{8,0},{9,1},... | collective-permute-start | bytes 26120 | tf_op jit(solution)/shard_map/ppermute | solution.py:263
  107.3 17.9 %copy-start.6 = (f32[136,16]{1,0:T(8,128)}, f32[136,16]{1,0:T(8,128)S(1)}, u32[]{:S(2)}) copy-start(f32[136,16]{1,0:T(8,128)S(1)} %add.114.first) | copy-start | bytes 26116
  107.3 17.9 %collective-permute-start.4 = (f32[136,16]{1,0:T(8,128)S(1)}, f32[136,16]{1,0:T(8,128)S(1)}, u32[]{:S(2)}, u32[]{:S(2)}) collective-permute-start(f32[136,16]{1,0:T(8,128)S(1)} %add.114.first), channel_id=1, source_target_pairs={{0,16},{1,17},{2,18},{3,19},{4,20},{5,21},{6,22},{7,23},{8,24},{9,... | collective-permute-start | bytes 26120 | tf_op jit(solution)/shard_map/ppermute | solution.py:263
  120.5 18.8 %copy-start = (f32[4,128,128]{2,1,0:T(8,128)S(1)}, f32[4,128,128]{2,1,0:T(8,128)}, u32[]{:S(2)}) copy-start(f32[4,128,128]{2,1,0:T(8,128)} %add_multiply_fusion.kinetic) | copy-start | bytes 786436
  120.5 53.0 %all-to-all-start.1 = ((f32[32,4,32,128]{3,2,1,0:T(8,128)}), f32[32,4,32,128]{3,2,1,0:T(8,128)S(1)}, u32[]{:S(2)}, u32[]{:S(2)}) async-start(f32[32,4,32,128]{3,2,1,0:T(8,128)} %get-tuple-element.6), calls=%async_computation.1 | async-start | bytes 4194304 | tf_op jit(solution)/shard_map/all_to_all | solution.py:415
  125.2 0.6 copy-start.10
  139.3 2.2 %copy-start.1 = (f32[8,2,4,128,128]{4,3,2,1,0:T(8,128)S(1)}, f32[8,2,4,128,128]{4,3,2,1,0:T(8,128)}, u32[]{:S(2)}) copy-start(f32[8,2,4,128,128]{4,3,2,1,0:T(8,128)} %psi.7) | copy-start | bytes 12582916
  141.5 2.2 %copy-start.2 = (f32[8,8,2,8192]{3,2,1,0:T(2,128)S(1)}, f32[8,8,2,8192]{3,2,1,0:T(2,128)}, u32[]{:S(2)}) copy-start(f32[8,8,2,8192]{3,2,1,0:T(2,128)} %param.13) | copy-start | bytes 12582916
  143.7 8.2 %copy-start.3 = (bf16[256,768]{1,0:T(8,128)(2,1)S(1)}, bf16[256,768]{1,0:T(8,128)(2,1)}, u32[]{:S(2)}) copy-start(bf16[256,768]{1,0:T(8,128)(2,1)} %constant.100.clone.y_table) | copy-start | bytes 1179652
  155.2 1.9 %copy-start.4 = (f32[8,2,4,128,128]{4,3,2,1,0:T(8,128)}, f32[8,2,4,128,128]{4,3,2,1,0:T(8,128)S(1)}, u32[]{:S(2)}) copy-start(f32[8,2,4,128,128]{4,3,2,1,0:T(8,128)S(1)} %base.1) | copy-start | bytes 12582916
  173.5 2.2 %copy-start.5 = (f32[8,2,4,128,128]{4,3,2,1,0:T(8,128)S(1)}, f32[8,2,4,128,128]{4,3,2,1,0:T(8,128)}, u32[]{:S(2)}) copy-start(f32[8,2,4,128,128]{4,3,2,1,0:T(8,128)} %copy-done.4) | copy-start | bytes 12582916

commit v13 on v12

--- a/solution.py
+++ b/solution.py
@@ -178,8 +178,7 @@
             out[weighted, b, a : a + 1, :] = line
 
 
-def to_planes_kernel(recv, base, y_table, *refs):
-    out = refs[-1]
+def to_planes_kernel(recv, base, y_table, out):
     bands, _, planes, span_y, span_z = base.shape
     each = recv.shape[2] // planes
     for band in range(bands):
@@ -464,7 +463,7 @@
         name="base",
     )(orbitals, beta, kinetic, coefs)
 
-    earlier = []
+    residual = base
     for c in range(parts):
         two_bands = pl.BlockSpec(
             (2, 2, planes, span_y, span_z), lambda j, c=c: (share * c + j, 0, 0, 0, 0)
@@ -477,15 +476,13 @@
                 pl.BlockSpec((devices, 2, block_rows, span_z), lambda j: (0, j, 0, 0)),
                 two_bands,
                 whole(fwd_y.shape),
-            ]
-            + [pl.BlockSpec(memory_space=pl.ANY)] * len(earlier),
+            ],
             out_specs=two_bands,
-            input_output_aliases={3: 0} if earlier else {},
+            input_output_aliases={1: 0},
             compiler_params=tail_params,
             cost_estimate=cost(8 * 10**9, 12 * 10**6),
             name="to_planes",
-        )(returned[c], base, fwd_y, *earlier)
-        earlier = [residual]
+        )(returned[c], residual, fwd_y)
     return (residual, jnp.stack([m_real, m_imag]))
 
 

time: 180 us -> 179 us (level)
  local copies, waits for them, and re-layouts: 14 us -> 9.86 us
  Pallas kernels: 52.8 us -> 54.7 us
    unnamed x34 -> x30, local copies, waits for them, and re-layouts: 9.65 us -> 5.52 us
where the time goes in v13:
time: 179 us; the launch traced here: 177 us
  waiting for transfers between devices  61.7 us (34%)
  Pallas kernels  54.7 us (31%)
  starting transfers between devices  34.9 us (19%)
  local copies, waits for them, and re-layouts  9.86 us (6%)
  other arithmetic  8.86 us (5%)
  matrix products  6.03 us (3%)
    all_to_all x2, waiting for transfers between devices, on_device(): lax.all_to_all(back, 'ga', split_axis=0, concat_axis=0, tiled=True)  27.2 us
    all_to_all x2, waiting for transfers between devices, on_device(): lax.all_to_all(sent, 'ga', split_axis=0, concat_axis=0, tiled=True)  23.3 us
    pallas_call x2, Pallas kernels, on_device(): pl.pallas_call(functools.partial(real_space_kernel, rows, planes), out_sh...  16.1 us
    ppermute x5, starting transfers between devices, partner(): return lax.ppermute(values, 'ga', [(d, d ^ k) for d in range(devices)])  13.9 us
    all_to_all x2, starting transfers between devices, on_device(): lax.all_to_all(sent, 'ga', split_axis=0, concat_axis=0, tiled=True)  11.7 us
    ppermute x5, waiting for transfers between devices, partner(): return lax.ppermute(values, 'ga', [(d, d ^ k) for d in range(devices)])  11.2 us
    pallas_call x1, Pallas kernels, on_device(): pl.pallas_call(functools.partial(project_kernel, slots), out_shape=jax.Sh...  10.1 us
    all_to_all x2, starting transfers between devices, on_device(): lax.all_to_all(back, 'ga', split_axis=0, concat_axis=0, tiled=True)  9.25 us
  transfers between devices with their start and end apart: 9, of which 8 were waited for; matrix products, arithmetic and copies ran while one was open for 11% of the time, Pallas kernels for 27%

profile of v13, /device:TPU:1, one launch (start us, length us, event | category | flops | bytes accessed | tf_op | source)
XLA Modules:
  0.0 176.9 jit_solution(7056523204071636796)
XLA Ops:
  0.6 3.0 %to_rows.3 = f32[32,2,32,128]{3,2,1,0:T(8,128)} custom-call(f32[8,2,4,128,128]{4,3,2,1,0:T(8,128)} %psi.7, bf16[256,768]{1,0:T(8,128)(2,1)} %constant.99.clone.y_table), custom_call_target="tpu_custom_call" | custom-call | flops 4000000000 | bytes 3000000 | tf_op jit(solution)/shard_map/to_rows/pallas_call | solution.py:315
  3.6 7.1 %all-to-all-start.2 = ((f32[32,2,32,128]{3,2,1,0:T(8,128)}), f32[32,2,32,128]{3,2,1,0:T(8,128)}, u32[]{:S(2)}, u32[]{:S(2)}) async-start(f32[32,2,32,128]{3,2,1,0:T(8,128)} %to_rows.3), calls=%async_computation.2 | async-start | bytes 2097152 | tf_op jit(solution)/shard_map/all_to_all | solution.py:330
  11.5 0.9 copy.118.inverse
  12.5 0.9 add_multiply_fusion.kinetic
  13.4 2.9 %to_rows.2 = f32[32,2,32,128]{3,2,1,0:T(8,128)} custom-call(f32[8,2,4,128,128]{4,3,2,1,0:T(8,128)} %psi.7, bf16[256,768]{1,0:T(8,128)(2,1)} %constant.99.clone.y_table), custom_call_target="tpu_custom_call" | custom-call | flops 4000000000 | bytes 3000000 | tf_op jit(solution)/shard_map/to_rows/pallas_call | solution.py:315
  16.4 19.8 %all-to-all-done.2.recv = f32[32,2,32,128]{3,2,1,0:T(8,128)} async-done(((f32[32,2,32,128]{3,2,1,0:T(8,128)}), f32[32,2,32,128]{3,2,1,0:T(8,128)}, u32[]{:S(2)}, u32[]{:S(2)}) %all-to-all-start.2) | async-done | bytes 1048608 | tf_op jit(solution)/shard_map/all_to_all | solution.py:330
  36.1 4.6 %all-to-all-start = ((f32[32,2,32,128]{3,2,1,0:T(8,128)}), f32[32,2,32,128]{3,2,1,0:T(8,128)}, u32[]{:S(2)}, u32[]{:S(2)}) async-start(f32[32,2,32,128]{3,2,1,0:T(8,128)} %to_rows.2), calls=%async_computation | async-start | bytes 2097152 | tf_op jit(solution)/shard_map/all_to_all | solution.py:330
  40.7 10.1 %project.1 = f32[8,32,16]{2,1,0:T(8,128)} custom-call(f32[8,2,4,128,128]{4,3,2,1,0:T(8,128)} %psi.7, f32[8,1024,128]{2,1,0:T(8,128)} %bitcast.74, f32[4,128,128]{2,1,0:T(8,128)} %add_multiply_fusion.kinetic), custom_call_target="tpu_custom_call" | custom-call | flops 8000000000 | bytes 8000000 | tf_op jit(solution)/shard_map/project/pallas_call | solution.py:362
  50.8 0.8 fusion.47
  52.1 0.8 copy.109
  52.9 0.7 pad_maximum_fusion.1.forward
  53.6 1.0 convolution_bitcast_fusion._
  54.6 8.0 %real_space.3 = (f32[32,4,32,128]{3,2,1,0:T(8,128)}, f32[4,512,128]{2,1,0:T(8,128)}) custom-call(f32[32,2,32,128]{3,2,1,0:T(8,128)} %all-to-all-done.2.recv, f32[512,128]{1,0:T(8,128)} %bitcast.76, bf16[256,768]{1,0:T(8,128)(2,1)} %copy.118.inverse, bf16[256,384]{1,0:T(8,128)(2,1)} %pad_maximum_fusion.1.forward, bf16[768,256]{1,0:T(8,128)(2,1)} %constant.101.clone.inv_z, ...), custom_call_target="tpu_custom_call" | custom-call | flops 4000000000 | bytes 8000000 | tf_op jit(solution)/shard_map/real_space/pallas_call | solution.py:390
  62.6 3.5 %all-to-all-done.recv = f32[32,2,32,128]{3,2,1,0:T(8,128)} async-done(((f32[32,2,32,128]{3,2,1,0:T(8,128)}), f32[32,2,32,128]{3,2,1,0:T(8,128)}, u32[]{:S(2)}, u32[]{:S(2)}) %all-to-all-start) | async-done | bytes 1048608 | tf_op jit(solution)/shard_map/all_to_all | solution.py:330
  66.1 4.6 %all-to-all-start.3 = ((f32[32,4,32,128]{3,2,1,0:T(8,128)}), f32[32,4,32,128]{3,2,1,0:T(8,128)}, u32[]{:S(2)}, u32[]{:S(2)}) async-start(f32[32,4,32,128]{3,2,1,0:T(8,128)} %get-tuple-element.7), calls=%async_computation.3 | async-start | bytes 4194304 | tf_op jit(solution)/shard_map/all_to_all | solution.py:414
  71.0 8.1 %real_space.2 = (f32[32,4,32,128]{3,2,1,0:T(8,128)}, f32[4,512,128]{2,1,0:T(8,128)}) custom-call(f32[32,2,32,128]{3,2,1,0:T(8,128)} %all-to-all-done.recv, f32[512,128]{1,0:T(8,128)} %bitcast.77, bf16[256,768]{1,0:T(8,128)(2,1)} %copy.118.inverse, bf16[256,384]{1,0:T(8,128)(2,1)} %pad_maximum_fusion.1.forward, bf16[768,256]{1,0:T(8,128)(2,1)} %constant.101.clone.inv_z, ...), custom_call_target="tpu_custom_call" | custom-call | flops 4000000000 | bytes 8000000 | tf_op jit(solution)/shard_map/real_space/pallas_call | solution.py:390
  79.1 5.2 %real_gram.1 = f32[2,8,8,128]{3,2,1,0:T(8,128)} custom-call(f32[4,512,128]{2,1,0:T(8,128)} %get-tuple-element.8.refs_0_, f32[4,512,128]{2,1,0:T(8,128)} %get-tuple-element.9.refs_1_, f32[512,128]{1,0:T(8,128)} %bitcast.78), custom_call_target="tpu_custom_call" | custom-call | flops 10000000 | bytes 2000000 | tf_op jit(solution)/shard_map/real_gram/pallas_call | solution.py:417
  84.2 0.9 reduce_sum.18
  85.6 0.9 collective-permute-done
  86.6 1.4 collective-permute-start.1
  88.0 2.4 %collective-permute-done.1 = f32[136,16]{1,0:T(8,128)S(1)} collective-permute-done((f32[136,16]{1,0:T(8,128)S(1)}, f32[136,16]{1,0:T(8,128)S(1)}, u32[]{:S(2)}, u32[]{:S(2)}) %collective-permute-start.1) | collective-permute-done | bytes 8736 | tf_op jit(solution)/shard_map/ppermute | solution.py:262
  90.4 6.1 %collective-permute-start.2 = (f32[136,16]{1,0:T(8,128)S(1)}, f32[136,16]{1,0:T(8,128)S(1)}, u32[]{:S(2)}, u32[]{:S(2)}) collective-permute-start(f32[136,16]{1,0:T(8,128)S(1)} %add.112), channel_id=1, source_target_pairs={{0,4},{1,5},{2,6},{3,7},{4,0},{5,1},{6,2},{7,3},{8,12},{9,13},{10,... | collective-permute-start | bytes 26120 | tf_op jit(solution)/shard_map/ppermute | solution.py:262
  96.5 2.3 %collective-permute-done.2 = f32[136,16]{1,0:T(8,128)S(1)} collective-permute-done((f32[136,16]{1,0:T(8,128)S(1)}, f32[136,16]{1,0:T(8,128)S(1)}, u32[]{:S(2)}, u32[]{:S(2)}) %collective-permute-start.2) | collective-permute-done | bytes 8736 | tf_op jit(solution)/shard_map/ppermute | solution.py:262
  98.8 2.8 %collective-permute-start.3 = (f32[136,16]{1,0:T(8,128)S(1)}, f32[136,16]{1,0:T(8,128)S(1)}, u32[]{:S(2)}, u32[]{:S(2)}) collective-permute-start(f32[136,16]{1,0:T(8,128)S(1)} %add.113), channel_id=1, source_target_pairs={{0,8},{1,9},{2,10},{3,11},{4,12},{5,13},{6,14},{7,15},{8,0},{9,1},... | collective-permute-start | bytes 26120 | tf_op jit(solution)/shard_map/ppermute | solution.py:262
  101.7 5.6 %collective-permute-done.3 = f32[136,16]{1,0:T(8,128)S(1)} collective-permute-done((f32[136,16]{1,0:T(8,128)S(1)}, f32[136,16]{1,0:T(8,128)S(1)}, u32[]{:S(2)}, u32[]{:S(2)}) %collective-permute-start.3) | collective-permute-done | bytes 8736 | tf_op jit(solution)/shard_map/ppermute | solution.py:262
  107.3 3.2 %collective-permute-start.4 = (f32[136,16]{1,0:T(8,128)S(1)}, f32[136,16]{1,0:T(8,128)S(1)}, u32[]{:S(2)}, u32[]{:S(2)}) collective-permute-start(f32[136,16]{1,0:T(8,128)S(1)} %add.114.first), channel_id=1, source_target_pairs={{0,16},{1,17},{2,18},{3,19},{4,20},{5,21},{6,22},{7,23},{8,24},{9,... | collective-permute-start | bytes 26120 | tf_op jit(solution)/shard_map/ppermute | solution.py:262
  110.7 9.8 %all-to-all-done.3._.recv = f32[32,4,32,128]{3,2,1,0:T(8,128)} async-done(((f32[32,4,32,128]{3,2,1,0:T(8,128)}), f32[32,4,32,128]{3,2,1,0:T(8,128)}, u32[]{:S(2)}, u32[]{:S(2)}) %all-to-all-start.3) | async-done | bytes 2097184 | tf_op jit(solution)/shard_map/all_to_all | solution.py:414
  120.5 4.7 %all-to-all-start.1 = ((f32[32,4,32,128]{3,2,1,0:T(8,128)}), f32[32,4,32,128]{3,2,1,0:T(8,128)S(1)}, u32[]{:S(2)}, u32[]{:S(2)}) async-start(f32[32,4,32,128]{3,2,1,0:T(8,128)} %get-tuple-element.6), calls=%async_computation.1 | async-start | bytes 4194304 | tf_op jit(solution)/shard_map/all_to_all | solution.py:414
  125.2 0.6 copy-done.8
  125.8 1.6 last_sum.1
  127.4 0.7 slice.119
  128.1 0.9 slice_multiply_fusion
  129.0 1.1 fusion.10
  130.1 1.1 fusion.16
  131.3 0.9 fusion.37
  132.1 0.7 cholesky.16
  132.9 0.6 compare_reduce_fusion
  133.5 0.6 fusion.27
  134.2 0.6 custom-call.10
  134.8 1.1 fusion.12
  135.9 1.1 convolution_subtract_fusion
  138.5 0.6 pad_maximum_fusion.6
  139.3 2.2 %copy-done.1 = f32[8,2,4,128,128]{4,3,2,1,0:T(8,128)S(1)} copy-done((f32[8,2,4,128,128]{4,3,2,1,0:T(8,128)S(1)}, f32[8,2,4,128,128]{4,3,2,1,0:T(8,128)}, u32[]{:S(2)}) %copy-start.1) | copy-done | bytes 4194328
  141.5 2.2 %copy-done.2 = f32[8,8,2,8192]{3,2,1,0:T(2,128)S(1)} copy-done((f32[8,8,2,8192]{3,2,1,0:T(2,128)S(1)}, f32[8,8,2,8192]{3,2,1,0:T(2,128)}, u32[]{:S(2)}) %copy-start.2) | copy-done | bytes 4194328
  143.6 8.7 %base.1 = f32[8,2,4,128,128]{4,3,2,1,0:T(8,128)} custom-call(f32[8,2,4,128,128]{4,3,2,1,0:T(8,128)S(1)} %copy-done.1, f32[8,1024,128]{2,1,0:T(8,128)S(1)} %bitcast.75, f32[4,128,128]{2,1,0:T(8,128)S(1)} %copy-done, f32[8,16,32]{2,1,0:T(8,128)S(1)} %pad_maximum_fusion.4.coefs), custom_call_target="tpu_custom_call" | custom-call | flops 8000000000 | bytes 12000000 | tf_op jit(solution)/shard_map/base/pallas_call | solution.py:454
  152.3 3.7 %to_planes.2.base = f32[8,2,4,128,128]{4,3,2,1,0:T(8,128)} custom-call(f32[32,4,32,128]{3,2,1,0:T(8,128)} %all-to-all-done.3._.recv, f32[8,2,4,128,128]{4,3,2,1,0:T(8,128)} %base.1, bf16[256,768]{1,0:T(8,128)(2,1)S(1)} %copy-done.3), custom_call_target="tpu_custom_call", output_to_operand_aliasing={{}: (1, {})} | custom-call | flops 8000000000 | bytes 12000000 | tf_op jit(solution)/shard_map/to_planes/pallas_call | solution.py:471
  156.1 17.4 %all-to-all-done.1.recv = f32[32,4,32,128]{3,2,1,0:T(8,128)S(1)} async-done(((f32[32,4,32,128]{3,2,1,0:T(8,128)}), f32[32,4,32,128]{3,2,1,0:T(8,128)S(1)}, u32[]{:S(2)}, u32[]{:S(2)}) %all-to-all-start.1) | async-done | bytes 2097184 | tf_op jit(solution)/shard_map/all_to_all | solution.py:414
  173.5 3.5 %to_planes.3 = f32[8,2,4,128,128]{4,3,2,1,0:T(8,128)} custom-call(f32[32,4,32,128]{3,2,1,0:T(8,128)S(1)} %all-to-all-done.1.recv, f32[8,2,4,128,128]{4,3,2,1,0:T(8,128)} %to_planes.2.base, bf16[256,768]{1,0:T(8,128)(2,1)S(1)} %copy-done.3), custom_call_target="tpu_custom_call", output_to_operand_aliasing={{}: (1, {})} | custom-call | flops 8000000000 | bytes 12000000 | tf_op jit(solution)/shard_map/to_planes/pallas_call | solution.py:471
  (74 shorter events, 4.1 us)
Async XLA Ops:
  0.6 10.1 %copy-start.10 = (s32[128]{0:T(128)S(1)}, s32[128]{0:T(128)}, u32[]{:S(2)}) copy-start(s32[128]{0:T(128)} %param.11) | copy-start | bytes 1540
  3.6 32.5 %all-to-all-start.2 = ((f32[32,2,32,128]{3,2,1,0:T(8,128)}), f32[32,2,32,128]{3,2,1,0:T(8,128)}, u32[]{:S(2)}, u32[]{:S(2)}) async-start(f32[32,2,32,128]{3,2,1,0:T(8,128)} %to_rows.3), calls=%async_computation.2 | async-start | bytes 2097152 | tf_op jit(solution)/shard_map/all_to_all | solution.py:330
  36.1 30.0 %all-to-all-start = ((f32[32,2,32,128]{3,2,1,0:T(8,128)}), f32[32,2,32,128]{3,2,1,0:T(8,128)}, u32[]{:S(2)}, u32[]{:S(2)}) async-start(f32[32,2,32,128]{3,2,1,0:T(8,128)} %to_rows.2), calls=%async_computation | async-start | bytes 2097152 | tf_op jit(solution)/shard_map/all_to_all | solution.py:330
  40.7 11.4 %copy-start.5 = (f32[128,4,128]{2,1,0:T(4,128)S(1)}, f32[128,4,128]{2,1,0:T(4,128)}, u32[]{:S(2)}) copy-start(f32[128,4,128]{2,1,0:T(4,128)} %param.12) | copy-start | bytes 786436
  40.7 12.9 %copy-start.11 = (s32[8,8]{1,0:T(8,128)S(1)}, s32[8,8]{1,0:T(8,128)}, u32[]{:S(2)}) copy-start(s32[8,8]{1,0:T(8,128)} %param.14) | copy-start | bytes 772
  62.6 8.1 %copy-start.7 = (f32[8,32,16]{2,1,0:T(8,128)S(1)}, f32[8,32,16]{2,1,0:T(8,128)}, u32[]{:S(2)}) copy-start(f32[8,32,16]{2,1,0:T(8,128)} %project.1) | copy-start | bytes 49156
  66.1 54.4 %all-to-all-start.3 = ((f32[32,4,32,128]{3,2,1,0:T(8,128)}), f32[32,4,32,128]{3,2,1,0:T(8,128)}, u32[]{:S(2)}, u32[]{:S(2)}) async-start(f32[32,4,32,128]{3,2,1,0:T(8,128)} %get-tuple-element.7), calls=%async_computation.3 | async-start | bytes 4194304 | tf_op jit(solution)/shard_map/all_to_all | solution.py:414
  70.9 14.2 %copy-start.6 = (f32[128,16]{1,0:T(8,128)S(1)}, f32[128,16]{1,0:T(8,128)}, u32[]{:S(2)}) copy-start(f32[128,16]{1,0:T(8,128)} %convolution_bitcast_fusion._) | copy-start | bytes 24580
  71.0 39.6 %copy-start.9 = (f32[32,4]{0,1:T(4,128)S(1)}, f32[32,4]{0,1:T(4,128)}, u32[]{:S(2)}) copy-start(f32[32,4]{0,1:T(4,128)} %param.15) | copy-start | bytes 1540
  85.3 1.3 collective-permute-start
  86.6 3.8 %collective-permute-start.1 = (f32[136,16]{1,0:T(8,128)S(1)}, f32[136,16]{1,0:T(8,128)S(1)}, u32[]{:S(2)}, u32[]{:S(2)}) collective-permute-start(f32[136,16]{1,0:T(8,128)S(1)} %fusion.51), channel_id=1, source_target_pairs={{0,2},{1,3},{2,0},{3,1},{4,6},{5,7},{6,4},{7,5},{8,10},{9,11},{10,... | collective-permute-start | bytes 26120 | tf_op jit(solution)/shard_map/ppermute | solution.py:262
  90.4 8.4 %collective-permute-start.2 = (f32[136,16]{1,0:T(8,128)S(1)}, f32[136,16]{1,0:T(8,128)S(1)}, u32[]{:S(2)}, u32[]{:S(2)}) collective-permute-start(f32[136,16]{1,0:T(8,128)S(1)} %add.112), channel_id=1, source_target_pairs={{0,4},{1,5},{2,6},{3,7},{4,0},{5,1},{6,2},{7,3},{8,12},{9,13},{10,... | collective-permute-start | bytes 26120 | tf_op jit(solution)/shard_map/ppermute | solution.py:262
  98.8 8.4 %collective-permute-start.3 = (f32[136,16]{1,0:T(8,128)S(1)}, f32[136,16]{1,0:T(8,128)S(1)}, u32[]{:S(2)}, u32[]{:S(2)}) collective-permute-start(f32[136,16]{1,0:T(8,128)S(1)} %add.113), channel_id=1, source_target_pairs={{0,8},{1,9},{2,10},{3,11},{4,12},{5,13},{6,14},{7,15},{8,0},{9,1},... | collective-permute-start | bytes 26120 | tf_op jit(solution)/shard_map/ppermute | solution.py:262
  107.3 17.9 %copy-start.4 = (f32[136,16]{1,0:T(8,128)}, f32[136,16]{1,0:T(8,128)S(1)}, u32[]{:S(2)}) copy-start(f32[136,16]{1,0:T(8,128)S(1)} %add.114.first) | copy-start | bytes 26116
  107.3 17.9 %collective-permute-start.4 = (f32[136,16]{1,0:T(8,128)S(1)}, f32[136,16]{1,0:T(8,128)S(1)}, u32[]{:S(2)}, u32[]{:S(2)}) collective-permute-start(f32[136,16]{1,0:T(8,128)S(1)} %add.114.first), channel_id=1, source_target_pairs={{0,16},{1,17},{2,18},{3,19},{4,20},{5,21},{6,22},{7,23},{8,24},{9,... | collective-permute-start | bytes 26120 | tf_op jit(solution)/shard_map/ppermute | solution.py:262
  120.5 18.8 %copy-start = (f32[4,128,128]{2,1,0:T(8,128)S(1)}, f32[4,128,128]{2,1,0:T(8,128)}, u32[]{:S(2)}) copy-start(f32[4,128,128]{2,1,0:T(8,128)} %add_multiply_fusion.kinetic) | copy-start | bytes 786436
  120.5 53.0 %all-to-all-start.1 = ((f32[32,4,32,128]{3,2,1,0:T(8,128)}), f32[32,4,32,128]{3,2,1,0:T(8,128)S(1)}, u32[]{:S(2)}, u32[]{:S(2)}) async-start(f32[32,4,32,128]{3,2,1,0:T(8,128)} %get-tuple-element.6), calls=%async_computation.1 | async-start | bytes 4194304 | tf_op jit(solution)/shard_map/all_to_all | solution.py:414
  125.2 0.6 copy-start.8
  139.3 2.2 %copy-start.1 = (f32[8,2,4,128,128]{4,3,2,1,0:T(8,128)S(1)}, f32[8,2,4,128,128]{4,3,2,1,0:T(8,128)}, u32[]{:S(2)}) copy-start(f32[8,2,4,128,128]{4,3,2,1,0:T(8,128)} %psi.7) | copy-start | bytes 12582916
  141.5 2.2 %copy-start.2 = (f32[8,8,2,8192]{3,2,1,0:T(2,128)S(1)}, f32[8,8,2,8192]{3,2,1,0:T(2,128)}, u32[]{:S(2)}) copy-start(f32[8,8,2,8192]{3,2,1,0:T(2,128)} %param.13) | copy-start | bytes 12582916
  143.6 8.7 %copy-start.3 = (bf16[256,768]{1,0:T(8,128)(2,1)S(1)}, bf16[256,768]{1,0:T(8,128)(2,1)}, u32[]{:S(2)}) copy-start(bf16[256,768]{1,0:T(8,128)(2,1)} %constant.100.clone.y_table) | copy-start | bytes 1179652

commit v14 on v12

--- a/solution.py
+++ b/solution.py
@@ -229,7 +229,7 @@
     out[height:] = rest[0:width] + rest[width:]
 
 
-def base_kernel(slots, psi, beta, kinetic, coefs, out):
+def base_kernel(slots, psi, beta, kinetic, coefs, *outs):
     bands, _, span, span_z = psi.shape
     psi_rows, beta_rows = block_rows_of(psi, beta, slots)
     values = jnp.concatenate(
@@ -237,11 +237,12 @@
     )
     high, low = split(coefs[...])
     summed = dot_left(jnp.concatenate([high, high, low], axis=1), values)
-    flat = out.reshape(bands * 2 * span, span_z)
+    height = 2 * bands // len(outs)
+    flat = [out.reshape(height * span, span_z) for out in outs]
     for y in range(span):
-        flat[pl.ds(y, 2 * bands, stride=span), :] = (
-            psi_rows[y] * kinetic[y : y + 1, :] + summed[:, y * span_z : (y + 1) * span_z]
-        )
+        values = psi_rows[y] * kinetic[y : y + 1, :] + summed[:, y * span_z : (y + 1) * span_z]
+        for i, out in enumerate(flat):
+            out[pl.ds(y, height, stride=span), :] = values[i * height : (i + 1) * height]
 
 
 def whole(shape):
@@ -452,13 +453,20 @@
     coefs = jnp.concatenate(
         [jnp.broadcast_to(from_psi, (blocks, 2 * bands, 2 * bands)), from_beta], axis=2
     )
+    held = bands // parts
     base = pl.pallas_call(
         functools.partial(base_kernel, slots),
-        out_shape=jax.ShapeDtypeStruct(orbitals.shape, f32),
+        out_shape=[jax.ShapeDtypeStruct((held,) + orbitals.shape[1:], f32)] * parts,
         grid=(blocks,),
         in_specs=block_specs
         + [pl.BlockSpec((None, 2 * bands, 2 * bands + 2 * slots), lambda g: (g, 0, 0))],
-        out_specs=block_specs[0],
+        out_specs=[
+            pl.BlockSpec(
+                (held, 2, None, block_span, span_z),
+                lambda g: (0, 0, g // per_plane, g % per_plane, 0),
+            )
+        ]
+        * parts,
         compiler_params=tail_params,
         cost_estimate=cost(8 * 10**9, 12 * 10**6),
         name="base",
@@ -466,25 +474,28 @@
 
     earlier = []
     for c in range(parts):
-        two_bands = pl.BlockSpec(
-            (2, 2, planes, span_y, span_z), lambda j, c=c: (share * c + j, 0, 0, 0, 0)
-        )
+
+        def two_bands(first):
+            return pl.BlockSpec(
+                (2, 2, planes, span_y, span_z), lambda j: (first + j, 0, 0, 0, 0)
+            )
+
         residual = pl.pallas_call(
             to_planes_kernel,
             out_shape=jax.ShapeDtypeStruct(orbitals.shape, f32),
             grid=(share,),
             in_specs=[
                 pl.BlockSpec((devices, 2, block_rows, span_z), lambda j: (0, j, 0, 0)),
-                two_bands,
+                two_bands(0),
                 whole(fwd_y.shape),
             ]
             + [pl.BlockSpec(memory_space=pl.ANY)] * len(earlier),
-            out_specs=two_bands,
+            out_specs=two_bands(share * c),
             input_output_aliases={3: 0} if earlier else {},
             compiler_params=tail_params,
             cost_estimate=cost(8 * 10**9, 12 * 10**6),
             name="to_planes",
-        )(returned[c], base, fwd_y, *earlier)
+        )(returned[c], base[c], fwd_y, *earlier)
         earlier = [residual]
     return (residual, jnp.stack([m_real, m_imag]))
 

time: 180 us -> 180 us (level)
  waiting for transfers between devices: 60.6 us -> 63.1 us
    ppermute x5, waiting for transfers between devices: 11.2 us -> 13.2 us  [partner(): return lax.ppermute(values, 'ga', [(d, d ^ k) for d in range(devices)])]
where the time goes in v14:
time: 180 us; the launch traced here: 177 us
  waiting for transfers between devices  63.1 us (35%)
  Pallas kernels  52.7 us (29%)
  starting transfers between devices  33 us (18%)
  local copies, waits for them, and re-layouts  12.8 us (7%)
  other arithmetic  8.88 us (5%)
  matrix products  6.01 us (3%)
    all_to_all x2, waiting for transfers between devices, on_device(): lax.all_to_all(back, 'ga', split_axis=0, concat_axis=0, tiled=True)  26.6 us
    all_to_all x2, waiting for transfers between devices, on_device(): lax.all_to_all(sent, 'ga', split_axis=0, concat_axis=0, tiled=True)  23.2 us
    pallas_call x2, Pallas kernels, on_device(): pl.pallas_call(functools.partial(real_space_kernel, rows, planes), out_sh...  16 us
    ppermute x5, waiting for transfers between devices, partner(): return lax.ppermute(values, 'ga', [(d, d ^ k) for d in range(devices)])  13.2 us
    ppermute x5, starting transfers between devices, partner(): return lax.ppermute(values, 'ga', [(d, d ^ k) for d in range(devices)])  12 us
    all_to_all x2, starting transfers between devices, on_device(): lax.all_to_all(sent, 'ga', split_axis=0, concat_axis=0, tiled=True)  11.7 us
    pallas_call x1, Pallas kernels, on_device(): pl.pallas_call(functools.partial(project_kernel, slots), out_shape=jax.Sh...  10.1 us
    all_to_all x2, starting transfers between devices, on_device(): lax.all_to_all(back, 'ga', split_axis=0, concat_axis=0, tiled=True)  9.25 us
  transfers between devices with their start and end apart: 9, of which 8 were waited for; matrix products, arithmetic and copies ran while one was open for 11% of the time, Pallas kernels for 27%

profile of v14, /device:TPU:1, one launch (start us, length us, event | category | flops | bytes accessed | tf_op | source)
XLA Modules:
  0.0 177.4 jit_solution(11232535572559390633)
XLA Ops:
  0.6 2.9 %to_rows.3 = f32[32,2,32,128]{3,2,1,0:T(8,128)} custom-call(f32[8,2,4,128,128]{4,3,2,1,0:T(8,128)} %psi.7, bf16[256,768]{1,0:T(8,128)(2,1)} %constant.99.clone.y_table), custom_call_target="tpu_custom_call" | custom-call | flops 4000000000 | bytes 3000000 | tf_op jit(solution)/shard_map/to_rows/pallas_call | solution.py:317
  3.6 7.2 %all-to-all-start.2 = ((f32[32,2,32,128]{3,2,1,0:T(8,128)}), f32[32,2,32,128]{3,2,1,0:T(8,128)}, u32[]{:S(2)}, u32[]{:S(2)}) async-start(f32[32,2,32,128]{3,2,1,0:T(8,128)} %to_rows.3), calls=%async_computation.2 | async-start | bytes 2097152 | tf_op jit(solution)/shard_map/all_to_all | solution.py:332
  11.5 0.9 copy.117.inverse
  12.5 0.9 add_multiply_fusion.kinetic
  13.4 3.0 %to_rows.2 = f32[32,2,32,128]{3,2,1,0:T(8,128)} custom-call(f32[8,2,4,128,128]{4,3,2,1,0:T(8,128)} %psi.7, bf16[256,768]{1,0:T(8,128)(2,1)} %constant.99.clone.y_table), custom_call_target="tpu_custom_call" | custom-call | flops 4000000000 | bytes 3000000 | tf_op jit(solution)/shard_map/to_rows/pallas_call | solution.py:317
  16.4 19.7 %all-to-all-done.2.recv = f32[32,2,32,128]{3,2,1,0:T(8,128)} async-done(((f32[32,2,32,128]{3,2,1,0:T(8,128)}), f32[32,2,32,128]{3,2,1,0:T(8,128)}, u32[]{:S(2)}, u32[]{:S(2)}) %all-to-all-start.2) | async-done | bytes 1048608 | tf_op jit(solution)/shard_map/all_to_all | solution.py:332
  36.1 4.6 %all-to-all-start = ((f32[32,2,32,128]{3,2,1,0:T(8,128)}), f32[32,2,32,128]{3,2,1,0:T(8,128)}, u32[]{:S(2)}, u32[]{:S(2)}) async-start(f32[32,2,32,128]{3,2,1,0:T(8,128)} %to_rows.2), calls=%async_computation | async-start | bytes 2097152 | tf_op jit(solution)/shard_map/all_to_all | solution.py:332
  40.7 10.1 %project.1 = f32[8,32,16]{2,1,0:T(8,128)} custom-call(f32[8,2,4,128,128]{4,3,2,1,0:T(8,128)} %psi.7, f32[8,1024,128]{2,1,0:T(8,128)} %bitcast.74, f32[4,128,128]{2,1,0:T(8,128)} %add_multiply_fusion.kinetic), custom_call_target="tpu_custom_call" | custom-call | flops 8000000000 | bytes 8000000 | tf_op jit(solution)/shard_map/project/pallas_call | solution.py:364
  50.8 0.8 fusion.47
  52.1 0.7 copy.108
  52.9 0.7 pad_maximum_fusion.1.forward
  53.6 0.9 convolution_bitcast_fusion._
  54.6 8.0 %real_space.3 = (f32[32,4,32,128]{3,2,1,0:T(8,128)}, f32[4,512,128]{2,1,0:T(8,128)}) custom-call(f32[32,2,32,128]{3,2,1,0:T(8,128)} %all-to-all-done.2.recv, f32[512,128]{1,0:T(8,128)} %bitcast.76, bf16[256,768]{1,0:T(8,128)(2,1)} %copy.117.inverse, bf16[256,384]{1,0:T(8,128)(2,1)} %pad_maximum_fusion.1.forward, bf16[768,256]{1,0:T(8,128)(2,1)} %constant.101.clone.inv_z, ...), custom_call_target="tpu_custom_call" | custom-call | flops 4000000000 | bytes 8000000 | tf_op jit(solution)/shard_map/real_space/pallas_call | solution.py:392
  62.5 3.5 %all-to-all-done.recv = f32[32,2,32,128]{3,2,1,0:T(8,128)} async-done(((f32[32,2,32,128]{3,2,1,0:T(8,128)}), f32[32,2,32,128]{3,2,1,0:T(8,128)}, u32[]{:S(2)}, u32[]{:S(2)}) %all-to-all-start) | async-done | bytes 1048608 | tf_op jit(solution)/shard_map/all_to_all | solution.py:332
  66.1 4.6 %all-to-all-start.3 = ((f32[32,4,32,128]{3,2,1,0:T(8,128)}), f32[32,4,32,128]{3,2,1,0:T(8,128)}, u32[]{:S(2)}, u32[]{:S(2)}) async-start(f32[32,4,32,128]{3,2,1,0:T(8,128)} %get-tuple-element.11), calls=%async_computation.3 | async-start | bytes 4194304 | tf_op jit(solution)/shard_map/all_to_all | solution.py:416
  70.9 8.0 %real_space.2 = (f32[32,4,32,128]{3,2,1,0:T(8,128)}, f32[4,512,128]{2,1,0:T(8,128)}) custom-call(f32[32,2,32,128]{3,2,1,0:T(8,128)} %all-to-all-done.recv, f32[512,128]{1,0:T(8,128)} %bitcast.77, bf16[256,768]{1,0:T(8,128)(2,1)} %copy.117.inverse, bf16[256,384]{1,0:T(8,128)(2,1)} %pad_maximum_fusion.1.forward, bf16[768,256]{1,0:T(8,128)(2,1)} %constant.101.clone.inv_z, ...), custom_call_target="tpu_custom_call" | custom-call | flops 4000000000 | bytes 8000000 | tf_op jit(solution)/shard_map/real_space/pallas_call | solution.py:392
  79.0 5.2 %real_gram.1 = f32[2,8,8,128]{3,2,1,0:T(8,128)} custom-call(f32[4,512,128]{2,1,0:T(8,128)} %get-tuple-element.9.refs_0_, f32[4,512,128]{2,1,0:T(8,128)} %get-tuple-element.10.refs_1_, f32[512,128]{1,0:T(8,128)} %bitcast.78), custom_call_target="tpu_custom_call" | custom-call | flops 10000000 | bytes 2000000 | tf_op jit(solution)/shard_map/real_gram/pallas_call | solution.py:419
  84.2 0.9 reduce_sum.18
  85.5 0.9 collective-permute-done
  86.5 1.4 collective-permute-start.1
  87.9 2.4 %collective-permute-done.1 = f32[136,16]{1,0:T(8,128)S(1)} collective-permute-done((f32[136,16]{1,0:T(8,128)S(1)}, f32[136,16]{1,0:T(8,128)S(1)}, u32[]{:S(2)}, u32[]{:S(2)}) %collective-permute-start.1) | collective-permute-done | bytes 8736 | tf_op jit(solution)/shard_map/ppermute | solution.py:264
  90.3 6.2 %collective-permute-start.2 = (f32[136,16]{1,0:T(8,128)S(1)}, f32[136,16]{1,0:T(8,128)S(1)}, u32[]{:S(2)}, u32[]{:S(2)}) collective-permute-start(f32[136,16]{1,0:T(8,128)S(1)} %add.112), channel_id=1, source_target_pairs={{0,4},{1,5},{2,6},{3,7},{4,0},{5,1},{6,2},{7,3},{8,12},{9,13},{10,... | collective-permute-start | bytes 26120 | tf_op jit(solution)/shard_map/ppermute | solution.py:264
  96.5 2.3 %collective-permute-done.2 = f32[136,16]{1,0:T(8,128)S(1)} collective-permute-done((f32[136,16]{1,0:T(8,128)S(1)}, f32[136,16]{1,0:T(8,128)S(1)}, u32[]{:S(2)}, u32[]{:S(2)}) %collective-permute-start.2) | collective-permute-done | bytes 8736 | tf_op jit(solution)/shard_map/ppermute | solution.py:264
  99.2 7.6 %collective-permute-done.3 = f32[136,16]{1,0:T(8,128)S(1)} collective-permute-done((f32[136,16]{1,0:T(8,128)S(1)}, f32[136,16]{1,0:T(8,128)S(1)}, u32[]{:S(2)}, u32[]{:S(2)}) %collective-permute-start.3) | collective-permute-done | bytes 8736 | tf_op jit(solution)/shard_map/ppermute | solution.py:264
  106.8 3.8 %collective-permute-start.4 = (f32[136,16]{1,0:T(8,128)S(1)}, f32[136,16]{1,0:T(8,128)S(1)}, u32[]{:S(2)}, u32[]{:S(2)}) collective-permute-start(f32[136,16]{1,0:T(8,128)S(1)} %add.114.first), channel_id=1, source_target_pairs={{0,16},{1,17},{2,18},{3,19},{4,20},{5,21},{6,22},{7,23},{8,24},{9,... | collective-permute-start | bytes 26120 | tf_op jit(solution)/shard_map/ppermute | solution.py:264
  110.7 9.8 %all-to-all-done.3._.recv = f32[32,4,32,128]{3,2,1,0:T(8,128)} async-done(((f32[32,4,32,128]{3,2,1,0:T(8,128)}), f32[32,4,32,128]{3,2,1,0:T(8,128)}, u32[]{:S(2)}, u32[]{:S(2)}) %all-to-all-start.3) | async-done | bytes 2097184 | tf_op jit(solution)/shard_map/all_to_all | solution.py:416
  120.5 4.7 %all-to-all-start.1 = ((f32[32,4,32,128]{3,2,1,0:T(8,128)}), f32[32,4,32,128]{3,2,1,0:T(8,128)S(1)}, u32[]{:S(2)}, u32[]{:S(2)}) async-start(f32[32,4,32,128]{3,2,1,0:T(8,128)} %get-tuple-element.8), calls=%async_computation.1 | async-start | bytes 4194304 | tf_op jit(solution)/shard_map/all_to_all | solution.py:416
  125.2 0.6 copy-done.10
  125.8 1.6 last_sum.1
  127.4 0.7 slice.119
  128.1 0.9 slice_multiply_fusion
  129.0 1.1 fusion.10
  130.1 1.1 fusion.16
  131.3 0.9 fusion.37
  132.1 0.7 cholesky.16
  132.9 0.6 compare_reduce_fusion
  133.5 0.6 fusion.27
  134.2 0.6 custom-call.10
  134.8 1.1 fusion.12
  135.9 1.1 convolution_subtract_fusion
  139.3 2.2 %copy-done.1 = f32[8,2,4,128,128]{4,3,2,1,0:T(8,128)S(1)} copy-done((f32[8,2,4,128,128]{4,3,2,1,0:T(8,128)S(1)}, f32[8,2,4,128,128]{4,3,2,1,0:T(8,128)}, u32[]{:S(2)}) %copy-start.1) | copy-done | bytes 4194328
  141.5 2.2 %copy-done.2 = f32[8,8,2,8192]{3,2,1,0:T(2,128)S(1)} copy-done((f32[8,8,2,8192]{3,2,1,0:T(2,128)S(1)}, f32[8,8,2,8192]{3,2,1,0:T(2,128)}, u32[]{:S(2)}) %copy-start.2) | copy-done | bytes 4194328
  143.7 8.2 %base.1 = (f32[4,2,4,128,128]{4,3,2,1,0:T(8,128)S(1)}, f32[4,2,4,128,128]{4,3,2,1,0:T(8,128)S(1)}) custom-call(f32[8,2,4,128,128]{4,3,2,1,0:T(8,128)S(1)} %copy-done.1, f32[8,1024,128]{2,1,0:T(8,128)S(1)} %bitcast.75, f32[4,128,128]{2,1,0:T(8,128)S(1)} %copy-done, f32[8,16,32]{2,1,0:T(8,128)S(1)} %pad_maximum_fusion.4.coefs), custom_call_target="tpu_custom_call" | custom-call | flops 8000000000 | bytes 12000000 | tf_op jit(solution)/shard_map/base/pallas_call | solution.py:457
  151.8 1.3 copy-done.4
  153.2 3.4 %to_planes.2.refs_0_ = f32[8,2,4,128,128]{4,3,2,1,0:T(8,128)} custom-call(f32[32,4,32,128]{3,2,1,0:T(8,128)} %all-to-all-done.3._.recv, f32[4,2,4,128,128]{4,3,2,1,0:T(8,128)S(1)} %get-tuple-element.13.base, bf16[256,768]{1,0:T(8,128)(2,1)S(1)} %copy-done.3), custom_call_target="tpu_custom_call" | custom-call | flops 8000000000 | bytes 12000000 | tf_op jit(solution)/shard_map/to_planes/pallas_call | solution.py:483
  156.6 16.9 %all-to-all-done.1.recv = f32[32,4,32,128]{3,2,1,0:T(8,128)S(1)} async-done(((f32[32,4,32,128]{3,2,1,0:T(8,128)}), f32[32,4,32,128]{3,2,1,0:T(8,128)S(1)}, u32[]{:S(2)}, u32[]{:S(2)}) %all-to-all-start.1) | async-done | bytes 2097184 | tf_op jit(solution)/shard_map/all_to_all | solution.py:416
  173.5 1.6 copy-done.5
  175.1 2.3 %to_planes.3 = f32[8,2,4,128,128]{4,3,2,1,0:T(8,128)} custom-call(f32[32,4,32,128]{3,2,1,0:T(8,128)S(1)} %all-to-all-done.1.recv, f32[4,2,4,128,128]{4,3,2,1,0:T(8,128)S(1)} %copy-done.5, bf16[256,768]{1,0:T(8,128)(2,1)S(1)} %copy-done.3, f32[8,2,4,128,128]{4,3,2,1,0:T(8,128)} %to_planes.2.refs_0_), custom_call_target="tpu_custom_call", output_to_operand_aliasing={{}: (3, {})} | custom-call | flops 8000000000 | bytes 12000000 | tf_op jit(solution)/shard_map/to_planes/pallas_call | solution.py:483
  (78 shorter events, 5.0 us)
Async XLA Ops:
  3.6 7.2 %copy-start.12 = (s32[128]{0:T(128)S(1)}, s32[128]{0:T(128)}, u32[]{:S(2)}) copy-start(s32[128]{0:T(128)} %param.11) | copy-start | bytes 1540
  3.6 32.5 %all-to-all-start.2 = ((f32[32,2,32,128]{3,2,1,0:T(8,128)}), f32[32,2,32,128]{3,2,1,0:T(8,128)}, u32[]{:S(2)}, u32[]{:S(2)}) async-start(f32[32,2,32,128]{3,2,1,0:T(8,128)} %to_rows.3), calls=%async_computation.2 | async-start | bytes 2097152 | tf_op jit(solution)/shard_map/all_to_all | solution.py:332
  36.1 30.0 %all-to-all-start = ((f32[32,2,32,128]{3,2,1,0:T(8,128)}), f32[32,2,32,128]{3,2,1,0:T(8,128)}, u32[]{:S(2)}, u32[]{:S(2)}) async-start(f32[32,2,32,128]{3,2,1,0:T(8,128)} %to_rows.2), calls=%async_computation | async-start | bytes 2097152 | tf_op jit(solution)/shard_map/all_to_all | solution.py:332
  40.7 11.4 %copy-start.7 = (f32[128,4,128]{2,1,0:T(4,128)S(1)}, f32[128,4,128]{2,1,0:T(4,128)}, u32[]{:S(2)}) copy-start(f32[128,4,128]{2,1,0:T(4,128)} %param.12) | copy-start | bytes 786436
  50.8 2.8 %copy-start.13 = (s32[8,8]{1,0:T(8,128)S(1)}, s32[8,8]{1,0:T(8,128)}, u32[]{:S(2)}) copy-start(s32[8,8]{1,0:T(8,128)} %param.14) | copy-start | bytes 772
  66.1 4.6 %copy-start.9 = (f32[8,32,16]{2,1,0:T(8,128)S(1)}, f32[8,32,16]{2,1,0:T(8,128)}, u32[]{:S(2)}) copy-start(f32[8,32,16]{2,1,0:T(8,128)} %project.1) | copy-start | bytes 49156
  66.1 54.4 %all-to-all-start.3 = ((f32[32,4,32,128]{3,2,1,0:T(8,128)}), f32[32,4,32,128]{3,2,1,0:T(8,128)}, u32[]{:S(2)}, u32[]{:S(2)}) async-start(f32[32,4,32,128]{3,2,1,0:T(8,128)} %get-tuple-element.11), calls=%async_computation.3 | async-start | bytes 4194304 | tf_op jit(solution)/shard_map/all_to_all | solution.py:416
  79.0 6.2 %copy-start.8 = (f32[128,16]{1,0:T(8,128)S(1)}, f32[128,16]{1,0:T(8,128)}, u32[]{:S(2)}) copy-start(f32[128,16]{1,0:T(8,128)} %convolution_bitcast_fusion._) | copy-start | bytes 24580
  79.0 31.6 %copy-start.11 = (f32[32,4]{0,1:T(4,128)S(1)}, f32[32,4]{0,1:T(4,128)}, u32[]{:S(2)}) copy-start(f32[32,4]{0,1:T(4,128)} %param.15) | copy-start | bytes 1540
  85.2 1.3 collective-permute-start
  86.5 3.7 %collective-permute-start.1 = (f32[136,16]{1,0:T(8,128)S(1)}, f32[136,16]{1,0:T(8,128)S(1)}, u32[]{:S(2)}, u32[]{:S(2)}) collective-permute-start(f32[136,16]{1,0:T(8,128)S(1)} %fusion.51), channel_id=1, source_target_pairs={{0,2},{1,3},{2,0},{3,1},{4,6},{5,7},{6,4},{7,5},{8,10},{9,11},{10,... | collective-permute-start | bytes 26120 | tf_op jit(solution)/shard_map/ppermute | solution.py:264
  90.3 8.5 %collective-permute-start.2 = (f32[136,16]{1,0:T(8,128)S(1)}, f32[136,16]{1,0:T(8,128)S(1)}, u32[]{:S(2)}, u32[]{:S(2)}) collective-permute-start(f32[136,16]{1,0:T(8,128)S(1)} %add.112), channel_id=1, source_target_pairs={{0,4},{1,5},{2,6},{3,7},{4,0},{5,1},{6,2},{7,3},{8,12},{9,13},{10,... | collective-permute-start | bytes 26120 | tf_op jit(solution)/shard_map/ppermute | solution.py:264
  98.8 7.9 %collective-permute-start.3 = (f32[136,16]{1,0:T(8,128)S(1)}, f32[136,16]{1,0:T(8,128)S(1)}, u32[]{:S(2)}, u32[]{:S(2)}) collective-permute-start(f32[136,16]{1,0:T(8,128)S(1)} %add.113), channel_id=1, source_target_pairs={{0,8},{1,9},{2,10},{3,11},{4,12},{5,13},{6,14},{7,15},{8,0},{9,1},... | collective-permute-start | bytes 26120 | tf_op jit(solution)/shard_map/ppermute | solution.py:264
  106.7 13.8 %copy-start.6 = (f32[136,16]{1,0:T(8,128)}, f32[136,16]{1,0:T(8,128)S(1)}, u32[]{:S(2)}) copy-start(f32[136,16]{1,0:T(8,128)S(1)} %add.114.first) | copy-start | bytes 26116
  106.8 18.4 %collective-permute-start.4 = (f32[136,16]{1,0:T(8,128)S(1)}, f32[136,16]{1,0:T(8,128)S(1)}, u32[]{:S(2)}, u32[]{:S(2)}) collective-permute-start(f32[136,16]{1,0:T(8,128)S(1)} %add.114.first), channel_id=1, source_target_pairs={{0,16},{1,17},{2,18},{3,19},{4,20},{5,21},{6,22},{7,23},{8,24},{9,... | collective-permute-start | bytes 26120 | tf_op jit(solution)/shard_map/ppermute | solution.py:264
  120.5 53.0 %all-to-all-start.1 = ((f32[32,4,32,128]{3,2,1,0:T(8,128)}), f32[32,4,32,128]{3,2,1,0:T(8,128)S(1)}, u32[]{:S(2)}, u32[]{:S(2)}) async-start(f32[32,4,32,128]{3,2,1,0:T(8,128)} %get-tuple-element.8), calls=%async_computation.1 | async-start | bytes 4194304 | tf_op jit(solution)/shard_map/all_to_all | solution.py:416
  125.2 14.1 %copy-start = (f32[4,128,128]{2,1,0:T(8,128)S(1)}, f32[4,128,128]{2,1,0:T(8,128)}, u32[]{:S(2)}) copy-start(f32[4,128,128]{2,1,0:T(8,128)} %add_multiply_fusion.kinetic) | copy-start | bytes 786436
  125.2 0.6 copy-start.10
  139.3 2.2 %copy-start.1 = (f32[8,2,4,128,128]{4,3,2,1,0:T(8,128)S(1)}, f32[8,2,4,128,128]{4,3,2,1,0:T(8,128)}, u32[]{:S(2)}) copy-start(f32[8,2,4,128,128]{4,3,2,1,0:T(8,128)} %psi.7) | copy-start | bytes 12582916
  141.5 2.2 %copy-start.2 = (f32[8,8,2,8192]{3,2,1,0:T(2,128)S(1)}, f32[8,8,2,8192]{3,2,1,0:T(2,128)}, u32[]{:S(2)}) copy-start(f32[8,8,2,8192]{3,2,1,0:T(2,128)} %param.13) | copy-start | bytes 12582916
  143.7 9.5 %copy-start.3 = (bf16[256,768]{1,0:T(8,128)(2,1)S(1)}, bf16[256,768]{1,0:T(8,128)(2,1)}, u32[]{:S(2)}) copy-start(bf16[256,768]{1,0:T(8,128)(2,1)} %constant.100.clone.y_table) | copy-start | bytes 1179652
  151.8 1.4 copy-start.4
  173.5 1.6 copy-start.5

commit v15 on v13

--- a/solution.py
+++ b/solution.py
@@ -301,8 +301,21 @@
     def cost(flops, moved):
         return pl.CostEstimate(flops=flops, bytes_accessed=moved, transcendentals=0)
 
+    layers = 4 if devices % 4 == 0 else 1
+    ranks = np.arange(devices).reshape(layers, -1).T.reshape(-1)
     order = np.arange(2 * span_y)
-    order = (order % 2) * span_y + order // 2
+    order = (order % 2) * span_y + (ranks[:, None] * rows + np.arange(rows)).reshape(-1)[order // 2]
+
+    def exchange(values):
+        return lax.all_to_all(
+            values,
+            "ga",
+            split_axis=0,
+            concat_axis=0,
+            axis_index_groups=[[int(rank) for rank in ranks]],
+            tiled=True,
+        )
+
     inv_y = left_const(left_table(span_y, 1.0)[order])
     fwd_y = left_const(left_table(span_y, -1.0)[:, order])
     inv_z = right_const(right_table(span_z, 1.0))
@@ -327,9 +340,9 @@
             cost_estimate=cost(4 * 10**9, 3 * 10**6),
             name="to_rows",
         )(orbitals, inv_y)
-        arrived.append(lax.all_to_all(sent, "ga", split_axis=0, concat_axis=0, tiled=True))
-
-    stored = plane_order.reshape(devices, planes).T.reshape(-1)
+        arrived.append(exchange(sent))
+
+    stored = plane_order.reshape(devices, planes)[ranks].T.reshape(-1)
     phases = (stored[:, None] * grid_x[None, :]) % span_x
     angles = phases.astype(f32) * (2.0 * math.pi / span_x)
     factor = 1.0 / math.sqrt(span_x)
@@ -411,7 +424,7 @@
             cost_estimate=cost(4 * 10**9, 8 * 10**6),
             name="real_space",
         )(arrived[c], pot, inv_x, fwd_x, inv_z, fwd_z, proj)
-        returned.append(lax.all_to_all(back, "ga", split_axis=0, concat_axis=0, tiled=True))
+        returned.append(exchange(back))
         fields.append(field)
 
     grams = pl.pallas_call(

time: 179 us -> 176 us (0.983)
  starting transfers between devices: 34.9 us -> 26 us
  waiting for transfers between devices: 61.7 us -> 67.9 us
    ppermute x5, waiting for transfers between devices: 11.2 us -> 16.6 us  [partner(): return lax.ppermute(values, 'ga', [(d, d ^ k) for d in range(devices)])]
    ppermute x5, starting transfers between devices: 13.9 us -> 9.05 us  [partner(): return lax.ppermute(values, 'ga', [(d, d ^ k) for d in range(devices)])]
    all_to_all x4, starting transfers between devices: 21 us -> 17 us  [exchange(): lax.all_to_all(values, 'ga', split_axis=0, concat_axis=0, axis_index_grou...]
    unnamed x30 -> x32, local copies, waits for them, and re-layouts: 5.52 us -> 5.53 us
  transfers between devices with their start and end apart: 9 -> 9, of which waited for: 8 -> 8; matrix products, arithmetic and copies ran while one was open for 11% -> 12% of each run, Pallas kernels for 27% -> 28%
where the time goes in v15:
time: 176 us; the launch traced here: 175 us
  waiting for transfers between devices  67.9 us (39%)
  Pallas kernels  54.7 us (31%)
  starting transfers between devices  26 us (15%)
  local copies, waits for them, and re-layouts  10.4 us (6%)
  other arithmetic  8.86 us (5%)
  matrix products  6.01 us (3%)
    all_to_all x4, waiting for transfers between devices, exchange(): lax.all_to_all(values, 'ga', split_axis=0, concat_axis=0, axis_index_grou...  51.2 us
    all_to_all x4, starting transfers between devices, exchange(): lax.all_to_all(values, 'ga', split_axis=0, concat_axis=0, axis_index_grou...  17 us
    ppermute x5, waiting for transfers between devices, partner(): return lax.ppermute(values, 'ga', [(d, d ^ k) for d in range(devices)])  16.6 us
    pallas_call x2, Pallas kernels, on_device(): pl.pallas_call(functools.partial(real_space_kernel, rows, planes), out_sh...  16.1 us
    pallas_call x1, Pallas kernels, on_device(): pl.pallas_call(functools.partial(project_kernel, slots), out_shape=jax.Sh...  10.1 us
    ppermute x5, starting transfers between devices, partner(): return lax.ppermute(values, 'ga', [(d, d ^ k) for d in range(devices)])  9.05 us
    pallas_call x1, Pallas kernels, on_device(): pl.pallas_call(functools.partial(base_kernel, slots), out_shape=jax.Shape...  8.68 us
    pallas_call x2, Pallas kernels, on_device(): pl.pallas_call(to_planes_kernel, out_shape=jax.ShapeDtypeStruct(orbitals....  7.21 us
  transfers between devices with their start and end apart: 9, of which 8 were waited for; matrix products, arithmetic and copies ran while one was open for 12% of the time, Pallas kernels for 28%

profile of v15, /device:TPU:1, one launch (start us, length us, event | category | flops | bytes accessed | tf_op | source)
XLA Modules:
  0.0 174.9 jit_solution(3562096723181844034)
XLA Ops:
  0.7 2.9 %to_rows.3 = f32[32,2,32,128]{3,2,1,0:T(8,128)} custom-call(f32[8,2,4,128,128]{4,3,2,1,0:T(8,128)} %psi.7, bf16[256,768]{1,0:T(8,128)(2,1)} %constant.105.clone.y_table), custom_call_target="tpu_custom_call" | custom-call | flops 4000000000 | bytes 3000000 | tf_op jit(solution)/shard_map/to_rows/pallas_call | solution.py:328
  3.6 7.2 %all-to-all-start.2 = ((f32[32,2,32,128]{3,2,1,0:T(8,128)}), f32[32,2,32,128]{3,2,1,0:T(8,128)}, u32[]{:S(2)}, u32[]{:S(2)}) async-start(f32[32,2,32,128]{3,2,1,0:T(8,128)} %to_rows.3), calls=%async_computation.2 | async-start | bytes 2097152 | tf_op jit(solution)/shard_map/all_to_all | solution.py:310
  12.1 0.9 copy.120.inverse
  13.2 0.9 add_multiply_fusion.kinetic
  14.0 3.0 %to_rows.2 = f32[32,2,32,128]{3,2,1,0:T(8,128)} custom-call(f32[8,2,4,128,128]{4,3,2,1,0:T(8,128)} %psi.7, bf16[256,768]{1,0:T(8,128)(2,1)} %constant.105.clone.y_table), custom_call_target="tpu_custom_call" | custom-call | flops 4000000000 | bytes 3000000 | tf_op jit(solution)/shard_map/to_rows/pallas_call | solution.py:328
  17.0 20.2 %all-to-all-done.2.recv = f32[32,2,32,128]{3,2,1,0:T(8,128)} async-done(((f32[32,2,32,128]{3,2,1,0:T(8,128)}), f32[32,2,32,128]{3,2,1,0:T(8,128)}, u32[]{:S(2)}, u32[]{:S(2)}) %all-to-all-start.2) | async-done | bytes 1048608 | tf_op jit(solution)/shard_map/all_to_all | solution.py:310
  37.2 3.2 %all-to-all-start = ((f32[32,2,32,128]{3,2,1,0:T(8,128)}), f32[32,2,32,128]{3,2,1,0:T(8,128)}, u32[]{:S(2)}, u32[]{:S(2)}) async-start(f32[32,2,32,128]{3,2,1,0:T(8,128)} %to_rows.2), calls=%async_computation | async-start | bytes 2097152 | tf_op jit(solution)/shard_map/all_to_all | solution.py:310
  40.4 10.1 %project.1 = f32[8,32,16]{2,1,0:T(8,128)} custom-call(f32[8,2,4,128,128]{4,3,2,1,0:T(8,128)} %psi.7, f32[8,1024,128]{2,1,0:T(8,128)} %bitcast.74, f32[4,128,128]{2,1,0:T(8,128)} %add_multiply_fusion.kinetic), custom_call_target="tpu_custom_call" | custom-call | flops 8000000000 | bytes 8000000 | tf_op jit(solution)/shard_map/project/pallas_call | solution.py:375
  50.5 0.8 fusion.47
  51.8 0.7 copy.111
  52.6 0.7 pad_maximum_fusion.1.forward
  53.3 0.9 convolution_bitcast_fusion._
  54.3 8.0 %real_space.3 = (f32[32,4,32,128]{3,2,1,0:T(8,128)}, f32[4,512,128]{2,1,0:T(8,128)}) custom-call(f32[32,2,32,128]{3,2,1,0:T(8,128)} %all-to-all-done.2.recv, f32[512,128]{1,0:T(8,128)} %bitcast.76, bf16[256,768]{1,0:T(8,128)(2,1)} %copy.120.inverse, bf16[256,384]{1,0:T(8,128)(2,1)} %pad_maximum_fusion.1.forward, bf16[768,256]{1,0:T(8,128)(2,1)} %constant.107.clone.inv_z, ...), custom_call_target="tpu_custom_call" | custom-call | flops 4000000000 | bytes 8000000 | tf_op jit(solution)/shard_map/real_space/pallas_call | solution.py:403
  62.2 4.6 %all-to-all-done.recv = f32[32,2,32,128]{3,2,1,0:T(8,128)} async-done(((f32[32,2,32,128]{3,2,1,0:T(8,128)}), f32[32,2,32,128]{3,2,1,0:T(8,128)}, u32[]{:S(2)}, u32[]{:S(2)}) %all-to-all-start) | async-done | bytes 1048608 | tf_op jit(solution)/shard_map/all_to_all | solution.py:310
  66.8 3.2 %all-to-all-start.3 = ((f32[32,4,32,128]{3,2,1,0:T(8,128)}), f32[32,4,32,128]{3,2,1,0:T(8,128)}, u32[]{:S(2)}, u32[]{:S(2)}) async-start(f32[32,4,32,128]{3,2,1,0:T(8,128)} %get-tuple-element.7), calls=%async_computation.3 | async-start | bytes 4194304 | tf_op jit(solution)/shard_map/all_to_all | solution.py:310
  70.3 8.1 %real_space.2 = (f32[32,4,32,128]{3,2,1,0:T(8,128)}, f32[4,512,128]{2,1,0:T(8,128)}) custom-call(f32[32,2,32,128]{3,2,1,0:T(8,128)} %all-to-all-done.recv, f32[512,128]{1,0:T(8,128)} %bitcast.77, bf16[256,768]{1,0:T(8,128)(2,1)} %copy.120.inverse, bf16[256,384]{1,0:T(8,128)(2,1)} %pad_maximum_fusion.1.forward, bf16[768,256]{1,0:T(8,128)(2,1)} %constant.107.clone.inv_z, ...), custom_call_target="tpu_custom_call" | custom-call | flops 4000000000 | bytes 8000000 | tf_op jit(solution)/shard_map/real_space/pallas_call | solution.py:403
  78.4 5.2 %real_gram.1 = f32[2,8,8,128]{3,2,1,0:T(8,128)} custom-call(f32[4,512,128]{2,1,0:T(8,128)} %get-tuple-element.8.refs_0_, f32[4,512,128]{2,1,0:T(8,128)} %get-tuple-element.9.refs_1_, f32[512,128]{1,0:T(8,128)} %bitcast.78), custom_call_target="tpu_custom_call" | custom-call | flops 10000000 | bytes 2000000 | tf_op jit(solution)/shard_map/real_gram/pallas_call | solution.py:430
  83.6 0.9 reduce_sum.18
  85.0 0.9 collective-permute-done
  86.0 1.4 collective-permute-start.1
  87.4 3.1 %collective-permute-done.1 = f32[136,16]{1,0:T(8,128)S(1)} collective-permute-done((f32[136,16]{1,0:T(8,128)S(1)}, f32[136,16]{1,0:T(8,128)S(1)}, u32[]{:S(2)}, u32[]{:S(2)}) %collective-permute-start.1) | collective-permute-done | bytes 8736 | tf_op jit(solution)/shard_map/ppermute | solution.py:262
  90.5 1.3 collective-permute-start.2
  91.8 3.2 %collective-permute-done.2 = f32[136,16]{1,0:T(8,128)S(1)} collective-permute-done((f32[136,16]{1,0:T(8,128)S(1)}, f32[136,16]{1,0:T(8,128)S(1)}, u32[]{:S(2)}, u32[]{:S(2)}) %collective-permute-start.2) | collective-permute-done | bytes 8736 | tf_op jit(solution)/shard_map/ppermute | solution.py:262
  94.9 1.5 collective-permute-start.3
  96.4 9.4 %collective-permute-done.3 = f32[136,16]{1,0:T(8,128)S(1)} collective-permute-done((f32[136,16]{1,0:T(8,128)S(1)}, f32[136,16]{1,0:T(8,128)S(1)}, u32[]{:S(2)}, u32[]{:S(2)}) %collective-permute-start.3) | collective-permute-done | bytes 8736 | tf_op jit(solution)/shard_map/ppermute | solution.py:262
  105.9 4.6 %collective-permute-start.4 = (f32[136,16]{1,0:T(8,128)S(1)}, f32[136,16]{1,0:T(8,128)S(1)}, u32[]{:S(2)}, u32[]{:S(2)}) collective-permute-start(f32[136,16]{1,0:T(8,128)S(1)} %add.122.first), channel_id=1, source_target_pairs={{0,16},{1,17},{2,18},{3,19},{4,20},{5,21},{6,22},{7,23},{8,24},{9,... | collective-permute-start | bytes 26120 | tf_op jit(solution)/shard_map/ppermute | solution.py:262
  110.7 9.2 %all-to-all-done.3._.recv = f32[32,4,32,128]{3,2,1,0:T(8,128)} async-done(((f32[32,4,32,128]{3,2,1,0:T(8,128)}), f32[32,4,32,128]{3,2,1,0:T(8,128)}, u32[]{:S(2)}, u32[]{:S(2)}) %all-to-all-start.3) | async-done | bytes 2097184 | tf_op jit(solution)/shard_map/all_to_all | solution.py:310
  119.8 3.4 %all-to-all-start.1 = ((f32[32,4,32,128]{3,2,1,0:T(8,128)}), f32[32,4,32,128]{3,2,1,0:T(8,128)S(1)}, u32[]{:S(2)}, u32[]{:S(2)}) async-start(f32[32,4,32,128]{3,2,1,0:T(8,128)} %get-tuple-element.6), calls=%async_computation.1 | async-start | bytes 4194304 | tf_op jit(solution)/shard_map/all_to_all | solution.py:310
  123.3 0.6 copy-done.8
  123.9 1.5 last_sum.1
  125.4 0.7 slice.121
  126.1 0.9 slice_multiply_fusion
  127.0 1.1 fusion.10
  128.2 1.1 fusion.16
  129.3 0.9 fusion.37
  130.2 0.7 cholesky.16
  130.9 0.6 compare_reduce_fusion
  131.6 0.6 fusion.27
  132.2 0.6 custom-call.10
  132.9 1.1 fusion.12
  134.0 1.1 convolution_subtract_fusion
  136.6 0.6 pad_maximum_fusion.6
  137.3 2.2 %copy-done.1 = f32[8,2,4,128,128]{4,3,2,1,0:T(8,128)S(1)} copy-done((f32[8,2,4,128,128]{4,3,2,1,0:T(8,128)S(1)}, f32[8,2,4,128,128]{4,3,2,1,0:T(8,128)}, u32[]{:S(2)}) %copy-start.1) | copy-done | bytes 4194328
  139.5 2.2 %copy-done.2 = f32[8,8,2,8192]{3,2,1,0:T(2,128)S(1)} copy-done((f32[8,8,2,8192]{3,2,1,0:T(2,128)S(1)}, f32[8,8,2,8192]{3,2,1,0:T(2,128)}, u32[]{:S(2)}) %copy-start.2) | copy-done | bytes 4194328
  141.7 8.7 %base.1 = f32[8,2,4,128,128]{4,3,2,1,0:T(8,128)} custom-call(f32[8,2,4,128,128]{4,3,2,1,0:T(8,128)S(1)} %copy-done.1, f32[8,1024,128]{2,1,0:T(8,128)S(1)} %bitcast.75, f32[4,128,128]{2,1,0:T(8,128)S(1)} %copy-done, f32[8,16,32]{2,1,0:T(8,128)S(1)} %pad_maximum_fusion.4.coefs), custom_call_target="tpu_custom_call" | custom-call | flops 8000000000 | bytes 12000000 | tf_op jit(solution)/shard_map/base/pallas_call | solution.py:467
  150.4 3.7 %to_planes.2.base = f32[8,2,4,128,128]{4,3,2,1,0:T(8,128)} custom-call(f32[32,4,32,128]{3,2,1,0:T(8,128)} %all-to-all-done.3._.recv, f32[8,2,4,128,128]{4,3,2,1,0:T(8,128)} %base.1, bf16[256,768]{1,0:T(8,128)(2,1)S(1)} %copy-done.3), custom_call_target="tpu_custom_call", output_to_operand_aliasing={{}: (1, {})} | custom-call | flops 8000000000 | bytes 12000000 | tf_op jit(solution)/shard_map/to_planes/pallas_call | solution.py:484
  154.1 17.3 %all-to-all-done.1.recv = f32[32,4,32,128]{3,2,1,0:T(8,128)S(1)} async-done(((f32[32,4,32,128]{3,2,1,0:T(8,128)}), f32[32,4,32,128]{3,2,1,0:T(8,128)S(1)}, u32[]{:S(2)}, u32[]{:S(2)}) %all-to-all-start.1) | async-done | bytes 2097184 | tf_op jit(solution)/shard_map/all_to_all | solution.py:310
  171.5 3.5 %to_planes.3 = f32[8,2,4,128,128]{4,3,2,1,0:T(8,128)} custom-call(f32[32,4,32,128]{3,2,1,0:T(8,128)S(1)} %all-to-all-done.1.recv, f32[8,2,4,128,128]{4,3,2,1,0:T(8,128)} %to_planes.2.base, bf16[256,768]{1,0:T(8,128)(2,1)S(1)} %copy-done.3), custom_call_target="tpu_custom_call", output_to_operand_aliasing={{}: (1, {})} | custom-call | flops 8000000000 | bytes 12000000 | tf_op jit(solution)/shard_map/to_planes/pallas_call | solution.py:484
  (78 shorter events, 4.6 us)
Async XLA Ops:
  0.6 10.3 %copy-start.11 = (s32[32]{0:T(128)S(1)}, s32[32]{0:T(128)}, u32[]{:S(2)}) copy-start(s32[32]{0:T(128)} %constant.116) | copy-start | bytes 388
  0.6 10.1 %copy-start.10 = (s32[128]{0:T(128)S(1)}, s32[128]{0:T(128)}, u32[]{:S(2)}) copy-start(s32[128]{0:T(128)} %param.13) | copy-start | bytes 1540
  3.6 33.6 %all-to-all-start.2 = ((f32[32,2,32,128]{3,2,1,0:T(8,128)}), f32[32,2,32,128]{3,2,1,0:T(8,128)}, u32[]{:S(2)}, u32[]{:S(2)}) async-start(f32[32,2,32,128]{3,2,1,0:T(8,128)} %to_rows.3), calls=%async_computation.2 | async-start | bytes 2097152 | tf_op jit(solution)/shard_map/all_to_all | solution.py:310
  37.2 29.6 %all-to-all-start = ((f32[32,2,32,128]{3,2,1,0:T(8,128)}), f32[32,2,32,128]{3,2,1,0:T(8,128)}, u32[]{:S(2)}, u32[]{:S(2)}) async-start(f32[32,2,32,128]{3,2,1,0:T(8,128)} %to_rows.2), calls=%async_computation | async-start | bytes 2097152 | tf_op jit(solution)/shard_map/all_to_all | solution.py:310
  40.4 11.4 %copy-start.5 = (f32[128,4,128]{2,1,0:T(4,128)S(1)}, f32[128,4,128]{2,1,0:T(4,128)}, u32[]{:S(2)}) copy-start(f32[128,4,128]{2,1,0:T(4,128)} %param.14) | copy-start | bytes 786436
  40.4 12.9 %copy-start.12 = (s32[8,8]{1,0:T(8,128)S(1)}, s32[8,8]{1,0:T(8,128)}, u32[]{:S(2)}) copy-start(s32[8,8]{1,0:T(8,128)} %param.16) | copy-start | bytes 772
  62.2 7.8 %copy-start.7 = (f32[8,32,16]{2,1,0:T(8,128)S(1)}, f32[8,32,16]{2,1,0:T(8,128)}, u32[]{:S(2)}) copy-start(f32[8,32,16]{2,1,0:T(8,128)} %project.1) | copy-start | bytes 49156
  66.8 53.1 %all-to-all-start.3 = ((f32[32,4,32,128]{3,2,1,0:T(8,128)}), f32[32,4,32,128]{3,2,1,0:T(8,128)}, u32[]{:S(2)}, u32[]{:S(2)}) async-start(f32[32,4,32,128]{3,2,1,0:T(8,128)} %get-tuple-element.7), calls=%async_computation.3 | async-start | bytes 4194304 | tf_op jit(solution)/shard_map/all_to_all | solution.py:310
  70.3 14.3 %copy-start.6 = (f32[128,16]{1,0:T(8,128)S(1)}, f32[128,16]{1,0:T(8,128)}, u32[]{:S(2)}) copy-start(f32[128,16]{1,0:T(8,128)} %convolution_bitcast_fusion._) | copy-start | bytes 24580
  70.3 40.2 %copy-start.9 = (f32[32,4]{0,1:T(4,128)S(1)}, f32[32,4]{0,1:T(4,128)}, u32[]{:S(2)}) copy-start(f32[32,4]{0,1:T(4,128)} %param.17) | copy-start | bytes 1540
  84.6 1.3 collective-permute-start
  86.0 4.5 %collective-permute-start.1 = (f32[136,16]{1,0:T(8,128)S(1)}, f32[136,16]{1,0:T(8,128)S(1)}, u32[]{:S(2)}, u32[]{:S(2)}) collective-permute-start(f32[136,16]{1,0:T(8,128)S(1)} %fusion.51), channel_id=1, source_target_pairs={{0,2},{1,3},{2,0},{3,1},{4,6},{5,7},{6,4},{7,5},{8,10},{9,11},{10,... | collective-permute-start | bytes 26120 | tf_op jit(solution)/shard_map/ppermute | solution.py:262
  90.5 4.4 %collective-permute-start.2 = (f32[136,16]{1,0:T(8,128)S(1)}, f32[136,16]{1,0:T(8,128)S(1)}, u32[]{:S(2)}, u32[]{:S(2)}) collective-permute-start(f32[136,16]{1,0:T(8,128)S(1)} %add.120), channel_id=1, source_target_pairs={{0,4},{1,5},{2,6},{3,7},{4,0},{5,1},{6,2},{7,3},{8,12},{9,13},{10,... | collective-permute-start | bytes 26120 | tf_op jit(solution)/shard_map/ppermute | solution.py:262
  94.9 10.9 %collective-permute-start.3 = (f32[136,16]{1,0:T(8,128)S(1)}, f32[136,16]{1,0:T(8,128)S(1)}, u32[]{:S(2)}, u32[]{:S(2)}) collective-permute-start(f32[136,16]{1,0:T(8,128)S(1)} %add.121), channel_id=1, source_target_pairs={{0,8},{1,9},{2,10},{3,11},{4,12},{5,13},{6,14},{7,15},{8,0},{9,1},... | collective-permute-start | bytes 26120 | tf_op jit(solution)/shard_map/ppermute | solution.py:262
  105.9 17.4 %copy-start.4 = (f32[136,16]{1,0:T(8,128)}, f32[136,16]{1,0:T(8,128)S(1)}, u32[]{:S(2)}) copy-start(f32[136,16]{1,0:T(8,128)S(1)} %add.122.first) | copy-start | bytes 26116
  105.9 17.4 %collective-permute-start.4 = (f32[136,16]{1,0:T(8,128)S(1)}, f32[136,16]{1,0:T(8,128)S(1)}, u32[]{:S(2)}, u32[]{:S(2)}) collective-permute-start(f32[136,16]{1,0:T(8,128)S(1)} %add.122.first), channel_id=1, source_target_pairs={{0,16},{1,17},{2,18},{3,19},{4,20},{5,21},{6,22},{7,23},{8,24},{9,... | collective-permute-start | bytes 26120 | tf_op jit(solution)/shard_map/ppermute | solution.py:262
  119.8 17.5 %copy-start = (f32[4,128,128]{2,1,0:T(8,128)S(1)}, f32[4,128,128]{2,1,0:T(8,128)}, u32[]{:S(2)}) copy-start(f32[4,128,128]{2,1,0:T(8,128)} %add_multiply_fusion.kinetic) | copy-start | bytes 786436
  119.8 51.6 %all-to-all-start.1 = ((f32[32,4,32,128]{3,2,1,0:T(8,128)}), f32[32,4,32,128]{3,2,1,0:T(8,128)S(1)}, u32[]{:S(2)}, u32[]{:S(2)}) async-start(f32[32,4,32,128]{3,2,1,0:T(8,128)} %get-tuple-element.6), calls=%async_computation.1 | async-start | bytes 4194304 | tf_op jit(solution)/shard_map/all_to_all | solution.py:310
  123.2 0.6 copy-start.8
  137.3 2.2 %copy-start.1 = (f32[8,2,4,128,128]{4,3,2,1,0:T(8,128)S(1)}, f32[8,2,4,128,128]{4,3,2,1,0:T(8,128)}, u32[]{:S(2)}) copy-start(f32[8,2,4,128,128]{4,3,2,1,0:T(8,128)} %psi.7) | copy-start | bytes 12582916
  139.5 2.2 %copy-start.2 = (f32[8,8,2,8192]{3,2,1,0:T(2,128)S(1)}, f32[8,8,2,8192]{3,2,1,0:T(2,128)}, u32[]{:S(2)}) copy-start(f32[8,8,2,8192]{3,2,1,0:T(2,128)} %param.15) | copy-start | bytes 12582916
  141.7 8.7 %copy-start.3 = (bf16[256,768]{1,0:T(8,128)(2,1)S(1)}, bf16[256,768]{1,0:T(8,128)(2,1)}, u32[]{:S(2)}) copy-start(bf16[256,768]{1,0:T(8,128)(2,1)} %constant.106.clone.y_table) | copy-start | bytes 1179652

commit v16 on v15

--- a/solution.py
+++ b/solution.py
@@ -302,7 +302,7 @@
         return pl.CostEstimate(flops=flops, bytes_accessed=moved, transcendentals=0)
 
     layers = 4 if devices % 4 == 0 else 1
-    ranks = np.arange(devices).reshape(layers, -1).T.reshape(-1)
+    ranks = np.arange(devices).reshape(layers, -1)[[0, 2, 1, 3] if layers == 4 else [0]].T.reshape(-1)
     order = np.arange(2 * span_y)
     order = (order % 2) * span_y + (ranks[:, None] * rows + np.arange(rows)).reshape(-1)[order // 2]
 

time: 176 us -> 182 us (1.034)
  starting transfers between devices: 26 us -> 33.7 us
  waiting for transfers between devices: 67.9 us -> 65.2 us
    ppermute x5, waiting for transfers between devices: 16.6 us -> 12.1 us  [partner(): return lax.ppermute(values, 'ga', [(d, d ^ k) for d in range(devices)])]
    ppermute x5, starting transfers between devices: 9.05 us -> 13.3 us  [partner(): return lax.ppermute(values, 'ga', [(d, d ^ k) for d in range(devices)])]
    all_to_all x4, starting transfers between devices: 17 us -> 20.4 us  [exchange(): lax.all_to_all(values, 'ga', split_axis=0, concat_axis=0, axis_index_grou...]
    all_to_all x4, waiting for transfers between devices: 51.2 us -> 53.1 us  [exchange(): lax.all_to_all(values, 'ga', split_axis=0, concat_axis=0, axis_index_grou...]
  transfers between devices with their start and end apart: 9 -> 9, of which waited for: 8 -> 8; matrix products, arithmetic and copies ran while one was open for 12% -> 11% of each run, Pallas kernels for 28% -> 27%
where the time goes in v16:
time: 182 us; the launch traced here: 180 us
  waiting for transfers between devices  65.2 us (36%)
  Pallas kernels  54.7 us (30%)
  starting transfers between devices  33.7 us (19%)
  local copies, waits for them, and re-layouts  10.4 us (6%)
  other arithmetic  8.86 us (5%)
  matrix products  6.01 us (3%)
    all_to_all x4, waiting for transfers between devices, exchange(): lax.all_to_all(values, 'ga', split_axis=0, concat_axis=0, axis_index_grou...  53.1 us
    all_to_all x4, starting transfers between devices, exchange(): lax.all_to_all(values, 'ga', split_axis=0, concat_axis=0, axis_index_grou...  20.4 us
    pallas_call x2, Pallas kernels, on_device(): pl.pallas_call(functools.partial(real_space_kernel, rows, planes), out_sh...  16.1 us
    ppermute x5, starting transfers between devices, partner(): return lax.ppermute(values, 'ga', [(d, d ^ k) for d in range(devices)])  13.3 us
    ppermute x5, waiting for transfers between devices, partner(): return lax.ppermute(values, 'ga', [(d, d ^ k) for d in range(devices)])  12.1 us
    pallas_call x1, Pallas kernels, on_device(): pl.pallas_call(functools.partial(project_kernel, slots), out_shape=jax.Sh...  10.1 us
    pallas_call x1, Pallas kernels, on_device(): pl.pallas_call(functools.partial(base_kernel, slots), out_shape=jax.Shape...  8.68 us
    pallas_call x2, Pallas kernels, on_device(): pl.pallas_call(to_planes_kernel, out_shape=jax.ShapeDtypeStruct(orbitals....  7.21 us
  transfers between devices with their start and end apart: 9, of which 8 were waited for; matrix products, arithmetic and copies ran while one was open for 11% of the time, Pallas kernels for 27%

profile of v16, /device:TPU:1, one launch (start us, length us, event | category | flops | bytes accessed | tf_op | source)
XLA Modules:
  0.0 179.9 jit_solution(77828272266597225)
XLA Ops:
  0.7 2.9 %to_rows.3 = f32[32,2,32,128]{3,2,1,0:T(8,128)} custom-call(f32[8,2,4,128,128]{4,3,2,1,0:T(8,128)} %psi.7, bf16[256,768]{1,0:T(8,128)(2,1)} %constant.105.clone.y_table), custom_call_target="tpu_custom_call" | custom-call | flops 4000000000 | bytes 3000000 | tf_op jit(solution)/shard_map/to_rows/pallas_call | solution.py:328
  3.6 7.2 %all-to-all-start.2 = ((f32[32,2,32,128]{3,2,1,0:T(8,128)}), f32[32,2,32,128]{3,2,1,0:T(8,128)}, u32[]{:S(2)}, u32[]{:S(2)}) async-start(f32[32,2,32,128]{3,2,1,0:T(8,128)} %to_rows.3), calls=%async_computation.2 | async-start | bytes 2097152 | tf_op jit(solution)/shard_map/all_to_all | solution.py:310
  12.1 0.9 copy.120.inverse
  13.2 0.9 add_multiply_fusion.kinetic
  14.0 3.0 %to_rows.2 = f32[32,2,32,128]{3,2,1,0:T(8,128)} custom-call(f32[8,2,4,128,128]{4,3,2,1,0:T(8,128)} %psi.7, bf16[256,768]{1,0:T(8,128)(2,1)} %constant.105.clone.y_table), custom_call_target="tpu_custom_call" | custom-call | flops 4000000000 | bytes 3000000 | tf_op jit(solution)/shard_map/to_rows/pallas_call | solution.py:328
  17.0 19.6 %all-to-all-done.2.recv = f32[32,2,32,128]{3,2,1,0:T(8,128)} async-done(((f32[32,2,32,128]{3,2,1,0:T(8,128)}), f32[32,2,32,128]{3,2,1,0:T(8,128)}, u32[]{:S(2)}, u32[]{:S(2)}) %all-to-all-start.2) | async-done | bytes 1048608 | tf_op jit(solution)/shard_map/all_to_all | solution.py:310
  36.6 4.9 %all-to-all-start = ((f32[32,2,32,128]{3,2,1,0:T(8,128)}), f32[32,2,32,128]{3,2,1,0:T(8,128)}, u32[]{:S(2)}, u32[]{:S(2)}) async-start(f32[32,2,32,128]{3,2,1,0:T(8,128)} %to_rows.2), calls=%async_computation | async-start | bytes 2097152 | tf_op jit(solution)/shard_map/all_to_all | solution.py:310
  41.6 10.1 %project.1 = f32[8,32,16]{2,1,0:T(8,128)} custom-call(f32[8,2,4,128,128]{4,3,2,1,0:T(8,128)} %psi.7, f32[8,1024,128]{2,1,0:T(8,128)} %bitcast.74, f32[4,128,128]{2,1,0:T(8,128)} %add_multiply_fusion.kinetic), custom_call_target="tpu_custom_call" | custom-call | flops 8000000000 | bytes 8000000 | tf_op jit(solution)/shard_map/project/pallas_call | solution.py:375
  51.7 0.8 fusion.47
  53.0 0.7 copy.111
  53.8 0.7 pad_maximum_fusion.1.forward
  54.5 0.9 convolution_bitcast_fusion._
  55.4 8.0 %real_space.3 = (f32[32,4,32,128]{3,2,1,0:T(8,128)}, f32[4,512,128]{2,1,0:T(8,128)}) custom-call(f32[32,2,32,128]{3,2,1,0:T(8,128)} %all-to-all-done.2.recv, f32[512,128]{1,0:T(8,128)} %bitcast.76, bf16[256,768]{1,0:T(8,128)(2,1)} %copy.120.inverse, bf16[256,384]{1,0:T(8,128)(2,1)} %pad_maximum_fusion.1.forward, bf16[768,256]{1,0:T(8,128)(2,1)} %constant.107.clone.inv_z, ...), custom_call_target="tpu_custom_call" | custom-call | flops 4000000000 | bytes 8000000 | tf_op jit(solution)/shard_map/real_space/pallas_call | solution.py:403
  63.4 4.1 %all-to-all-done.recv = f32[32,2,32,128]{3,2,1,0:T(8,128)} async-done(((f32[32,2,32,128]{3,2,1,0:T(8,128)}), f32[32,2,32,128]{3,2,1,0:T(8,128)}, u32[]{:S(2)}, u32[]{:S(2)}) %all-to-all-start) | async-done | bytes 1048608 | tf_op jit(solution)/shard_map/all_to_all | solution.py:310
  67.5 5.1 %all-to-all-start.3 = ((f32[32,4,32,128]{3,2,1,0:T(8,128)}), f32[32,4,32,128]{3,2,1,0:T(8,128)}, u32[]{:S(2)}, u32[]{:S(2)}) async-start(f32[32,4,32,128]{3,2,1,0:T(8,128)} %get-tuple-element.7), calls=%async_computation.3 | async-start | bytes 4194304 | tf_op jit(solution)/shard_map/all_to_all | solution.py:310
  72.9 8.1 %real_space.2 = (f32[32,4,32,128]{3,2,1,0:T(8,128)}, f32[4,512,128]{2,1,0:T(8,128)}) custom-call(f32[32,2,32,128]{3,2,1,0:T(8,128)} %all-to-all-done.recv, f32[512,128]{1,0:T(8,128)} %bitcast.77, bf16[256,768]{1,0:T(8,128)(2,1)} %copy.120.inverse, bf16[256,384]{1,0:T(8,128)(2,1)} %pad_maximum_fusion.1.forward, bf16[768,256]{1,0:T(8,128)(2,1)} %constant.107.clone.inv_z, ...), custom_call_target="tpu_custom_call" | custom-call | flops 4000000000 | bytes 8000000 | tf_op jit(solution)/shard_map/real_space/pallas_call | solution.py:403
  81.0 5.2 %real_gram.1 = f32[2,8,8,128]{3,2,1,0:T(8,128)} custom-call(f32[4,512,128]{2,1,0:T(8,128)} %get-tuple-element.8.refs_0_, f32[4,512,128]{2,1,0:T(8,128)} %get-tuple-element.9.refs_1_, f32[512,128]{1,0:T(8,128)} %bitcast.78), custom_call_target="tpu_custom_call" | custom-call | flops 10000000 | bytes 2000000 | tf_op jit(solution)/shard_map/real_gram/pallas_call | solution.py:430
  86.2 0.9 reduce_sum.18
  87.7 0.9 collective-permute-done
  88.7 1.3 collective-permute-start.1
  90.0 2.9 %collective-permute-done.1 = f32[136,16]{1,0:T(8,128)S(1)} collective-permute-done((f32[136,16]{1,0:T(8,128)S(1)}, f32[136,16]{1,0:T(8,128)S(1)}, u32[]{:S(2)}, u32[]{:S(2)}) %collective-permute-start.1) | collective-permute-done | bytes 8736 | tf_op jit(solution)/shard_map/ppermute | solution.py:262
  92.9 1.3 collective-permute-start.2
  94.2 3.1 %collective-permute-done.2 = f32[136,16]{1,0:T(8,128)S(1)} collective-permute-done((f32[136,16]{1,0:T(8,128)S(1)}, f32[136,16]{1,0:T(8,128)S(1)}, u32[]{:S(2)}, u32[]{:S(2)}) %collective-permute-start.2) | collective-permute-done | bytes 8736 | tf_op jit(solution)/shard_map/ppermute | solution.py:262
  97.4 7.7 %collective-permute-start.3 = (f32[136,16]{1,0:T(8,128)S(1)}, f32[136,16]{1,0:T(8,128)S(1)}, u32[]{:S(2)}, u32[]{:S(2)}) collective-permute-start(f32[136,16]{1,0:T(8,128)S(1)} %add.121), channel_id=1, source_target_pairs={{0,8},{1,9},{2,10},{3,11},{4,12},{5,13},{6,14},{7,15},{8,0},{9,1},... | collective-permute-start | bytes 26120 | tf_op jit(solution)/shard_map/ppermute | solution.py:262
  105.0 5.2 %collective-permute-done.3 = f32[136,16]{1,0:T(8,128)S(1)} collective-permute-done((f32[136,16]{1,0:T(8,128)S(1)}, f32[136,16]{1,0:T(8,128)S(1)}, u32[]{:S(2)}, u32[]{:S(2)}) %collective-permute-start.3) | collective-permute-done | bytes 8736 | tf_op jit(solution)/shard_map/ppermute | solution.py:262
  110.2 2.6 %collective-permute-start.4 = (f32[136,16]{1,0:T(8,128)S(1)}, f32[136,16]{1,0:T(8,128)S(1)}, u32[]{:S(2)}, u32[]{:S(2)}) collective-permute-start(f32[136,16]{1,0:T(8,128)S(1)} %add.122.first), channel_id=1, source_target_pairs={{0,16},{1,17},{2,18},{3,19},{4,20},{5,21},{6,22},{7,23},{8,24},{9,... | collective-permute-start | bytes 26120 | tf_op jit(solution)/shard_map/ppermute | solution.py:262
  113.0 10.9 %all-to-all-done.3._.recv = f32[32,4,32,128]{3,2,1,0:T(8,128)} async-done(((f32[32,4,32,128]{3,2,1,0:T(8,128)}), f32[32,4,32,128]{3,2,1,0:T(8,128)}, u32[]{:S(2)}, u32[]{:S(2)}) %all-to-all-start.3) | async-done | bytes 2097184 | tf_op jit(solution)/shard_map/all_to_all | solution.py:310
  123.9 3.2 %all-to-all-start.1 = ((f32[32,4,32,128]{3,2,1,0:T(8,128)}), f32[32,4,32,128]{3,2,1,0:T(8,128)S(1)}, u32[]{:S(2)}, u32[]{:S(2)}) async-start(f32[32,4,32,128]{3,2,1,0:T(8,128)} %get-tuple-element.6), calls=%async_computation.1 | async-start | bytes 4194304 | tf_op jit(solution)/shard_map/all_to_all | solution.py:310
  127.2 0.6 copy-done.8
  127.8 1.5 last_sum.1
  129.3 0.7 slice.121
  130.0 0.9 slice_multiply_fusion
  130.9 1.1 fusion.10
  132.1 1.1 fusion.16
  133.2 0.9 fusion.37
  134.1 0.7 cholesky.16
  134.8 0.6 compare_reduce_fusion
  135.5 0.6 fusion.27
  136.1 0.6 custom-call.10
  136.8 1.1 fusion.12
  137.9 1.1 convolution_subtract_fusion
  140.5 0.6 pad_maximum_fusion.6
  141.2 2.2 %copy-done.1 = f32[8,2,4,128,128]{4,3,2,1,0:T(8,128)S(1)} copy-done((f32[8,2,4,128,128]{4,3,2,1,0:T(8,128)S(1)}, f32[8,2,4,128,128]{4,3,2,1,0:T(8,128)}, u32[]{:S(2)}) %copy-start.1) | copy-done | bytes 4194328
  143.4 2.2 %copy-done.2 = f32[8,8,2,8192]{3,2,1,0:T(2,128)S(1)} copy-done((f32[8,8,2,8192]{3,2,1,0:T(2,128)S(1)}, f32[8,8,2,8192]{3,2,1,0:T(2,128)}, u32[]{:S(2)}) %copy-start.2) | copy-done | bytes 4194328
  145.6 8.7 %base.1 = f32[8,2,4,128,128]{4,3,2,1,0:T(8,128)} custom-call(f32[8,2,4,128,128]{4,3,2,1,0:T(8,128)S(1)} %copy-done.1, f32[8,1024,128]{2,1,0:T(8,128)S(1)} %bitcast.75, f32[4,128,128]{2,1,0:T(8,128)S(1)} %copy-done, f32[8,16,32]{2,1,0:T(8,128)S(1)} %pad_maximum_fusion.4.coefs), custom_call_target="tpu_custom_call" | custom-call | flops 8000000000 | bytes 12000000 | tf_op jit(solution)/shard_map/base/pallas_call | solution.py:467
  154.3 3.7 %to_planes.2.base = f32[8,2,4,128,128]{4,3,2,1,0:T(8,128)} custom-call(f32[32,4,32,128]{3,2,1,0:T(8,128)} %all-to-all-done.3._.recv, f32[8,2,4,128,128]{4,3,2,1,0:T(8,128)} %base.1, bf16[256,768]{1,0:T(8,128)(2,1)S(1)} %copy-done.3), custom_call_target="tpu_custom_call", output_to_operand_aliasing={{}: (1, {})} | custom-call | flops 8000000000 | bytes 12000000 | tf_op jit(solution)/shard_map/to_planes/pallas_call | solution.py:484
  158.0 18.4 %all-to-all-done.1.recv = f32[32,4,32,128]{3,2,1,0:T(8,128)S(1)} async-done(((f32[32,4,32,128]{3,2,1,0:T(8,128)}), f32[32,4,32,128]{3,2,1,0:T(8,128)S(1)}, u32[]{:S(2)}, u32[]{:S(2)}) %all-to-all-start.1) | async-done | bytes 2097184 | tf_op jit(solution)/shard_map/all_to_all | solution.py:310
  176.4 3.5 %to_planes.3 = f32[8,2,4,128,128]{4,3,2,1,0:T(8,128)} custom-call(f32[32,4,32,128]{3,2,1,0:T(8,128)S(1)} %all-to-all-done.1.recv, f32[8,2,4,128,128]{4,3,2,1,0:T(8,128)} %to_planes.2.base, bf16[256,768]{1,0:T(8,128)(2,1)S(1)} %copy-done.3), custom_call_target="tpu_custom_call", output_to_operand_aliasing={{}: (1, {})} | custom-call | flops 8000000000 | bytes 12000000 | tf_op jit(solution)/shard_map/to_planes/pallas_call | solution.py:484
  (78 shorter events, 4.8 us)
Async XLA Ops:
  0.6 10.3 %copy-start.11 = (s32[32]{0:T(128)S(1)}, s32[32]{0:T(128)}, u32[]{:S(2)}) copy-start(s32[32]{0:T(128)} %constant.116) | copy-start | bytes 388
  0.6 10.1 %copy-start.10 = (s32[128]{0:T(128)S(1)}, s32[128]{0:T(128)}, u32[]{:S(2)}) copy-start(s32[128]{0:T(128)} %param.13) | copy-start | bytes 1540
  3.6 33.0 %all-to-all-start.2 = ((f32[32,2,32,128]{3,2,1,0:T(8,128)}), f32[32,2,32,128]{3,2,1,0:T(8,128)}, u32[]{:S(2)}, u32[]{:S(2)}) async-start(f32[32,2,32,128]{3,2,1,0:T(8,128)} %to_rows.3), calls=%async_computation.2 | async-start | bytes 2097152 | tf_op jit(solution)/shard_map/all_to_all | solution.py:310
  36.6 30.9 %all-to-all-start = ((f32[32,2,32,128]{3,2,1,0:T(8,128)}), f32[32,2,32,128]{3,2,1,0:T(8,128)}, u32[]{:S(2)}, u32[]{:S(2)}) async-start(f32[32,2,32,128]{3,2,1,0:T(8,128)} %to_rows.2), calls=%async_computation | async-start | bytes 2097152 | tf_op jit(solution)/shard_map/all_to_all | solution.py:310
  41.6 11.4 %copy-start.5 = (f32[128,4,128]{2,1,0:T(4,128)S(1)}, f32[128,4,128]{2,1,0:T(4,128)}, u32[]{:S(2)}) copy-start(f32[128,4,128]{2,1,0:T(4,128)} %param.14) | copy-start | bytes 786436
  41.6 12.9 %copy-start.12 = (s32[8,8]{1,0:T(8,128)S(1)}, s32[8,8]{1,0:T(8,128)}, u32[]{:S(2)}) copy-start(s32[8,8]{1,0:T(8,128)} %param.16) | copy-start | bytes 772
  63.4 9.2 %copy-start.7 = (f32[8,32,16]{2,1,0:T(8,128)S(1)}, f32[8,32,16]{2,1,0:T(8,128)}, u32[]{:S(2)}) copy-start(f32[8,32,16]{2,1,0:T(8,128)} %project.1) | copy-start | bytes 49156
  67.5 56.4 %all-to-all-start.3 = ((f32[32,4,32,128]{3,2,1,0:T(8,128)}), f32[32,4,32,128]{3,2,1,0:T(8,128)}, u32[]{:S(2)}, u32[]{:S(2)}) async-start(f32[32,4,32,128]{3,2,1,0:T(8,128)} %get-tuple-element.7), calls=%async_computation.3 | async-start | bytes 4194304 | tf_op jit(solution)/shard_map/all_to_all | solution.py:310
  72.9 14.3 %copy-start.6 = (f32[128,16]{1,0:T(8,128)S(1)}, f32[128,16]{1,0:T(8,128)}, u32[]{:S(2)}) copy-start(f32[128,16]{1,0:T(8,128)} %convolution_bitcast_fusion._) | copy-start | bytes 24580
  72.9 39.9 %copy-start.9 = (f32[32,4]{0,1:T(4,128)S(1)}, f32[32,4]{0,1:T(4,128)}, u32[]{:S(2)}) copy-start(f32[32,4]{0,1:T(4,128)} %param.17) | copy-start | bytes 1540
  87.2 1.4 collective-permute-start
  88.7 4.2 %collective-permute-start.1 = (f32[136,16]{1,0:T(8,128)S(1)}, f32[136,16]{1,0:T(8,128)S(1)}, u32[]{:S(2)}, u32[]{:S(2)}) collective-permute-start(f32[136,16]{1,0:T(8,128)S(1)} %fusion.51), channel_id=1, source_target_pairs={{0,2},{1,3},{2,0},{3,1},{4,6},{5,7},{6,4},{7,5},{8,10},{9,11},{10,... | collective-permute-start | bytes 26120 | tf_op jit(solution)/shard_map/ppermute | solution.py:262
  92.9 4.5 %collective-permute-start.2 = (f32[136,16]{1,0:T(8,128)S(1)}, f32[136,16]{1,0:T(8,128)S(1)}, u32[]{:S(2)}, u32[]{:S(2)}) collective-permute-start(f32[136,16]{1,0:T(8,128)S(1)} %add.120), channel_id=1, source_target_pairs={{0,4},{1,5},{2,6},{3,7},{4,0},{5,1},{6,2},{7,3},{8,12},{9,13},{10,... | collective-permute-start | bytes 26120 | tf_op jit(solution)/shard_map/ppermute | solution.py:262
  97.4 12.8 %collective-permute-start.3 = (f32[136,16]{1,0:T(8,128)S(1)}, f32[136,16]{1,0:T(8,128)S(1)}, u32[]{:S(2)}, u32[]{:S(2)}) collective-permute-start(f32[136,16]{1,0:T(8,128)S(1)} %add.121), channel_id=1, source_target_pairs={{0,8},{1,9},{2,10},{3,11},{4,12},{5,13},{6,14},{7,15},{8,0},{9,1},... | collective-permute-start | bytes 26120 | tf_op jit(solution)/shard_map/ppermute | solution.py:262
  110.2 17.0 %copy-start.4 = (f32[136,16]{1,0:T(8,128)}, f32[136,16]{1,0:T(8,128)S(1)}, u32[]{:S(2)}) copy-start(f32[136,16]{1,0:T(8,128)S(1)} %add.122.first) | copy-start | bytes 26116
  110.2 16.9 %collective-permute-start.4 = (f32[136,16]{1,0:T(8,128)S(1)}, f32[136,16]{1,0:T(8,128)S(1)}, u32[]{:S(2)}, u32[]{:S(2)}) collective-permute-start(f32[136,16]{1,0:T(8,128)S(1)} %add.122.first), channel_id=1, source_target_pairs={{0,16},{1,17},{2,18},{3,19},{4,20},{5,21},{6,22},{7,23},{8,24},{9,... | collective-permute-start | bytes 26120 | tf_op jit(solution)/shard_map/ppermute | solution.py:262
  123.9 17.3 %copy-start = (f32[4,128,128]{2,1,0:T(8,128)S(1)}, f32[4,128,128]{2,1,0:T(8,128)}, u32[]{:S(2)}) copy-start(f32[4,128,128]{2,1,0:T(8,128)} %add_multiply_fusion.kinetic) | copy-start | bytes 786436
  123.9 52.5 %all-to-all-start.1 = ((f32[32,4,32,128]{3,2,1,0:T(8,128)}), f32[32,4,32,128]{3,2,1,0:T(8,128)S(1)}, u32[]{:S(2)}, u32[]{:S(2)}) async-start(f32[32,4,32,128]{3,2,1,0:T(8,128)} %get-tuple-element.6), calls=%async_computation.1 | async-start | bytes 4194304 | tf_op jit(solution)/shard_map/all_to_all | solution.py:310
  127.2 0.6 copy-start.8
  141.2 2.2 %copy-start.1 = (f32[8,2,4,128,128]{4,3,2,1,0:T(8,128)S(1)}, f32[8,2,4,128,128]{4,3,2,1,0:T(8,128)}, u32[]{:S(2)}) copy-start(f32[8,2,4,128,128]{4,3,2,1,0:T(8,128)} %psi.7) | copy-start | bytes 12582916
  143.4 2.2 %copy-start.2 = (f32[8,8,2,8192]{3,2,1,0:T(2,128)S(1)}, f32[8,8,2,8192]{3,2,1,0:T(2,128)}, u32[]{:S(2)}) copy-start(f32[8,8,2,8192]{3,2,1,0:T(2,128)} %param.15) | copy-start | bytes 12582916
  145.6 8.7 %copy-start.3 = (bf16[256,768]{1,0:T(8,128)(2,1)S(1)}, bf16[256,768]{1,0:T(8,128)(2,1)}, u32[]{:S(2)}) copy-start(bf16[256,768]{1,0:T(8,128)(2,1)} %constant.106.clone.y_table) | copy-start | bytes 1179652

commit v17 on v16

--- a/solution.py
+++ b/solution.py
@@ -302,7 +302,7 @@
         return pl.CostEstimate(flops=flops, bytes_accessed=moved, transcendentals=0)
 
     layers = 4 if devices % 4 == 0 else 1
-    ranks = np.arange(devices).reshape(layers, -1)[[0, 2, 1, 3] if layers == 4 else [0]].T.reshape(-1)
+    ranks = np.arange(devices).reshape(layers, -1)[[0, 1, 3, 2] if layers == 4 else [0]].T.reshape(-1)
     order = np.arange(2 * span_y)
     order = (order % 2) * span_y + (ranks[:, None] * rows + np.arange(rows)).reshape(-1)[order // 2]
 

time: 182 us -> 181 us (level)
  starting transfers between devices: 33.7 us -> 30.9 us
where the time goes in v17:
time: 181 us; the launch traced here: 179 us
  waiting for transfers between devices  67 us (37%)
  Pallas kernels  54.7 us (30%)
  starting transfers between devices  30.9 us (17%)
  local copies, waits for them, and re-layouts  10.4 us (6%)
  other arithmetic  8.86 us (5%)
  matrix products  6.01 us (3%)
    all_to_all x4, waiting for transfers between devices, exchange(): lax.all_to_all(values, 'ga', split_axis=0, concat_axis=0, axis_index_grou...  53.3 us
    all_to_all x4, starting transfers between devices, exchange(): lax.all_to_all(values, 'ga', split_axis=0, concat_axis=0, axis_index_grou...  19.2 us
    pallas_call x2, Pallas kernels, on_device(): pl.pallas_call(functools.partial(real_space_kernel, rows, planes), out_sh...  16.1 us
    ppermute x5, waiting for transfers between devices, partner(): return lax.ppermute(values, 'ga', [(d, d ^ k) for d in range(devices)])  13.7 us
    ppermute x5, starting transfers between devices, partner(): return lax.ppermute(values, 'ga', [(d, d ^ k) for d in range(devices)])  11.6 us
    pallas_call x1, Pallas kernels, on_device(): pl.pallas_call(functools.partial(project_kernel, slots), out_shape=jax.Sh...  10.1 us
    pallas_call x1, Pallas kernels, on_device(): pl.pallas_call(functools.partial(base_kernel, slots), out_shape=jax.Shape...  8.68 us
    pallas_call x2, Pallas kernels, on_device(): pl.pallas_call(to_planes_kernel, out_shape=jax.ShapeDtypeStruct(orbitals....  7.19 us
  transfers between devices with their start and end apart: 9, of which 8 were waited for; matrix products, arithmetic and copies ran while one was open for 11% of the time, Pallas kernels for 27%

profile of v17, /device:TPU:1, one launch (start us, length us, event | category | flops | bytes accessed | tf_op | source)
XLA Modules:
  0.0 178.8 jit_solution(17131196854443632388)
XLA Ops:
  0.7 2.9 %to_rows.3 = f32[32,2,32,128]{3,2,1,0:T(8,128)} custom-call(f32[8,2,4,128,128]{4,3,2,1,0:T(8,128)} %psi.7, bf16[256,768]{1,0:T(8,128)(2,1)} %constant.105.clone.y_table), custom_call_target="tpu_custom_call" | custom-call | flops 4000000000 | bytes 3000000 | tf_op jit(solution)/shard_map/to_rows/pallas_call | solution.py:328
  3.6 7.2 %all-to-all-start.2 = ((f32[32,2,32,128]{3,2,1,0:T(8,128)}), f32[32,2,32,128]{3,2,1,0:T(8,128)}, u32[]{:S(2)}, u32[]{:S(2)}) async-start(f32[32,2,32,128]{3,2,1,0:T(8,128)} %to_rows.3), calls=%async_computation.2 | async-start | bytes 2097152 | tf_op jit(solution)/shard_map/all_to_all | solution.py:310
  12.1 0.9 copy.120.inverse
  13.2 0.9 add_multiply_fusion.kinetic
  14.0 3.0 %to_rows.2 = f32[32,2,32,128]{3,2,1,0:T(8,128)} custom-call(f32[8,2,4,128,128]{4,3,2,1,0:T(8,128)} %psi.7, bf16[256,768]{1,0:T(8,128)(2,1)} %constant.105.clone.y_table), custom_call_target="tpu_custom_call" | custom-call | flops 4000000000 | bytes 3000000 | tf_op jit(solution)/shard_map/to_rows/pallas_call | solution.py:328
  17.0 20.1 %all-to-all-done.2.recv = f32[32,2,32,128]{3,2,1,0:T(8,128)} async-done(((f32[32,2,32,128]{3,2,1,0:T(8,128)}), f32[32,2,32,128]{3,2,1,0:T(8,128)}, u32[]{:S(2)}, u32[]{:S(2)}) %all-to-all-start.2) | async-done | bytes 1048608 | tf_op jit(solution)/shard_map/all_to_all | solution.py:310
  37.0 4.1 %all-to-all-start = ((f32[32,2,32,128]{3,2,1,0:T(8,128)}), f32[32,2,32,128]{3,2,1,0:T(8,128)}, u32[]{:S(2)}, u32[]{:S(2)}) async-start(f32[32,2,32,128]{3,2,1,0:T(8,128)} %to_rows.2), calls=%async_computation | async-start | bytes 2097152 | tf_op jit(solution)/shard_map/all_to_all | solution.py:310
  41.1 10.1 %project.1 = f32[8,32,16]{2,1,0:T(8,128)} custom-call(f32[8,2,4,128,128]{4,3,2,1,0:T(8,128)} %psi.7, f32[8,1024,128]{2,1,0:T(8,128)} %bitcast.74, f32[4,128,128]{2,1,0:T(8,128)} %add_multiply_fusion.kinetic), custom_call_target="tpu_custom_call" | custom-call | flops 8000000000 | bytes 8000000 | tf_op jit(solution)/shard_map/project/pallas_call | solution.py:375
  51.2 0.8 fusion.47
  52.6 0.7 copy.111
  53.3 0.7 pad_maximum_fusion.1.forward
  54.0 0.9 convolution_bitcast_fusion._
  55.0 8.0 %real_space.3 = (f32[32,4,32,128]{3,2,1,0:T(8,128)}, f32[4,512,128]{2,1,0:T(8,128)}) custom-call(f32[32,2,32,128]{3,2,1,0:T(8,128)} %all-to-all-done.2.recv, f32[512,128]{1,0:T(8,128)} %bitcast.76, bf16[256,768]{1,0:T(8,128)(2,1)} %copy.120.inverse, bf16[256,384]{1,0:T(8,128)(2,1)} %pad_maximum_fusion.1.forward, bf16[768,256]{1,0:T(8,128)(2,1)} %constant.107.clone.inv_z, ...), custom_call_target="tpu_custom_call" | custom-call | flops 4000000000 | bytes 8000000 | tf_op jit(solution)/shard_map/real_space/pallas_call | solution.py:403
  63.0 4.6 %all-to-all-done.recv = f32[32,2,32,128]{3,2,1,0:T(8,128)} async-done(((f32[32,2,32,128]{3,2,1,0:T(8,128)}), f32[32,2,32,128]{3,2,1,0:T(8,128)}, u32[]{:S(2)}, u32[]{:S(2)}) %all-to-all-start) | async-done | bytes 1048608 | tf_op jit(solution)/shard_map/all_to_all | solution.py:310
  67.5 4.2 %all-to-all-start.3 = ((f32[32,4,32,128]{3,2,1,0:T(8,128)}), f32[32,4,32,128]{3,2,1,0:T(8,128)}, u32[]{:S(2)}, u32[]{:S(2)}) async-start(f32[32,4,32,128]{3,2,1,0:T(8,128)} %get-tuple-element.7), calls=%async_computation.3 | async-start | bytes 4194304 | tf_op jit(solution)/shard_map/all_to_all | solution.py:310
  72.0 8.1 %real_space.2 = (f32[32,4,32,128]{3,2,1,0:T(8,128)}, f32[4,512,128]{2,1,0:T(8,128)}) custom-call(f32[32,2,32,128]{3,2,1,0:T(8,128)} %all-to-all-done.recv, f32[512,128]{1,0:T(8,128)} %bitcast.77, bf16[256,768]{1,0:T(8,128)(2,1)} %copy.120.inverse, bf16[256,384]{1,0:T(8,128)(2,1)} %pad_maximum_fusion.1.forward, bf16[768,256]{1,0:T(8,128)(2,1)} %constant.107.clone.inv_z, ...), custom_call_target="tpu_custom_call" | custom-call | flops 4000000000 | bytes 8000000 | tf_op jit(solution)/shard_map/real_space/pallas_call | solution.py:403
  80.1 5.2 %real_gram.1 = f32[2,8,8,128]{3,2,1,0:T(8,128)} custom-call(f32[4,512,128]{2,1,0:T(8,128)} %get-tuple-element.8.refs_0_, f32[4,512,128]{2,1,0:T(8,128)} %get-tuple-element.9.refs_1_, f32[512,128]{1,0:T(8,128)} %bitcast.78), custom_call_target="tpu_custom_call" | custom-call | flops 10000000 | bytes 2000000 | tf_op jit(solution)/shard_map/real_gram/pallas_call | solution.py:430
  85.3 0.9 reduce_sum.18
  86.8 0.9 collective-permute-done
  87.8 1.3 collective-permute-start.1
  89.1 3.0 %collective-permute-done.1 = f32[136,16]{1,0:T(8,128)S(1)} collective-permute-done((f32[136,16]{1,0:T(8,128)S(1)}, f32[136,16]{1,0:T(8,128)S(1)}, u32[]{:S(2)}, u32[]{:S(2)}) %collective-permute-start.1) | collective-permute-done | bytes 8736 | tf_op jit(solution)/shard_map/ppermute | solution.py:262
  92.1 1.3 collective-permute-start.2
  93.4 2.5 %collective-permute-done.2 = f32[136,16]{1,0:T(8,128)S(1)} collective-permute-done((f32[136,16]{1,0:T(8,128)S(1)}, f32[136,16]{1,0:T(8,128)S(1)}, u32[]{:S(2)}, u32[]{:S(2)}) %collective-permute-start.2) | collective-permute-done | bytes 8736 | tf_op jit(solution)/shard_map/ppermute | solution.py:262
  95.9 4.1 %collective-permute-start.3 = (f32[136,16]{1,0:T(8,128)S(1)}, f32[136,16]{1,0:T(8,128)S(1)}, u32[]{:S(2)}, u32[]{:S(2)}) collective-permute-start(f32[136,16]{1,0:T(8,128)S(1)} %add.121), channel_id=1, source_target_pairs={{0,8},{1,9},{2,10},{3,11},{4,12},{5,13},{6,14},{7,15},{8,0},{9,1},... | collective-permute-start | bytes 26120 | tf_op jit(solution)/shard_map/ppermute | solution.py:262
  100.0 7.2 %collective-permute-done.3 = f32[136,16]{1,0:T(8,128)S(1)} collective-permute-done((f32[136,16]{1,0:T(8,128)S(1)}, f32[136,16]{1,0:T(8,128)S(1)}, u32[]{:S(2)}, u32[]{:S(2)}) %collective-permute-start.3) | collective-permute-done | bytes 8736 | tf_op jit(solution)/shard_map/ppermute | solution.py:262
  107.3 4.5 %collective-permute-start.4 = (f32[136,16]{1,0:T(8,128)S(1)}, f32[136,16]{1,0:T(8,128)S(1)}, u32[]{:S(2)}, u32[]{:S(2)}) collective-permute-start(f32[136,16]{1,0:T(8,128)S(1)} %add.122.first), channel_id=1, source_target_pairs={{0,16},{1,17},{2,18},{3,19},{4,20},{5,21},{6,22},{7,23},{8,24},{9,... | collective-permute-start | bytes 26120 | tf_op jit(solution)/shard_map/ppermute | solution.py:262
  112.0 10.4 %all-to-all-done.3._.recv = f32[32,4,32,128]{3,2,1,0:T(8,128)} async-done(((f32[32,4,32,128]{3,2,1,0:T(8,128)}), f32[32,4,32,128]{3,2,1,0:T(8,128)}, u32[]{:S(2)}, u32[]{:S(2)}) %all-to-all-start.3) | async-done | bytes 2097184 | tf_op jit(solution)/shard_map/all_to_all | solution.py:310
  122.4 3.8 %all-to-all-start.1 = ((f32[32,4,32,128]{3,2,1,0:T(8,128)}), f32[32,4,32,128]{3,2,1,0:T(8,128)S(1)}, u32[]{:S(2)}, u32[]{:S(2)}) async-start(f32[32,4,32,128]{3,2,1,0:T(8,128)} %get-tuple-element.6), calls=%async_computation.1 | async-start | bytes 4194304 | tf_op jit(solution)/shard_map/all_to_all | solution.py:310
  126.2 0.6 copy-done.8
  126.9 1.5 last_sum.1
  128.4 0.7 slice.121
  129.1 0.9 slice_multiply_fusion
  130.0 1.1 fusion.10
  131.1 1.1 fusion.16
  132.3 0.9 fusion.37
  133.2 0.7 cholesky.16
  133.9 0.6 compare_reduce_fusion
  134.6 0.6 fusion.27
  135.2 0.6 custom-call.10
  135.9 1.1 fusion.12
  137.0 1.1 convolution_subtract_fusion
  139.6 0.6 pad_maximum_fusion.6
  140.3 2.2 %copy-done.1 = f32[8,2,4,128,128]{4,3,2,1,0:T(8,128)S(1)} copy-done((f32[8,2,4,128,128]{4,3,2,1,0:T(8,128)S(1)}, f32[8,2,4,128,128]{4,3,2,1,0:T(8,128)}, u32[]{:S(2)}) %copy-start.1) | copy-done | bytes 4194328
  142.5 2.2 %copy-done.2 = f32[8,8,2,8192]{3,2,1,0:T(2,128)S(1)} copy-done((f32[8,8,2,8192]{3,2,1,0:T(2,128)S(1)}, f32[8,8,2,8192]{3,2,1,0:T(2,128)}, u32[]{:S(2)}) %copy-start.2) | copy-done | bytes 4194328
  144.7 8.7 %base.1 = f32[8,2,4,128,128]{4,3,2,1,0:T(8,128)} custom-call(f32[8,2,4,128,128]{4,3,2,1,0:T(8,128)S(1)} %copy-done.1, f32[8,1024,128]{2,1,0:T(8,128)S(1)} %bitcast.75, f32[4,128,128]{2,1,0:T(8,128)S(1)} %copy-done, f32[8,16,32]{2,1,0:T(8,128)S(1)} %pad_maximum_fusion.4.coefs), custom_call_target="tpu_custom_call" | custom-call | flops 8000000000 | bytes 12000000 | tf_op jit(solution)/shard_map/base/pallas_call | solution.py:467
  153.4 3.7 %to_planes.2.base = f32[8,2,4,128,128]{4,3,2,1,0:T(8,128)} custom-call(f32[32,4,32,128]{3,2,1,0:T(8,128)} %all-to-all-done.3._.recv, f32[8,2,4,128,128]{4,3,2,1,0:T(8,128)} %base.1, bf16[256,768]{1,0:T(8,128)(2,1)S(1)} %copy-done.3), custom_call_target="tpu_custom_call", output_to_operand_aliasing={{}: (1, {})} | custom-call | flops 8000000000 | bytes 12000000 | tf_op jit(solution)/shard_map/to_planes/pallas_call | solution.py:484
  157.1 18.2 %all-to-all-done.1.recv = f32[32,4,32,128]{3,2,1,0:T(8,128)S(1)} async-done(((f32[32,4,32,128]{3,2,1,0:T(8,128)}), f32[32,4,32,128]{3,2,1,0:T(8,128)S(1)}, u32[]{:S(2)}, u32[]{:S(2)}) %all-to-all-start.1) | async-done | bytes 2097184 | tf_op jit(solution)/shard_map/all_to_all | solution.py:310
  175.4 3.5 %to_planes.3 = f32[8,2,4,128,128]{4,3,2,1,0:T(8,128)} custom-call(f32[32,4,32,128]{3,2,1,0:T(8,128)S(1)} %all-to-all-done.1.recv, f32[8,2,4,128,128]{4,3,2,1,0:T(8,128)} %to_planes.2.base, bf16[256,768]{1,0:T(8,128)(2,1)S(1)} %copy-done.3), custom_call_target="tpu_custom_call", output_to_operand_aliasing={{}: (1, {})} | custom-call | flops 8000000000 | bytes 12000000 | tf_op jit(solution)/shard_map/to_planes/pallas_call | solution.py:484
  (78 shorter events, 4.8 us)
Async XLA Ops:
  0.6 10.3 %copy-start.11 = (s32[32]{0:T(128)S(1)}, s32[32]{0:T(128)}, u32[]{:S(2)}) copy-start(s32[32]{0:T(128)} %constant.116) | copy-start | bytes 388
  0.6 10.1 %copy-start.10 = (s32[128]{0:T(128)S(1)}, s32[128]{0:T(128)}, u32[]{:S(2)}) copy-start(s32[128]{0:T(128)} %param.13) | copy-start | bytes 1540
  3.6 33.4 %all-to-all-start.2 = ((f32[32,2,32,128]{3,2,1,0:T(8,128)}), f32[32,2,32,128]{3,2,1,0:T(8,128)}, u32[]{:S(2)}, u32[]{:S(2)}) async-start(f32[32,2,32,128]{3,2,1,0:T(8,128)} %to_rows.3), calls=%async_computation.2 | async-start | bytes 2097152 | tf_op jit(solution)/shard_map/all_to_all | solution.py:310
  37.0 30.5 %all-to-all-start = ((f32[32,2,32,128]{3,2,1,0:T(8,128)}), f32[32,2,32,128]{3,2,1,0:T(8,128)}, u32[]{:S(2)}, u32[]{:S(2)}) async-start(f32[32,2,32,128]{3,2,1,0:T(8,128)} %to_rows.2), calls=%async_computation | async-start | bytes 2097152 | tf_op jit(solution)/shard_map/all_to_all | solution.py:310
  41.1 11.4 %copy-start.5 = (f32[128,4,128]{2,1,0:T(4,128)S(1)}, f32[128,4,128]{2,1,0:T(4,128)}, u32[]{:S(2)}) copy-start(f32[128,4,128]{2,1,0:T(4,128)} %param.14) | copy-start | bytes 786436
  41.1 12.9 %copy-start.12 = (s32[8,8]{1,0:T(8,128)S(1)}, s32[8,8]{1,0:T(8,128)}, u32[]{:S(2)}) copy-start(s32[8,8]{1,0:T(8,128)} %param.16) | copy-start | bytes 772
  63.0 8.7 %copy-start.7 = (f32[8,32,16]{2,1,0:T(8,128)S(1)}, f32[8,32,16]{2,1,0:T(8,128)}, u32[]{:S(2)}) copy-start(f32[8,32,16]{2,1,0:T(8,128)} %project.1) | copy-start | bytes 49156
  67.5 54.9 %all-to-all-start.3 = ((f32[32,4,32,128]{3,2,1,0:T(8,128)}), f32[32,4,32,128]{3,2,1,0:T(8,128)}, u32[]{:S(2)}, u32[]{:S(2)}) async-start(f32[32,4,32,128]{3,2,1,0:T(8,128)} %get-tuple-element.7), calls=%async_computation.3 | async-start | bytes 4194304 | tf_op jit(solution)/shard_map/all_to_all | solution.py:310
  72.0 14.3 %copy-start.6 = (f32[128,16]{1,0:T(8,128)S(1)}, f32[128,16]{1,0:T(8,128)}, u32[]{:S(2)}) copy-start(f32[128,16]{1,0:T(8,128)} %convolution_bitcast_fusion._) | copy-start | bytes 24580
  72.0 39.8 %copy-start.9 = (f32[32,4]{0,1:T(4,128)S(1)}, f32[32,4]{0,1:T(4,128)}, u32[]{:S(2)}) copy-start(f32[32,4]{0,1:T(4,128)} %param.17) | copy-start | bytes 1540
  86.3 1.4 collective-permute-start
  87.8 4.3 %collective-permute-start.1 = (f32[136,16]{1,0:T(8,128)S(1)}, f32[136,16]{1,0:T(8,128)S(1)}, u32[]{:S(2)}, u32[]{:S(2)}) collective-permute-start(f32[136,16]{1,0:T(8,128)S(1)} %fusion.51), channel_id=1, source_target_pairs={{0,2},{1,3},{2,0},{3,1},{4,6},{5,7},{6,4},{7,5},{8,10},{9,11},{10,... | collective-permute-start | bytes 26120 | tf_op jit(solution)/shard_map/ppermute | solution.py:262
  92.1 3.8 %collective-permute-start.2 = (f32[136,16]{1,0:T(8,128)S(1)}, f32[136,16]{1,0:T(8,128)S(1)}, u32[]{:S(2)}, u32[]{:S(2)}) collective-permute-start(f32[136,16]{1,0:T(8,128)S(1)} %add.120), channel_id=1, source_target_pairs={{0,4},{1,5},{2,6},{3,7},{4,0},{5,1},{6,2},{7,3},{8,12},{9,13},{10,... | collective-permute-start | bytes 26120 | tf_op jit(solution)/shard_map/ppermute | solution.py:262
  95.9 11.3 %collective-permute-start.3 = (f32[136,16]{1,0:T(8,128)S(1)}, f32[136,16]{1,0:T(8,128)S(1)}, u32[]{:S(2)}, u32[]{:S(2)}) collective-permute-start(f32[136,16]{1,0:T(8,128)S(1)} %add.121), channel_id=1, source_target_pairs={{0,8},{1,9},{2,10},{3,11},{4,12},{5,13},{6,14},{7,15},{8,0},{9,1},... | collective-permute-start | bytes 26120 | tf_op jit(solution)/shard_map/ppermute | solution.py:262
  107.3 19.0 %copy-start.4 = (f32[136,16]{1,0:T(8,128)}, f32[136,16]{1,0:T(8,128)S(1)}, u32[]{:S(2)}) copy-start(f32[136,16]{1,0:T(8,128)S(1)} %add.122.first) | copy-start | bytes 26116
  107.3 18.9 %collective-permute-start.4 = (f32[136,16]{1,0:T(8,128)S(1)}, f32[136,16]{1,0:T(8,128)S(1)}, u32[]{:S(2)}, u32[]{:S(2)}) collective-permute-start(f32[136,16]{1,0:T(8,128)S(1)} %add.122.first), channel_id=1, source_target_pairs={{0,16},{1,17},{2,18},{3,19},{4,20},{5,21},{6,22},{7,23},{8,24},{9,... | collective-permute-start | bytes 26120 | tf_op jit(solution)/shard_map/ppermute | solution.py:262
  122.4 17.9 %copy-start = (f32[4,128,128]{2,1,0:T(8,128)S(1)}, f32[4,128,128]{2,1,0:T(8,128)}, u32[]{:S(2)}) copy-start(f32[4,128,128]{2,1,0:T(8,128)} %add_multiply_fusion.kinetic) | copy-start | bytes 786436
  122.4 53.0 %all-to-all-start.1 = ((f32[32,4,32,128]{3,2,1,0:T(8,128)}), f32[32,4,32,128]{3,2,1,0:T(8,128)S(1)}, u32[]{:S(2)}, u32[]{:S(2)}) async-start(f32[32,4,32,128]{3,2,1,0:T(8,128)} %get-tuple-element.6), calls=%async_computation.1 | async-start | bytes 4194304 | tf_op jit(solution)/shard_map/all_to_all | solution.py:310
  126.2 0.6 copy-start.8
  140.3 2.2 %copy-start.1 = (f32[8,2,4,128,128]{4,3,2,1,0:T(8,128)S(1)}, f32[8,2,4,128,128]{4,3,2,1,0:T(8,128)}, u32[]{:S(2)}) copy-start(f32[8,2,4,128,128]{4,3,2,1,0:T(8,128)} %psi.7) | copy-start | bytes 12582916
  142.5 2.2 %copy-start.2 = (f32[8,8,2,8192]{3,2,1,0:T(2,128)S(1)}, f32[8,8,2,8192]{3,2,1,0:T(2,128)}, u32[]{:S(2)}) copy-start(f32[8,8,2,8192]{3,2,1,0:T(2,128)} %param.15) | copy-start | bytes 12582916
  144.7 8.7 %copy-start.3 = (bf16[256,768]{1,0:T(8,128)(2,1)S(1)}, bf16[256,768]{1,0:T(8,128)(2,1)}, u32[]{:S(2)}) copy-start(bf16[256,768]{1,0:T(8,128)(2,1)} %constant.106.clone.y_table) | copy-start | bytes 1179652

commit v18 on v17

--- a/solution.py
+++ b/solution.py
@@ -302,7 +302,8 @@
         return pl.CostEstimate(flops=flops, bytes_accessed=moved, transcendentals=0)
 
     layers = 4 if devices % 4 == 0 else 1
-    ranks = np.arange(devices).reshape(layers, -1)[[0, 1, 3, 2] if layers == 4 else [0]].T.reshape(-1)
+    cores = 2 if devices % 8 == 0 else 1
+    ranks = np.arange(devices).reshape(layers, -1, cores).T.reshape(-1)
     order = np.arange(2 * span_y)
     order = (order % 2) * span_y + (ranks[:, None] * rows + np.arange(rows)).reshape(-1)[order // 2]
 

time: 181 us -> 178 us (0.983)
  starting transfers between devices: 30.9 us -> 27.5 us
    ppermute x5, starting transfers between devices: 11.6 us -> 7.68 us  [partner(): return lax.ppermute(values, 'ga', [(d, d ^ k) for d in range(devices)])]
    ppermute x5, waiting for transfers between devices: 13.7 us -> 17.6 us  [partner(): return lax.ppermute(values, 'ga', [(d, d ^ k) for d in range(devices)])]
    all_to_all x4, waiting for transfers between devices: 53.3 us -> 49.6 us  [exchange(): lax.all_to_all(values, 'ga', split_axis=0, concat_axis=0, axis_index_grou...]
  transfers between devices with their start and end apart: 9 -> 9, of which waited for: 8 -> 8; matrix products, arithmetic and copies ran while one was open for 11% -> 12% of each run, Pallas kernels for 27% -> 27%
where the time goes in v18:
time: 178 us; the launch traced here: 176 us
  waiting for transfers between devices  67.2 us (38%)
  Pallas kernels  54.7 us (31%)
  starting transfers between devices  27.5 us (15%)
  local copies, waits for them, and re-layouts  10.4 us (6%)
  other arithmetic  8.86 us (5%)
  matrix products  6.01 us (3%)
    all_to_all x4, waiting for transfers between devices, exchange(): lax.all_to_all(values, 'ga', split_axis=0, concat_axis=0, axis_index_grou...  49.6 us
    all_to_all x4, starting transfers between devices, exchange(): lax.all_to_all(values, 'ga', split_axis=0, concat_axis=0, axis_index_grou...  19.8 us
    ppermute x5, waiting for transfers between devices, partner(): return lax.ppermute(values, 'ga', [(d, d ^ k) for d in range(devices)])  17.6 us
    pallas_call x2, Pallas kernels, on_device(): pl.pallas_call(functools.partial(real_space_kernel, rows, planes), out_sh...  16.1 us
    pallas_call x1, Pallas kernels, on_device(): pl.pallas_call(functools.partial(project_kernel, slots), out_shape=jax.Sh...  10.1 us
    pallas_call x1, Pallas kernels, on_device(): pl.pallas_call(functools.partial(base_kernel, slots), out_shape=jax.Shape...  8.68 us
    ppermute x5, starting transfers between devices, partner(): return lax.ppermute(values, 'ga', [(d, d ^ k) for d in range(devices)])  7.68 us
    pallas_call x2, Pallas kernels, on_device(): pl.pallas_call(to_planes_kernel, out_shape=jax.ShapeDtypeStruct(orbitals....  7.2 us
  transfers between devices with their start and end apart: 9, of which 8 were waited for; matrix products, arithmetic and copies ran while one was open for 12% of the time, Pallas kernels for 27%

profile of v18, /device:TPU:1, one launch (start us, length us, event | category | flops | bytes accessed | tf_op | source)
XLA Modules:
  0.0 175.7 jit_solution(17483447376163623387)
XLA Ops:
  0.7 2.9 %to_rows.3 = f32[32,2,32,128]{3,2,1,0:T(8,128)} custom-call(f32[8,2,4,128,128]{4,3,2,1,0:T(8,128)} %psi.7, bf16[256,768]{1,0:T(8,128)(2,1)} %constant.105.clone.y_table), custom_call_target="tpu_custom_call" | custom-call | flops 4000000000 | bytes 3000000 | tf_op jit(solution)/shard_map/to_rows/pallas_call | solution.py:329
  3.6 7.2 %all-to-all-start.2 = ((f32[32,2,32,128]{3,2,1,0:T(8,128)}), f32[32,2,32,128]{3,2,1,0:T(8,128)}, u32[]{:S(2)}, u32[]{:S(2)}) async-start(f32[32,2,32,128]{3,2,1,0:T(8,128)} %to_rows.3), calls=%async_computation.2 | async-start | bytes 2097152 | tf_op jit(solution)/shard_map/all_to_all | solution.py:311
  10.9 0.6 gather_fusion
  12.1 0.9 copy.120.inverse
  13.2 0.9 add_multiply_fusion.kinetic
  14.0 3.0 %to_rows.2 = f32[32,2,32,128]{3,2,1,0:T(8,128)} custom-call(f32[8,2,4,128,128]{4,3,2,1,0:T(8,128)} %psi.7, bf16[256,768]{1,0:T(8,128)(2,1)} %constant.105.clone.y_table), custom_call_target="tpu_custom_call" | custom-call | flops 4000000000 | bytes 3000000 | tf_op jit(solution)/shard_map/to_rows/pallas_call | solution.py:329
  17.0 19.6 %all-to-all-done.2.recv = f32[32,2,32,128]{3,2,1,0:T(8,128)} async-done(((f32[32,2,32,128]{3,2,1,0:T(8,128)}), f32[32,2,32,128]{3,2,1,0:T(8,128)}, u32[]{:S(2)}, u32[]{:S(2)}) %all-to-all-start.2) | async-done | bytes 1048608 | tf_op jit(solution)/shard_map/all_to_all | solution.py:311
  36.6 4.1 %all-to-all-start = ((f32[32,2,32,128]{3,2,1,0:T(8,128)}), f32[32,2,32,128]{3,2,1,0:T(8,128)}, u32[]{:S(2)}, u32[]{:S(2)}) async-start(f32[32,2,32,128]{3,2,1,0:T(8,128)} %to_rows.2), calls=%async_computation | async-start | bytes 2097152 | tf_op jit(solution)/shard_map/all_to_all | solution.py:311
  40.8 10.1 %project.1 = f32[8,32,16]{2,1,0:T(8,128)} custom-call(f32[8,2,4,128,128]{4,3,2,1,0:T(8,128)} %psi.7, f32[8,1024,128]{2,1,0:T(8,128)} %bitcast.74, f32[4,128,128]{2,1,0:T(8,128)} %add_multiply_fusion.kinetic), custom_call_target="tpu_custom_call" | custom-call | flops 8000000000 | bytes 8000000 | tf_op jit(solution)/shard_map/project/pallas_call | solution.py:376
  50.9 0.8 fusion.47
  52.2 0.7 copy.111
  53.0 0.7 pad_maximum_fusion.1.forward
  53.7 0.9 convolution_bitcast_fusion._
  54.6 8.0 %real_space.3 = (f32[32,4,32,128]{3,2,1,0:T(8,128)}, f32[4,512,128]{2,1,0:T(8,128)}) custom-call(f32[32,2,32,128]{3,2,1,0:T(8,128)} %all-to-all-done.2.recv, f32[512,128]{1,0:T(8,128)} %bitcast.76, bf16[256,768]{1,0:T(8,128)(2,1)} %copy.120.inverse, bf16[256,384]{1,0:T(8,128)(2,1)} %pad_maximum_fusion.1.forward, bf16[768,256]{1,0:T(8,128)(2,1)} %constant.107.clone.inv_z, ...), custom_call_target="tpu_custom_call" | custom-call | flops 4000000000 | bytes 8000000 | tf_op jit(solution)/shard_map/real_space/pallas_call | solution.py:404
  62.6 4.2 %all-to-all-done.recv = f32[32,2,32,128]{3,2,1,0:T(8,128)} async-done(((f32[32,2,32,128]{3,2,1,0:T(8,128)}), f32[32,2,32,128]{3,2,1,0:T(8,128)}, u32[]{:S(2)}, u32[]{:S(2)}) %all-to-all-start) | async-done | bytes 1048608 | tf_op jit(solution)/shard_map/all_to_all | solution.py:311
  66.8 4.2 %all-to-all-start.3 = ((f32[32,4,32,128]{3,2,1,0:T(8,128)}), f32[32,4,32,128]{3,2,1,0:T(8,128)}, u32[]{:S(2)}, u32[]{:S(2)}) async-start(f32[32,4,32,128]{3,2,1,0:T(8,128)} %get-tuple-element.7), calls=%async_computation.3 | async-start | bytes 4194304 | tf_op jit(solution)/shard_map/all_to_all | solution.py:311
  71.3 8.1 %real_space.2 = (f32[32,4,32,128]{3,2,1,0:T(8,128)}, f32[4,512,128]{2,1,0:T(8,128)}) custom-call(f32[32,2,32,128]{3,2,1,0:T(8,128)} %all-to-all-done.recv, f32[512,128]{1,0:T(8,128)} %bitcast.77, bf16[256,768]{1,0:T(8,128)(2,1)} %copy.120.inverse, bf16[256,384]{1,0:T(8,128)(2,1)} %pad_maximum_fusion.1.forward, bf16[768,256]{1,0:T(8,128)(2,1)} %constant.107.clone.inv_z, ...), custom_call_target="tpu_custom_call" | custom-call | flops 4000000000 | bytes 8000000 | tf_op jit(solution)/shard_map/real_space/pallas_call | solution.py:404
  79.4 5.2 %real_gram.1 = f32[2,8,8,128]{3,2,1,0:T(8,128)} custom-call(f32[4,512,128]{2,1,0:T(8,128)} %get-tuple-element.8.refs_0_, f32[4,512,128]{2,1,0:T(8,128)} %get-tuple-element.9.refs_1_, f32[512,128]{1,0:T(8,128)} %bitcast.78), custom_call_target="tpu_custom_call" | custom-call | flops 10000000 | bytes 2000000 | tf_op jit(solution)/shard_map/real_gram/pallas_call | solution.py:431
  84.6 0.9 reduce_sum.18
  86.1 0.9 collective-permute-done
  87.1 1.3 collective-permute-start.1
  88.4 4.1 %collective-permute-done.1 = f32[136,16]{1,0:T(8,128)S(1)} collective-permute-done((f32[136,16]{1,0:T(8,128)S(1)}, f32[136,16]{1,0:T(8,128)S(1)}, u32[]{:S(2)}, u32[]{:S(2)}) %collective-permute-start.1) | collective-permute-done | bytes 8736 | tf_op jit(solution)/shard_map/ppermute | solution.py:262
  92.5 1.4 collective-permute-start.2
  93.9 5.0 %collective-permute-done.2 = f32[136,16]{1,0:T(8,128)S(1)} collective-permute-done((f32[136,16]{1,0:T(8,128)S(1)}, f32[136,16]{1,0:T(8,128)S(1)}, u32[]{:S(2)}, u32[]{:S(2)}) %collective-permute-start.2) | collective-permute-done | bytes 8736 | tf_op jit(solution)/shard_map/ppermute | solution.py:262
  99.0 7.6 %collective-permute-done.3 = f32[136,16]{1,0:T(8,128)S(1)} collective-permute-done((f32[136,16]{1,0:T(8,128)S(1)}, f32[136,16]{1,0:T(8,128)S(1)}, u32[]{:S(2)}, u32[]{:S(2)}) %collective-permute-start.3) | collective-permute-done | bytes 8736 | tf_op jit(solution)/shard_map/ppermute | solution.py:262
  106.6 4.5 %collective-permute-start.4 = (f32[136,16]{1,0:T(8,128)S(1)}, f32[136,16]{1,0:T(8,128)S(1)}, u32[]{:S(2)}, u32[]{:S(2)}) collective-permute-start(f32[136,16]{1,0:T(8,128)S(1)} %add.122.first), channel_id=1, source_target_pairs={{0,16},{1,17},{2,18},{3,19},{4,20},{5,21},{6,22},{7,23},{8,24},{9,... | collective-permute-start | bytes 26120 | tf_op jit(solution)/shard_map/ppermute | solution.py:262
  111.3 9.1 %all-to-all-done.3._.recv = f32[32,4,32,128]{3,2,1,0:T(8,128)} async-done(((f32[32,4,32,128]{3,2,1,0:T(8,128)}), f32[32,4,32,128]{3,2,1,0:T(8,128)}, u32[]{:S(2)}, u32[]{:S(2)}) %all-to-all-start.3) | async-done | bytes 2097184 | tf_op jit(solution)/shard_map/all_to_all | solution.py:311
  120.3 4.3 %all-to-all-start.1 = ((f32[32,4,32,128]{3,2,1,0:T(8,128)}), f32[32,4,32,128]{3,2,1,0:T(8,128)S(1)}, u32[]{:S(2)}, u32[]{:S(2)}) async-start(f32[32,4,32,128]{3,2,1,0:T(8,128)} %get-tuple-element.6), calls=%async_computation.1 | async-start | bytes 4194304 | tf_op jit(solution)/shard_map/all_to_all | solution.py:311
  124.7 0.6 copy-done.8
  125.3 1.5 last_sum.1
  126.9 0.7 slice.121
  127.5 0.9 slice_multiply_fusion
  128.5 1.1 fusion.10
  129.6 1.1 fusion.16
  130.7 0.9 fusion.37
  131.6 0.7 cholesky.16
  132.4 0.6 compare_reduce_fusion
  133.0 0.6 fusion.27
  133.7 0.6 custom-call.10
  134.3 1.1 fusion.12
  135.4 1.1 convolution_subtract_fusion
  138.0 0.6 pad_maximum_fusion.6
  138.8 2.2 %copy-done.1 = f32[8,2,4,128,128]{4,3,2,1,0:T(8,128)S(1)} copy-done((f32[8,2,4,128,128]{4,3,2,1,0:T(8,128)S(1)}, f32[8,2,4,128,128]{4,3,2,1,0:T(8,128)}, u32[]{:S(2)}) %copy-start.1) | copy-done | bytes 4194328
  140.9 2.2 %copy-done.2 = f32[8,8,2,8192]{3,2,1,0:T(2,128)S(1)} copy-done((f32[8,8,2,8192]{3,2,1,0:T(2,128)S(1)}, f32[8,8,2,8192]{3,2,1,0:T(2,128)}, u32[]{:S(2)}) %copy-start.2) | copy-done | bytes 4194328
  143.1 8.7 %base.1 = f32[8,2,4,128,128]{4,3,2,1,0:T(8,128)} custom-call(f32[8,2,4,128,128]{4,3,2,1,0:T(8,128)S(1)} %copy-done.1, f32[8,1024,128]{2,1,0:T(8,128)S(1)} %bitcast.75, f32[4,128,128]{2,1,0:T(8,128)S(1)} %copy-done, f32[8,16,32]{2,1,0:T(8,128)S(1)} %pad_maximum_fusion.4.coefs), custom_call_target="tpu_custom_call" | custom-call | flops 8000000000 | bytes 12000000 | tf_op jit(solution)/shard_map/base/pallas_call | solution.py:468
  151.8 3.7 %to_planes.2.base = f32[8,2,4,128,128]{4,3,2,1,0:T(8,128)} custom-call(f32[32,4,32,128]{3,2,1,0:T(8,128)} %all-to-all-done.3._.recv, f32[8,2,4,128,128]{4,3,2,1,0:T(8,128)} %base.1, bf16[256,768]{1,0:T(8,128)(2,1)S(1)} %copy-done.3), custom_call_target="tpu_custom_call", output_to_operand_aliasing={{}: (1, {})} | custom-call | flops 8000000000 | bytes 12000000 | tf_op jit(solution)/shard_map/to_planes/pallas_call | solution.py:485
  155.6 16.7 %all-to-all-done.1.recv = f32[32,4,32,128]{3,2,1,0:T(8,128)S(1)} async-done(((f32[32,4,32,128]{3,2,1,0:T(8,128)}), f32[32,4,32,128]{3,2,1,0:T(8,128)S(1)}, u32[]{:S(2)}, u32[]{:S(2)}) %all-to-all-start.1) | async-done | bytes 2097184 | tf_op jit(solution)/shard_map/all_to_all | solution.py:311
  172.3 3.5 %to_planes.3 = f32[8,2,4,128,128]{4,3,2,1,0:T(8,128)} custom-call(f32[32,4,32,128]{3,2,1,0:T(8,128)S(1)} %all-to-all-done.1.recv, f32[8,2,4,128,128]{4,3,2,1,0:T(8,128)} %to_planes.2.base, bf16[256,768]{1,0:T(8,128)(2,1)S(1)} %copy-done.3), custom_call_target="tpu_custom_call", output_to_operand_aliasing={{}: (1, {})} | custom-call | flops 8000000000 | bytes 12000000 | tf_op jit(solution)/shard_map/to_planes/pallas_call | solution.py:485
  (78 shorter events, 4.3 us)
Async XLA Ops:
  0.6 10.3 %copy-start.11 = (s32[32]{0:T(128)S(1)}, s32[32]{0:T(128)}, u32[]{:S(2)}) copy-start(s32[32]{0:T(128)} %constant.116) | copy-start | bytes 388
  0.6 10.1 %copy-start.10 = (s32[128]{0:T(128)S(1)}, s32[128]{0:T(128)}, u32[]{:S(2)}) copy-start(s32[128]{0:T(128)} %param.13) | copy-start | bytes 1540
  3.6 33.0 %all-to-all-start.2 = ((f32[32,2,32,128]{3,2,1,0:T(8,128)}), f32[32,2,32,128]{3,2,1,0:T(8,128)}, u32[]{:S(2)}, u32[]{:S(2)}) async-start(f32[32,2,32,128]{3,2,1,0:T(8,128)} %to_rows.3), calls=%async_computation.2 | async-start | bytes 2097152 | tf_op jit(solution)/shard_map/all_to_all | solution.py:311
  36.6 30.1 %all-to-all-start = ((f32[32,2,32,128]{3,2,1,0:T(8,128)}), f32[32,2,32,128]{3,2,1,0:T(8,128)}, u32[]{:S(2)}, u32[]{:S(2)}) async-start(f32[32,2,32,128]{3,2,1,0:T(8,128)} %to_rows.2), calls=%async_computation | async-start | bytes 2097152 | tf_op jit(solution)/shard_map/all_to_all | solution.py:311
  40.8 11.4 %copy-start.5 = (f32[128,4,128]{2,1,0:T(4,128)S(1)}, f32[128,4,128]{2,1,0:T(4,128)}, u32[]{:S(2)}) copy-start(f32[128,4,128]{2,1,0:T(4,128)} %param.14) | copy-start | bytes 786436
  40.8 12.9 %copy-start.12 = (s32[8,8]{1,0:T(8,128)S(1)}, s32[8,8]{1,0:T(8,128)}, u32[]{:S(2)}) copy-start(s32[8,8]{1,0:T(8,128)} %param.16) | copy-start | bytes 772
  62.6 8.4 %copy-start.7 = (f32[8,32,16]{2,1,0:T(8,128)S(1)}, f32[8,32,16]{2,1,0:T(8,128)}, u32[]{:S(2)}) copy-start(f32[8,32,16]{2,1,0:T(8,128)} %project.1) | copy-start | bytes 49156
  66.8 53.6 %all-to-all-start.3 = ((f32[32,4,32,128]{3,2,1,0:T(8,128)}), f32[32,4,32,128]{3,2,1,0:T(8,128)}, u32[]{:S(2)}, u32[]{:S(2)}) async-start(f32[32,4,32,128]{3,2,1,0:T(8,128)} %get-tuple-element.7), calls=%async_computation.3 | async-start | bytes 4194304 | tf_op jit(solution)/shard_map/all_to_all | solution.py:311
  71.3 14.3 %copy-start.6 = (f32[128,16]{1,0:T(8,128)S(1)}, f32[128,16]{1,0:T(8,128)}, u32[]{:S(2)}) copy-start(f32[128,16]{1,0:T(8,128)} %convolution_bitcast_fusion._) | copy-start | bytes 24580
  71.3 39.8 %copy-start.9 = (f32[32,4]{0,1:T(4,128)S(1)}, f32[32,4]{0,1:T(4,128)}, u32[]{:S(2)}) copy-start(f32[32,4]{0,1:T(4,128)} %param.17) | copy-start | bytes 1540
  85.6 1.4 collective-permute-start
  87.1 5.4 %collective-permute-start.1 = (f32[136,16]{1,0:T(8,128)S(1)}, f32[136,16]{1,0:T(8,128)S(1)}, u32[]{:S(2)}, u32[]{:S(2)}) collective-permute-start(f32[136,16]{1,0:T(8,128)S(1)} %fusion.51), channel_id=1, source_target_pairs={{0,2},{1,3},{2,0},{3,1},{4,6},{5,7},{6,4},{7,5},{8,10},{9,11},{10,... | collective-permute-start | bytes 26120 | tf_op jit(solution)/shard_map/ppermute | solution.py:262
  92.5 6.3 %collective-permute-start.2 = (f32[136,16]{1,0:T(8,128)S(1)}, f32[136,16]{1,0:T(8,128)S(1)}, u32[]{:S(2)}, u32[]{:S(2)}) collective-permute-start(f32[136,16]{1,0:T(8,128)S(1)} %add.120), channel_id=1, source_target_pairs={{0,4},{1,5},{2,6},{3,7},{4,0},{5,1},{6,2},{7,3},{8,12},{9,13},{10,... | collective-permute-start | bytes 26120 | tf_op jit(solution)/shard_map/ppermute | solution.py:262
  98.9 7.7 %collective-permute-start.3 = (f32[136,16]{1,0:T(8,128)S(1)}, f32[136,16]{1,0:T(8,128)S(1)}, u32[]{:S(2)}, u32[]{:S(2)}) collective-permute-start(f32[136,16]{1,0:T(8,128)S(1)} %add.121), channel_id=1, source_target_pairs={{0,8},{1,9},{2,10},{3,11},{4,12},{5,13},{6,14},{7,15},{8,0},{9,1},... | collective-permute-start | bytes 26120 | tf_op jit(solution)/shard_map/ppermute | solution.py:262
  106.6 18.1 %copy-start.4 = (f32[136,16]{1,0:T(8,128)}, f32[136,16]{1,0:T(8,128)S(1)}, u32[]{:S(2)}) copy-start(f32[136,16]{1,0:T(8,128)S(1)} %add.122.first) | copy-start | bytes 26116
  106.6 18.1 %collective-permute-start.4 = (f32[136,16]{1,0:T(8,128)S(1)}, f32[136,16]{1,0:T(8,128)S(1)}, u32[]{:S(2)}, u32[]{:S(2)}) collective-permute-start(f32[136,16]{1,0:T(8,128)S(1)} %add.122.first), channel_id=1, source_target_pairs={{0,16},{1,17},{2,18},{3,19},{4,20},{5,21},{6,22},{7,23},{8,24},{9,... | collective-permute-start | bytes 26120 | tf_op jit(solution)/shard_map/ppermute | solution.py:262
  120.3 18.4 %copy-start = (f32[4,128,128]{2,1,0:T(8,128)S(1)}, f32[4,128,128]{2,1,0:T(8,128)}, u32[]{:S(2)}) copy-start(f32[4,128,128]{2,1,0:T(8,128)} %add_multiply_fusion.kinetic) | copy-start | bytes 786436
  120.3 51.9 %all-to-all-start.1 = ((f32[32,4,32,128]{3,2,1,0:T(8,128)}), f32[32,4,32,128]{3,2,1,0:T(8,128)S(1)}, u32[]{:S(2)}, u32[]{:S(2)}) async-start(f32[32,4,32,128]{3,2,1,0:T(8,128)} %get-tuple-element.6), calls=%async_computation.1 | async-start | bytes 4194304 | tf_op jit(solution)/shard_map/all_to_all | solution.py:311
  124.7 0.6 copy-start.8
  138.8 2.2 %copy-start.1 = (f32[8,2,4,128,128]{4,3,2,1,0:T(8,128)S(1)}, f32[8,2,4,128,128]{4,3,2,1,0:T(8,128)}, u32[]{:S(2)}) copy-start(f32[8,2,4,128,128]{4,3,2,1,0:T(8,128)} %psi.7) | copy-start | bytes 12582916
  140.9 2.2 %copy-start.2 = (f32[8,8,2,8192]{3,2,1,0:T(2,128)S(1)}, f32[8,8,2,8192]{3,2,1,0:T(2,128)}, u32[]{:S(2)}) copy-start(f32[8,8,2,8192]{3,2,1,0:T(2,128)} %param.15) | copy-start | bytes 12582916
  143.1 8.7 %copy-start.3 = (bf16[256,768]{1,0:T(8,128)(2,1)S(1)}, bf16[256,768]{1,0:T(8,128)(2,1)}, u32[]{:S(2)}) copy-start(bf16[256,768]{1,0:T(8,128)(2,1)} %constant.106.clone.y_table) | copy-start | bytes 1179652

commit v19 on v18

--- a/solution.py
+++ b/solution.py
@@ -303,7 +303,7 @@
 
     layers = 4 if devices % 4 == 0 else 1
     cores = 2 if devices % 8 == 0 else 1
-    ranks = np.arange(devices).reshape(layers, -1, cores).T.reshape(-1)
+    ranks = np.arange(devices).reshape(layers, -1, cores).transpose(1, 0, 2).reshape(-1)
     order = np.arange(2 * span_y)
     order = (order % 2) * span_y + (ranks[:, None] * rows + np.arange(rows)).reshape(-1)[order // 2]
 

time: 178 us -> 182 us (1.022)
  waiting for transfers between devices: 67.2 us -> 73.1 us
    all_to_all x4, waiting for transfers between devices: 49.6 us -> 56.4 us  [exchange(): lax.all_to_all(values, 'ga', split_axis=0, concat_axis=0, axis_index_grou...]
    all_to_all x4, starting transfers between devices: 19.8 us -> 17.6 us  [exchange(): lax.all_to_all(values, 'ga', split_axis=0, concat_axis=0, axis_index_grou...]
  transfers between devices with their start and end apart: 9 -> 9, of which waited for: 8 -> 8; matrix products, arithmetic and copies ran while one was open for 12% -> 11% of each run, Pallas kernels for 27% -> 27%
where the time goes in v19:
time: 182 us; the launch traced here: 180 us
  waiting for transfers between devices  73.1 us (40%)
  Pallas kernels  54.7 us (30%)
  starting transfers between devices  26.1 us (14%)
  local copies, waits for them, and re-layouts  10.4 us (6%)
  other arithmetic  8.86 us (5%)
  matrix products  6.01 us (3%)
    all_to_all x4, waiting for transfers between devices, exchange(): lax.all_to_all(values, 'ga', split_axis=0, concat_axis=0, axis_index_grou...  56.4 us
    all_to_all x4, starting transfers between devices, exchange(): lax.all_to_all(values, 'ga', split_axis=0, concat_axis=0, axis_index_grou...  17.6 us
    ppermute x5, waiting for transfers between devices, partner(): return lax.ppermute(values, 'ga', [(d, d ^ k) for d in range(devices)])  16.8 us
    pallas_call x2, Pallas kernels, on_device(): pl.pallas_call(functools.partial(real_space_kernel, rows, planes), out_sh...  16.1 us
    pallas_call x1, Pallas kernels, on_device(): pl.pallas_call(functools.partial(project_kernel, slots), out_shape=jax.Sh...  10.1 us
    pallas_call x1, Pallas kernels, on_device(): pl.pallas_call(functools.partial(base_kernel, slots), out_shape=jax.Shape...  8.68 us
    ppermute x5, starting transfers between devices, partner(): return lax.ppermute(values, 'ga', [(d, d ^ k) for d in range(devices)])  8.48 us
    pallas_call x2, Pallas kernels, on_device(): pl.pallas_call(to_planes_kernel, out_shape=jax.ShapeDtypeStruct(orbitals....  7.21 us
  transfers between devices with their start and end apart: 9, of which 8 were waited for; matrix products, arithmetic and copies ran while one was open for 11% of the time, Pallas kernels for 27%

profile of v19, /device:TPU:1, one launch (start us, length us, event | category | flops | bytes accessed | tf_op | source)
XLA Modules:
  0.0 180.3 jit_solution(4807655278576645976)
XLA Ops:
  0.7 2.9 %to_rows.3 = f32[32,2,32,128]{3,2,1,0:T(8,128)} custom-call(f32[8,2,4,128,128]{4,3,2,1,0:T(8,128)} %psi.7, bf16[256,768]{1,0:T(8,128)(2,1)} %constant.105.clone.y_table), custom_call_target="tpu_custom_call" | custom-call | flops 4000000000 | bytes 3000000 | tf_op jit(solution)/shard_map/to_rows/pallas_call | solution.py:329
  3.6 7.2 %all-to-all-start.2 = ((f32[32,2,32,128]{3,2,1,0:T(8,128)}), f32[32,2,32,128]{3,2,1,0:T(8,128)}, u32[]{:S(2)}, u32[]{:S(2)}) async-start(f32[32,2,32,128]{3,2,1,0:T(8,128)} %to_rows.3), calls=%async_computation.2 | async-start | bytes 2097152 | tf_op jit(solution)/shard_map/all_to_all | solution.py:311
  10.9 0.6 gather_fusion
  12.1 0.9 copy.120.inverse
  13.2 0.9 add_multiply_fusion.kinetic
  14.0 3.0 %to_rows.2 = f32[32,2,32,128]{3,2,1,0:T(8,128)} custom-call(f32[8,2,4,128,128]{4,3,2,1,0:T(8,128)} %psi.7, bf16[256,768]{1,0:T(8,128)(2,1)} %constant.105.clone.y_table), custom_call_target="tpu_custom_call" | custom-call | flops 4000000000 | bytes 3000000 | tf_op jit(solution)/shard_map/to_rows/pallas_call | solution.py:329
  17.0 20.8 %all-to-all-done.2.recv = f32[32,2,32,128]{3,2,1,0:T(8,128)} async-done(((f32[32,2,32,128]{3,2,1,0:T(8,128)}), f32[32,2,32,128]{3,2,1,0:T(8,128)}, u32[]{:S(2)}, u32[]{:S(2)}) %all-to-all-start.2) | async-done | bytes 1048608 | tf_op jit(solution)/shard_map/all_to_all | solution.py:311
  37.8 3.7 %all-to-all-start = ((f32[32,2,32,128]{3,2,1,0:T(8,128)}), f32[32,2,32,128]{3,2,1,0:T(8,128)}, u32[]{:S(2)}, u32[]{:S(2)}) async-start(f32[32,2,32,128]{3,2,1,0:T(8,128)} %to_rows.2), calls=%async_computation | async-start | bytes 2097152 | tf_op jit(solution)/shard_map/all_to_all | solution.py:311
  41.6 10.1 %project.1 = f32[8,32,16]{2,1,0:T(8,128)} custom-call(f32[8,2,4,128,128]{4,3,2,1,0:T(8,128)} %psi.7, f32[8,1024,128]{2,1,0:T(8,128)} %bitcast.74, f32[4,128,128]{2,1,0:T(8,128)} %add_multiply_fusion.kinetic), custom_call_target="tpu_custom_call" | custom-call | flops 8000000000 | bytes 8000000 | tf_op jit(solution)/shard_map/project/pallas_call | solution.py:376
  51.7 0.8 fusion.47
  53.0 0.7 copy.111
  53.8 0.7 pad_maximum_fusion.1.forward
  54.5 0.9 convolution_bitcast_fusion._
  55.4 8.0 %real_space.3 = (f32[32,4,32,128]{3,2,1,0:T(8,128)}, f32[4,512,128]{2,1,0:T(8,128)}) custom-call(f32[32,2,32,128]{3,2,1,0:T(8,128)} %all-to-all-done.2.recv, f32[512,128]{1,0:T(8,128)} %bitcast.76, bf16[256,768]{1,0:T(8,128)(2,1)} %copy.120.inverse, bf16[256,384]{1,0:T(8,128)(2,1)} %pad_maximum_fusion.1.forward, bf16[768,256]{1,0:T(8,128)(2,1)} %constant.107.clone.inv_z, ...), custom_call_target="tpu_custom_call" | custom-call | flops 4000000000 | bytes 8000000 | tf_op jit(solution)/shard_map/real_space/pallas_call | solution.py:404
  63.4 5.3 %all-to-all-done.recv = f32[32,2,32,128]{3,2,1,0:T(8,128)} async-done(((f32[32,2,32,128]{3,2,1,0:T(8,128)}), f32[32,2,32,128]{3,2,1,0:T(8,128)}, u32[]{:S(2)}, u32[]{:S(2)}) %all-to-all-start) | async-done | bytes 1048608 | tf_op jit(solution)/shard_map/all_to_all | solution.py:311
  68.8 3.9 %all-to-all-start.3 = ((f32[32,4,32,128]{3,2,1,0:T(8,128)}), f32[32,4,32,128]{3,2,1,0:T(8,128)}, u32[]{:S(2)}, u32[]{:S(2)}) async-start(f32[32,4,32,128]{3,2,1,0:T(8,128)} %get-tuple-element.7), calls=%async_computation.3 | async-start | bytes 4194304 | tf_op jit(solution)/shard_map/all_to_all | solution.py:311
  72.9 8.1 %real_space.2 = (f32[32,4,32,128]{3,2,1,0:T(8,128)}, f32[4,512,128]{2,1,0:T(8,128)}) custom-call(f32[32,2,32,128]{3,2,1,0:T(8,128)} %all-to-all-done.recv, f32[512,128]{1,0:T(8,128)} %bitcast.77, bf16[256,768]{1,0:T(8,128)(2,1)} %copy.120.inverse, bf16[256,384]{1,0:T(8,128)(2,1)} %pad_maximum_fusion.1.forward, bf16[768,256]{1,0:T(8,128)(2,1)} %constant.107.clone.inv_z, ...), custom_call_target="tpu_custom_call" | custom-call | flops 4000000000 | bytes 8000000 | tf_op jit(solution)/shard_map/real_space/pallas_call | solution.py:404
  81.0 5.2 %real_gram.1 = f32[2,8,8,128]{3,2,1,0:T(8,128)} custom-call(f32[4,512,128]{2,1,0:T(8,128)} %get-tuple-element.8.refs_0_, f32[4,512,128]{2,1,0:T(8,128)} %get-tuple-element.9.refs_1_, f32[512,128]{1,0:T(8,128)} %bitcast.78), custom_call_target="tpu_custom_call" | custom-call | flops 10000000 | bytes 2000000 | tf_op jit(solution)/shard_map/real_gram/pallas_call | solution.py:431
  86.2 0.9 reduce_sum.18
  87.7 0.9 collective-permute-done
  88.7 1.3 collective-permute-start.1
  90.0 4.1 %collective-permute-done.1 = f32[136,16]{1,0:T(8,128)S(1)} collective-permute-done((f32[136,16]{1,0:T(8,128)S(1)}, f32[136,16]{1,0:T(8,128)S(1)}, u32[]{:S(2)}, u32[]{:S(2)}) %collective-permute-start.1) | collective-permute-done | bytes 8736 | tf_op jit(solution)/shard_map/ppermute | solution.py:262
  94.1 2.2 %collective-permute-start.2 = (f32[136,16]{1,0:T(8,128)S(1)}, f32[136,16]{1,0:T(8,128)S(1)}, u32[]{:S(2)}, u32[]{:S(2)}) collective-permute-start(f32[136,16]{1,0:T(8,128)S(1)} %add.120), channel_id=1, source_target_pairs={{0,4},{1,5},{2,6},{3,7},{4,0},{5,1},{6,2},{7,3},{8,12},{9,13},{10,... | collective-permute-start | bytes 26120 | tf_op jit(solution)/shard_map/ppermute | solution.py:262
  96.2 2.0 %collective-permute-done.2 = f32[136,16]{1,0:T(8,128)S(1)} collective-permute-done((f32[136,16]{1,0:T(8,128)S(1)}, f32[136,16]{1,0:T(8,128)S(1)}, u32[]{:S(2)}, u32[]{:S(2)}) %collective-permute-start.2) | collective-permute-done | bytes 8736 | tf_op jit(solution)/shard_map/ppermute | solution.py:262
  98.3 9.8 %collective-permute-done.3 = f32[136,16]{1,0:T(8,128)S(1)} collective-permute-done((f32[136,16]{1,0:T(8,128)S(1)}, f32[136,16]{1,0:T(8,128)S(1)}, u32[]{:S(2)}, u32[]{:S(2)}) %collective-permute-start.3) | collective-permute-done | bytes 8736 | tf_op jit(solution)/shard_map/ppermute | solution.py:262
  108.2 4.5 %collective-permute-start.4 = (f32[136,16]{1,0:T(8,128)S(1)}, f32[136,16]{1,0:T(8,128)S(1)}, u32[]{:S(2)}, u32[]{:S(2)}) collective-permute-start(f32[136,16]{1,0:T(8,128)S(1)} %add.122.first), channel_id=1, source_target_pairs={{0,16},{1,17},{2,18},{3,19},{4,20},{5,21},{6,22},{7,23},{8,24},{9,... | collective-permute-start | bytes 26120 | tf_op jit(solution)/shard_map/ppermute | solution.py:262
  112.8 11.4 %all-to-all-done.3._.recv = f32[32,4,32,128]{3,2,1,0:T(8,128)} async-done(((f32[32,4,32,128]{3,2,1,0:T(8,128)}), f32[32,4,32,128]{3,2,1,0:T(8,128)}, u32[]{:S(2)}, u32[]{:S(2)}) %all-to-all-start.3) | async-done | bytes 2097184 | tf_op jit(solution)/shard_map/all_to_all | solution.py:311
  124.3 2.9 %all-to-all-start.1 = ((f32[32,4,32,128]{3,2,1,0:T(8,128)}), f32[32,4,32,128]{3,2,1,0:T(8,128)S(1)}, u32[]{:S(2)}, u32[]{:S(2)}) async-start(f32[32,4,32,128]{3,2,1,0:T(8,128)} %get-tuple-element.6), calls=%async_computation.1 | async-start | bytes 4194304 | tf_op jit(solution)/shard_map/all_to_all | solution.py:311
  127.2 0.6 copy-done.8
  127.8 1.5 last_sum.1
  129.4 0.7 slice.121
  130.0 0.9 slice_multiply_fusion
  131.0 1.1 fusion.10
  132.1 1.1 fusion.16
  133.2 0.9 fusion.37
  134.1 0.7 cholesky.16
  134.9 0.6 compare_reduce_fusion
  135.5 0.6 fusion.27
  136.2 0.6 custom-call.10
  136.8 1.1 fusion.12
  137.9 1.1 convolution_subtract_fusion
  140.5 0.6 pad_maximum_fusion.6
  141.3 2.2 %copy-done.1 = f32[8,2,4,128,128]{4,3,2,1,0:T(8,128)S(1)} copy-done((f32[8,2,4,128,128]{4,3,2,1,0:T(8,128)S(1)}, f32[8,2,4,128,128]{4,3,2,1,0:T(8,128)}, u32[]{:S(2)}) %copy-start.1) | copy-done | bytes 4194328
  143.4 2.2 %copy-done.2 = f32[8,8,2,8192]{3,2,1,0:T(2,128)S(1)} copy-done((f32[8,8,2,8192]{3,2,1,0:T(2,128)S(1)}, f32[8,8,2,8192]{3,2,1,0:T(2,128)}, u32[]{:S(2)}) %copy-start.2) | copy-done | bytes 4194328
  145.6 8.7 %base.1 = f32[8,2,4,128,128]{4,3,2,1,0:T(8,128)} custom-call(f32[8,2,4,128,128]{4,3,2,1,0:T(8,128)S(1)} %copy-done.1, f32[8,1024,128]{2,1,0:T(8,128)S(1)} %bitcast.75, f32[4,128,128]{2,1,0:T(8,128)S(1)} %copy-done, f32[8,16,32]{2,1,0:T(8,128)S(1)} %pad_maximum_fusion.4.coefs), custom_call_target="tpu_custom_call" | custom-call | flops 8000000000 | bytes 12000000 | tf_op jit(solution)/shard_map/base/pallas_call | solution.py:468
  154.3 3.7 %to_planes.2.base = f32[8,2,4,128,128]{4,3,2,1,0:T(8,128)} custom-call(f32[32,4,32,128]{3,2,1,0:T(8,128)} %all-to-all-done.3._.recv, f32[8,2,4,128,128]{4,3,2,1,0:T(8,128)} %base.1, bf16[256,768]{1,0:T(8,128)(2,1)S(1)} %copy-done.3), custom_call_target="tpu_custom_call", output_to_operand_aliasing={{}: (1, {})} | custom-call | flops 8000000000 | bytes 12000000 | tf_op jit(solution)/shard_map/to_planes/pallas_call | solution.py:485
  158.1 18.7 %all-to-all-done.1.recv = f32[32,4,32,128]{3,2,1,0:T(8,128)S(1)} async-done(((f32[32,4,32,128]{3,2,1,0:T(8,128)}), f32[32,4,32,128]{3,2,1,0:T(8,128)S(1)}, u32[]{:S(2)}, u32[]{:S(2)}) %all-to-all-start.1) | async-done | bytes 2097184 | tf_op jit(solution)/shard_map/all_to_all | solution.py:311
  176.8 3.5 %to_planes.3 = f32[8,2,4,128,128]{4,3,2,1,0:T(8,128)} custom-call(f32[32,4,32,128]{3,2,1,0:T(8,128)S(1)} %all-to-all-done.1.recv, f32[8,2,4,128,128]{4,3,2,1,0:T(8,128)} %to_planes.2.base, bf16[256,768]{1,0:T(8,128)(2,1)S(1)} %copy-done.3), custom_call_target="tpu_custom_call", output_to_operand_aliasing={{}: (1, {})} | custom-call | flops 8000000000 | bytes 12000000 | tf_op jit(solution)/shard_map/to_planes/pallas_call | solution.py:485
  (78 shorter events, 4.3 us)
Async XLA Ops:
  0.6 10.3 %copy-start.11 = (s32[32]{0:T(128)S(1)}, s32[32]{0:T(128)}, u32[]{:S(2)}) copy-start(s32[32]{0:T(128)} %constant.116) | copy-start | bytes 388
  0.6 10.1 %copy-start.10 = (s32[128]{0:T(128)S(1)}, s32[128]{0:T(128)}, u32[]{:S(2)}) copy-start(s32[128]{0:T(128)} %param.13) | copy-start | bytes 1540
  3.6 34.2 %all-to-all-start.2 = ((f32[32,2,32,128]{3,2,1,0:T(8,128)}), f32[32,2,32,128]{3,2,1,0:T(8,128)}, u32[]{:S(2)}, u32[]{:S(2)}) async-start(f32[32,2,32,128]{3,2,1,0:T(8,128)} %to_rows.3), calls=%async_computation.2 | async-start | bytes 2097152 | tf_op jit(solution)/shard_map/all_to_all | solution.py:311
  37.8 30.9 %all-to-all-start = ((f32[32,2,32,128]{3,2,1,0:T(8,128)}), f32[32,2,32,128]{3,2,1,0:T(8,128)}, u32[]{:S(2)}, u32[]{:S(2)}) async-start(f32[32,2,32,128]{3,2,1,0:T(8,128)} %to_rows.2), calls=%async_computation | async-start | bytes 2097152 | tf_op jit(solution)/shard_map/all_to_all | solution.py:311
  41.6 11.4 %copy-start.5 = (f32[128,4,128]{2,1,0:T(4,128)S(1)}, f32[128,4,128]{2,1,0:T(4,128)}, u32[]{:S(2)}) copy-start(f32[128,4,128]{2,1,0:T(4,128)} %param.14) | copy-start | bytes 786436
  41.6 12.9 %copy-start.12 = (s32[8,8]{1,0:T(8,128)S(1)}, s32[8,8]{1,0:T(8,128)}, u32[]{:S(2)}) copy-start(s32[8,8]{1,0:T(8,128)} %param.16) | copy-start | bytes 772
  63.4 9.2 %copy-start.7 = (f32[8,32,16]{2,1,0:T(8,128)S(1)}, f32[8,32,16]{2,1,0:T(8,128)}, u32[]{:S(2)}) copy-start(f32[8,32,16]{2,1,0:T(8,128)} %project.1) | copy-start | bytes 49156
  68.8 55.5 %all-to-all-start.3 = ((f32[32,4,32,128]{3,2,1,0:T(8,128)}), f32[32,4,32,128]{3,2,1,0:T(8,128)}, u32[]{:S(2)}, u32[]{:S(2)}) async-start(f32[32,4,32,128]{3,2,1,0:T(8,128)} %get-tuple-element.7), calls=%async_computation.3 | async-start | bytes 4194304 | tf_op jit(solution)/shard_map/all_to_all | solution.py:311
  72.9 14.3 %copy-start.6 = (f32[128,16]{1,0:T(8,128)S(1)}, f32[128,16]{1,0:T(8,128)}, u32[]{:S(2)}) copy-start(f32[128,16]{1,0:T(8,128)} %convolution_bitcast_fusion._) | copy-start | bytes 24580
  72.9 39.7 %copy-start.9 = (f32[32,4]{0,1:T(4,128)S(1)}, f32[32,4]{0,1:T(4,128)}, u32[]{:S(2)}) copy-start(f32[32,4]{0,1:T(4,128)} %param.17) | copy-start | bytes 1540
  87.2 1.4 collective-permute-start
  88.7 5.4 %collective-permute-start.1 = (f32[136,16]{1,0:T(8,128)S(1)}, f32[136,16]{1,0:T(8,128)S(1)}, u32[]{:S(2)}, u32[]{:S(2)}) collective-permute-start(f32[136,16]{1,0:T(8,128)S(1)} %fusion.51), channel_id=1, source_target_pairs={{0,2},{1,3},{2,0},{3,1},{4,6},{5,7},{6,4},{7,5},{8,10},{9,11},{10,... | collective-permute-start | bytes 26120 | tf_op jit(solution)/shard_map/ppermute | solution.py:262
  94.1 4.1 %collective-permute-start.2 = (f32[136,16]{1,0:T(8,128)S(1)}, f32[136,16]{1,0:T(8,128)S(1)}, u32[]{:S(2)}, u32[]{:S(2)}) collective-permute-start(f32[136,16]{1,0:T(8,128)S(1)} %add.120), channel_id=1, source_target_pairs={{0,4},{1,5},{2,6},{3,7},{4,0},{5,1},{6,2},{7,3},{8,12},{9,13},{10,... | collective-permute-start | bytes 26120 | tf_op jit(solution)/shard_map/ppermute | solution.py:262
  98.2 9.9 %collective-permute-start.3 = (f32[136,16]{1,0:T(8,128)S(1)}, f32[136,16]{1,0:T(8,128)S(1)}, u32[]{:S(2)}, u32[]{:S(2)}) collective-permute-start(f32[136,16]{1,0:T(8,128)S(1)} %add.121), channel_id=1, source_target_pairs={{0,8},{1,9},{2,10},{3,11},{4,12},{5,13},{6,14},{7,15},{8,0},{9,1},... | collective-permute-start | bytes 26120 | tf_op jit(solution)/shard_map/ppermute | solution.py:262
  108.1 19.0 %copy-start.4 = (f32[136,16]{1,0:T(8,128)}, f32[136,16]{1,0:T(8,128)S(1)}, u32[]{:S(2)}) copy-start(f32[136,16]{1,0:T(8,128)S(1)} %add.122.first) | copy-start | bytes 26116
  108.2 19.0 %collective-permute-start.4 = (f32[136,16]{1,0:T(8,128)S(1)}, f32[136,16]{1,0:T(8,128)S(1)}, u32[]{:S(2)}, u32[]{:S(2)}) collective-permute-start(f32[136,16]{1,0:T(8,128)S(1)} %add.122.first), channel_id=1, source_target_pairs={{0,16},{1,17},{2,18},{3,19},{4,20},{5,21},{6,22},{7,23},{8,24},{9,... | collective-permute-start | bytes 26120 | tf_op jit(solution)/shard_map/ppermute | solution.py:262
  124.3 17.0 %copy-start = (f32[4,128,128]{2,1,0:T(8,128)S(1)}, f32[4,128,128]{2,1,0:T(8,128)}, u32[]{:S(2)}) copy-start(f32[4,128,128]{2,1,0:T(8,128)} %add_multiply_fusion.kinetic) | copy-start | bytes 786436
  124.3 52.5 %all-to-all-start.1 = ((f32[32,4,32,128]{3,2,1,0:T(8,128)}), f32[32,4,32,128]{3,2,1,0:T(8,128)S(1)}, u32[]{:S(2)}, u32[]{:S(2)}) async-start(f32[32,4,32,128]{3,2,1,0:T(8,128)} %get-tuple-element.6), calls=%async_computation.1 | async-start | bytes 4194304 | tf_op jit(solution)/shard_map/all_to_all | solution.py:311
  127.2 0.6 copy-start.8
  141.3 2.2 %copy-start.1 = (f32[8,2,4,128,128]{4,3,2,1,0:T(8,128)S(1)}, f32[8,2,4,128,128]{4,3,2,1,0:T(8,128)}, u32[]{:S(2)}) copy-start(f32[8,2,4,128,128]{4,3,2,1,0:T(8,128)} %psi.7) | copy-start | bytes 12582916
  143.4 2.2 %copy-start.2 = (f32[8,8,2,8192]{3,2,1,0:T(2,128)S(1)}, f32[8,8,2,8192]{3,2,1,0:T(2,128)}, u32[]{:S(2)}) copy-start(f32[8,8,2,8192]{3,2,1,0:T(2,128)} %param.15) | copy-start | bytes 12582916
  145.6 8.7 %copy-start.3 = (bf16[256,768]{1,0:T(8,128)(2,1)S(1)}, bf16[256,768]{1,0:T(8,128)(2,1)}, u32[]{:S(2)}) copy-start(bf16[256,768]{1,0:T(8,128)(2,1)} %constant.106.clone.y_table) | copy-start | bytes 1179652

commit v20 on v17

--- a/solution.py
+++ b/solution.py
@@ -302,7 +302,10 @@
         return pl.CostEstimate(flops=flops, bytes_accessed=moved, transcendentals=0)
 
     layers = 4 if devices % 4 == 0 else 1
-    ranks = np.arange(devices).reshape(layers, -1)[[0, 1, 3, 2] if layers == 4 else [0]].T.reshape(-1)
+    ranks = np.arange(devices).reshape(layers, -1).T
+    if devices % 32 == 0:
+        ranks = ranks.reshape(4, -1, layers)[[0, 1, 3, 2]]
+    ranks = ranks.reshape(-1)
     order = np.arange(2 * span_y)
     order = (order % 2) * span_y + (ranks[:, None] * rows + np.arange(rows)).reshape(-1)[order // 2]
 

time: 181 us -> 176 us (0.972)
  starting transfers between devices: 30.9 us -> 23.8 us
  waiting for transfers between devices: 67 us -> 69.9 us
    ppermute x5, starting transfers between devices: 11.6 us -> 7.03 us  [partner(): return lax.ppermute(values, 'ga', [(d, d ^ k) for d in range(devices)])]
    ppermute x5, waiting for transfers between devices: 13.7 us -> 18.1 us  [partner(): return lax.ppermute(values, 'ga', [(d, d ^ k) for d in range(devices)])]
    all_to_all x4, starting transfers between devices: 19.2 us -> 16.8 us  [exchange(): lax.all_to_all(values, 'ga', split_axis=0, concat_axis=0, axis_index_grou...]
  transfers between devices with their start and end apart: 9 -> 9, of which waited for: 8 -> 8; matrix products, arithmetic and copies ran while one was open for 11% -> 12% of each run, Pallas kernels for 27% -> 28%
where the time goes in v20:
time: 176 us; the launch traced here: 175 us
  waiting for transfers between devices  69.9 us (40%)
  Pallas kernels  54.7 us (31%)
  starting transfers between devices  23.8 us (14%)
  local copies, waits for them, and re-layouts  10.4 us (6%)
  other arithmetic  8.86 us (5%)
  matrix products  6.01 us (3%)
    all_to_all x4, waiting for transfers between devices, exchange(): lax.all_to_all(values, 'ga', split_axis=0, concat_axis=0, axis_index_grou...  51.7 us
    ppermute x5, waiting for transfers between devices, partner(): return lax.ppermute(values, 'ga', [(d, d ^ k) for d in range(devices)])  18.1 us
    all_to_all x4, starting transfers between devices, exchange(): lax.all_to_all(values, 'ga', split_axis=0, concat_axis=0, axis_index_grou...  16.8 us
    pallas_call x2, Pallas kernels, on_device(): pl.pallas_call(functools.partial(real_space_kernel, rows, planes), out_sh...  16.1 us
    pallas_call x1, Pallas kernels, on_device(): pl.pallas_call(functools.partial(project_kernel, slots), out_shape=jax.Sh...  10.1 us
    pallas_call x1, Pallas kernels, on_device(): pl.pallas_call(functools.partial(base_kernel, slots), out_shape=jax.Shape...  8.68 us
    pallas_call x2, Pallas kernels, on_device(): pl.pallas_call(to_planes_kernel, out_shape=jax.ShapeDtypeStruct(orbitals....  7.21 us
    ppermute x5, starting transfers between devices, partner(): return lax.ppermute(values, 'ga', [(d, d ^ k) for d in range(devices)])  7.03 us
  transfers between devices with their start and end apart: 9, of which 8 were waited for; matrix products, arithmetic and copies ran while one was open for 12% of the time, Pallas kernels for 28%

profile of v20, /device:TPU:1, one launch (start us, length us, event | category | flops | bytes accessed | tf_op | source)
XLA Modules:
  0.0 174.7 jit_solution(3885194679538488014)
XLA Ops:
  0.7 2.9 %to_rows.3 = f32[32,2,32,128]{3,2,1,0:T(8,128)} custom-call(f32[8,2,4,128,128]{4,3,2,1,0:T(8,128)} %psi.7, bf16[256,768]{1,0:T(8,128)(2,1)} %constant.105.clone.y_table), custom_call_target="tpu_custom_call" | custom-call | flops 4000000000 | bytes 3000000 | tf_op jit(solution)/shard_map/to_rows/pallas_call | solution.py:331
  3.6 7.2 %all-to-all-start.2 = ((f32[32,2,32,128]{3,2,1,0:T(8,128)}), f32[32,2,32,128]{3,2,1,0:T(8,128)}, u32[]{:S(2)}, u32[]{:S(2)}) async-start(f32[32,2,32,128]{3,2,1,0:T(8,128)} %to_rows.3), calls=%async_computation.2 | async-start | bytes 2097152 | tf_op jit(solution)/shard_map/all_to_all | solution.py:313
  10.9 0.6 gather_fusion
  12.1 0.9 copy.120.inverse
  13.2 0.9 add_multiply_fusion.kinetic
  14.0 3.0 %to_rows.2 = f32[32,2,32,128]{3,2,1,0:T(8,128)} custom-call(f32[8,2,4,128,128]{4,3,2,1,0:T(8,128)} %psi.7, bf16[256,768]{1,0:T(8,128)(2,1)} %constant.105.clone.y_table), custom_call_target="tpu_custom_call" | custom-call | flops 4000000000 | bytes 3000000 | tf_op jit(solution)/shard_map/to_rows/pallas_call | solution.py:331
  17.0 20.2 %all-to-all-done.2.recv = f32[32,2,32,128]{3,2,1,0:T(8,128)} async-done(((f32[32,2,32,128]{3,2,1,0:T(8,128)}), f32[32,2,32,128]{3,2,1,0:T(8,128)}, u32[]{:S(2)}, u32[]{:S(2)}) %all-to-all-start.2) | async-done | bytes 1048608 | tf_op jit(solution)/shard_map/all_to_all | solution.py:313
  37.2 3.2 %all-to-all-start = ((f32[32,2,32,128]{3,2,1,0:T(8,128)}), f32[32,2,32,128]{3,2,1,0:T(8,128)}, u32[]{:S(2)}, u32[]{:S(2)}) async-start(f32[32,2,32,128]{3,2,1,0:T(8,128)} %to_rows.2), calls=%async_computation | async-start | bytes 2097152 | tf_op jit(solution)/shard_map/all_to_all | solution.py:313
  40.4 10.1 %project.1 = f32[8,32,16]{2,1,0:T(8,128)} custom-call(f32[8,2,4,128,128]{4,3,2,1,0:T(8,128)} %psi.7, f32[8,1024,128]{2,1,0:T(8,128)} %bitcast.74, f32[4,128,128]{2,1,0:T(8,128)} %add_multiply_fusion.kinetic), custom_call_target="tpu_custom_call" | custom-call | flops 8000000000 | bytes 8000000 | tf_op jit(solution)/shard_map/project/pallas_call | solution.py:378
  50.5 0.8 fusion.47
  51.8 0.7 copy.111
  52.6 0.7 pad_maximum_fusion.1.forward
  53.3 0.9 convolution_bitcast_fusion._
  54.3 8.0 %real_space.3 = (f32[32,4,32,128]{3,2,1,0:T(8,128)}, f32[4,512,128]{2,1,0:T(8,128)}) custom-call(f32[32,2,32,128]{3,2,1,0:T(8,128)} %all-to-all-done.2.recv, f32[512,128]{1,0:T(8,128)} %bitcast.76, bf16[256,768]{1,0:T(8,128)(2,1)} %copy.120.inverse, bf16[256,384]{1,0:T(8,128)(2,1)} %pad_maximum_fusion.1.forward, bf16[768,256]{1,0:T(8,128)(2,1)} %constant.107.clone.inv_z, ...), custom_call_target="tpu_custom_call" | custom-call | flops 4000000000 | bytes 8000000 | tf_op jit(solution)/shard_map/real_space/pallas_call | solution.py:406
  62.2 4.6 %all-to-all-done.recv = f32[32,2,32,128]{3,2,1,0:T(8,128)} async-done(((f32[32,2,32,128]{3,2,1,0:T(8,128)}), f32[32,2,32,128]{3,2,1,0:T(8,128)}, u32[]{:S(2)}, u32[]{:S(2)}) %all-to-all-start) | async-done | bytes 1048608 | tf_op jit(solution)/shard_map/all_to_all | solution.py:313
  66.8 3.2 %all-to-all-start.3 = ((f32[32,4,32,128]{3,2,1,0:T(8,128)}), f32[32,4,32,128]{3,2,1,0:T(8,128)}, u32[]{:S(2)}, u32[]{:S(2)}) async-start(f32[32,4,32,128]{3,2,1,0:T(8,128)} %get-tuple-element.7), calls=%async_computation.3 | async-start | bytes 4194304 | tf_op jit(solution)/shard_map/all_to_all | solution.py:313
  70.3 8.1 %real_space.2 = (f32[32,4,32,128]{3,2,1,0:T(8,128)}, f32[4,512,128]{2,1,0:T(8,128)}) custom-call(f32[32,2,32,128]{3,2,1,0:T(8,128)} %all-to-all-done.recv, f32[512,128]{1,0:T(8,128)} %bitcast.77, bf16[256,768]{1,0:T(8,128)(2,1)} %copy.120.inverse, bf16[256,384]{1,0:T(8,128)(2,1)} %pad_maximum_fusion.1.forward, bf16[768,256]{1,0:T(8,128)(2,1)} %constant.107.clone.inv_z, ...), custom_call_target="tpu_custom_call" | custom-call | flops 4000000000 | bytes 8000000 | tf_op jit(solution)/shard_map/real_space/pallas_call | solution.py:406
  78.4 5.2 %real_gram.1 = f32[2,8,8,128]{3,2,1,0:T(8,128)} custom-call(f32[4,512,128]{2,1,0:T(8,128)} %get-tuple-element.8.refs_0_, f32[4,512,128]{2,1,0:T(8,128)} %get-tuple-element.9.refs_1_, f32[512,128]{1,0:T(8,128)} %bitcast.78), custom_call_target="tpu_custom_call" | custom-call | flops 10000000 | bytes 2000000 | tf_op jit(solution)/shard_map/real_gram/pallas_call | solution.py:433
  83.6 0.9 reduce_sum.18
  85.0 0.9 collective-permute-done
  86.0 1.4 collective-permute-start.1
  87.4 4.2 %collective-permute-done.1 = f32[136,16]{1,0:T(8,128)S(1)} collective-permute-done((f32[136,16]{1,0:T(8,128)S(1)}, f32[136,16]{1,0:T(8,128)S(1)}, u32[]{:S(2)}, u32[]{:S(2)}) %collective-permute-start.1) | collective-permute-done | bytes 8736 | tf_op jit(solution)/shard_map/ppermute | solution.py:262
  92.1 2.7 %collective-permute-done.2 = f32[136,16]{1,0:T(8,128)S(1)} collective-permute-done((f32[136,16]{1,0:T(8,128)S(1)}, f32[136,16]{1,0:T(8,128)S(1)}, u32[]{:S(2)}, u32[]{:S(2)}) %collective-permute-start.2) | collective-permute-done | bytes 8736 | tf_op jit(solution)/shard_map/ppermute | solution.py:262
  94.8 0.7 collective-permute-start.3
  95.6 10.3 %collective-permute-done.3 = f32[136,16]{1,0:T(8,128)S(1)} collective-permute-done((f32[136,16]{1,0:T(8,128)S(1)}, f32[136,16]{1,0:T(8,128)S(1)}, u32[]{:S(2)}, u32[]{:S(2)}) %collective-permute-start.3) | collective-permute-done | bytes 8736 | tf_op jit(solution)/shard_map/ppermute | solution.py:262
  105.8 4.1 %collective-permute-start.4 = (f32[136,16]{1,0:T(8,128)S(1)}, f32[136,16]{1,0:T(8,128)S(1)}, u32[]{:S(2)}, u32[]{:S(2)}) collective-permute-start(f32[136,16]{1,0:T(8,128)S(1)} %add.122.first), channel_id=1, source_target_pairs={{0,16},{1,17},{2,18},{3,19},{4,20},{5,21},{6,22},{7,23},{8,24},{9,... | collective-permute-start | bytes 26120 | tf_op jit(solution)/shard_map/ppermute | solution.py:262
  110.1 9.7 %all-to-all-done.3._.recv = f32[32,4,32,128]{3,2,1,0:T(8,128)} async-done(((f32[32,4,32,128]{3,2,1,0:T(8,128)}), f32[32,4,32,128]{3,2,1,0:T(8,128)}, u32[]{:S(2)}, u32[]{:S(2)}) %all-to-all-start.3) | async-done | bytes 2097184 | tf_op jit(solution)/shard_map/all_to_all | solution.py:313
  119.8 3.2 %all-to-all-start.1 = ((f32[32,4,32,128]{3,2,1,0:T(8,128)}), f32[32,4,32,128]{3,2,1,0:T(8,128)S(1)}, u32[]{:S(2)}, u32[]{:S(2)}) async-start(f32[32,4,32,128]{3,2,1,0:T(8,128)} %get-tuple-element.6), calls=%async_computation.1 | async-start | bytes 4194304 | tf_op jit(solution)/shard_map/all_to_all | solution.py:313
  123.0 0.6 copy-done.8
  123.6 1.5 last_sum.1
  125.2 0.7 slice.121
  125.9 0.9 slice_multiply_fusion
  126.8 1.1 fusion.10
  127.9 1.1 fusion.16
  129.1 0.9 fusion.37
  129.9 0.7 cholesky.16
  130.7 0.6 compare_reduce_fusion
  131.3 0.6 fusion.27
  132.0 0.6 custom-call.10
  132.6 1.1 fusion.12
  133.7 1.1 convolution_subtract_fusion
  136.3 0.6 pad_maximum_fusion.6
  137.1 2.2 %copy-done.1 = f32[8,2,4,128,128]{4,3,2,1,0:T(8,128)S(1)} copy-done((f32[8,2,4,128,128]{4,3,2,1,0:T(8,128)S(1)}, f32[8,2,4,128,128]{4,3,2,1,0:T(8,128)}, u32[]{:S(2)}) %copy-start.1) | copy-done | bytes 4194328
  139.3 2.2 %copy-done.2 = f32[8,8,2,8192]{3,2,1,0:T(2,128)S(1)} copy-done((f32[8,8,2,8192]{3,2,1,0:T(2,128)S(1)}, f32[8,8,2,8192]{3,2,1,0:T(2,128)}, u32[]{:S(2)}) %copy-start.2) | copy-done | bytes 4194328
  141.4 8.7 %base.1 = f32[8,2,4,128,128]{4,3,2,1,0:T(8,128)} custom-call(f32[8,2,4,128,128]{4,3,2,1,0:T(8,128)S(1)} %copy-done.1, f32[8,1024,128]{2,1,0:T(8,128)S(1)} %bitcast.75, f32[4,128,128]{2,1,0:T(8,128)S(1)} %copy-done, f32[8,16,32]{2,1,0:T(8,128)S(1)} %pad_maximum_fusion.4.coefs), custom_call_target="tpu_custom_call" | custom-call | flops 8000000000 | bytes 12000000 | tf_op jit(solution)/shard_map/base/pallas_call | solution.py:470
  150.1 3.7 %to_planes.2.base = f32[8,2,4,128,128]{4,3,2,1,0:T(8,128)} custom-call(f32[32,4,32,128]{3,2,1,0:T(8,128)} %all-to-all-done.3._.recv, f32[8,2,4,128,128]{4,3,2,1,0:T(8,128)} %base.1, bf16[256,768]{1,0:T(8,128)(2,1)S(1)} %copy-done.3), custom_call_target="tpu_custom_call", output_to_operand_aliasing={{}: (1, {})} | custom-call | flops 8000000000 | bytes 12000000 | tf_op jit(solution)/shard_map/to_planes/pallas_call | solution.py:487
  153.9 17.3 %all-to-all-done.1.recv = f32[32,4,32,128]{3,2,1,0:T(8,128)S(1)} async-done(((f32[32,4,32,128]{3,2,1,0:T(8,128)}), f32[32,4,32,128]{3,2,1,0:T(8,128)S(1)}, u32[]{:S(2)}, u32[]{:S(2)}) %all-to-all-start.1) | async-done | bytes 2097184 | tf_op jit(solution)/shard_map/all_to_all | solution.py:313
  171.2 3.5 %to_planes.3 = f32[8,2,4,128,128]{4,3,2,1,0:T(8,128)} custom-call(f32[32,4,32,128]{3,2,1,0:T(8,128)S(1)} %all-to-all-done.1.recv, f32[8,2,4,128,128]{4,3,2,1,0:T(8,128)} %to_planes.2.base, bf16[256,768]{1,0:T(8,128)(2,1)S(1)} %copy-done.3), custom_call_target="tpu_custom_call", output_to_operand_aliasing={{}: (1, {})} | custom-call | flops 8000000000 | bytes 12000000 | tf_op jit(solution)/shard_map/to_planes/pallas_call | solution.py:487
  (78 shorter events, 4.6 us)
Async XLA Ops:
  0.6 10.3 %copy-start.11 = (s32[32]{0:T(128)S(1)}, s32[32]{0:T(128)}, u32[]{:S(2)}) copy-start(s32[32]{0:T(128)} %constant.116) | copy-start | bytes 388
  0.6 10.1 %copy-start.10 = (s32[128]{0:T(128)S(1)}, s32[128]{0:T(128)}, u32[]{:S(2)}) copy-start(s32[128]{0:T(128)} %param.13) | copy-start | bytes 1540
  3.6 33.6 %all-to-all-start.2 = ((f32[32,2,32,128]{3,2,1,0:T(8,128)}), f32[32,2,32,128]{3,2,1,0:T(8,128)}, u32[]{:S(2)}, u32[]{:S(2)}) async-start(f32[32,2,32,128]{3,2,1,0:T(8,128)} %to_rows.3), calls=%async_computation.2 | async-start | bytes 2097152 | tf_op jit(solution)/shard_map/all_to_all | solution.py:313
  37.2 29.6 %all-to-all-start = ((f32[32,2,32,128]{3,2,1,0:T(8,128)}), f32[32,2,32,128]{3,2,1,0:T(8,128)}, u32[]{:S(2)}, u32[]{:S(2)}) async-start(f32[32,2,32,128]{3,2,1,0:T(8,128)} %to_rows.2), calls=%async_computation | async-start | bytes 2097152 | tf_op jit(solution)/shard_map/all_to_all | solution.py:313
  40.4 11.4 %copy-start.5 = (f32[128,4,128]{2,1,0:T(4,128)S(1)}, f32[128,4,128]{2,1,0:T(4,128)}, u32[]{:S(2)}) copy-start(f32[128,4,128]{2,1,0:T(4,128)} %param.14) | copy-start | bytes 786436
  40.4 12.9 %copy-start.12 = (s32[8,8]{1,0:T(8,128)S(1)}, s32[8,8]{1,0:T(8,128)}, u32[]{:S(2)}) copy-start(s32[8,8]{1,0:T(8,128)} %param.16) | copy-start | bytes 772
  62.2 7.8 %copy-start.7 = (f32[8,32,16]{2,1,0:T(8,128)S(1)}, f32[8,32,16]{2,1,0:T(8,128)}, u32[]{:S(2)}) copy-start(f32[8,32,16]{2,1,0:T(8,128)} %project.1) | copy-start | bytes 49156
  66.8 53.0 %all-to-all-start.3 = ((f32[32,4,32,128]{3,2,1,0:T(8,128)}), f32[32,4,32,128]{3,2,1,0:T(8,128)}, u32[]{:S(2)}, u32[]{:S(2)}) async-start(f32[32,4,32,128]{3,2,1,0:T(8,128)} %get-tuple-element.7), calls=%async_computation.3 | async-start | bytes 4194304 | tf_op jit(solution)/shard_map/all_to_all | solution.py:313
  70.3 14.3 %copy-start.6 = (f32[128,16]{1,0:T(8,128)S(1)}, f32[128,16]{1,0:T(8,128)}, u32[]{:S(2)}) copy-start(f32[128,16]{1,0:T(8,128)} %convolution_bitcast_fusion._) | copy-start | bytes 24580
  70.3 39.6 %copy-start.9 = (f32[32,4]{0,1:T(4,128)S(1)}, f32[32,4]{0,1:T(4,128)}, u32[]{:S(2)}) copy-start(f32[32,4]{0,1:T(4,128)} %param.17) | copy-start | bytes 1540
  84.6 1.3 collective-permute-start
  86.0 5.6 %collective-permute-start.1 = (f32[136,16]{1,0:T(8,128)S(1)}, f32[136,16]{1,0:T(8,128)S(1)}, u32[]{:S(2)}, u32[]{:S(2)}) collective-permute-start(f32[136,16]{1,0:T(8,128)S(1)} %fusion.51), channel_id=1, source_target_pairs={{0,2},{1,3},{2,0},{3,1},{4,6},{5,7},{6,4},{7,5},{8,10},{9,11},{10,... | collective-permute-start | bytes 26120 | tf_op jit(solution)/shard_map/ppermute | solution.py:262
  91.6 3.2 %collective-permute-start.2 = (f32[136,16]{1,0:T(8,128)S(1)}, f32[136,16]{1,0:T(8,128)S(1)}, u32[]{:S(2)}, u32[]{:S(2)}) collective-permute-start(f32[136,16]{1,0:T(8,128)S(1)} %add.120), channel_id=1, source_target_pairs={{0,4},{1,5},{2,6},{3,7},{4,0},{5,1},{6,2},{7,3},{8,12},{9,13},{10,... | collective-permute-start | bytes 26120 | tf_op jit(solution)/shard_map/ppermute | solution.py:262
  94.8 11.0 %collective-permute-start.3 = (f32[136,16]{1,0:T(8,128)S(1)}, f32[136,16]{1,0:T(8,128)S(1)}, u32[]{:S(2)}, u32[]{:S(2)}) collective-permute-start(f32[136,16]{1,0:T(8,128)S(1)} %add.121), channel_id=1, source_target_pairs={{0,8},{1,9},{2,10},{3,11},{4,12},{5,13},{6,14},{7,15},{8,0},{9,1},... | collective-permute-start | bytes 26120 | tf_op jit(solution)/shard_map/ppermute | solution.py:262
  105.8 17.2 %copy-start.4 = (f32[136,16]{1,0:T(8,128)}, f32[136,16]{1,0:T(8,128)S(1)}, u32[]{:S(2)}) copy-start(f32[136,16]{1,0:T(8,128)S(1)} %add.122.first) | copy-start | bytes 26116
  105.8 17.1 %collective-permute-start.4 = (f32[136,16]{1,0:T(8,128)S(1)}, f32[136,16]{1,0:T(8,128)S(1)}, u32[]{:S(2)}, u32[]{:S(2)}) collective-permute-start(f32[136,16]{1,0:T(8,128)S(1)} %add.122.first), channel_id=1, source_target_pairs={{0,16},{1,17},{2,18},{3,19},{4,20},{5,21},{6,22},{7,23},{8,24},{9,... | collective-permute-start | bytes 26120 | tf_op jit(solution)/shard_map/ppermute | solution.py:262
  119.8 17.3 %copy-start = (f32[4,128,128]{2,1,0:T(8,128)S(1)}, f32[4,128,128]{2,1,0:T(8,128)}, u32[]{:S(2)}) copy-start(f32[4,128,128]{2,1,0:T(8,128)} %add_multiply_fusion.kinetic) | copy-start | bytes 786436
  119.8 51.4 %all-to-all-start.1 = ((f32[32,4,32,128]{3,2,1,0:T(8,128)}), f32[32,4,32,128]{3,2,1,0:T(8,128)S(1)}, u32[]{:S(2)}, u32[]{:S(2)}) async-start(f32[32,4,32,128]{3,2,1,0:T(8,128)} %get-tuple-element.6), calls=%async_computation.1 | async-start | bytes 4194304 | tf_op jit(solution)/shard_map/all_to_all | solution.py:313
  123.0 0.6 copy-start.8
  137.1 2.2 %copy-start.1 = (f32[8,2,4,128,128]{4,3,2,1,0:T(8,128)S(1)}, f32[8,2,4,128,128]{4,3,2,1,0:T(8,128)}, u32[]{:S(2)}) copy-start(f32[8,2,4,128,128]{4,3,2,1,0:T(8,128)} %psi.7) | copy-start | bytes 12582916
  139.3 2.2 %copy-start.2 = (f32[8,8,2,8192]{3,2,1,0:T(2,128)S(1)}, f32[8,8,2,8192]{3,2,1,0:T(2,128)}, u32[]{:S(2)}) copy-start(f32[8,8,2,8192]{3,2,1,0:T(2,128)} %param.15) | copy-start | bytes 12582916
  141.4 8.7 %copy-start.3 = (bf16[256,768]{1,0:T(8,128)(2,1)S(1)}, bf16[256,768]{1,0:T(8,128)(2,1)}, u32[]{:S(2)}) copy-start(bf16[256,768]{1,0:T(8,128)(2,1)} %constant.106.clone.y_table) | copy-start | bytes 1179652

commit v21 on v20

--- a/solution.py
+++ b/solution.py
@@ -305,7 +305,8 @@
     ranks = np.arange(devices).reshape(layers, -1).T
     if devices % 32 == 0:
         ranks = ranks.reshape(4, -1, layers)[[0, 1, 3, 2]]
-    ranks = ranks.reshape(-1)
+    ranks = ranks.reshape(-1, layers)
+    ranks = np.stack([np.roll(one, -i) for i, one in enumerate(ranks)]).reshape(-1)
     order = np.arange(2 * span_y)
     order = (order % 2) * span_y + (ranks[:, None] * rows + np.arange(rows)).reshape(-1)[order // 2]
 

time: 176 us -> 181 us (1.028)
  waiting for transfers between devices: 69.9 us -> 77.8 us
  starting transfers between devices: 23.8 us -> 20.5 us
    all_to_all x4, waiting for transfers between devices: 51.7 us -> 57.9 us  [exchange(): lax.all_to_all(values, 'ga', split_axis=0, concat_axis=0, axis_index_grou...]
    ppermute x5, starting transfers between devices: 7.03 us -> 4.44 us  [partner(): return lax.ppermute(values, 'ga', [(d, d ^ k) for d in range(devices)])]
  transfers between devices with their start and end apart: 9 -> 9, of which waited for: 8 -> 8; matrix products, arithmetic and copies ran while one was open for 12% -> 11% of each run, Pallas kernels for 28% -> 27%
where the time goes in v21:
time: 181 us; the launch traced here: 179 us
  waiting for transfers between devices  77.8 us (43%)
  Pallas kernels  54.7 us (30%)
  starting transfers between devices  20.5 us (11%)
  local copies, waits for them, and re-layouts  10.4 us (6%)
  other arithmetic  8.86 us (5%)
  matrix products  6.01 us (3%)
    all_to_all x4, waiting for transfers between devices, exchange(): lax.all_to_all(values, 'ga', split_axis=0, concat_axis=0, axis_index_grou...  57.9 us
    ppermute x5, waiting for transfers between devices, partner(): return lax.ppermute(values, 'ga', [(d, d ^ k) for d in range(devices)])  19.9 us
    all_to_all x4, starting transfers between devices, exchange(): lax.all_to_all(values, 'ga', split_axis=0, concat_axis=0, axis_index_grou...  16.1 us
    pallas_call x2, Pallas kernels, on_device(): pl.pallas_call(functools.partial(real_space_kernel, rows, planes), out_sh...  16.1 us
    pallas_call x1, Pallas kernels, on_device(): pl.pallas_call(functools.partial(project_kernel, slots), out_shape=jax.Sh...  10.1 us
    pallas_call x1, Pallas kernels, on_device(): pl.pallas_call(functools.partial(base_kernel, slots), out_shape=jax.Shape...  8.68 us
    pallas_call x2, Pallas kernels, on_device(): pl.pallas_call(to_planes_kernel, out_shape=jax.ShapeDtypeStruct(orbitals....  7.21 us
    pallas_call x2, Pallas kernels, on_device(): pl.pallas_call(to_rows_kernel, out_shape=jax.ShapeDtypeStruct((devices, s...  5.92 us
  transfers between devices with their start and end apart: 9, of which 8 were waited for; matrix products, arithmetic and copies ran while one was open for 11% of the time, Pallas kernels for 27%

profile of v21, /device:TPU:1, one launch (start us, length us, event | category | flops | bytes accessed | tf_op | source)
XLA Modules:
  0.0 179.4 jit_solution(10613093337963498267)
XLA Ops:
  0.7 2.9 %to_rows.3 = f32[32,2,32,128]{3,2,1,0:T(8,128)} custom-call(f32[8,2,4,128,128]{4,3,2,1,0:T(8,128)} %psi.7, bf16[256,768]{1,0:T(8,128)(2,1)} %constant.105.clone.y_table), custom_call_target="tpu_custom_call" | custom-call | flops 4000000000 | bytes 3000000 | tf_op jit(solution)/shard_map/to_rows/pallas_call | solution.py:332
  3.6 7.2 %all-to-all-start.2 = ((f32[32,2,32,128]{3,2,1,0:T(8,128)}), f32[32,2,32,128]{3,2,1,0:T(8,128)}, u32[]{:S(2)}, u32[]{:S(2)}) async-start(f32[32,2,32,128]{3,2,1,0:T(8,128)} %to_rows.3), calls=%async_computation.2 | async-start | bytes 2097152 | tf_op jit(solution)/shard_map/all_to_all | solution.py:314
  10.9 0.6 gather_fusion
  11.6 0.4 fusion.24
  12.1 0.9 copy.120.inverse
  13.2 0.9 add_multiply_fusion.kinetic
  14.0 3.0 %to_rows.2 = f32[32,2,32,128]{3,2,1,0:T(8,128)} custom-call(f32[8,2,4,128,128]{4,3,2,1,0:T(8,128)} %psi.7, bf16[256,768]{1,0:T(8,128)(2,1)} %constant.105.clone.y_table), custom_call_target="tpu_custom_call" | custom-call | flops 4000000000 | bytes 3000000 | tf_op jit(solution)/shard_map/to_rows/pallas_call | solution.py:332
  17.0 21.5 %all-to-all-done.2.recv = f32[32,2,32,128]{3,2,1,0:T(8,128)} async-done(((f32[32,2,32,128]{3,2,1,0:T(8,128)}), f32[32,2,32,128]{3,2,1,0:T(8,128)}, u32[]{:S(2)}, u32[]{:S(2)}) %all-to-all-start.2) | async-done | bytes 1048608 | tf_op jit(solution)/shard_map/all_to_all | solution.py:314
  38.4 3.1 %all-to-all-start = ((f32[32,2,32,128]{3,2,1,0:T(8,128)}), f32[32,2,32,128]{3,2,1,0:T(8,128)}, u32[]{:S(2)}, u32[]{:S(2)}) async-start(f32[32,2,32,128]{3,2,1,0:T(8,128)} %to_rows.2), calls=%async_computation | async-start | bytes 2097152 | tf_op jit(solution)/shard_map/all_to_all | solution.py:314
  41.6 10.1 %project.1 = f32[8,32,16]{2,1,0:T(8,128)} custom-call(f32[8,2,4,128,128]{4,3,2,1,0:T(8,128)} %psi.7, f32[8,1024,128]{2,1,0:T(8,128)} %bitcast.74, f32[4,128,128]{2,1,0:T(8,128)} %add_multiply_fusion.kinetic), custom_call_target="tpu_custom_call" | custom-call | flops 8000000000 | bytes 8000000 | tf_op jit(solution)/shard_map/project/pallas_call | solution.py:379
  51.7 0.8 fusion.47
  53.0 0.7 copy.111
  53.8 0.7 pad_maximum_fusion.1.forward
  54.5 0.9 convolution_bitcast_fusion._
  55.4 8.0 %real_space.3 = (f32[32,4,32,128]{3,2,1,0:T(8,128)}, f32[4,512,128]{2,1,0:T(8,128)}) custom-call(f32[32,2,32,128]{3,2,1,0:T(8,128)} %all-to-all-done.2.recv, f32[512,128]{1,0:T(8,128)} %bitcast.76, bf16[256,768]{1,0:T(8,128)(2,1)} %copy.120.inverse, bf16[256,384]{1,0:T(8,128)(2,1)} %pad_maximum_fusion.1.forward, bf16[768,256]{1,0:T(8,128)(2,1)} %constant.107.clone.inv_z, ...), custom_call_target="tpu_custom_call" | custom-call | flops 4000000000 | bytes 8000000 | tf_op jit(solution)/shard_map/real_space/pallas_call | solution.py:407
  63.4 5.2 %all-to-all-done.recv = f32[32,2,32,128]{3,2,1,0:T(8,128)} async-done(((f32[32,2,32,128]{3,2,1,0:T(8,128)}), f32[32,2,32,128]{3,2,1,0:T(8,128)}, u32[]{:S(2)}, u32[]{:S(2)}) %all-to-all-start) | async-done | bytes 1048608 | tf_op jit(solution)/shard_map/all_to_all | solution.py:314
  68.6 3.2 %all-to-all-start.3 = ((f32[32,4,32,128]{3,2,1,0:T(8,128)}), f32[32,4,32,128]{3,2,1,0:T(8,128)}, u32[]{:S(2)}, u32[]{:S(2)}) async-start(f32[32,4,32,128]{3,2,1,0:T(8,128)} %get-tuple-element.7), calls=%async_computation.3 | async-start | bytes 4194304 | tf_op jit(solution)/shard_map/all_to_all | solution.py:314
  72.1 8.1 %real_space.2 = (f32[32,4,32,128]{3,2,1,0:T(8,128)}, f32[4,512,128]{2,1,0:T(8,128)}) custom-call(f32[32,2,32,128]{3,2,1,0:T(8,128)} %all-to-all-done.recv, f32[512,128]{1,0:T(8,128)} %bitcast.77, bf16[256,768]{1,0:T(8,128)(2,1)} %copy.120.inverse, bf16[256,384]{1,0:T(8,128)(2,1)} %pad_maximum_fusion.1.forward, bf16[768,256]{1,0:T(8,128)(2,1)} %constant.107.clone.inv_z, ...), custom_call_target="tpu_custom_call" | custom-call | flops 4000000000 | bytes 8000000 | tf_op jit(solution)/shard_map/real_space/pallas_call | solution.py:407
  80.2 5.2 %real_gram.1 = f32[2,8,8,128]{3,2,1,0:T(8,128)} custom-call(f32[4,512,128]{2,1,0:T(8,128)} %get-tuple-element.8.refs_0_, f32[4,512,128]{2,1,0:T(8,128)} %get-tuple-element.9.refs_1_, f32[512,128]{1,0:T(8,128)} %bitcast.78), custom_call_target="tpu_custom_call" | custom-call | flops 10000000 | bytes 2000000 | tf_op jit(solution)/shard_map/real_gram/pallas_call | solution.py:434
  85.4 0.9 reduce_sum.18
  86.5 1.2 collective-permute-done
  87.8 0.7 collective-permute-start.1
  88.5 6.5 %collective-permute-done.1 = f32[136,16]{1,0:T(8,128)S(1)} collective-permute-done((f32[136,16]{1,0:T(8,128)S(1)}, f32[136,16]{1,0:T(8,128)S(1)}, u32[]{:S(2)}, u32[]{:S(2)}) %collective-permute-start.1) | collective-permute-done | bytes 8736 | tf_op jit(solution)/shard_map/ppermute | solution.py:262
  95.0 3.6 %collective-permute-done.2 = f32[136,16]{1,0:T(8,128)S(1)} collective-permute-done((f32[136,16]{1,0:T(8,128)S(1)}, f32[136,16]{1,0:T(8,128)S(1)}, u32[]{:S(2)}, u32[]{:S(2)}) %collective-permute-start.2) | collective-permute-done | bytes 8736 | tf_op jit(solution)/shard_map/ppermute | solution.py:262
  98.7 8.6 %collective-permute-done.3 = f32[136,16]{1,0:T(8,128)S(1)} collective-permute-done((f32[136,16]{1,0:T(8,128)S(1)}, f32[136,16]{1,0:T(8,128)S(1)}, u32[]{:S(2)}, u32[]{:S(2)}) %collective-permute-start.3) | collective-permute-done | bytes 8736 | tf_op jit(solution)/shard_map/ppermute | solution.py:262
  107.3 3.6 %collective-permute-start.4 = (f32[136,16]{1,0:T(8,128)S(1)}, f32[136,16]{1,0:T(8,128)S(1)}, u32[]{:S(2)}, u32[]{:S(2)}) collective-permute-start(f32[136,16]{1,0:T(8,128)S(1)} %add.122.first), channel_id=1, source_target_pairs={{0,16},{1,17},{2,18},{3,19},{4,20},{5,21},{6,22},{7,23},{8,24},{9,... | collective-permute-start | bytes 26120 | tf_op jit(solution)/shard_map/ppermute | solution.py:262
  111.2 12.1 %all-to-all-done.3._.recv = f32[32,4,32,128]{3,2,1,0:T(8,128)} async-done(((f32[32,4,32,128]{3,2,1,0:T(8,128)}), f32[32,4,32,128]{3,2,1,0:T(8,128)}, u32[]{:S(2)}, u32[]{:S(2)}) %all-to-all-start.3) | async-done | bytes 2097184 | tf_op jit(solution)/shard_map/all_to_all | solution.py:314
  123.3 2.6 %all-to-all-start.1 = ((f32[32,4,32,128]{3,2,1,0:T(8,128)}), f32[32,4,32,128]{3,2,1,0:T(8,128)S(1)}, u32[]{:S(2)}, u32[]{:S(2)}) async-start(f32[32,4,32,128]{3,2,1,0:T(8,128)} %get-tuple-element.6), calls=%async_computation.1 | async-start | bytes 4194304 | tf_op jit(solution)/shard_map/all_to_all | solution.py:314
  125.9 0.6 copy-done.8
  126.5 1.5 last_sum.1
  128.1 0.7 slice.121
  128.8 0.9 slice_multiply_fusion
  129.7 1.1 fusion.10
  130.8 1.1 fusion.16
  132.0 0.9 fusion.37
  132.9 0.7 cholesky.16
  133.6 0.6 compare_reduce_fusion
  134.2 0.6 fusion.27
  134.9 0.6 custom-call.10
  135.5 1.1 fusion.12
  136.7 1.1 convolution_subtract_fusion
  139.3 0.6 pad_maximum_fusion.6
  140.0 2.2 %copy-done.1 = f32[8,2,4,128,128]{4,3,2,1,0:T(8,128)S(1)} copy-done((f32[8,2,4,128,128]{4,3,2,1,0:T(8,128)S(1)}, f32[8,2,4,128,128]{4,3,2,1,0:T(8,128)}, u32[]{:S(2)}) %copy-start.1) | copy-done | bytes 4194328
  142.2 2.2 %copy-done.2 = f32[8,8,2,8192]{3,2,1,0:T(2,128)S(1)} copy-done((f32[8,8,2,8192]{3,2,1,0:T(2,128)S(1)}, f32[8,8,2,8192]{3,2,1,0:T(2,128)}, u32[]{:S(2)}) %copy-start.2) | copy-done | bytes 4194328
  144.4 8.7 %base.1 = f32[8,2,4,128,128]{4,3,2,1,0:T(8,128)} custom-call(f32[8,2,4,128,128]{4,3,2,1,0:T(8,128)S(1)} %copy-done.1, f32[8,1024,128]{2,1,0:T(8,128)S(1)} %bitcast.75, f32[4,128,128]{2,1,0:T(8,128)S(1)} %copy-done, f32[8,16,32]{2,1,0:T(8,128)S(1)} %pad_maximum_fusion.4.coefs), custom_call_target="tpu_custom_call" | custom-call | flops 8000000000 | bytes 12000000 | tf_op jit(solution)/shard_map/base/pallas_call | solution.py:471
  153.1 3.7 %to_planes.2.base = f32[8,2,4,128,128]{4,3,2,1,0:T(8,128)} custom-call(f32[32,4,32,128]{3,2,1,0:T(8,128)} %all-to-all-done.3._.recv, f32[8,2,4,128,128]{4,3,2,1,0:T(8,128)} %base.1, bf16[256,768]{1,0:T(8,128)(2,1)S(1)} %copy-done.3), custom_call_target="tpu_custom_call", output_to_operand_aliasing={{}: (1, {})} | custom-call | flops 8000000000 | bytes 12000000 | tf_op jit(solution)/shard_map/to_planes/pallas_call | solution.py:488
  156.8 19.2 %all-to-all-done.1.recv = f32[32,4,32,128]{3,2,1,0:T(8,128)S(1)} async-done(((f32[32,4,32,128]{3,2,1,0:T(8,128)}), f32[32,4,32,128]{3,2,1,0:T(8,128)S(1)}, u32[]{:S(2)}, u32[]{:S(2)}) %all-to-all-start.1) | async-done | bytes 2097184 | tf_op jit(solution)/shard_map/all_to_all | solution.py:314
  176.0 3.5 %to_planes.3 = f32[8,2,4,128,128]{4,3,2,1,0:T(8,128)} custom-call(f32[32,4,32,128]{3,2,1,0:T(8,128)S(1)} %all-to-all-done.1.recv, f32[8,2,4,128,128]{4,3,2,1,0:T(8,128)} %to_planes.2.base, bf16[256,768]{1,0:T(8,128)(2,1)S(1)} %copy-done.3), custom_call_target="tpu_custom_call", output_to_operand_aliasing={{}: (1, {})} | custom-call | flops 8000000000 | bytes 12000000 | tf_op jit(solution)/shard_map/to_planes/pallas_call | solution.py:488
  (78 shorter events, 3.5 us)
Async XLA Ops:
  0.6 10.3 %copy-start.11 = (s32[32]{0:T(128)S(1)}, s32[32]{0:T(128)}, u32[]{:S(2)}) copy-start(s32[32]{0:T(128)} %constant.116) | copy-start | bytes 388
  0.6 10.1 %copy-start.10 = (s32[128]{0:T(128)S(1)}, s32[128]{0:T(128)}, u32[]{:S(2)}) copy-start(s32[128]{0:T(128)} %param.13) | copy-start | bytes 1540
  3.6 34.9 %all-to-all-start.2 = ((f32[32,2,32,128]{3,2,1,0:T(8,128)}), f32[32,2,32,128]{3,2,1,0:T(8,128)}, u32[]{:S(2)}, u32[]{:S(2)}) async-start(f32[32,2,32,128]{3,2,1,0:T(8,128)} %to_rows.3), calls=%async_computation.2 | async-start | bytes 2097152 | tf_op jit(solution)/shard_map/all_to_all | solution.py:314
  38.4 30.2 %all-to-all-start = ((f32[32,2,32,128]{3,2,1,0:T(8,128)}), f32[32,2,32,128]{3,2,1,0:T(8,128)}, u32[]{:S(2)}, u32[]{:S(2)}) async-start(f32[32,2,32,128]{3,2,1,0:T(8,128)} %to_rows.2), calls=%async_computation | async-start | bytes 2097152 | tf_op jit(solution)/shard_map/all_to_all | solution.py:314
  41.6 11.4 %copy-start.5 = (f32[128,4,128]{2,1,0:T(4,128)S(1)}, f32[128,4,128]{2,1,0:T(4,128)}, u32[]{:S(2)}) copy-start(f32[128,4,128]{2,1,0:T(4,128)} %param.14) | copy-start | bytes 786436
  41.6 12.9 %copy-start.12 = (s32[8,8]{1,0:T(8,128)S(1)}, s32[8,8]{1,0:T(8,128)}, u32[]{:S(2)}) copy-start(s32[8,8]{1,0:T(8,128)} %param.16) | copy-start | bytes 772
  63.4 8.4 %copy-start.7 = (f32[8,32,16]{2,1,0:T(8,128)S(1)}, f32[8,32,16]{2,1,0:T(8,128)}, u32[]{:S(2)}) copy-start(f32[8,32,16]{2,1,0:T(8,128)} %project.1) | copy-start | bytes 49156
  68.6 54.7 %all-to-all-start.3 = ((f32[32,4,32,128]{3,2,1,0:T(8,128)}), f32[32,4,32,128]{3,2,1,0:T(8,128)}, u32[]{:S(2)}, u32[]{:S(2)}) async-start(f32[32,4,32,128]{3,2,1,0:T(8,128)} %get-tuple-element.7), calls=%async_computation.3 | async-start | bytes 4194304 | tf_op jit(solution)/shard_map/all_to_all | solution.py:314
  72.1 14.3 %copy-start.6 = (f32[128,16]{1,0:T(8,128)S(1)}, f32[128,16]{1,0:T(8,128)}, u32[]{:S(2)}) copy-start(f32[128,16]{1,0:T(8,128)} %convolution_bitcast_fusion._) | copy-start | bytes 24580
  72.1 38.8 %copy-start.9 = (f32[32,4]{0,1:T(4,128)S(1)}, f32[32,4]{0,1:T(4,128)}, u32[]{:S(2)}) copy-start(f32[32,4]{0,1:T(4,128)} %param.17) | copy-start | bytes 1540
  86.5 1.3 collective-permute-start
  87.8 7.1 %collective-permute-start.1 = (f32[136,16]{1,0:T(8,128)S(1)}, f32[136,16]{1,0:T(8,128)S(1)}, u32[]{:S(2)}, u32[]{:S(2)}) collective-permute-start(f32[136,16]{1,0:T(8,128)S(1)} %fusion.51), channel_id=1, source_target_pairs={{0,2},{1,3},{2,0},{3,1},{4,6},{5,7},{6,4},{7,5},{8,10},{9,11},{10,... | collective-permute-start | bytes 26120 | tf_op jit(solution)/shard_map/ppermute | solution.py:262
  95.0 3.7 %collective-permute-start.2 = (f32[136,16]{1,0:T(8,128)S(1)}, f32[136,16]{1,0:T(8,128)S(1)}, u32[]{:S(2)}, u32[]{:S(2)}) collective-permute-start(f32[136,16]{1,0:T(8,128)S(1)} %add.120), channel_id=1, source_target_pairs={{0,4},{1,5},{2,6},{3,7},{4,0},{5,1},{6,2},{7,3},{8,12},{9,13},{10,... | collective-permute-start | bytes 26120 | tf_op jit(solution)/shard_map/ppermute | solution.py:262
  98.6 8.7 %collective-permute-start.3 = (f32[136,16]{1,0:T(8,128)S(1)}, f32[136,16]{1,0:T(8,128)S(1)}, u32[]{:S(2)}, u32[]{:S(2)}) collective-permute-start(f32[136,16]{1,0:T(8,128)S(1)} %add.121), channel_id=1, source_target_pairs={{0,8},{1,9},{2,10},{3,11},{4,12},{5,13},{6,14},{7,15},{8,0},{9,1},... | collective-permute-start | bytes 26120 | tf_op jit(solution)/shard_map/ppermute | solution.py:262
  107.3 18.6 %copy-start.4 = (f32[136,16]{1,0:T(8,128)}, f32[136,16]{1,0:T(8,128)S(1)}, u32[]{:S(2)}) copy-start(f32[136,16]{1,0:T(8,128)S(1)} %add.122.first) | copy-start | bytes 26116
  107.3 18.6 %collective-permute-start.4 = (f32[136,16]{1,0:T(8,128)S(1)}, f32[136,16]{1,0:T(8,128)S(1)}, u32[]{:S(2)}, u32[]{:S(2)}) collective-permute-start(f32[136,16]{1,0:T(8,128)S(1)} %add.122.first), channel_id=1, source_target_pairs={{0,16},{1,17},{2,18},{3,19},{4,20},{5,21},{6,22},{7,23},{8,24},{9,... | collective-permute-start | bytes 26120 | tf_op jit(solution)/shard_map/ppermute | solution.py:262
  123.3 16.7 %copy-start = (f32[4,128,128]{2,1,0:T(8,128)S(1)}, f32[4,128,128]{2,1,0:T(8,128)}, u32[]{:S(2)}) copy-start(f32[4,128,128]{2,1,0:T(8,128)} %add_multiply_fusion.kinetic) | copy-start | bytes 786436
  123.3 52.7 %all-to-all-start.1 = ((f32[32,4,32,128]{3,2,1,0:T(8,128)}), f32[32,4,32,128]{3,2,1,0:T(8,128)S(1)}, u32[]{:S(2)}, u32[]{:S(2)}) async-start(f32[32,4,32,128]{3,2,1,0:T(8,128)} %get-tuple-element.6), calls=%async_computation.1 | async-start | bytes 4194304 | tf_op jit(solution)/shard_map/all_to_all | solution.py:314
  125.9 0.6 copy-start.8
  140.0 2.2 %copy-start.1 = (f32[8,2,4,128,128]{4,3,2,1,0:T(8,128)S(1)}, f32[8,2,4,128,128]{4,3,2,1,0:T(8,128)}, u32[]{:S(2)}) copy-start(f32[8,2,4,128,128]{4,3,2,1,0:T(8,128)} %psi.7) | copy-start | bytes 12582916
  142.2 2.2 %copy-start.2 = (f32[8,8,2,8192]{3,2,1,0:T(2,128)S(1)}, f32[8,8,2,8192]{3,2,1,0:T(2,128)}, u32[]{:S(2)}) copy-start(f32[8,8,2,8192]{3,2,1,0:T(2,128)} %param.15) | copy-start | bytes 12582916
  144.4 8.7 %copy-start.3 = (bf16[256,768]{1,0:T(8,128)(2,1)S(1)}, bf16[256,768]{1,0:T(8,128)(2,1)}, u32[]{:S(2)}) copy-start(bf16[256,768]{1,0:T(8,128)(2,1)} %constant.106.clone.y_table) | copy-start | bytes 1179652

commit v22 on v20

--- a/solution.py
+++ b/solution.py
@@ -304,7 +304,7 @@
     layers = 4 if devices % 4 == 0 else 1
     ranks = np.arange(devices).reshape(layers, -1).T
     if devices % 32 == 0:
-        ranks = ranks.reshape(4, -1, layers)[[0, 1, 3, 2]]
+        ranks = ranks.reshape(4, -1, layers)[[0, 1, 3, 2]].transpose(1, 0, 2)
     ranks = ranks.reshape(-1)
     order = np.arange(2 * span_y)
     order = (order % 2) * span_y + (ranks[:, None] * rows + np.arange(rows)).reshape(-1)[order // 2]

time: 176 us -> 178 us (1.011)
  starting transfers between devices: 23.8 us -> 30.7 us
  waiting for transfers between devices: 69.9 us -> 64 us
    all_to_all x4, starting transfers between devices: 16.8 us -> 20.4 us  [exchange(): lax.all_to_all(values, 'ga', split_axis=0, concat_axis=0, axis_index_grou...]
    ppermute x5, starting transfers between devices: 7.03 us -> 10.3 us  [partner(): return lax.ppermute(values, 'ga', [(d, d ^ k) for d in range(devices)])]
    ppermute x5, waiting for transfers between devices: 18.1 us -> 15 us  [partner(): return lax.ppermute(values, 'ga', [(d, d ^ k) for d in range(devices)])]
    all_to_all x4, waiting for transfers between devices: 51.7 us -> 49 us  [exchange(): lax.all_to_all(values, 'ga', split_axis=0, concat_axis=0, axis_index_grou...]
  transfers between devices with their start and end apart: 9 -> 9, of which waited for: 8 -> 8; matrix products, arithmetic and copies ran while one was open for 12% -> 12% of each run, Pallas kernels for 28% -> 27%
where the time goes in v22:
time: 178 us; the launch traced here: 176 us
  waiting for transfers between devices  64 us (36%)
  Pallas kernels  54.7 us (31%)
  starting transfers between devices  30.7 us (17%)
  local copies, waits for them, and re-layouts  10.4 us (6%)
  other arithmetic  8.86 us (5%)
  matrix products  6.01 us (3%)
    all_to_all x4, waiting for transfers between devices, exchange(): lax.all_to_all(values, 'ga', split_axis=0, concat_axis=0, axis_index_grou...  49 us
    all_to_all x4, starting transfers between devices, exchange(): lax.all_to_all(values, 'ga', split_axis=0, concat_axis=0, axis_index_grou...  20.4 us
    pallas_call x2, Pallas kernels, on_device(): pl.pallas_call(functools.partial(real_space_kernel, rows, planes), out_sh...  16.1 us
    ppermute x5, waiting for transfers between devices, partner(): return lax.ppermute(values, 'ga', [(d, d ^ k) for d in range(devices)])  15 us
    ppermute x5, starting transfers between devices, partner(): return lax.ppermute(values, 'ga', [(d, d ^ k) for d in range(devices)])  10.3 us
    pallas_call x1, Pallas kernels, on_device(): pl.pallas_call(functools.partial(project_kernel, slots), out_shape=jax.Sh...  10.1 us
    pallas_call x1, Pallas kernels, on_device(): pl.pallas_call(functools.partial(base_kernel, slots), out_shape=jax.Shape...  8.68 us
    pallas_call x2, Pallas kernels, on_device(): pl.pallas_call(to_planes_kernel, out_shape=jax.ShapeDtypeStruct(orbitals....  7.21 us
  transfers between devices with their start and end apart: 9, of which 8 were waited for; matrix products, arithmetic and copies ran while one was open for 12% of the time, Pallas kernels for 27%

profile of v22, /device:TPU:1, one launch (start us, length us, event | category | flops | bytes accessed | tf_op | source)
XLA Modules:
  0.0 175.7 jit_solution(16298827144480867581)
XLA Ops:
  0.7 2.9 %to_rows.3 = f32[32,2,32,128]{3,2,1,0:T(8,128)} custom-call(f32[8,2,4,128,128]{4,3,2,1,0:T(8,128)} %psi.7, bf16[256,768]{1,0:T(8,128)(2,1)} %constant.105.clone.y_table), custom_call_target="tpu_custom_call" | custom-call | flops 4000000000 | bytes 3000000 | tf_op jit(solution)/shard_map/to_rows/pallas_call | solution.py:331
  3.6 7.2 %all-to-all-start.2 = ((f32[32,2,32,128]{3,2,1,0:T(8,128)}), f32[32,2,32,128]{3,2,1,0:T(8,128)}, u32[]{:S(2)}, u32[]{:S(2)}) async-start(f32[32,2,32,128]{3,2,1,0:T(8,128)} %to_rows.3), calls=%async_computation.2 | async-start | bytes 2097152 | tf_op jit(solution)/shard_map/all_to_all | solution.py:313
  12.1 0.9 copy.120.inverse
  13.2 0.9 add_multiply_fusion.kinetic
  14.0 3.0 %to_rows.2 = f32[32,2,32,128]{3,2,1,0:T(8,128)} custom-call(f32[8,2,4,128,128]{4,3,2,1,0:T(8,128)} %psi.7, bf16[256,768]{1,0:T(8,128)(2,1)} %constant.105.clone.y_table), custom_call_target="tpu_custom_call" | custom-call | flops 4000000000 | bytes 3000000 | tf_op jit(solution)/shard_map/to_rows/pallas_call | solution.py:331
  17.0 19.3 %all-to-all-done.2.recv = f32[32,2,32,128]{3,2,1,0:T(8,128)} async-done(((f32[32,2,32,128]{3,2,1,0:T(8,128)}), f32[32,2,32,128]{3,2,1,0:T(8,128)}, u32[]{:S(2)}, u32[]{:S(2)}) %all-to-all-start.2) | async-done | bytes 1048608 | tf_op jit(solution)/shard_map/all_to_all | solution.py:313
  36.3 4.4 %all-to-all-start = ((f32[32,2,32,128]{3,2,1,0:T(8,128)}), f32[32,2,32,128]{3,2,1,0:T(8,128)}, u32[]{:S(2)}, u32[]{:S(2)}) async-start(f32[32,2,32,128]{3,2,1,0:T(8,128)} %to_rows.2), calls=%async_computation | async-start | bytes 2097152 | tf_op jit(solution)/shard_map/all_to_all | solution.py:313
  40.8 10.1 %project.1 = f32[8,32,16]{2,1,0:T(8,128)} custom-call(f32[8,2,4,128,128]{4,3,2,1,0:T(8,128)} %psi.7, f32[8,1024,128]{2,1,0:T(8,128)} %bitcast.74, f32[4,128,128]{2,1,0:T(8,128)} %add_multiply_fusion.kinetic), custom_call_target="tpu_custom_call" | custom-call | flops 8000000000 | bytes 8000000 | tf_op jit(solution)/shard_map/project/pallas_call | solution.py:378
  50.9 0.8 fusion.47
  52.2 0.7 copy.111
  53.0 0.7 pad_maximum_fusion.1.forward
  53.7 0.9 convolution_bitcast_fusion._
  54.6 8.0 %real_space.3 = (f32[32,4,32,128]{3,2,1,0:T(8,128)}, f32[4,512,128]{2,1,0:T(8,128)}) custom-call(f32[32,2,32,128]{3,2,1,0:T(8,128)} %all-to-all-done.2.recv, f32[512,128]{1,0:T(8,128)} %bitcast.76, bf16[256,768]{1,0:T(8,128)(2,1)} %copy.120.inverse, bf16[256,384]{1,0:T(8,128)(2,1)} %pad_maximum_fusion.1.forward, bf16[768,256]{1,0:T(8,128)(2,1)} %constant.107.clone.inv_z, ...), custom_call_target="tpu_custom_call" | custom-call | flops 4000000000 | bytes 8000000 | tf_op jit(solution)/shard_map/real_space/pallas_call | solution.py:406
  62.6 3.9 %all-to-all-done.recv = f32[32,2,32,128]{3,2,1,0:T(8,128)} async-done(((f32[32,2,32,128]{3,2,1,0:T(8,128)}), f32[32,2,32,128]{3,2,1,0:T(8,128)}, u32[]{:S(2)}, u32[]{:S(2)}) %all-to-all-start) | async-done | bytes 1048608 | tf_op jit(solution)/shard_map/all_to_all | solution.py:313
  66.5 4.5 %all-to-all-start.3 = ((f32[32,4,32,128]{3,2,1,0:T(8,128)}), f32[32,4,32,128]{3,2,1,0:T(8,128)}, u32[]{:S(2)}, u32[]{:S(2)}) async-start(f32[32,4,32,128]{3,2,1,0:T(8,128)} %get-tuple-element.7), calls=%async_computation.3 | async-start | bytes 4194304 | tf_op jit(solution)/shard_map/all_to_all | solution.py:313
  71.3 8.1 %real_space.2 = (f32[32,4,32,128]{3,2,1,0:T(8,128)}, f32[4,512,128]{2,1,0:T(8,128)}) custom-call(f32[32,2,32,128]{3,2,1,0:T(8,128)} %all-to-all-done.recv, f32[512,128]{1,0:T(8,128)} %bitcast.77, bf16[256,768]{1,0:T(8,128)(2,1)} %copy.120.inverse, bf16[256,384]{1,0:T(8,128)(2,1)} %pad_maximum_fusion.1.forward, bf16[768,256]{1,0:T(8,128)(2,1)} %constant.107.clone.inv_z, ...), custom_call_target="tpu_custom_call" | custom-call | flops 4000000000 | bytes 8000000 | tf_op jit(solution)/shard_map/real_space/pallas_call | solution.py:406
  79.4 5.2 %real_gram.1 = f32[2,8,8,128]{3,2,1,0:T(8,128)} custom-call(f32[4,512,128]{2,1,0:T(8,128)} %get-tuple-element.8.refs_0_, f32[4,512,128]{2,1,0:T(8,128)} %get-tuple-element.9.refs_1_, f32[512,128]{1,0:T(8,128)} %bitcast.78), custom_call_target="tpu_custom_call" | custom-call | flops 10000000 | bytes 2000000 | tf_op jit(solution)/shard_map/real_gram/pallas_call | solution.py:433
  84.6 0.9 reduce_sum.18
  86.1 0.9 collective-permute-done
  87.1 1.3 collective-permute-start.1
  88.4 2.4 %collective-permute-done.1 = f32[136,16]{1,0:T(8,128)S(1)} collective-permute-done((f32[136,16]{1,0:T(8,128)S(1)}, f32[136,16]{1,0:T(8,128)S(1)}, u32[]{:S(2)}, u32[]{:S(2)}) %collective-permute-start.1) | collective-permute-done | bytes 8736 | tf_op jit(solution)/shard_map/ppermute | solution.py:262
  90.8 3.2 %collective-permute-start.2 = (f32[136,16]{1,0:T(8,128)S(1)}, f32[136,16]{1,0:T(8,128)S(1)}, u32[]{:S(2)}, u32[]{:S(2)}) collective-permute-start(f32[136,16]{1,0:T(8,128)S(1)} %add.120), channel_id=1, source_target_pairs={{0,4},{1,5},{2,6},{3,7},{4,0},{5,1},{6,2},{7,3},{8,12},{9,13},{10,... | collective-permute-start | bytes 26120 | tf_op jit(solution)/shard_map/ppermute | solution.py:262
  94.0 3.3 %collective-permute-done.2 = f32[136,16]{1,0:T(8,128)S(1)} collective-permute-done((f32[136,16]{1,0:T(8,128)S(1)}, f32[136,16]{1,0:T(8,128)S(1)}, u32[]{:S(2)}, u32[]{:S(2)}) %collective-permute-start.2) | collective-permute-done | bytes 8736 | tf_op jit(solution)/shard_map/ppermute | solution.py:262
  97.3 0.8 collective-permute-start.3
  98.1 8.4 %collective-permute-done.3 = f32[136,16]{1,0:T(8,128)S(1)} collective-permute-done((f32[136,16]{1,0:T(8,128)S(1)}, f32[136,16]{1,0:T(8,128)S(1)}, u32[]{:S(2)}, u32[]{:S(2)}) %collective-permute-start.3) | collective-permute-done | bytes 8736 | tf_op jit(solution)/shard_map/ppermute | solution.py:262
  106.6 4.5 %collective-permute-start.4 = (f32[136,16]{1,0:T(8,128)S(1)}, f32[136,16]{1,0:T(8,128)S(1)}, u32[]{:S(2)}, u32[]{:S(2)}) collective-permute-start(f32[136,16]{1,0:T(8,128)S(1)} %add.122.first), channel_id=1, source_target_pairs={{0,16},{1,17},{2,18},{3,19},{4,20},{5,21},{6,22},{7,23},{8,24},{9,... | collective-permute-start | bytes 26120 | tf_op jit(solution)/shard_map/ppermute | solution.py:262
  111.3 9.1 %all-to-all-done.3._.recv = f32[32,4,32,128]{3,2,1,0:T(8,128)} async-done(((f32[32,4,32,128]{3,2,1,0:T(8,128)}), f32[32,4,32,128]{3,2,1,0:T(8,128)}, u32[]{:S(2)}, u32[]{:S(2)}) %all-to-all-start.3) | async-done | bytes 2097184 | tf_op jit(solution)/shard_map/all_to_all | solution.py:313
  120.3 4.3 %all-to-all-start.1 = ((f32[32,4,32,128]{3,2,1,0:T(8,128)}), f32[32,4,32,128]{3,2,1,0:T(8,128)S(1)}, u32[]{:S(2)}, u32[]{:S(2)}) async-start(f32[32,4,32,128]{3,2,1,0:T(8,128)} %get-tuple-element.6), calls=%async_computation.1 | async-start | bytes 4194304 | tf_op jit(solution)/shard_map/all_to_all | solution.py:313
  124.7 0.6 copy-done.8
  125.3 1.5 last_sum.1
  126.9 0.7 slice.121
  127.5 0.9 slice_multiply_fusion
  128.5 1.1 fusion.10
  129.6 1.1 fusion.16
  130.7 0.9 fusion.37
  131.6 0.7 cholesky.16
  132.4 0.6 compare_reduce_fusion
  133.0 0.6 fusion.27
  133.7 0.6 custom-call.10
  134.3 1.1 fusion.12
  135.4 1.1 convolution_subtract_fusion
  138.0 0.6 pad_maximum_fusion.6
  138.8 2.2 %copy-done.1 = f32[8,2,4,128,128]{4,3,2,1,0:T(8,128)S(1)} copy-done((f32[8,2,4,128,128]{4,3,2,1,0:T(8,128)S(1)}, f32[8,2,4,128,128]{4,3,2,1,0:T(8,128)}, u32[]{:S(2)}) %copy-start.1) | copy-done | bytes 4194328
  140.9 2.2 %copy-done.2 = f32[8,8,2,8192]{3,2,1,0:T(2,128)S(1)} copy-done((f32[8,8,2,8192]{3,2,1,0:T(2,128)S(1)}, f32[8,8,2,8192]{3,2,1,0:T(2,128)}, u32[]{:S(2)}) %copy-start.2) | copy-done | bytes 4194328
  143.1 8.7 %base.1 = f32[8,2,4,128,128]{4,3,2,1,0:T(8,128)} custom-call(f32[8,2,4,128,128]{4,3,2,1,0:T(8,128)S(1)} %copy-done.1, f32[8,1024,128]{2,1,0:T(8,128)S(1)} %bitcast.75, f32[4,128,128]{2,1,0:T(8,128)S(1)} %copy-done, f32[8,16,32]{2,1,0:T(8,128)S(1)} %pad_maximum_fusion.4.coefs), custom_call_target="tpu_custom_call" | custom-call | flops 8000000000 | bytes 12000000 | tf_op jit(solution)/shard_map/base/pallas_call | solution.py:470
  151.8 3.7 %to_planes.2.base = f32[8,2,4,128,128]{4,3,2,1,0:T(8,128)} custom-call(f32[32,4,32,128]{3,2,1,0:T(8,128)} %all-to-all-done.3._.recv, f32[8,2,4,128,128]{4,3,2,1,0:T(8,128)} %base.1, bf16[256,768]{1,0:T(8,128)(2,1)S(1)} %copy-done.3), custom_call_target="tpu_custom_call", output_to_operand_aliasing={{}: (1, {})} | custom-call | flops 8000000000 | bytes 12000000 | tf_op jit(solution)/shard_map/to_planes/pallas_call | solution.py:487
  155.6 16.7 %all-to-all-done.1.recv = f32[32,4,32,128]{3,2,1,0:T(8,128)S(1)} async-done(((f32[32,4,32,128]{3,2,1,0:T(8,128)}), f32[32,4,32,128]{3,2,1,0:T(8,128)S(1)}, u32[]{:S(2)}, u32[]{:S(2)}) %all-to-all-start.1) | async-done | bytes 2097184 | tf_op jit(solution)/shard_map/all_to_all | solution.py:313
  172.3 3.5 %to_planes.3 = f32[8,2,4,128,128]{4,3,2,1,0:T(8,128)} custom-call(f32[32,4,32,128]{3,2,1,0:T(8,128)S(1)} %all-to-all-done.1.recv, f32[8,2,4,128,128]{4,3,2,1,0:T(8,128)} %to_planes.2.base, bf16[256,768]{1,0:T(8,128)(2,1)S(1)} %copy-done.3), custom_call_target="tpu_custom_call", output_to_operand_aliasing={{}: (1, {})} | custom-call | flops 8000000000 | bytes 12000000 | tf_op jit(solution)/shard_map/to_planes/pallas_call | solution.py:487
  (78 shorter events, 4.8 us)
Async XLA Ops:
  0.6 10.3 %copy-start.11 = (s32[32]{0:T(128)S(1)}, s32[32]{0:T(128)}, u32[]{:S(2)}) copy-start(s32[32]{0:T(128)} %constant.116) | copy-start | bytes 388
  0.6 10.1 %copy-start.10 = (s32[128]{0:T(128)S(1)}, s32[128]{0:T(128)}, u32[]{:S(2)}) copy-start(s32[128]{0:T(128)} %param.13) | copy-start | bytes 1540
  3.6 32.7 %all-to-all-start.2 = ((f32[32,2,32,128]{3,2,1,0:T(8,128)}), f32[32,2,32,128]{3,2,1,0:T(8,128)}, u32[]{:S(2)}, u32[]{:S(2)}) async-start(f32[32,2,32,128]{3,2,1,0:T(8,128)} %to_rows.3), calls=%async_computation.2 | async-start | bytes 2097152 | tf_op jit(solution)/shard_map/all_to_all | solution.py:313
  36.3 30.1 %all-to-all-start = ((f32[32,2,32,128]{3,2,1,0:T(8,128)}), f32[32,2,32,128]{3,2,1,0:T(8,128)}, u32[]{:S(2)}, u32[]{:S(2)}) async-start(f32[32,2,32,128]{3,2,1,0:T(8,128)} %to_rows.2), calls=%async_computation | async-start | bytes 2097152 | tf_op jit(solution)/shard_map/all_to_all | solution.py:313
  40.8 11.4 %copy-start.5 = (f32[128,4,128]{2,1,0:T(4,128)S(1)}, f32[128,4,128]{2,1,0:T(4,128)}, u32[]{:S(2)}) copy-start(f32[128,4,128]{2,1,0:T(4,128)} %param.14) | copy-start | bytes 786436
  40.8 12.9 %copy-start.12 = (s32[8,8]{1,0:T(8,128)S(1)}, s32[8,8]{1,0:T(8,128)}, u32[]{:S(2)}) copy-start(s32[8,8]{1,0:T(8,128)} %param.16) | copy-start | bytes 772
  62.6 8.4 %copy-start.7 = (f32[8,32,16]{2,1,0:T(8,128)S(1)}, f32[8,32,16]{2,1,0:T(8,128)}, u32[]{:S(2)}) copy-start(f32[8,32,16]{2,1,0:T(8,128)} %project.1) | copy-start | bytes 49156
  66.5 53.8 %all-to-all-start.3 = ((f32[32,4,32,128]{3,2,1,0:T(8,128)}), f32[32,4,32,128]{3,2,1,0:T(8,128)}, u32[]{:S(2)}, u32[]{:S(2)}) async-start(f32[32,4,32,128]{3,2,1,0:T(8,128)} %get-tuple-element.7), calls=%async_computation.3 | async-start | bytes 4194304 | tf_op jit(solution)/shard_map/all_to_all | solution.py:313
  71.3 14.3 %copy-start.6 = (f32[128,16]{1,0:T(8,128)S(1)}, f32[128,16]{1,0:T(8,128)}, u32[]{:S(2)}) copy-start(f32[128,16]{1,0:T(8,128)} %convolution_bitcast_fusion._) | copy-start | bytes 24580
  71.3 39.8 %copy-start.9 = (f32[32,4]{0,1:T(4,128)S(1)}, f32[32,4]{0,1:T(4,128)}, u32[]{:S(2)}) copy-start(f32[32,4]{0,1:T(4,128)} %param.17) | copy-start | bytes 1540
  85.6 1.4 collective-permute-start
  87.1 3.7 %collective-permute-start.1 = (f32[136,16]{1,0:T(8,128)S(1)}, f32[136,16]{1,0:T(8,128)S(1)}, u32[]{:S(2)}, u32[]{:S(2)}) collective-permute-start(f32[136,16]{1,0:T(8,128)S(1)} %fusion.51), channel_id=1, source_target_pairs={{0,2},{1,3},{2,0},{3,1},{4,6},{5,7},{6,4},{7,5},{8,10},{9,11},{10,... | collective-permute-start | bytes 26120 | tf_op jit(solution)/shard_map/ppermute | solution.py:262
  90.8 6.5 %collective-permute-start.2 = (f32[136,16]{1,0:T(8,128)S(1)}, f32[136,16]{1,0:T(8,128)S(1)}, u32[]{:S(2)}, u32[]{:S(2)}) collective-permute-start(f32[136,16]{1,0:T(8,128)S(1)} %add.120), channel_id=1, source_target_pairs={{0,4},{1,5},{2,6},{3,7},{4,0},{5,1},{6,2},{7,3},{8,12},{9,13},{10,... | collective-permute-start | bytes 26120 | tf_op jit(solution)/shard_map/ppermute | solution.py:262
  97.3 9.3 %collective-permute-start.3 = (f32[136,16]{1,0:T(8,128)S(1)}, f32[136,16]{1,0:T(8,128)S(1)}, u32[]{:S(2)}, u32[]{:S(2)}) collective-permute-start(f32[136,16]{1,0:T(8,128)S(1)} %add.121), channel_id=1, source_target_pairs={{0,8},{1,9},{2,10},{3,11},{4,12},{5,13},{6,14},{7,15},{8,0},{9,1},... | collective-permute-start | bytes 26120 | tf_op jit(solution)/shard_map/ppermute | solution.py:262
  106.6 18.1 %copy-start.4 = (f32[136,16]{1,0:T(8,128)}, f32[136,16]{1,0:T(8,128)S(1)}, u32[]{:S(2)}) copy-start(f32[136,16]{1,0:T(8,128)S(1)} %add.122.first) | copy-start | bytes 26116
  106.6 18.1 %collective-permute-start.4 = (f32[136,16]{1,0:T(8,128)S(1)}, f32[136,16]{1,0:T(8,128)S(1)}, u32[]{:S(2)}, u32[]{:S(2)}) collective-permute-start(f32[136,16]{1,0:T(8,128)S(1)} %add.122.first), channel_id=1, source_target_pairs={{0,16},{1,17},{2,18},{3,19},{4,20},{5,21},{6,22},{7,23},{8,24},{9,... | collective-permute-start | bytes 26120 | tf_op jit(solution)/shard_map/ppermute | solution.py:262
  120.3 18.4 %copy-start = (f32[4,128,128]{2,1,0:T(8,128)S(1)}, f32[4,128,128]{2,1,0:T(8,128)}, u32[]{:S(2)}) copy-start(f32[4,128,128]{2,1,0:T(8,128)} %add_multiply_fusion.kinetic) | copy-start | bytes 786436
  120.3 51.9 %all-to-all-start.1 = ((f32[32,4,32,128]{3,2,1,0:T(8,128)}), f32[32,4,32,128]{3,2,1,0:T(8,128)S(1)}, u32[]{:S(2)}, u32[]{:S(2)}) async-start(f32[32,4,32,128]{3,2,1,0:T(8,128)} %get-tuple-element.6), calls=%async_computation.1 | async-start | bytes 4194304 | tf_op jit(solution)/shard_map/all_to_all | solution.py:313
  124.7 0.6 copy-start.8
  138.8 2.2 %copy-start.1 = (f32[8,2,4,128,128]{4,3,2,1,0:T(8,128)S(1)}, f32[8,2,4,128,128]{4,3,2,1,0:T(8,128)}, u32[]{:S(2)}) copy-start(f32[8,2,4,128,128]{4,3,2,1,0:T(8,128)} %psi.7) | copy-start | bytes 12582916
  140.9 2.2 %copy-start.2 = (f32[8,8,2,8192]{3,2,1,0:T(2,128)S(1)}, f32[8,8,2,8192]{3,2,1,0:T(2,128)}, u32[]{:S(2)}) copy-start(f32[8,8,2,8192]{3,2,1,0:T(2,128)} %param.15) | copy-start | bytes 12582916
  143.1 8.7 %copy-start.3 = (bf16[256,768]{1,0:T(8,128)(2,1)S(1)}, bf16[256,768]{1,0:T(8,128)(2,1)}, u32[]{:S(2)}) copy-start(bf16[256,768]{1,0:T(8,128)(2,1)} %constant.106.clone.y_table) | copy-start | bytes 1179652
